TPU v7x, 32 devices: a whole 2x2x4 slice. The times are simulated.
32 devices in a mesh: dp: 4 (over y, core), tensor: 8 (over z, x).
Axes of the slice: x: 2, y: 2, z: 4, core: 2. Of those that a mesh axis runs over, the one named last changes fastest.
Arguments:
- embedded: bfloat16 [2, 8192, 1024], P(None, ('dp', 'tensor')), may hold values from -6 to 6
- token_table: bfloat16 [30, 1024], replicated, may hold values from -6 to 6
- masked_pos: int32 [2, 8, 204], P(None, 'dp'), may hold values from 0 to 1024, as said below
- replace_ids: int32 [2, 8, 204], P(None, 'dp'), may hold values from 0 to 29
- w_query: bfloat16 [1024, 1024], P(None, 'tensor'), may hold values from -0.1875 to 0.1875
- b_query: bfloat16 [1024], P('tensor'), may hold values from -3 to 3
- w_key: bfloat16 [1024, 1024], P(None, 'tensor'), may hold values from -0.25 to 0.25
- w_value: bfloat16 [1024, 1024], P(None, 'tensor'), may hold values from -0.1875 to 0.1875
- b_value: bfloat16 [1024], P('tensor'), may hold values from -3 to 3
- w_out: bfloat16 [1024, 1024], P('tensor'), may hold values from -2 to 2
- b_out: bfloat16 [1024], replicated, may hold values from -3 to 3
- ln1_gain: bfloat16 [1024], replicated, may hold values from 0.5 to 1.5
- ln1_bias: bfloat16 [1024], replicated, may hold values from -2 to 2
- w_up: bfloat16 [1024, 4096], P(None, 'tensor'), may hold values from -0.1875 to 0.1875
- b_up: bfloat16 [4096], P('tensor'), may hold values from -3 to 3
- w_down: bfloat16 [4096, 1024], P('tensor'), may hold values from -0.09375 to 0.09375
- b_down: bfloat16 [1024], replicated, may hold values from -3 to 3
- ln2_gain: bfloat16 [1024], replicated, may hold values from 0.5 to 1.5
- ln2_bias: bfloat16 [1024], replicated, may hold values from -2 to 2
- grad_masked: bfloat16 [2, 8, 204, 1024], P(None, 'dp'), may hold values from -6 to 6
Outputs:
- layer_out: bfloat16 [2, 8192, 1024], P(None, ('dp', 'tensor'))
- grad_embedded: float32 [2, 8192, 1024], P(None, ('dp', 'tensor'))
- grad_token_table: float32 [30, 1024], replicated
- grad_w_query: float32 [1024, 1024], P(None, 'tensor')
- grad_b_query: float32 [1024], P('tensor')
- grad_w_key: float32 [1024, 1024], P(None, 'tensor')
- grad_w_value: float32 [1024, 1024], P(None, 'tensor')
- grad_b_value: float32 [1024], P('tensor')
- grad_w_out: float32 [1024, 1024], P('tensor')
- grad_b_out: float32 [1024], replicated
- grad_ln1_gain: float32 [1024], replicated
- grad_ln1_bias: float32 [1024], replicated
- grad_w_up: float32 [1024, 4096], P(None, 'tensor')
- grad_b_up: float32 [4096], P('tensor')
- grad_w_down: float32 [4096, 1024], P('tensor')
- grad_b_down: float32 [1024], replicated
- grad_ln2_gain: float32 [1024], replicated
- grad_ln2_bias: float32 [1024], replicated
Inputs may be any that keep to these rules, and one draw needn't show every extreme that they name: `masked_pos`: in each row of a micro-batch, the used slots come first and hold distinct positions below 1024; the other slots hold 1024. Between half of 204 and 204 slots of a row are used, and some row uses all 204.
All inputs are finite; a program needn't handle non-finite values.
Results may differ from a plain program's by a relative error of at most 0.018.
The roundings to bfloat16 on the way count: a program that leaves them out, or rounds other values in their place, can miss the bound.
Values may be sent and summed in bfloat16 or wider, within the bound.
No kernel may reach another device: no remote copies, remote signals or barrier semaphores. Data moves between devices by JAX's collectives and lax.ppermute only.
A program may use at most 320 MiB of HBM per device.

v0:
```python
import jax
import jax.numpy as jnp
from jax import lax
from jax.sharding import PartitionSpec as P

HD = 64
LEN = 1024


EPSILON = 1e-12
ROWS_DIMS = (((0,), (0,)), ((), ()))
LAST_DIMS = (((1,), (1,)), ((), ()))


def layer_norm(values, gain_vec, bias_vec):
    row_mean = jnp.mean(values, axis=-1, keepdims=True)
    centred = values - row_mean
    row_var = jnp.mean(centred * centred, axis=-1, keepdims=True)
    return centred * lax.rsqrt(row_var + EPSILON) * gain_vec + bias_vec


def gelu_exact(values):
    return jax.nn.gelu(values, approximate=False)


def product(left_mat, right_mat):
    return jnp.dot(left_mat, right_mat, preferred_element_type=jnp.float32)


def over_rows(left_mat, right_mat):
    return lax.dot_general(left_mat, right_mat, ROWS_DIMS, preferred_element_type=jnp.float32)


def against(left_mat, right_mat):
    return lax.dot_general(left_mat, right_mat, LAST_DIMS, preferred_element_type=jnp.float32)


def shards(
    embedded,
    token_table,
    masked_pos,
    replace_ids,
    w_query,
    b_query,
    w_key,
    w_value,
    b_value,
    w_out,
    b_out,
    ln1_gain,
    ln1_bias,
    w_up,
    b_up,
    w_down,
    b_down,
    ln2_gain,
    ln2_bias,
    grad_masked,
):
    dev_rank = lax.axis_index("tensor")
    tensor_count = lax.axis_size("tensor")
    micro_count, row_count, model_width = embedded.shape
    local_width = w_query.shape[1]
    local_heads = local_width // HD
    group_rows = row_count * tensor_count
    seq_count = group_rows // LEN
    vocab_count = token_table.shape[0]
    att_scale = HD ** (-0.5)
    w_joint = jnp.concatenate([w_query, w_key, w_value], axis=1)
    b_joint = jnp.concatenate(
        [
            b_query.astype(jnp.float32),
            jnp.zeros((local_width,), jnp.float32),
            b_value.astype(jnp.float32),
        ]
    )
    gain_one = ln1_gain.astype(jnp.float32)
    bias_one = ln1_bias.astype(jnp.float32)
    gain_two = ln2_gain.astype(jnp.float32)
    bias_two = ln2_bias.astype(jnp.float32)
    b_out_f = b_out.astype(jnp.float32)
    b_down_f = b_down.astype(jnp.float32)
    row_index = dev_rank * row_count + jnp.arange(row_count, dtype=jnp.int32)
    seq_of_row = row_index // LEN
    pos_of_row = row_index % LEN
    slot_seq = lax.broadcasted_iota(jnp.int32, masked_pos.shape[1:], 0).reshape(-1)
    vocab_iota = jnp.arange(vocab_count, dtype=jnp.int32)
    w_up_all, b_up_all, w_down_all = (w_up, b_up, w_down)
    up_width = w_up_all.shape[1]
    b_up_f = b_up_all.astype(jnp.float32)
    acc_joint = jnp.zeros((model_width, 3 * local_width), jnp.float32)
    acc_bjoint = jnp.zeros((3 * local_width,), jnp.float32)
    acc_out = jnp.zeros((local_width, model_width), jnp.float32)
    acc_up = jnp.zeros((model_width, up_width), jnp.float32)
    acc_bup = jnp.zeros((up_width,), jnp.float32)
    acc_down = jnp.zeros((up_width, model_width), jnp.float32)
    acc_table = jnp.zeros((vocab_count, model_width), jnp.float32)
    acc_bout = jnp.zeros((model_width,), jnp.float32)
    acc_gone = jnp.zeros((model_width,), jnp.float32)
    acc_bone = jnp.zeros((model_width,), jnp.float32)
    acc_bdown = jnp.zeros((model_width,), jnp.float32)
    acc_gtwo = jnp.zeros((model_width,), jnp.float32)
    acc_btwo = jnp.zeros((model_width,), jnp.float32)
    out_list = []
    grad_list = []
    for batch_step in range(micro_count):
        slot_pos = masked_pos[batch_step].reshape(-1)
        slot_ids = replace_ids[batch_step].reshape(-1)
        matches = (seq_of_row[:, None] == slot_seq[None, :]) & (
            pos_of_row[:, None] == slot_pos[None, :]
        )
        replaced = jnp.any(matches, axis=1)
        row_ids = jnp.sum(jnp.where(matches, slot_ids[None, :], 0), axis=1)
        table_hot = ((row_ids[:, None] == vocab_iota[None, :]) & replaced[:, None]).astype(
            jnp.float32
        )
        inserted = product(table_hot.astype(jnp.bfloat16), token_table)
        placed = jnp.where(replaced[:, None], inserted, embedded[batch_step].astype(jnp.float32))
        sent_rows = placed.astype(jnp.bfloat16)
        gathered = lax.all_gather(sent_rows, "tensor", axis=0, tiled=True)
        joint_proj = (product(gathered, w_joint) + b_joint).astype(jnp.bfloat16)
        head_shape = (seq_count, LEN, local_heads, HD)
        query_heads = joint_proj[:, :local_width].reshape(head_shape)
        key_heads = joint_proj[:, local_width : 2 * local_width].reshape(head_shape)
        value_heads = joint_proj[:, 2 * local_width :].reshape(head_shape)
        scores = (
            jnp.einsum(
                "sqhd,skhd->shqk", query_heads, key_heads, preferred_element_type=jnp.float32
            )
            * att_scale
        )
        row_top = jnp.max(scores, axis=-1, keepdims=True)
        exp_scores = jnp.exp(scores - row_top)
        exp_total = jnp.sum(exp_scores, axis=-1, keepdims=True)
        log_total = row_top + jnp.log(exp_total)
        probs_low = (exp_scores / exp_total).astype(jnp.bfloat16)
        mixed_heads = jnp.einsum(
            "shqk,skhd->sqhd", probs_low, value_heads, preferred_element_type=jnp.float32
        )
        heads_out = mixed_heads.astype(jnp.bfloat16).reshape(group_rows, local_width)
        attended = lax.psum_scatter(
            product(heads_out, w_out), "tensor", scatter_dimension=0, tiled=True
        )
        pre_one = placed + attended + b_out_f
        first_norm, ln1_pull = jax.vjp(layer_norm, pre_one, gain_one, bias_one)
        first_sent = first_norm.astype(jnp.bfloat16)
        ffn_rows = lax.all_gather(first_sent, "tensor", axis=0, tiled=True)
        upper_proj = product(ffn_rows, w_up_all) + b_up_f
        hidden, gelu_pull = jax.vjp(gelu_exact, upper_proj)
        hidden_low = hidden.astype(jnp.bfloat16)
        ffn_out = lax.psum_scatter(
            product(hidden_low, w_down_all).astype(jnp.bfloat16),
            "tensor",
            scatter_dimension=0,
            tiled=True,
        ).astype(jnp.float32)
        pre_two = first_norm + ffn_out + b_down_f
        output_norm, ln2_pull = jax.vjp(layer_norm, pre_two, gain_two, bias_two)
        out_list.append(output_norm.astype(jnp.bfloat16))
        cot_rows = product(
            matches.astype(jnp.bfloat16), grad_masked[batch_step].reshape(-1, model_width)
        )
        d_pre_two, d_gain_two, d_bias_two = ln2_pull(cot_rows)
        acc_gtwo = acc_gtwo + d_gain_two
        acc_btwo = acc_btwo + d_bias_two
        acc_bdown = acc_bdown + jnp.sum(d_pre_two, axis=0)
        d_fed = d_pre_two.astype(jnp.bfloat16)
        fed_grad = lax.all_gather(d_fed, "tensor", axis=0, tiled=True)
        acc_down = acc_down + over_rows(hidden_low, fed_grad)
        d_hidden = against(fed_grad, w_down_all)
        d_upper = gelu_pull(d_hidden)[0].astype(jnp.bfloat16)
        acc_up = acc_up + over_rows(ffn_rows, d_upper)
        acc_bup = acc_bup + jnp.sum(d_upper.astype(jnp.float32), axis=0)
        back_ffn = lax.psum_scatter(
            against(d_upper, w_up_all), "tensor", scatter_dimension=0, tiled=True
        )
        d_first = d_pre_two + back_ffn
        d_pre_one, d_gain_one, d_bias_one = ln1_pull(d_first)
        acc_gone = acc_gone + d_gain_one
        acc_bone = acc_bone + d_bias_one
        acc_bout = acc_bout + jnp.sum(d_pre_one, axis=0)
        d_attended = d_pre_one.astype(jnp.bfloat16)
        attn_grad = lax.all_gather(d_attended, "tensor", axis=0, tiled=True)
        acc_out = acc_out + over_rows(heads_out, attn_grad)
        d_heads = against(attn_grad, w_out).astype(jnp.bfloat16).reshape(head_shape)
        scores_again = (
            jnp.einsum(
                "sqhd,skhd->shqk", query_heads, key_heads, preferred_element_type=jnp.float32
            )
            * att_scale
        )
        attn_probs = jnp.exp(scores_again - log_total)
        d_probs = jnp.einsum(
            "sqhd,skhd->shqk", d_heads, value_heads, preferred_element_type=jnp.float32
        )
        d_value = jnp.einsum(
            "shqk,sqhd->skhd",
            attn_probs.astype(jnp.bfloat16),
            d_heads,
            preferred_element_type=jnp.float32,
        ).astype(jnp.bfloat16)
        row_dot = jnp.sum(d_probs * attn_probs, axis=-1, keepdims=True)
        d_scores = (attn_probs * (d_probs - row_dot)).astype(jnp.bfloat16)
        d_query = (
            jnp.einsum("shqk,skhd->sqhd", d_scores, key_heads, preferred_element_type=jnp.float32)
            * att_scale
        ).astype(jnp.bfloat16)
        d_key = (
            jnp.einsum("shqk,sqhd->skhd", d_scores, query_heads, preferred_element_type=jnp.float32)
            * att_scale
        ).astype(jnp.bfloat16)
        d_joint = jnp.concatenate(
            [
                d_query.reshape(group_rows, local_width),
                d_key.reshape(group_rows, local_width),
                d_value.reshape(group_rows, local_width),
            ],
            axis=1,
        )
        acc_joint = acc_joint + over_rows(gathered, d_joint)
        acc_bjoint = acc_bjoint + jnp.sum(d_joint.astype(jnp.float32), axis=0)
        back_attn = lax.psum_scatter(
            against(d_joint, w_joint).astype(jnp.bfloat16),
            "tensor",
            scatter_dimension=0,
            tiled=True,
        ).astype(jnp.float32)
        d_placed = d_pre_one + back_attn
        grad_list.append(jnp.where(replaced[:, None], 0.0, d_placed))
        acc_table = acc_table + lax.dot_general(
            table_hot,
            d_placed,
            ROWS_DIMS,
            precision=lax.Precision.HIGHEST,
            preferred_element_type=jnp.float32,
        )
    summed = (
        lax.psum(acc_joint.astype(jnp.bfloat16), "dp").astype(jnp.float32),
        lax.psum(acc_bjoint.astype(jnp.bfloat16), "dp").astype(jnp.float32),
        lax.psum(acc_out.astype(jnp.bfloat16), "dp").astype(jnp.float32),
        lax.psum(acc_up.astype(jnp.bfloat16), "dp").astype(jnp.float32),
        lax.psum(acc_bup.astype(jnp.bfloat16), "dp").astype(jnp.float32),
        lax.psum(acc_down.astype(jnp.bfloat16), "dp").astype(jnp.float32),
    )
    shared = lax.psum(
        (acc_table, acc_bout, acc_gone, acc_bone, acc_bdown, acc_gtwo, acc_btwo), ("dp", "tensor")
    )
    grad_joint, grad_bjoint, grad_w_out, grad_w_up, grad_b_up, grad_w_down = summed
    grad_table, grad_b_out, grad_gone, grad_bone, grad_b_down, grad_gtwo, grad_btwo = shared
    return (
        jnp.stack(out_list),
        jnp.stack(grad_list),
        grad_table,
        grad_joint[:, :local_width],
        grad_bjoint[:local_width],
        grad_joint[:, local_width : 2 * local_width],
        grad_joint[:, 2 * local_width :],
        grad_bjoint[2 * local_width :],
        grad_w_out,
        grad_b_out,
        grad_gone,
        grad_bone,
        grad_w_up,
        grad_b_up,
        grad_w_down,
        grad_b_down,
        grad_gtwo,
        grad_btwo,
    )


def solution(mesh):
    return jax.shard_map(
        shards,
        mesh=mesh,
        in_specs=(
            P(None, ("dp", "tensor"), None),
            P(),
            P(None, "dp", None),
            P(None, "dp", None),
            P(None, "tensor"),
            P("tensor"),
            P(None, "tensor"),
            P(None, "tensor"),
            P("tensor"),
            P("tensor", None),
            P(),
            P(),
            P(),
            P(None, "tensor"),
            P("tensor"),
            P("tensor", None),
            P(),
            P(),
            P(),
            P(None, "dp", None, None),
        ),
        out_specs=(
            P(None, ("dp", "tensor"), None),
            P(None, ("dp", "tensor"), None),
            P(),
            P(None, "tensor"),
            P("tensor"),
            P(None, "tensor"),
            P(None, "tensor"),
            P("tensor"),
            P("tensor", None),
            P(),
            P(),
            P(),
            P(None, "tensor"),
            P("tensor"),
            P("tensor", None),
            P(),
            P(),
            P(),
        ),
        check_vma=False,
    )
```

profile of v0, /device:TPU:0, one launch (start us, length us, event | category | flops | bytes accessed | tf_op | source)
XLA Modules:
  0.0 1904.7 jit_solution(8807117701652538047)
XLA Ops:
  16.2 73.2 %all-gather.13.cloned.1.call-done = bf16[2048,1024]{1,0:T(8,128)(2,1)} async-done(((bf16[256,1024]{1,0:T(8,128)(2,1)}), bf16[2048,1024]{1,0:T(8,128)(2,1)}) %all-gather.13.cloned.1.call-update) | async-done | bytes 4194320 | tf_op jit(solution)/shard_map/all_gather | solution.py:120
  89.4 4.5 add_convert_fusion.2
  96.5 2.7 reshape.301
  99.9 2.6 reshape.300
  104.4 8.1 multiply_reduce_fusion.2
  112.6 8.6 fusion.1
  121.2 8.2 fusion.45
  130.9 4.5 fusion.107
  135.9 27.8 %all-gather.9.cloned.1.call-done = bf16[2048,1024]{1,0:T(8,128)(2,1)} async-done(((bf16[256,1024]{1,0:T(8,128)(2,1)}), bf16[2048,1024]{1,0:T(8,128)(2,1)}) %all-gather.9.cloned.1.call-update) | async-done | bytes 4194320 | tf_op jit(solution)/shard_map/all_gather | solution.py:120
  163.7 4.5 add_convert_fusion.3
  170.7 2.6 reshape.298
  174.1 2.6 reshape.297
  178.6 8.1 multiply_reduce_fusion.3
  186.8 8.7 fusion
  195.5 7.8 fusion.44
  204.8 4.5 fusion.106
  210.0 104.7 %reduce-scatter.13.cloned.1.call-done = f32[256,1024]{1,0:T(8,128)} async-done(((f32[2048,1024]{1,0:T(8,128)}), f32[256,1024]{1,0:T(8,128)}) %reduce-scatter.13.cloned.1.call-update) | async-done | bytes 1048592 | tf_op jit(solution)/shard_map/reduce_scatter | solution.py:141
  314.7 152.0 %reduce-scatter.9.cloned.1.call-done = f32[256,1024]{1,0:T(8,128)} async-done(((f32[2048,1024]{1,0:T(8,128)}), f32[256,1024]{1,0:T(8,128)}) %reduce-scatter.9.cloned.1.call-update) | async-done | bytes 1048592 | tf_op jit(solution)/shard_map/reduce_scatter | solution.py:141
  471.8 71.9 %all-gather.15.cloned.1.call-done = bf16[2048,1024]{1,0:T(8,128)(2,1)} async-done(((bf16[256,1024]{1,0:T(8,128)(2,1)}), bf16[2048,1024]{1,0:T(8,128)(2,1)}) %all-gather.15.cloned.1.call-update) | async-done | bytes 4194320 | tf_op jit(solution)/shard_map/all_gather | solution.py:147
  543.7 6.5 fusion.108
  550.2 67.7 %all-gather.11.cloned.1.call-done = bf16[2048,1024]{1,0:T(8,128)(2,1)} async-done(((bf16[256,1024]{1,0:T(8,128)(2,1)}), bf16[2048,1024]{1,0:T(8,128)(2,1)}) %all-gather.11.cloned.1.call-update) | async-done | bytes 4194320 | tf_op jit(solution)/shard_map/all_gather | solution.py:147
  617.9 23.5 %multiply_convert_fusion.3 = (bf16[2048,512]{1,0:T(8,128)(2,1)S(1)}, f32[2048,512]{1,0:T(8,128)}, bf16[2048,512]{1,0:T(8,128)(2,1)}, f32[2048,512]{1,0:T(8,128)}, f32[2048,512]{1,0:T(8,128)}) fusion(f32[512]{0:T(512)S(1)} %convert_element_type.260, f32[2048,512]{1,0:T(8,128)} %fusion.108, bf16[2048,1024]{1,0:T(8,128)(2,1)} %all-gather.11.cloned.1.call-done, ...), kind=kOutput, calls=%fused_computation.41 | convolution fusion | flops 2285895680 | bytes 26216448 | tf_op jit(solution)/shard_map/dot_general | solution.py:27
  642.8 4.3 convolution_convert_fusion.3
  647.4 6.2 convolution_convert_fusion.2
  654.3 3.4 fusion.97
  665.7 2.8 fusion.56
  668.5 65.2 %reduce-scatter.11.cloned.1.call-done = bf16[256,1024]{1,0:T(8,128)(2,1)} async-done(((bf16[2048,1024]{1,0:T(8,128)(2,1)}), bf16[256,1024]{1,0:T(8,128)(2,1)}) %reduce-scatter.11.cloned.1.call-update) | async-done | bytes 524304 | tf_op jit(solution)/shard_map/reduce_scatter | solution.py:151
  733.6 91.8 %reduce-scatter.15.cloned.1.call-done = bf16[256,1024]{1,0:T(8,128)(2,1)} async-done(((bf16[2048,1024]{1,0:T(8,128)(2,1)}), bf16[256,1024]{1,0:T(8,128)(2,1)}) %reduce-scatter.15.cloned.1.call-update) | async-done | bytes 524304 | tf_op jit(solution)/shard_map/reduce_scatter | solution.py:151
  836.0 70.6 %all-gather.21.cloned.1.call-done = bf16[2048,1024]{1,0:T(8,128)(2,1)} async-done(((bf16[256,1024]{1,0:T(8,128)(2,1)}), bf16[2048,1024]{1,0:T(8,128)(2,1)}) %all-gather.21.cloned.1.call-update) | async-done | bytes 4194320 | tf_op jit(solution)/shard_map/all_gather | solution.py:168
  906.6 6.8 fusion.110
  913.4 67.4 %all-gather.17.cloned.1.call-done = bf16[2048,1024]{1,0:T(8,128)(2,1)} async-done(((bf16[256,1024]{1,0:T(8,128)(2,1)}), bf16[2048,1024]{1,0:T(8,128)(2,1)}) %all-gather.17.cloned.1.call-update) | async-done | bytes 4194320 | tf_op jit(solution)/shard_map/all_gather | solution.py:168
  980.9 13.6 convert_reduce_fusion.1
  995.8 5.6 fusion.109
  1001.5 7.5 fusion.111
  1009.1 139.8 %reduce-scatter.17.cloned.1.call-done = f32[256,1024]{1,0:T(8,128)} async-done(((f32[2048,1024]{1,0:T(8,128)}), f32[256,1024]{1,0:T(8,128)}) %reduce-scatter.17.cloned.1.call-update) | async-done | bytes 1048592 | tf_op jit(solution)/shard_map/reduce_scatter | solution.py:174
  1148.9 152.0 %reduce-scatter.21.cloned.1.call-done = f32[256,1024]{1,0:T(8,128)} async-done(((f32[2048,1024]{1,0:T(8,128)}), f32[256,1024]{1,0:T(8,128)}) %reduce-scatter.21.cloned.1.call-update) | async-done | bytes 1048592 | tf_op jit(solution)/shard_map/reduce_scatter | solution.py:174
  1300.9 3.1 multiply_reduce_fusion.7
  1307.8 6.6 fusion.115
  1315.4 5.4 fusion.114
  1320.8 3.4 add_convert_fusion.4
  1324.3 3.3 add_convert_fusion.5
  1327.6 52.4 %all-gather.19.cloned.1.call-done = bf16[2048,1024]{1,0:T(8,128)(2,1)} async-done(((bf16[256,1024]{1,0:T(8,128)(2,1)}), bf16[2048,1024]{1,0:T(8,128)(2,1)}) %all-gather.19.cloned.1.call-update) | async-done | bytes 4194320 | tf_op jit(solution)/shard_map/all_gather | solution.py:183
  1380.1 3.4 convolution_convert_fusion.5
  1387.5 11.4 multiply_reduce_fusion.1
  1398.9 15.9 multiply_convert_fusion.1
  1414.8 7.0 fusion.42
  1421.8 5.8 fusion.43
  1427.6 3.9 fusion.37
  1431.5 22.2 %all-gather.23.cloned.1.call-done = bf16[2048,1024]{1,0:T(8,128)(2,1)} async-done(((bf16[256,1024]{1,0:T(8,128)(2,1)}), bf16[2048,1024]{1,0:T(8,128)(2,1)}) %all-gather.23.cloned.1.call-update) | async-done | bytes 4194320 | tf_op jit(solution)/shard_map/all_gather | solution.py:183
  1453.7 3.4 convolution_convert_fusion.4
  1461.0 8.3 fusion.34
  1469.4 12.8 multiply_reduce_fusion
  1482.2 11.3 multiply_convert_fusion
  1493.6 6.2 fusion.40
  1513.7 3.5 add_convert_fusion.6
  1517.3 5.8 convolution_convert_fusion.1
  1523.2 5.8 convolution_convert_fusion
  1533.2 6.6 all-reduce.1
  1540.9 43.9 %all-reduce.8.cloned.1.call-done = (bf16[1024,384]{1,0:T(8,128)(2,1)}, bf16[128,1024]{1,0:T(8,128)(2,1)}, bf16[1024,512]{1,0:T(8,128)(2,1)}, bf16[512,1024]{1,0:T(8,128)(2,1)}) async-done(((bf16[1024,384]{1,0:T(8,128)(2,1)}, bf16[128,1024]{1,0:T(8,128)(2,1)}, bf16[1024,512]{1,0:T(8,128)(2,1)}, bf16[512,1024]{1,0:T(8,128)(2,1)}), (bf16[1024,384]{1,0:T(8,128)(2,1)}, bf16[128,1024]{1,0:T(8,128)(2,1)}, ...) | async-done | bytes 3145744 | tf_op jit(solution)/shard_map/psum | solution.py:238
  1586.7 2.9 convert_element_type.319
  1592.4 83.9 %reduce-scatter.19.cloned.1.call-done = bf16[256,1024]{1,0:T(8,128)(2,1)} async-done(((bf16[2048,1024]{1,0:T(8,128)(2,1)}), bf16[256,1024]{1,0:T(8,128)(2,1)}) %reduce-scatter.19.cloned.1.call-update) | async-done | bytes 524304 | tf_op jit(solution)/shard_map/reduce_scatter | solution.py:222
  1678.0 89.9 %reduce-scatter.23.cloned.1.call-done = bf16[256,1024]{1,0:T(8,128)(2,1)} async-done(((bf16[2048,1024]{1,0:T(8,128)(2,1)}), bf16[256,1024]{1,0:T(8,128)(2,1)}) %reduce-scatter.23.cloned.1.call-update) | async-done | bytes 524304 | tf_op jit(solution)/shard_map/reduce_scatter | solution.py:222
  1774.4 41.0 %all-reduce = (f32[1024]{0:T(1024)}, f32[1024]{0:T(1024)}, f32[1024]{0:T(1024)}, f32[1024]{0:T(1024)}, f32[1024]{0:T(1024)}, /*index=5*/f32[1024]{0:T(1024)}) all-reduce(f32[1024]{0:T(1024)S(1)} %add.312, f32[1024]{0:T(1024)S(1)} %add.313, f32[1024]{0:T(1024)S(1)} %add.314, ...), channel_id=1, replica_groups=mesh['dp'=4,'tensor'=8] {'dp','tensor'}, use_global_device_ids=true, to_apply=%region_42.43 | all-reduce | flops 6144 | bytes 49152 | tf_op jit(solution)/shard_map/psum | solution.py:245
  1815.3 80.8 %all-reduce.6.cloned.1.call-done = f32[30,1024]{1,0:T(8,128)} async-done(((f32[30,1024]{1,0:T(8,128)}), f32[30,1024]{1,0:T(8,128)}) %all-reduce.6.cloned.1.call-update) | async-done | bytes 122896 | tf_op jit(solution)/shard_map/psum | solution.py:245
  (347 shorter events, 96.2 us)
Async XLA Ops:
  7.2 536.5 %copy-start = (bf16[1024,512]{1,0:T(8,128)(2,1)S(1)}, bf16[1024,512]{1,0:T(8,128)(2,1)}, u32[]{:S(2)}) copy-start(bf16[1024,512]{1,0:T(8,128)(2,1)} %param.33) | copy-start | bytes 3145732
  7.2 8.6 copy-start.78
  7.2 8.6 copy-start.79
  7.2 8.7 copy-start.38
  7.2 8.8 copy-start.39
  7.2 8.8 copy-start.40
  7.3 82.1 %all-gather.13.cloned.1.call-start = ((), (), s32[]{:S(2)}) async-start(), calls=%async_computation.12 | async-start | bytes 4718592 | tf_op jit(solution)/shard_map/all_gather | solution.py:120
  7.3 8.5 copy-start.54
  7.3 8.5 copy-start.56
  7.4 8.4 copy-start.48
  8.4 7.5 copy-start.50
  8.4 7.5 copy-start.52
  13.1 150.6 %all-gather.9.cloned.1.call-start = ((), (), s32[]{:S(2)}) async-start(), calls=%async_computation.8 | async-start | bytes 4718592 | tf_op jit(solution)/shard_map/all_gather | solution.py:120
  15.8 299.0 %reduce-scatter.13.cloned.1.call-start = ((), (), s32[]{:S(2)}) async-start(), calls=%async_computation.13 | async-start | bytes 9437184 | tf_op jit(solution)/shard_map/reduce_scatter | solution.py:141
  16.2 77.7 %copy-start.43 = (bf16[1024,384]{1,0:T(8,128)(2,1)}, bf16[1024,384]{1,0:T(8,128)(2,1)S(1)}, u32[]{:S(2)}) copy-start(bf16[1024,384]{1,0:T(8,128)(2,1)S(1)} %constant_dynamic-update-slice_fusion) | copy-start | bytes 2359300
  96.5 16.1 copy-start.10
  99.9 12.6 copy-start.12
  112.6 8.6 copy-start.41
  112.6 8.6 copy-start.25
  121.2 8.2 copy-start.46
  121.2 9.7 copy-start.36
  135.4 28.3 %copy-start.44 = (bf16[1024,384]{1,0:T(8,128)(2,1)S(1)}, bf16[1024,384]{1,0:T(8,128)(2,1)}, u32[]{:S(2)}) copy-start(bf16[1024,384]{1,0:T(8,128)(2,1)} %copy-done.43) | copy-start | bytes 2359300
  135.5 331.2 %reduce-scatter.9.cloned.1.call-start = ((), (), s32[]{:S(2)}) async-start(), calls=%async_computation.9 | async-start | bytes 9437184 | tf_op jit(solution)/shard_map/reduce_scatter | solution.py:141
  170.7 16.1 copy-start.14
  174.1 12.7 copy-start.16
  186.8 8.7 copy-start.27
  209.3 334.4 %all-gather.15.cloned.1.call-start = ((), (), s32[]{:S(2)}) async-start(), calls=%async_computation.14 | async-start | bytes 4718592 | tf_op jit(solution)/shard_map/all_gather | solution.py:147
  471.2 146.8 %all-gather.11.cloned.1.call-start = ((), (), s32[]{:S(2)}) async-start(), calls=%async_computation.10 | async-start | bytes 4718592 | tf_op jit(solution)/shard_map/all_gather | solution.py:147
  471.7 261.9 %reduce-scatter.11.cloned.1.call-start = ((), (), s32[]{:S(2)}) async-start(), calls=%async_computation.11 | async-start | bytes 4718592 | tf_op jit(solution)/shard_map/reduce_scatter | solution.py:151
  617.9 24.9 %copy-start.77 = (bf16[512,1024]{1,0:T(8,128)(2,1)S(1)}, bf16[512,1024]{1,0:T(8,128)(2,1)}, u32[]{:S(2)}) copy-start(bf16[512,1024]{1,0:T(8,128)(2,1)} %param.35) | copy-start | bytes 3145732
  647.2 178.3 %reduce-scatter.15.cloned.1.call-start = ((), (), s32[]{:S(2)}) async-start(), calls=%async_computation.15 | async-start | bytes 4718592 | tf_op jit(solution)/shard_map/reduce_scatter | solution.py:151
  653.6 253.0 %all-gather.21.cloned.1.call-start = ((), (), s32[]{:S(2)}) async-start(), calls=%async_computation.20 | async-start | bytes 4718592 | tf_op jit(solution)/shard_map/all_gather | solution.py:168
  657.8 7.9 copy-start.49
  657.8 7.9 copy-start.51
  657.8 7.9 copy-start.55
  657.8 7.9 copy-start.57
  665.6 162.4 %copy-start.53 = (s32[408]{0:T(512)S(1)}, s32[408]{0:T(512)}, u32[]{:S(2)}) copy-start(s32[408]{0:T(512)} %copy-done.52) | copy-start | bytes 4900
  833.3 147.6 %all-gather.17.cloned.1.call-start = ((), (), s32[]{:S(2)}) async-start(), calls=%async_computation.16 | async-start | bytes 4718592 | tf_op jit(solution)/shard_map/all_gather | solution.py:168
  835.6 313.3 %reduce-scatter.17.cloned.1.call-start = ((), (), s32[]{:S(2)}) async-start(), calls=%async_computation.17 | async-start | bytes 9437184 | tf_op jit(solution)/shard_map/reduce_scatter | solution.py:174
  1001.4 299.5 %reduce-scatter.21.cloned.1.call-start = ((), (), s32[]{:S(2)}) async-start(), calls=%async_computation.21 | async-start | bytes 9437184 | tf_op jit(solution)/shard_map/reduce_scatter | solution.py:174
  1009.0 371.1 %all-gather.19.cloned.1.call-start = ((), (), s32[]{:S(2)}) async-start(), calls=%async_computation.18 | async-start | bytes 4718592 | tf_op jit(solution)/shard_map/all_gather | solution.py:183
  1307.5 146.2 %all-gather.23.cloned.1.call-start = ((), (), s32[]{:S(2)}) async-start(), calls=%async_computation.22 | async-start | bytes 4718592 | tf_op jit(solution)/shard_map/all_gather | solution.py:183
  1315.3 269.5 %all-reduce.8.cloned.1.call-start = ((), (), s32[]{:S(2)}) async-start(), calls=%async_computation.25 | async-start | bytes 6291456 | tf_op jit(solution)/shard_map/psum | solution.py:238
  1327.6 59.9 %copy-start.28 = (bf16[2,1024,2,64]{1,3,2,0:T(8,128)(2,1)S(1)}, bf16[2,1024,2,64]{1,3,2,0:T(8,128)(2,1)}, u32[]{:S(2)}) copy-start(bf16[2,1024,2,64]{1,3,2,0:T(8,128)(2,1)} %copy.109) | copy-start | bytes 1572868
  1398.9 15.9 copy-start.17
  1398.9 28.7 %slice-start.4 = ((s8[16777216]{0:T(1024)(128)(4,1)}), s8[4194304]{0:T(1024)(128)(4,1)S(1)}, s32[]{:S(2)}) async-start(s8[16777216]{0:T(1024)(128)(4,1)} %bitcast.144), calls=%async_computation.30 | async-start | bytes 8388608
  1398.9 28.7 %slice-start.5 = ((s8[16777216]{0:T(1024)(128)(4,1)}), s8[4194304]{0:T(1024)(128)(4,1)S(1)}, s32[]{:S(2)}) async-start(s8[16777216]{0:T(1024)(128)(4,1)} %bitcast.144), calls=%async_computation.31 | async-start | bytes 8388608
  1398.9 28.7 %slice-start.6 = ((s8[16777216]{0:T(1024)(128)(4,1)}), s8[4194304]{0:T(1024)(128)(4,1)S(1)}, s32[]{:S(2)}) async-start(s8[16777216]{0:T(1024)(128)(4,1)} %bitcast.144), calls=%async_computation.32 | async-start | bytes 8388608
  1414.8 7.0 copy-start.15
  1414.8 12.8 slice-start.7
  1461.0 8.4 copy-start.26
  1461.0 21.2 %slice-start = ((s8[16777216]{0:T(1024)(128)(4,1)}), s8[4194304]{0:T(1024)(128)(4,1)S(1)}, s32[]{:S(2)}) async-start(s8[16777216]{0:T(1024)(128)(4,1)} %bitcast.142), calls=%async_computation.26 | async-start | bytes 8388608
  1461.0 21.2 %slice-start.1 = ((s8[16777216]{0:T(1024)(128)(4,1)}), s8[4194304]{0:T(1024)(128)(4,1)S(1)}, s32[]{:S(2)}) async-start(s8[16777216]{0:T(1024)(128)(4,1)} %bitcast.142), calls=%async_computation.27 | async-start | bytes 8388608
  1469.4 12.8 slice-start.2
  1469.4 12.9 slice-start.3
  1482.2 11.3 copy-start.13
  1517.2 159.0 %reduce-scatter.19.cloned.1.call-start = ((), (), s32[]{:S(2)}) async-start(), calls=%async_computation.19 | async-start | bytes 4718592 | tf_op jit(solution)/shard_map/reduce_scatter | solution.py:222
  1523.1 244.8 %reduce-scatter.23.cloned.1.call-start = ((), (), s32[]{:S(2)}) async-start(), calls=%async_computation.23 | async-start | bytes 4718592 | tf_op jit(solution)/shard_map/reduce_scatter | solution.py:222
  1529.0 367.1 %all-reduce.6.cloned.1.call-start = ((), (), s32[]{:S(2)}) async-start(), calls=%async_computation.24 | async-start | bytes 262144 | tf_op jit(solution)/shard_map/psum | solution.py:245
  1586.7 89.6 %copy-start.4 = (f32[256,1024]{1,0:T(8,128)S(1)}, f32[256,1024]{1,0:T(8,128)}, u32[]{:S(2)}) copy-start(f32[256,1024]{1,0:T(8,128)} %copy-done.3) | copy-start | bytes 3145732
  1586.7 89.6 %copy-start.61 = (s32[256]{0:T(256)S(1)}, s32[256]{0:T(256)}, u32[]{:S(2)}) copy-start(s32[256]{0:T(256)} %copy-done.60) | copy-start | bytes 3076
  1586.7 89.6 %copy-start.63 = (pred[256]{0:T(512)(128)(4,1)S(1)}, pred[256]{0:T(512)(128)(4,1)}, u32[]{:S(2)}) copy-start(pred[256]{0:T(512)(128)(4,1)} %copy-done.62) | copy-start | bytes 772
  1589.6 178.3 %copy-start.59 = (s32[256]{0:T(256)S(1)}, s32[256]{0:T(256)}, u32[]{:S(2)}) copy-start(s32[256]{0:T(256)} %copy-done.58) | copy-start | bytes 3076
  1589.7 178.3 %copy-start.65 = (pred[256]{0:T(512)(128)(4,1)S(1)}, pred[256]{0:T(512)(128)(4,1)}, u32[]{:S(2)}) copy-start(pred[256]{0:T(512)(128)(4,1)} %copy-done.64) | copy-start | bytes 772
  (46 other events, 139.3 us)
Sparse Core Ops, SparseCore 0:
  13.2 76.0 all-gather.12
  92.0 71.6 all-gather.8
  167.4 147.2 reduce-scatter.12
  318.6 148.0 reduce-scatter.8
  471.3 72.3 all-gather.14
  546.2 71.6 all-gather.10
  647.3 86.3 reduce-scatter.10
  737.7 87.6 reduce-scatter.14
  833.4 73.1 all-gather.20
  909.2 71.6 all-gather.16
  1001.6 147.2 reduce-scatter.16
  1152.8 148.0 reduce-scatter.20
  1307.6 72.3 all-gather.18
  1382.0 71.6 all-gather.22
  1517.4 67.3 all-reduce.7
  1588.3 87.9 reduce-scatter.18
  1680.2 87.6 reduce-scatter.22
  1773.9 122.1 all-reduce.5
where the time goes:
time: 1910 us; the launch traced here: 1900 us
  waiting for transfers between devices  1460 us (76%)
  matrix products  240 us (13%)
  other arithmetic  78 us (4%)
  local copies, waits for them, and re-layouts  63.3 us (3%)
  blocking collectives  47.5 us (2%)
    reduce_scatter x2, waiting for transfers between devices, shards(): lax.psum_scatter(against(d_upper, w_up_all), 'tensor', scatter_dimension=...  292 us
    reduce_scatter x2, waiting for transfers between devices, shards(): lax.psum_scatter(product(heads_out, w_out), 'tensor', scatter_dimension=0...  257 us
    reduce_scatter x2, waiting for transfers between devices, shards(): lax.psum_scatter(against(d_joint, w_joint).astype(jnp.bfloat16), 'tensor'...  174 us
    reduce_scatter x2, waiting for transfers between devices, shards(): lax.psum_scatter(product(hidden_low, w_down_all).astype(jnp.bfloat16), 't...  157 us
    all_gather x2, waiting for transfers between devices, shards(): ffn_rows = lax.all_gather(first_sent, 'tensor', axis=0, tiled=True)  140 us
    all_gather x2, waiting for transfers between devices, shards(): fed_grad = lax.all_gather(d_fed, 'tensor', axis=0, tiled=True)  138 us
    all_gather x2, waiting for transfers between devices, shards(): gathered = lax.all_gather(sent_rows, 'tensor', axis=0, tiled=True)  101 us
    psum x1, waiting for transfers between devices, shards(): lax.psum((acc_table, acc_bout, acc_gone, acc_bone, acc_bdown, acc_gtwo, a...  80.8 us
  transfers between devices with their start and end apart: 18, of which 18 were waited for; matrix products, arithmetic and copies ran while one was open for 12% of the time, Pallas kernels for 0%

commit v1 on v0

v1 whole, which is shorter than its diff:
```python
import jax
import jax.numpy as jnp
from jax import lax
from jax.experimental import pallas as pl
from jax.experimental.pallas import tpu as pltpu
from jax.sharding import PartitionSpec as P

HD = 64
LEN = 1024
EPSILON = 1e-12
SCALE = HD ** (-0.5)
ROWS_DIMS = (((0,), (0,)), ((), ()))
LAST_DIMS = (((1,), (1,)), ((), ()))
BF = jnp.bfloat16
F32 = jnp.float32
PAD = 16
Q_ROWS = 256
VMEM_BYTES = 48 * 1024 * 1024


def product(left_mat, right_mat):
    return jnp.dot(left_mat, right_mat, preferred_element_type=F32)


def over_rows(left_mat, right_mat):
    return lax.dot_general(left_mat, right_mat, ROWS_DIMS, preferred_element_type=F32)


def against(left_mat, right_mat):
    return lax.dot_general(left_mat, right_mat, LAST_DIMS, preferred_element_type=F32)


def swap(values, axis, bit):
    count = lax.axis_size(axis)
    return lax.ppermute(values, axis, [(i, i ^ bit) for i in range(count)])


def attn_forward_kernel(q_ref, k_ref, v_ref, o_ref):
    for head in range(2):
        lanes = pl.ds(head * HD, HD)
        scores = against(q_ref[:, lanes], k_ref[:, lanes])
        top = jnp.max(scores, axis=-1, keepdims=True)
        weights = jnp.exp((scores - top) * SCALE)
        total = jnp.sum(weights, axis=-1, keepdims=True)
        mixed = product(weights.astype(BF), v_ref[:, lanes])
        o_ref[:, lanes] = (mixed / total).astype(BF)


def attn_forward(joint, width):
    rows = joint.shape[0]
    pairs = width // 128
    return pl.pallas_call(
        attn_forward_kernel,
        out_shape=jax.ShapeDtypeStruct((rows, width), BF),
        grid=(pairs, rows // Q_ROWS),
        in_specs=[
            pl.BlockSpec((Q_ROWS, 128), lambda g, i: (i, g)),
            pl.BlockSpec((rows, 128), lambda g, i: (0, pairs + g)),
            pl.BlockSpec((rows, 128), lambda g, i: (0, 2 * pairs + g)),
        ],
        out_specs=pl.BlockSpec((Q_ROWS, 128), lambda g, i: (i, g)),
        compiler_params=pltpu.CompilerParams(vmem_limit_bytes=VMEM_BYTES),
        cost_estimate=pl.CostEstimate(
            flops=16 * rows * rows * width,
            bytes_accessed=8 * rows * width,
            transcendentals=rows * rows * width // HD,
        ),
        name="attn_forward",
    )(joint, joint, joint)


def attn_backward_kernel(
    q_ref, k_ref, v_ref, g_ref, dq_ref, dk_ref, dv_ref, kt_ref, dk_acc, dv_acc
):
    step = pl.program_id(1)

    @pl.when(step == 0)
    def _():
        kt_ref[...] = k_ref[...].T
        dk_acc[...] = jnp.zeros_like(dk_acc)
        dv_acc[...] = jnp.zeros_like(dv_acc)

    dq_parts = []
    for head in range(2):
        lanes = pl.ds(head * HD, HD)
        queries = q_ref[:, lanes]
        grads = g_ref[:, lanes]
        scores = against(k_ref[:, lanes], queries)
        top = jnp.max(scores, axis=0, keepdims=True)
        weights = jnp.exp((scores - top) * SCALE)
        probs = weights * (1.0 / jnp.sum(weights, axis=0, keepdims=True))
        d_probs = against(v_ref[:, lanes], grads)
        row_dot = jnp.sum(probs * d_probs, axis=0, keepdims=True)
        d_scores = (probs * (d_probs - row_dot)).astype(BF)
        dv_acc[:, lanes] += product(probs.astype(BF), grads)
        dk_acc[:, lanes] += product(d_scores, queries)
        dq_parts.append(product(kt_ref[lanes, :], d_scores))
    dq_ref[...] = (jnp.concatenate(dq_parts, axis=0).T * SCALE).astype(BF)

    @pl.when(step == pl.num_programs(1) - 1)
    def _():
        dk_ref[...] = (dk_acc[...] * SCALE).astype(BF)
        dv_ref[...] = dv_acc[...].astype(BF)


def attn_backward(joint, d_heads, width):
    rows = joint.shape[0]
    pairs = width // 128
    shape = jax.ShapeDtypeStruct((rows, width), BF)
    block = pl.BlockSpec((Q_ROWS, 128), lambda g, i: (i, g))
    whole = pl.BlockSpec((rows, 128), lambda g, i: (0, g))
    return pl.pallas_call(
        attn_backward_kernel,
        out_shape=(shape, shape, shape),
        grid=(pairs, rows // Q_ROWS),
        in_specs=[
            block,
            pl.BlockSpec((rows, 128), lambda g, i: (0, pairs + g)),
            pl.BlockSpec((rows, 128), lambda g, i: (0, 2 * pairs + g)),
            block,
        ],
        out_specs=(block, whole, whole),
        scratch_shapes=[
            pltpu.VMEM((128, rows), BF),
            pltpu.VMEM((rows, 128), F32),
            pltpu.VMEM((rows, 128), F32),
        ],
        compiler_params=pltpu.CompilerParams(vmem_limit_bytes=VMEM_BYTES),
        cost_estimate=pl.CostEstimate(
            flops=40 * rows * rows * width,
            bytes_accessed=14 * rows * width,
            transcendentals=rows * rows * width // HD,
        ),
        name="attn_backward",
    )(joint, joint, joint, d_heads)


def norm_forward(values):
    row_mean = jnp.mean(values, axis=-1, keepdims=True)
    centred = values - row_mean
    row_var = jnp.mean(centred * centred, axis=-1, keepdims=True)
    scale = lax.rsqrt(row_var + EPSILON)
    return centred * scale, scale


def norm_backward(normed, scale, gain_vec, grads):
    d_normed = grads * gain_vec
    mean_d = jnp.mean(d_normed, axis=-1, keepdims=True)
    mean_dn = jnp.mean(d_normed * normed, axis=-1, keepdims=True)
    return (d_normed - mean_d - normed * mean_dn) * scale


def shards(
    embedded,
    token_table,
    masked_pos,
    replace_ids,
    w_query,
    b_query,
    w_key,
    w_value,
    b_value,
    w_out,
    b_out,
    ln1_gain,
    ln1_bias,
    w_up,
    b_up,
    w_down,
    b_down,
    ln2_gain,
    ln2_bias,
    grad_masked,
):
    rank = lax.axis_index("tensor")
    count = lax.axis_size("tensor")
    dp_count = lax.axis_size("dp")
    core = lax.axis_index("dp") % 2
    micro_count, row_count, width = embedded.shape
    local_width = w_query.shape[1]
    ff_local = w_up.shape[1]
    vocab_count = token_table.shape[0]
    parts = LEN // row_count
    groups = count // parts
    part = rank % parts
    group = rank // parts
    part_width = width // parts
    own_first = core == 0

    def by_core(mine, other, axis=0):
        return jnp.where(
            own_first,
            jnp.concatenate([mine, other], axis=axis),
            jnp.concatenate([other, mine], axis=axis),
        )

    order = list(range(0, count, 2)) + list(range(count - 1, 0, -2))
    ring_fw = [(order[i], order[(i + 1) % count]) for i in range(count)]
    ring_bw = [(b, a) for a, b in ring_fw]
    far = count // 2
    ring_pos = jnp.where(rank % 2 == 0, rank // 2, count - 1 - rank // 2)

    def forward(values):
        return lax.ppermute(values, "tensor", ring_fw)

    def backward(values):
        return lax.ppermute(values, "tensor", ring_bw)

    slot_pos = lax.dynamic_index_in_dim(masked_pos, group, 1, keepdims=False)
    slot_ids = lax.dynamic_index_in_dim(replace_ids, group, 1, keepdims=False)
    slot_grads = lax.dynamic_index_in_dim(grad_masked, group, 1, keepdims=False)
    vocab_iota = jnp.arange(vocab_count, dtype=jnp.int32)

    def replacement(positions, step):
        matches = positions[:, None] == slot_pos[step][None, :]
        replaced = jnp.any(matches, axis=1)
        row_ids = jnp.sum(jnp.where(matches, slot_ids[step][None, :], 0), axis=1)
        hot = (row_ids[:, None] == vocab_iota[None, :]) & replaced[:, None]
        return matches, replaced, hot

    row_iota = jnp.arange(row_count, dtype=jnp.int32)
    placed_list, replaced_list, hot_list, cot_list, seq_hot_list = [], [], [], [], []
    for step in range(micro_count):
        matches, replaced, hot = replacement(part * row_count + row_iota, step)
        inserted = product(hot.astype(BF), token_table)
        placed_list.append(
            jnp.where(replaced[:, None], inserted, embedded[step].astype(F32)).astype(BF)
        )
        replaced_list.append(replaced)
        hot_list.append(hot.astype(F32))
        cot_list.append(product(matches.astype(BF), slot_grads[step]))
        seq_pos = jnp.concatenate([(part ^ j) * row_count + row_iota for j in range(parts)])
        seq_hot_list.append(replacement(seq_pos, step)[2].astype(BF))

    half_rows = width // 2
    joint_half = jnp.concatenate(
        [
            lax.dynamic_slice_in_dim(jnp.concatenate([w_query, w_key, w_value], axis=1), core * half_rows, half_rows, 0),
            jnp.pad(
                jnp.concatenate([b_query, jnp.zeros_like(b_query), b_value])[None, :],
                ((0, PAD - 1), (0, 0)),
            ),
        ],
        axis=0,
    )
    spread = [
        [(groups * p + i, p + parts * ((i + k) % groups)) for p in range(parts) for i in range(groups)]
        for k in range(groups)
    ]
    full_w, full_b = [], []
    for k in range(groups):
        mine = lax.ppermute(joint_half, "tensor", spread[k])
        other = swap(mine[:half_rows], "dp", 1)
        full_w.append(by_core(mine[:half_rows], other))
        full_b.append(mine[half_rows])
    stack_w, stack_b = jnp.stack(full_w), jnp.stack(full_b)
    shard_w = [lax.dynamic_index_in_dim(stack_w, (group - i) % groups, 0, keepdims=False) for i in range(groups)]
    shard_b = [lax.dynamic_index_in_dim(stack_b, (group - i) % groups, 0, keepdims=False) for i in range(groups)]
    w_seq = jnp.concatenate(
        [w[:, a * local_width : (a + 1) * local_width] for a in range(3) for w in shard_w], axis=1
    )
    b_seq = jnp.concatenate(
        [b[a * local_width : (a + 1) * local_width] for a in range(3) for b in shard_b]
    ).astype(F32)

    half_count = row_count // 2
    x_seqs, joints, heads_list = [], [], []
    for step in range(micro_count):
        sent = placed_list[step]
        from_one = swap(sent, "tensor", 1)
        from_two = swap(sent, "tensor", 2)
        from_three_a = swap(from_one[:half_count], "tensor", 2)
        from_three_b = swap(from_two[half_count:], "tensor", 1)
        x_seq = jnp.concatenate([sent, from_one, from_two, from_three_a, from_three_b], axis=0)
        x_seqs.append(x_seq)
        joints.append((product(x_seq, w_seq) + b_seq).astype(BF))

    w_out_all = lax.all_gather(w_out, "tensor", axis=0, tiled=True)

    ff_half = ff_local // 2
    up_t = w_up.T
    piece = jnp.concatenate(
        [
            lax.dynamic_slice_in_dim(up_t, core * ff_half, ff_half, 0),
            jnp.pad(
                lax.dynamic_slice_in_dim(b_up, core * ff_half, ff_half, 0)[None, :],
                ((0, PAD - 1), (0, width - ff_half)),
            ),
            lax.dynamic_slice_in_dim(w_down, core * ff_half, ff_half, 0),
        ],
        axis=0,
    )
    cut = ff_half + PAD
    piece = lax.optimization_barrier((piece, x_seqs, w_seq))[0]
    got = {0: piece}
    fw = bw = piece
    for s in range(1, far):
        fw, bw = forward(fw), backward(bw)
        got[-s], got[s] = fw, bw
    got[far] = jnp.concatenate([forward(fw[:cut]), backward(bw[cut:])], axis=0)
    offsets = [0] + [sign * s for s in range(1, far) for sign in (-1, 1)] + [far]
    slots = {}
    blocks = []
    for o in offsets:
        slots[o] = len(blocks)
        blocks.append(got[o])
        blocks.append(swap(got[o], "dp", 1))
    up_all = jnp.concatenate([b[:ff_half] for b in blocks], axis=0)
    down_all = jnp.concatenate([b[cut:] for b in blocks], axis=0)
    b_up_all = jnp.concatenate([b[ff_half, :ff_half] for b in blocks]).astype(F32)

    for step in range(micro_count):
        heads = attn_forward(joints[step], part_width)
        pieces = [heads[:row_count]] + [
            swap(heads[j * row_count : (j + 1) * row_count], "tensor", j) for j in range(1, parts)
        ]
        stacked = jnp.stack(pieces)
        heads_list.append(
            jnp.concatenate(
                [lax.dynamic_index_in_dim(stacked, part ^ j, 0, keepdims=False) for j in range(parts)],
                axis=1,
            )
        )

    placed = jnp.concatenate(placed_list, axis=0).astype(F32)
    replaced = jnp.concatenate(replaced_list, axis=0)
    cot = jnp.concatenate(cot_list, axis=0)
    heads_out = jnp.concatenate(heads_list, axis=0)
    gain_one, gain_two = ln1_gain.astype(F32), ln2_gain.astype(F32)
    norm_one, scale_one = norm_forward(placed + product(heads_out, w_out_all) + b_out.astype(F32))
    first = norm_one * gain_one + ln1_bias.astype(F32)
    first_low = first.astype(BF)
    upper = against(first_low, up_all) + b_up_all
    hidden_low = jax.nn.gelu(upper, approximate=False).astype(BF)
    fed = product(hidden_low, down_all) + b_down.astype(F32)
    norm_two, scale_two = norm_forward(first + fed)
    layer_out = (norm_two * gain_two + ln2_bias.astype(F32)).astype(BF)

    d_pre_two = norm_backward(norm_two, scale_two, gain_two, cot)
    d_fed = d_pre_two.astype(BF)
    d_hidden = against(d_fed, down_all)
    phi = jnp.exp(-0.5 * upper * upper) * (0.5 / jnp.pi) ** 0.5
    big_phi = 0.5 * (1.0 + lax.erf(upper * 0.5**0.5))
    d_upper = (d_hidden * (big_phi + upper * phi)).astype(BF)
    d_first = d_pre_two + product(d_upper, up_all)
    d_pre_one = norm_backward(norm_one, scale_one, gain_one, d_first)
    d_attended = d_pre_one.astype(BF)
    d_heads = against(d_attended, w_out_all).astype(BF)

    d_joints = []
    for step in range(micro_count):
        own = d_heads[step * row_count : (step + 1) * row_count]
        cols = [
            lax.dynamic_slice_in_dim(own, (part ^ j) * part_width, part_width, 1) for j in range(parts)
        ]
        seq_grads = jnp.concatenate(
            [cols[0]] + [swap(cols[j], "tensor", j) for j in range(1, parts)], axis=0
        )
        d_joints.append(jnp.concatenate(attn_backward(joints[step], seq_grads, part_width), axis=1))

    def ff_block(index):
        cols = slice(index * ff_half, (index + 1) * ff_half)
        return jnp.concatenate(
            [over_rows(d_upper[:, cols], first_low), over_rows(hidden_low[:, cols], d_fed)], axis=0
        )

    def ff_share(offset):
        other = swap(ff_block(slots[offset] + 1).astype(BF), "dp", 1)
        return ff_block(slots[offset]) + other.astype(F32)

    share = ff_share(far)
    fw = forward(share[:ff_half].astype(BF))
    bw = backward(share[ff_half:].astype(BF))
    for s in range(far - 1, 0, -1):
        fw_add, bw_add = fw.astype(F32), bw.astype(F32)
        if s == far - 1:
            fw_add = jnp.pad(fw_add, ((0, ff_half), (0, 0)))
            bw_add = jnp.pad(bw_add, ((ff_half, 0), (0, 0)))
        fw = forward((ff_share(s) + fw_add).astype(BF))
        bw = backward((ff_share(-s) + bw_add).astype(BF))
    ff_sum = (ff_share(0) + fw.astype(F32) + bw.astype(F32)).astype(BF)

    def over_dp(values):
        bit = 2
        while bit < dp_count:
            values = (values.astype(F32) + swap(values, "dp", bit).astype(F32)).astype(BF)
            bit *= 2
        return values

    ff_sum = over_dp(ff_sum)
    ff_other = swap(ff_sum, "dp", 1)
    grad_w_up = by_core(ff_sum[:ff_half], ff_other[:ff_half]).astype(F32).T
    grad_w_down = by_core(ff_sum[ff_half:], ff_other[ff_half:]).astype(F32)

    grad_w_out = lax.psum(
        lax.psum_scatter(
            over_rows(heads_out, d_attended).astype(BF), "tensor", scatter_dimension=0, tiled=True
        ),
        "dp",
    ).astype(F32)

    d_w_seq = sum(over_rows(x_seqs[m], d_joints[m]) for m in range(micro_count))
    other_half = lax.dynamic_slice_in_dim(d_w_seq, (1 - core) * half_rows, half_rows, 0).astype(BF)
    my_half = lax.dynamic_slice_in_dim(d_w_seq, core * half_rows, half_rows, 0)
    my_half = (my_half + swap(other_half, "dp", 1).astype(F32)).astype(BF)
    by_shard = jnp.stack(
        [
            jnp.concatenate(
                [
                    my_half[:, a * part_width + i * local_width : a * part_width + (i + 1) * local_width]
                    for a in range(3)
                ],
                axis=1,
            )
            for i in range(groups)
        ]
    )
    joint_sum = sum(
        lax.ppermute(
            lax.dynamic_index_in_dim(by_shard, (group - k) % groups, 0, keepdims=False),
            "tensor",
            [(b, a) for a, b in spread[k]],
        ).astype(F32)
        for k in range(groups)
    )
    joint_sum = over_dp(joint_sum.astype(BF))
    grad_joint = by_core(joint_sum, swap(joint_sum, "dp", 1)).astype(F32)

    grad_list = []
    for step in range(micro_count):
        share = against(d_joints[step], w_seq)
        rows = [share[j * row_count : (j + 1) * row_count] for j in range(parts)]
        to_two = swap(rows[3][:half_count].astype(BF), "tensor", 2).astype(F32)
        to_one = swap(rows[3][half_count:].astype(BF), "tensor", 1).astype(F32)
        via_one = rows[1] + jnp.pad(to_two, ((0, half_count), (0, 0)))
        via_two = rows[2] + jnp.pad(to_one, ((half_count, 0), (0, 0)))
        total = (
            rows[0]
            + swap(via_one.astype(BF), "tensor", 1).astype(F32)
            + swap(via_two.astype(BF), "tensor", 2).astype(F32)
        )
        mine = slice(step * row_count, (step + 1) * row_count)
        grad_list.append(jnp.where(replaced[mine, None], 0.0, d_pre_one[mine] + total))

    def over_all(values):
        for axis, size in (("dp", dp_count), ("tensor", count)):
            bit = 1
            while bit < size:
                values = values + swap(values, axis, bit)
                bit *= 2
        return values

    rel_b_up = jnp.sum(d_upper.astype(F32), axis=0).reshape(count, 2, ff_half)
    rel_b_up = jnp.where(own_first, rel_b_up, rel_b_up[:, ::-1]).reshape(count, ff_local)
    slot_of = [0] * count
    for o in offsets:
        slot_of[o % count] = slots[o] // 2
    place = jnp.array([order.index(s) for s in range(count)], jnp.int32)
    wanted = jnp.array(slot_of, jnp.int32)[(place - ring_pos) % count]
    all_b_up = rel_b_up[wanted].reshape(-1, width)
    early = jnp.concatenate(
        [
            all_b_up,
            jnp.sum(d_pre_one, axis=0)[None],
            jnp.sum(d_first * norm_one, axis=0)[None],
            jnp.sum(d_first, axis=0)[None],
            jnp.sum(d_pre_two, axis=0)[None],
            jnp.sum(cot * norm_two, axis=0)[None],
            jnp.sum(cot, axis=0)[None],
        ],
        axis=0,
    )
    early = over_all(early)
    b_rows = all_b_up.shape[0]
    grad_b_up = lax.dynamic_slice_in_dim(early[:b_rows].reshape(-1), rank * ff_local, ff_local, 0)
    grad_b_out, grad_gone, grad_bone, grad_b_down, grad_gtwo, grad_btwo = (
        early[b_rows + i] for i in range(6)
    )
    table = jnp.zeros((vocab_count, width), F32)
    for step in range(micro_count):
        table = table + lax.dot_general(
            hot_list[step],
            d_pre_one[step * row_count : (step + 1) * row_count],
            ROWS_DIMS,
            precision=lax.Precision.HIGHEST,
            preferred_element_type=F32,
        )
    hot_sum = sum(over_rows(seq_hot_list[m], d_joints[m]) for m in range(micro_count))
    table = table + lax.dot_general(
        hot_sum,
        w_seq.astype(F32),
        LAST_DIMS,
        precision=lax.Precision.HIGHEST,
        preferred_element_type=F32,
    )
    d_b_seq = sum(jnp.sum(d_joints[m].astype(F32), axis=0) for m in range(micro_count))
    empty = jnp.zeros((width,), F32)
    d_b_query = lax.dynamic_update_slice_in_dim(empty, d_b_seq[:part_width], part * part_width, 0)
    d_b_value = lax.dynamic_update_slice_in_dim(empty, d_b_seq[2 * part_width :], part * part_width, 0)
    late = over_all(jnp.concatenate([table, d_b_query[None], d_b_value[None]], axis=0))
    grad_table = late[:vocab_count]
    grad_b_query = lax.dynamic_slice_in_dim(late[vocab_count], rank * local_width, local_width, 0)
    grad_b_value = lax.dynamic_slice_in_dim(late[vocab_count + 1], rank * local_width, local_width, 0)

    return (
        layer_out.reshape(micro_count, row_count, width),
        jnp.stack(grad_list),
        grad_table,
        grad_joint[:, :local_width],
        grad_b_query,
        grad_joint[:, local_width : 2 * local_width],
        grad_joint[:, 2 * local_width :],
        grad_b_value,
        grad_w_out,
        grad_b_out,
        grad_gone,
        grad_bone,
        grad_w_up,
        grad_b_up,
        grad_w_down,
        grad_b_down,
        grad_gtwo,
        grad_btwo,
    )


def solution(mesh):
    return jax.shard_map(
        shards,
        mesh=mesh,
        in_specs=(
            P(None, ("dp", "tensor"), None),
            P(),
            P(None, "dp", None),
            P(None, "dp", None),
            P(None, "tensor"),
            P("tensor"),
            P(None, "tensor"),
            P(None, "tensor"),
            P("tensor"),
            P("tensor", None),
            P(),
            P(),
            P(),
            P(None, "tensor"),
            P("tensor"),
            P("tensor", None),
            P(),
            P(),
            P(),
            P(None, "dp", None, None),
        ),
        out_specs=(
            P(None, ("dp", "tensor"), None),
            P(None, ("dp", "tensor"), None),
            P(),
            P(None, "tensor"),
            P("tensor"),
            P(None, "tensor"),
            P(None, "tensor"),
            P("tensor"),
            P("tensor", None),
            P(),
            P(),
            P(),
            P(None, "tensor"),
            P("tensor"),
            P("tensor", None),
            P(),
            P(),
            P(),
        ),
        check_vma=False,
    )
```

time: 1910 us -> 678 us (0.35)
  waiting for transfers between devices: 1460 us -> 223 us
  matrix products: 240 us -> 127 us
  starting transfers between devices: 2.11 us -> 76.4 us
  Pallas kernels: 0 us -> 66.8 us
  blocking collectives: 47.5 us -> 0 us
  local copies, waits for them, and re-layouts: 63.3 us -> 100 us
  other arithmetic: 78 us -> 57.6 us
    reduce_scatter x8 -> x1, waiting for transfers between devices: 879 us -> 0.02 us  [shards(): lax.psum_scatter(over_rows(heads_out, d_attended).astype(BF), 'tensor', s...]
    all_gather x8 -> x1, waiting for transfers between devices: 453 us -> 0.01 us  [shards(): w_out_all = lax.all_gather(w_out, 'tensor', axis=0, tiled=True)]
    ppermute x0 -> x81, waiting for transfers between devices: none -> 193 us  [the longest x61 116 us: swap(): return lax.ppermute(values, axis, [(i, i ^ bit) for i in range(count)])]
    dot_general x42 -> x54, matrix products: 240 us -> 127 us  [the longest x37 52.6 us: over_rows(): lax.dot_general(left_mat, right_mat, ROWS_DIMS, preferred_element_type=F32)]
    psum x2 -> x1, waiting for transfers between devices: 125 us -> 29.9 us  [shards(): lax.psum(lax.psum_scatter(over_rows(heads_out, d_attended).astype(BF), 't...]
    ppermute x0 -> x81, starting transfers between devices: none -> 76.3 us  [the longest x61 53.1 us: swap(): return lax.ppermute(values, axis, [(i, i ^ bit) for i in range(count)])]
    pallas_call x0 -> x4, Pallas kernels: none -> 66.8 us  [the longest x2 45.1 us: attn_backward(): pl.pallas_call(attn_backward_kernel, out_shape=(shape, shape, shape), gri...]
    psum x2 -> x0, blocking collectives: 47.5 us -> none  [the longest x1 41 us: shards(): lax.psum((acc_table, acc_bout, acc_gone, acc_bone, acc_bdown, acc_gtwo, a...]
  transfers between devices with their start and end apart: 18 -> 84, of which waited for: 18 -> 27; matrix products, arithmetic and copies ran while one was open for 12% -> 24% of each run, Pallas kernels for 0% -> 10%
where the time goes in v1:
time: 678 us; the launch traced here: 668 us
  waiting for transfers between devices  223 us (33%)
  matrix products  127 us (19%)
  local copies, waits for them, and re-layouts  100 us (15%)
  starting transfers between devices  76.4 us (11%)
  Pallas kernels  66.8 us (10%)
  other arithmetic  57.6 us (8%)
  between operations  16.5 us (2%)
    ppermute x61, waiting for transfers between devices, swap(): return lax.ppermute(values, axis, [(i, i ^ bit) for i in range(count)])  116 us
    unnamed x288, local copies, waits for them, and re-layouts  57.1 us
    ppermute x8, waiting for transfers between devices, backward(): return lax.ppermute(values, 'tensor', ring_bw)  54.2 us
    ppermute x61, starting transfers between devices, swap(): return lax.ppermute(values, axis, [(i, i ^ bit) for i in range(count)])  53.1 us
    dot_general x37, matrix products, over_rows(): lax.dot_general(left_mat, right_mat, ROWS_DIMS, preferred_element_type=F32)  52.6 us
    pallas_call x2, Pallas kernels, attn_backward(): pl.pallas_call(attn_backward_kernel, out_shape=(shape, shape, shape), gri...  45.1 us
    dot_general x5, matrix products, against(): lax.dot_general(left_mat, right_mat, LAST_DIMS, preferred_element_type=F32)  42.6 us
    psum x1, waiting for transfers between devices, shards(): lax.psum(lax.psum_scatter(over_rows(heads_out, d_attended).astype(BF), 't...  29.9 us
  transfers between devices with their start and end apart: 84, of which 27 were waited for; matrix products, arithmetic and copies ran while one was open for 24% of the time, Pallas kernels for 10%

profile of v1, /device:TPU:0, one launch (start us, length us, event | category | flops | bytes accessed | tf_op | source)
XLA Modules:
  0.0 667.9 jit_solution(3736487757546278876)
XLA Ops:
  8.6 2.4 constant_dynamic-update-slice_fusion.4
  11.0 2.9 collective-permute-start
  17.1 4.9 collective-permute-start.4
  22.0 2.4 constant_dynamic-update-slice_fusion.9
  24.4 2.1 collective-permute-start.11
  27.0 3.1 constant_dynamic-slice_fusion.19
  38.0 5.0 collective-permute-start.12
  54.9 5.3 collective-permute-done.12
  60.6 16.4 %collective-permute-done.2 = bf16[128,1024]{1,0:T(8,128)(2,1)S(1)} collective-permute-done((bf16[128,1024]{1,0:T(8,128)(2,1)S(1)}, bf16[128,1024]{1,0:T(8,128)(2,1)S(1)}, u32[]{:S(2)}, u32[]{:S(2)}) %collective-permute-start.2) | collective-permute-done | bytes 262176 | tf_op jit(solution)/shard_map/ppermute | solution.py:35
  77.1 8.5 %collective-permute-done.13 = bf16[128,1024]{1,0:T(8,128)(2,1)S(1)} collective-permute-done((bf16[128,1024]{1,0:T(8,128)(2,1)S(1)}, bf16[128,1024]{1,0:T(8,128)(2,1)S(1)}, u32[]{:S(2)}, u32[]{:S(2)}) %collective-permute-start.13) | collective-permute-done | bytes 262176 | tf_op jit(solution)/shard_map/ppermute | solution.py:35
  85.6 2.0 maximum_select_fusion.2
  89.1 2.5 collective-permute-start.21
  95.3 10.9 %attn_forward.3 = bf16[1024,256]{1,0:T(8,128)(2,1)S(1)} custom-call(bf16[1024,768]{1,0:T(8,128)(2,1)S(1)} %add_convert_fusion.q_ref.k_ref.v_ref, bf16[1024,768]{1,0:T(8,128)(2,1)S(1)} %add_convert_fusion.q_ref.k_ref.v_ref, bf16[1024,768]{1,0:T(8,128)(2,1)S(1)} %add_convert_fusion.q_ref.k_ref.v_ref), custom_call_target="tpu_custom_call" | custom-call | flops 4294967296 | bytes 2097152 | tf_op jit(solution)/shard_map/attn_forward/pallas_call | solution.py:52
  107.8 10.9 %attn_forward.2 = bf16[1024,256]{1,0:T(8,128)(2,1)S(1)} custom-call(bf16[1024,768]{1,0:T(8,128)(2,1)S(1)} %add_convert_fusion.1.q_ref.k_ref.v_ref, bf16[1024,768]{1,0:T(8,128)(2,1)S(1)} %add_convert_fusion.1.q_ref.k_ref.v_ref, bf16[1024,768]{1,0:T(8,128)(2,1)S(1)} %add_convert_fusion.1.q_ref.k_ref.v_ref), custom_call_target="tpu_custom_call" | custom-call | flops 4294967296 | bytes 2097152 | tf_op jit(solution)/shard_map/attn_forward/pallas_call | solution.py:52
  119.4 2.0 collective-permute-start.15
  123.9 2.5 collective-permute-done.15
  143.0 2.2 slice_dynamic-update-slice_fusion.12
  145.2 2.3 slice_dynamic-update-slice_fusion.11
  153.2 9.6 %collective-permute-done.23 = bf16[528,1024]{1,0:T(8,128)(2,1)} collective-permute-done((bf16[528,1024]{1,0:T(8,128)(2,1)}, bf16[528,1024]{1,0:T(8,128)(2,1)}, u32[]{:S(2)}, u32[]{:S(2)}) %collective-permute-start.23) | collective-permute-done | bytes 1081376 | tf_op jit(solution)/shard_map/ppermute | solution.py:204
  167.2 2.2 slice_dynamic-update-slice_fusion.10
  170.4 2.3 slice_dynamic-update-slice_fusion.8
  172.7 2.2 slice_dynamic-update-slice_fusion.7
  176.2 3.2 fusion.171
  179.8 11.7 %collective-permute-done.27 = bf16[528,1024]{1,0:T(8,128)(2,1)} collective-permute-done((bf16[528,1024]{1,0:T(8,128)(2,1)}, bf16[528,1024]{1,0:T(8,128)(2,1)}, u32[]{:S(2)}, u32[]{:S(2)}) %collective-permute-start.27) | collective-permute-done | bytes 1081376 | tf_op jit(solution)/shard_map/ppermute | solution.py:204
  194.4 2.2 slice_dynamic-update-slice_fusion.6
  196.6 2.2 slice_dynamic-update-slice_fusion.5
  198.8 2.2 slice_dynamic-update-slice_fusion.4
  201.1 2.2 slice_dynamic-update-slice_fusion.3
  204.4 2.5 constant_dynamic-update-slice_fusion.11
  211.9 10.4 %collective-permute-done.32 = bf16[256,1024]{1,0:T(8,128)(2,1)} collective-permute-done((bf16[256,1024]{1,0:T(8,128)(2,1)}, bf16[256,1024]{1,0:T(8,128)(2,1)}, u32[]{:S(2)}, u32[]{:S(2)}) %collective-permute-start.32) | collective-permute-done | bytes 524320 | tf_op jit(solution)/shard_map/ppermute | solution.py:207
  222.4 2.3 pad_maximum_fusion.2
  228.2 2.3 slice_dynamic-update-slice_fusion.1
  235.2 2.3 slice_dynamic-update-slice_fusion
  237.5 25.6 %fusion.2 = (bf16[512,4096]{1,0:T(8,128)(2,1)S(1)}, f32[512,4096]{1,0:T(8,128)}) fusion(f32[4096]{0:T(1024)S(1)} %convert_element_type.282, bf16[512,1024]{1,0:T(8,128)(2,1)S(1)} %fusion.34, bf16[4096,1024]{1,0:T(8,128)(2,1)} %get-tuple-element.124), kind=kOutput, calls=%fused_computation.6 | convolution fusion | flops 4433379328 | bytes 22036480 | tf_op jit(solution)/shard_map/dot_general | solution.py:30
  263.1 4.8 fusion.172
  273.0 10.0 %convert_reduce_fusion = (f32[4096]{0:T(1024)}, bf16[512,4096]{1,0:T(8,128)(2,1)S(1)}) fusion(f32[512,4096]{1,0:T(8,128)} %get-tuple-element.227, f32[4096]{0:T(1024)S(1)} %convert_element_type.282, bf16[512,1024]{1,0:T(8,128)(2,1)S(1)} %convert_element_type.288, bf16[4096,1024]{1,0:T(8,128)(2,1)S(1)} %copy-done.80), kind=kOutput, calls=%fused_computation.13 | convolution fusion | flops 4322226176 | bytes 22052864 | tf_op jit(solution)/shard_map/dot_general | solution.py:30
  283.0 10.1 %multiply_reduce_fusion.1 = (f32[1024]{0:T(1024)}, f32[512]{0:T(512)S(1)}, f32[512]{0:T(512)S(1)}, f32[1024]{0:T(1024)}, f32[512,1024]{1,0:T(8,128)S(1)}) fusion(f32[512,1024]{1,0:T(8,128)S(1)} %copy-done.11, f32[512]{0:T(512)S(1)} %add_rsqrt_fusion.1, f32[512]{0:T(512)S(1)} %broadcast_multiply_fusion.5, f32[1024]{0:T(1024)S(1)} %convert_element_type.279, ...), kind=kOutput, calls=%fused_computation.66 | convolution fusion | flops 4300207104 | bytes 18894848 | tf_op jit(solution)/shard_map/dot_general | solution.py:22
  295.3 2.6 convolution_convert_fusion
  297.9 2.5 fusion.124
  300.4 2.4 fusion.126
  304.3 2.5 fusion.96
  355.6 2.3 pad_maximum_fusion.7
  366.4 2.1 collective-permute-start.60
  375.4 22.4 %attn_backward.2 = (bf16[1024,256]{1,0:T(8,128)(2,1)S(1)}, bf16[1024,256]{1,0:T(8,128)(2,1)S(1)}, bf16[1024,256]{1,0:T(8,128)(2,1)S(1)}) custom-call(bf16[1024,768]{1,0:T(8,128)(2,1)S(1)} %copy-done.5, bf16[1024,768]{1,0:T(8,128)(2,1)S(1)} %copy-done.5, bf16[1024,768]{1,0:T(8,128)(2,1)S(1)} %copy-done.5, bf16[1024,256]{1,0:T(8,128)(2,1)S(1)} %pad_maximum_fusion.13.g_ref), custom_call_target="tpu_custom_call" | custom-call | flops 10737418240 | bytes 3670016 | tf_op jit(solution)/shard_map/attn_backward/pallas_call | solution.py:112
  403.9 22.6 %attn_backward.3 = (bf16[1024,256]{1,0:T(8,128)(2,1)S(1)}, bf16[1024,256]{1,0:T(8,128)(2,1)S(1)}, bf16[1024,256]{1,0:T(8,128)(2,1)S(1)}) custom-call(bf16[1024,768]{1,0:T(8,128)(2,1)S(1)} %copy-done.3, bf16[1024,768]{1,0:T(8,128)(2,1)S(1)} %copy-done.3, bf16[1024,768]{1,0:T(8,128)(2,1)S(1)} %copy-done.3, bf16[1024,256]{1,0:T(8,128)(2,1)S(1)} %pad_maximum_fusion.14.g_ref), custom_call_target="tpu_custom_call" | custom-call | flops 10737418240 | bytes 3670016 | tf_op jit(solution)/shard_map/attn_backward/pallas_call | solution.py:112
  431.1 3.8 fusion.174
  441.6 11.1 %collective-permute-done.75 = bf16[256,1024]{1,0:T(8,128)(2,1)S(1)} collective-permute-done((bf16[256,1024]{1,0:T(8,128)(2,1)S(1)}, bf16[256,1024]{1,0:T(8,128)(2,1)S(1)}, u32[]{:S(2)}, u32[]{:S(2)}) %collective-permute-start.75) | collective-permute-done | bytes 524320 | tf_op jit(solution)/shard_map/ppermute | solution.py:207
  460.0 2.0 convolution_add_fusion
  462.7 17.5 %collective-permute-done.76 = bf16[512,1024]{1,0:T(8,128)(2,1)S(1)} collective-permute-done((bf16[512,1024]{1,0:T(8,128)(2,1)S(1)}, bf16[512,1024]{1,0:T(8,128)(2,1)S(1)}, u32[]{:S(2)}, u32[]{:S(2)}) %collective-permute-start.76) | collective-permute-done | bytes 1048608 | tf_op jit(solution)/shard_map/ppermute | solution.py:207
  484.7 4.2 collective-permute-done.62
  491.5 3.3 collective-permute-done.49
  497.3 19.8 %collective-permute-done.50 = f32[32,1024]{1,0:T(8,128)S(1)} collective-permute-done((f32[32,1024]{1,0:T(8,128)S(1)}, f32[32,1024]{1,0:T(8,128)S(1)}, u32[]{:S(2)}, u32[]{:S(2)}) %collective-permute-start.50) | collective-permute-done | bytes 131104 | tf_op jit(solution)/shard_map/ppermute | solution.py:35
  522.6 3.7 collective-permute-done.37
  537.9 14.8 %collective-permute-done.78 = bf16[512,1024]{1,0:T(8,128)(2,1)} collective-permute-done((bf16[512,1024]{1,0:T(8,128)(2,1)}, bf16[512,1024]{1,0:T(8,128)(2,1)}, u32[]{:S(2)}, u32[]{:S(2)}) %collective-permute-start.78) | collective-permute-done | bytes 1048608 | tf_op jit(solution)/shard_map/ppermute | solution.py:207
  554.0 2.2 collective-permute-start.54
  556.2 2.9 fusion.20
  559.1 16.1 %collective-permute-done.44 = bf16[128,1024]{1,0:T(8,128)(2,1)} collective-permute-done((bf16[128,1024]{1,0:T(8,128)(2,1)}, bf16[128,1024]{1,0:T(8,128)(2,1)}, u32[]{:S(2)}, u32[]{:S(2)}) %collective-permute-start.44) | collective-permute-done | bytes 262176 | tf_op jit(solution)/shard_map/ppermute | solution.py:35
  577.9 3.2 collective-permute-done.52
  581.1 3.9 collective-permute-start.38
  588.9 17.1 %collective-permute-done.56 = bf16[512,384]{1,0:T(8,128)(2,1)S(1)} collective-permute-done((bf16[512,384]{1,0:T(8,128)(2,1)S(1)}, bf16[512,384]{1,0:T(8,128)(2,1)S(1)}, u32[]{:S(2)}, u32[]{:S(2)}) %collective-permute-start.56) | collective-permute-done | bytes 393248 | tf_op jit(solution)/shard_map/ppermute | solution.py:35
  607.2 9.0 %collective-permute-done.45 = bf16[256,1024]{1,0:T(8,128)(2,1)S(1)} collective-permute-done((bf16[256,1024]{1,0:T(8,128)(2,1)S(1)}, bf16[256,1024]{1,0:T(8,128)(2,1)S(1)}, u32[]{:S(2)}, u32[]{:S(2)}) %collective-permute-start.45) | collective-permute-done | bytes 524320 | tf_op jit(solution)/shard_map/ppermute | solution.py:35
  620.7 29.9 %all-reduce.10.cloned.1.call-done = bf16[128,1024]{1,0:T(8,128)(2,1)} async-done(((bf16[128,1024]{1,0:T(8,128)(2,1)}), bf16[128,1024]{1,0:T(8,128)(2,1)}) %all-reduce.10.cloned.1.call-update) | async-done | bytes 262160 | tf_op jit(solution)/shard_map/psum | solution.py:395
  653.3 2.1 fusion.164
  657.6 3.3 fusion.52
  (624 shorter events, 223.3 us)
Async XLA Ops:
  7.2 168.9 %all-gather.2.cloned.1.call-start = ((), (), s32[]{:S(2)}) async-start(), calls=%async_computation.1 | async-start | bytes 2359296 | tf_op jit(solution)/shard_map/all_gather | solution.py:278
  11.0 37.0 %collective-permute-start = (bf16[256,1024]{1,0:T(8,128)(2,1)}, bf16[256,1024]{1,0:T(8,128)(2,1)}, u32[]{:S(2)}, u32[]{:S(2)}) collective-permute-start(bf16[256,1024]{1,0:T(8,128)(2,1)} %get-tuple-element.221), channel_id=1, source_target_pairs={{0,1},{1,0},{2,3},{3,2},{4,5},{5,4},{6,7},{7,6},{8,9},{9,8},{10,11... | collective-permute-start | bytes 1572872 | tf_op jit(solution)/shard_map/ppermute | solution.py:35
  13.9 37.5 %collective-permute-start.1 = (bf16[256,1024]{1,0:T(8,128)(2,1)}, bf16[256,1024]{1,0:T(8,128)(2,1)S(1)}, u32[]{:S(2)}, u32[]{:S(2)}) collective-permute-start(bf16[256,1024]{1,0:T(8,128)(2,1)} %get-tuple-element.221), channel_id=1, source_target_pairs={{0,2},{1,3},{2,0},{3,1},{4,6},{5,7},{6,4},{7,5},{8,10},{9,11},{10,... | collective-permute-start | bytes 1572872 | tf_op jit(solution)/shard_map/ppermute | solution.py:35
  17.1 20.9 %collective-permute-start.4 = (bf16[528,384]{1,0:T(8,128)(2,1)}, bf16[528,384]{1,0:T(8,128)(2,1)}, u32[]{:S(2)}, u32[]{:S(2)}) collective-permute-start(bf16[528,384]{1,0:T(8,128)(2,1)} %fusion.73), channel_id=1, source_target_pairs={{0,0},{1,4},{2,1},{3,5},{4,2},{5,6},{6,3},{7,7},{8,8},{9,12},{10,9... | collective-permute-start | bytes 1216520 | tf_op jit(solution)/shard_map/ppermute | solution.py:252
  22.0 22.7 %collective-permute-start.6 = (bf16[528,384]{1,0:T(8,128)(2,1)}, bf16[528,384]{1,0:T(8,128)(2,1)}, u32[]{:S(2)}, u32[]{:S(2)}) collective-permute-start(bf16[528,384]{1,0:T(8,128)(2,1)} %fusion.73), channel_id=1, source_target_pairs={{0,4},{1,0},{2,5},{3,1},{4,6},{5,2},{6,7},{7,3},{8,12},{9,8},{10,1... | collective-permute-start | bytes 1216520 | tf_op jit(solution)/shard_map/ppermute | solution.py:252
  24.4 28.2 %collective-permute-start.11 = (bf16[256,1024]{1,0:T(8,128)(2,1)}, bf16[256,1024]{1,0:T(8,128)(2,1)}, u32[]{:S(2)}, u32[]{:S(2)}) collective-permute-start(bf16[256,1024]{1,0:T(8,128)(2,1)} %get-tuple-element.223), channel_id=1, source_target_pairs={{0,1},{1,0},{2,3},{3,2},{4,5},{5,4},{6,7},{7,6},{8,9},{9,8},{10,11... | collective-permute-start | bytes 1572872 | tf_op jit(solution)/shard_map/ppermute | solution.py:35
  26.5 593.0 %reduce-scatter.2.cloned.1.call-start = ((), (), s32[]{:S(2)}) async-start(), calls=%async_computation.2 | async-start | bytes 2359296 | tf_op jit(solution)/shard_map/reduce_scatter | solution.py:396
  38.0 22.2 %collective-permute-start.12 = (bf16[256,1024]{1,0:T(8,128)(2,1)}, bf16[256,1024]{1,0:T(8,128)(2,1)S(1)}, u32[]{:S(2)}, u32[]{:S(2)}) collective-permute-start(bf16[256,1024]{1,0:T(8,128)(2,1)} %get-tuple-element.223), channel_id=1, source_target_pairs={{0,2},{1,3},{2,0},{3,1},{4,6},{5,7},{6,4},{7,5},{8,10},{9,11},{10,... | collective-permute-start | bytes 1572872 | tf_op jit(solution)/shard_map/ppermute | solution.py:35
  44.7 40.9 %collective-permute-start.5 = (bf16[512,384]{1,0:T(8,128)(2,1)S(1)}, bf16[512,384]{1,0:T(8,128)(2,1)}, u32[]{:S(2)}, u32[]{:S(2)}) collective-permute-start(bf16[512,384]{1,0:T(8,128)(2,1)S(1)} %get-tuple-element.197), channel_id=1, source_target_pairs={{0,8},{8,0},{16,24},{24,16},{1,9},{9,1},{17,25},{25,17},{2,10},{10... | collective-permute-start | bytes 1179656 | tf_op jit(solution)/shard_map/ppermute | solution.py:35
  48.0 39.6 %collective-permute-start.7 = (bf16[512,384]{1,0:T(8,128)(2,1)S(1)}, bf16[512,384]{1,0:T(8,128)(2,1)S(1)}, u32[]{:S(2)}, u32[]{:S(2)}) collective-permute-start(bf16[512,384]{1,0:T(8,128)(2,1)S(1)} %get-tuple-element.195), channel_id=1, source_target_pairs={{0,8},{8,0},{16,24},{24,16},{1,9},{9,1},{17,25},{25,17},{2,10},{10... | collective-permute-start | bytes 1179656 | tf_op jit(solution)/shard_map/ppermute | solution.py:35
  51.4 25.6 %collective-permute-start.2 = (bf16[128,1024]{1,0:T(8,128)(2,1)S(1)}, bf16[128,1024]{1,0:T(8,128)(2,1)S(1)}, u32[]{:S(2)}, u32[]{:S(2)}) collective-permute-start(bf16[128,1024]{1,0:T(8,128)(2,1)S(1)} %slice.665), channel_id=1, source_target_pairs={{0,2},{1,3},{2,0},{3,1},{4,6},{5,7},{6,4},{7,5},{8,10},{9,11},{10,... | collective-permute-start | bytes 786440 | tf_op jit(solution)/shard_map/ppermute | solution.py:35
  52.6 24.4 %collective-permute-start.3 = (bf16[128,1024]{1,0:T(8,128)(2,1)S(1)}, bf16[128,1024]{1,0:T(8,128)(2,1)S(1)}, u32[]{:S(2)}, u32[]{:S(2)}) collective-permute-start(bf16[128,1024]{1,0:T(8,128)(2,1)S(1)} %slice.666), channel_id=1, source_target_pairs={{0,1},{1,0},{2,3},{3,2},{4,5},{5,4},{6,7},{7,6},{8,9},{9,8},{10,11... | collective-permute-start | bytes 786440 | tf_op jit(solution)/shard_map/ppermute | solution.py:35
  60.2 25.3 %collective-permute-start.13 = (bf16[128,1024]{1,0:T(8,128)(2,1)S(1)}, bf16[128,1024]{1,0:T(8,128)(2,1)S(1)}, u32[]{:S(2)}, u32[]{:S(2)}) collective-permute-start(bf16[128,1024]{1,0:T(8,128)(2,1)S(1)} %slice.687), channel_id=1, source_target_pairs={{0,2},{1,3},{2,0},{3,1},{4,6},{5,7},{6,4},{7,5},{8,10},{9,11},{10,... | collective-permute-start | bytes 786440 | tf_op jit(solution)/shard_map/ppermute | solution.py:35
  89.0 48.3 %collective-permute-start.18 = (bf16[528,1024]{1,0:T(8,128)(2,1)S(1)}, bf16[528,1024]{1,0:T(8,128)(2,1)}, u32[]{:S(2)}, u32[]{:S(2)}) collective-permute-start(bf16[528,1024]{1,0:T(8,128)(2,1)S(1)} %fusion.39), channel_id=1, source_target_pairs={{0,8},{8,0},{16,24},{24,16},{1,9},{9,1},{17,25},{25,17},{2,10},{10... | collective-permute-start | bytes 3244040 | tf_op jit(solution)/shard_map/ppermute | solution.py:35
  89.1 46.2 %collective-permute-start.19 = (bf16[528,1024]{1,0:T(8,128)(2,1)S(1)}, bf16[528,1024]{1,0:T(8,128)(2,1)}, u32[]{:S(2)}, u32[]{:S(2)}) collective-permute-start(bf16[528,1024]{1,0:T(8,128)(2,1)S(1)} %fusion.39), channel_id=1, source_target_pairs={{0,2},{2,4},{4,6},{6,7},{7,5},{5,3},{3,1},{1,0},{8,10},{10,12},{12... | collective-permute-start | bytes 3244040 | tf_op jit(solution)/shard_map/ppermute | solution.py:204
  89.1 46.9 %collective-permute-start.21 = (bf16[528,1024]{1,0:T(8,128)(2,1)S(1)}, bf16[528,1024]{1,0:T(8,128)(2,1)S(1)}, u32[]{:S(2)}, u32[]{:S(2)}) collective-permute-start(bf16[528,1024]{1,0:T(8,128)(2,1)S(1)} %fusion.39), channel_id=1, source_target_pairs={{2,0},{4,2},{6,4},{7,6},{5,7},{3,5},{1,3},{0,1},{10,8},{12,10},{14... | collective-permute-start | bytes 3244040 | tf_op jit(solution)/shard_map/ppermute | solution.py:207
  106.2 13.2 %collective-permute-start.17 = (bf16[256,256]{1,0:T(8,128)(2,1)S(1)}, bf16[256,256]{1,0:T(8,128)(2,1)S(1)}, u32[]{:S(2)}, u32[]{:S(2)}) collective-permute-start(bf16[256,256]{1,0:T(8,128)(2,1)S(1)} %get-tuple-element.191), channel_id=1, source_target_pairs={{0,3},{1,2},{2,1},{3,0},{4,7},{5,6},{6,5},{7,4},{8,11},{9,10},{10,... | collective-permute-start | bytes 393224 | tf_op jit(solution)/shard_map/ppermute | solution.py:35
  106.3 15.2 %collective-permute-start.16 = (bf16[256,256]{1,0:T(8,128)(2,1)S(1)}, bf16[256,256]{1,0:T(8,128)(2,1)S(1)}, u32[]{:S(2)}, u32[]{:S(2)}) collective-permute-start(bf16[256,256]{1,0:T(8,128)(2,1)S(1)} %get-tuple-element.192), channel_id=1, source_target_pairs={{0,2},{1,3},{2,0},{3,1},{4,6},{5,7},{6,4},{7,5},{8,10},{9,11},{10,... | collective-permute-start | bytes 393224 | tf_op jit(solution)/shard_map/ppermute | solution.py:35
  136.1 15.0 %collective-permute-start.22 = (bf16[528,1024]{1,0:T(8,128)(2,1)S(1)}, bf16[528,1024]{1,0:T(8,128)(2,1)}, u32[]{:S(2)}, u32[]{:S(2)}) collective-permute-start(bf16[528,1024]{1,0:T(8,128)(2,1)S(1)} %collective-permute-done.21), channel_id=1, source_target_pairs={{0,8},{8,0},{16,24},{24,16},{1,9},{9,1},{17,25},{25,17},{2,10},{10... | collective-permute-start | bytes 3244040 | tf_op jit(solution)/shard_map/ppermute | solution.py:35
  136.6 26.2 %collective-permute-start.23 = (bf16[528,1024]{1,0:T(8,128)(2,1)}, bf16[528,1024]{1,0:T(8,128)(2,1)}, u32[]{:S(2)}, u32[]{:S(2)}) collective-permute-start(bf16[528,1024]{1,0:T(8,128)(2,1)} %collective-permute-done.19), channel_id=1, source_target_pairs={{0,2},{2,4},{4,6},{6,7},{7,5},{5,3},{3,1},{1,0},{8,10},{10,12},{12... | collective-permute-start | bytes 3244040 | tf_op jit(solution)/shard_map/ppermute | solution.py:204
  139.4 26.5 %collective-permute-start.25 = (bf16[528,1024]{1,0:T(8,128)(2,1)S(1)}, bf16[528,1024]{1,0:T(8,128)(2,1)}, u32[]{:S(2)}, u32[]{:S(2)}) collective-permute-start(bf16[528,1024]{1,0:T(8,128)(2,1)S(1)} %collective-permute-done.21), channel_id=1, source_target_pairs={{2,0},{4,2},{6,4},{7,6},{5,7},{3,5},{1,3},{0,1},{10,8},{12,10},{14... | collective-permute-start | bytes 3244040 | tf_op jit(solution)/shard_map/ppermute | solution.py:207
  164.9 29.5 %collective-permute-start.24 = (bf16[528,1024]{1,0:T(8,128)(2,1)}, bf16[528,1024]{1,0:T(8,128)(2,1)}, u32[]{:S(2)}, u32[]{:S(2)}) collective-permute-start(bf16[528,1024]{1,0:T(8,128)(2,1)} %collective-permute-done.23), channel_id=1, source_target_pairs={{0,8},{8,0},{16,24},{24,16},{1,9},{9,1},{17,25},{25,17},{2,10},{10... | collective-permute-start | bytes 3244040 | tf_op jit(solution)/shard_map/ppermute | solution.py:35
  164.9 26.6 %collective-permute-start.27 = (bf16[528,1024]{1,0:T(8,128)(2,1)}, bf16[528,1024]{1,0:T(8,128)(2,1)}, u32[]{:S(2)}, u32[]{:S(2)}) collective-permute-start(bf16[528,1024]{1,0:T(8,128)(2,1)} %collective-permute-done.23), channel_id=1, source_target_pairs={{0,2},{2,4},{4,6},{6,7},{7,5},{5,3},{3,1},{1,0},{8,10},{10,12},{12... | collective-permute-start | bytes 3244040 | tf_op jit(solution)/shard_map/ppermute | solution.py:204
  165.9 32.9 %collective-permute-start.26 = (bf16[528,1024]{1,0:T(8,128)(2,1)}, bf16[528,1024]{1,0:T(8,128)(2,1)}, u32[]{:S(2)}, u32[]{:S(2)}) collective-permute-start(bf16[528,1024]{1,0:T(8,128)(2,1)} %collective-permute-done.25), channel_id=1, source_target_pairs={{0,8},{8,0},{16,24},{24,16},{1,9},{9,1},{17,25},{25,17},{2,10},{10... | collective-permute-start | bytes 3244040 | tf_op jit(solution)/shard_map/ppermute | solution.py:35
  165.9 28.3 %collective-permute-start.29 = (bf16[528,1024]{1,0:T(8,128)(2,1)}, bf16[528,1024]{1,0:T(8,128)(2,1)}, u32[]{:S(2)}, u32[]{:S(2)}) collective-permute-start(bf16[528,1024]{1,0:T(8,128)(2,1)} %collective-permute-done.25), channel_id=1, source_target_pairs={{2,0},{4,2},{6,4},{7,6},{5,7},{3,5},{1,3},{0,1},{10,8},{12,10},{14... | collective-permute-start | bytes 3244040 | tf_op jit(solution)/shard_map/ppermute | solution.py:207
  193.4 18.5 %collective-permute-start.31 = (bf16[272,1024]{1,0:T(8,128)(2,1)}, bf16[272,1024]{1,0:T(8,128)(2,1)}, u32[]{:S(2)}, u32[]{:S(2)}) collective-permute-start(bf16[272,1024]{1,0:T(8,128)(2,1)} %slice.706), channel_id=1, source_target_pairs={{0,2},{2,4},{4,6},{6,7},{7,5},{5,3},{3,1},{1,0},{8,10},{10,12},{12... | collective-permute-start | bytes 1671176 | tf_op jit(solution)/shard_map/ppermute | solution.py:204
  194.1 33.0 %collective-permute-start.30 = (bf16[528,1024]{1,0:T(8,128)(2,1)}, bf16[528,1024]{1,0:T(8,128)(2,1)}, u32[]{:S(2)}, u32[]{:S(2)}) collective-permute-start(bf16[528,1024]{1,0:T(8,128)(2,1)} %collective-permute-done.29), channel_id=1, source_target_pairs={{0,8},{8,0},{16,24},{24,16},{1,9},{9,1},{17,25},{25,17},{2,10},{10... | collective-permute-start | bytes 3244040 | tf_op jit(solution)/shard_map/ppermute | solution.py:35
  207.0 15.4 %collective-permute-start.32 = (bf16[256,1024]{1,0:T(8,128)(2,1)}, bf16[256,1024]{1,0:T(8,128)(2,1)}, u32[]{:S(2)}, u32[]{:S(2)}) collective-permute-start(bf16[256,1024]{1,0:T(8,128)(2,1)} %get-tuple-element.128), channel_id=1, source_target_pairs={{2,0},{4,2},{6,4},{7,6},{5,7},{3,5},{1,3},{0,1},{10,8},{12,10},{14... | collective-permute-start | bytes 1572872 | tf_op jit(solution)/shard_map/ppermute | solution.py:207
  345.4 26.8 %collective-permute-start.36 = (bf16[256,256]{1,0:T(8,128)(2,1)}, bf16[256,256]{1,0:T(8,128)(2,1)}, u32[]{:S(2)}, u32[]{:S(2)}) collective-permute-start(bf16[256,256]{1,0:T(8,128)(2,1)} %get-tuple-element.171), channel_id=1, source_target_pairs={{0,3},{1,2},{2,1},{3,0},{4,7},{5,6},{6,5},{7,4},{8,11},{9,10},{10,... | collective-permute-start | bytes 393224 | tf_op jit(solution)/shard_map/ppermute | solution.py:35
  346.3 27.5 %collective-permute-start.35 = (bf16[256,256]{1,0:T(8,128)(2,1)}, bf16[256,256]{1,0:T(8,128)(2,1)}, u32[]{:S(2)}, u32[]{:S(2)}) collective-permute-start(bf16[256,256]{1,0:T(8,128)(2,1)} %get-tuple-element.172), channel_id=1, source_target_pairs={{0,2},{1,3},{2,0},{3,1},{4,6},{5,7},{6,4},{7,5},{8,10},{9,11},{10,... | collective-permute-start | bytes 393224 | tf_op jit(solution)/shard_map/ppermute | solution.py:35
  347.4 26.4 %collective-permute-start.34 = (bf16[256,256]{1,0:T(8,128)(2,1)}, bf16[256,256]{1,0:T(8,128)(2,1)}, u32[]{:S(2)}, u32[]{:S(2)}) collective-permute-start(bf16[256,256]{1,0:T(8,128)(2,1)} %get-tuple-element.173), channel_id=1, source_target_pairs={{0,1},{1,0},{2,3},{3,2},{4,5},{5,4},{6,7},{7,6},{8,9},{9,8},{10,11... | collective-permute-start | bytes 393224 | tf_op jit(solution)/shard_map/ppermute | solution.py:35
  349.7 52.5 %collective-permute-start.43 = (bf16[256,256]{1,0:T(8,128)(2,1)}, bf16[256,256]{1,0:T(8,128)(2,1)}, u32[]{:S(2)}, u32[]{:S(2)}) collective-permute-start(bf16[256,256]{1,0:T(8,128)(2,1)} %get-tuple-element.175), channel_id=1, source_target_pairs={{0,3},{1,2},{2,1},{3,0},{4,7},{5,6},{6,5},{7,4},{8,11},{9,10},{10,... | collective-permute-start | bytes 393224 | tf_op jit(solution)/shard_map/ppermute | solution.py:35
  350.9 299.7 %all-reduce.10.cloned.1.call-start = ((), (), s32[]{:S(2)}) async-start(), calls=%async_computation.3 | async-start | bytes 524288 | tf_op jit(solution)/shard_map/psum | solution.py:395
  371.4 31.0 %collective-permute-start.42 = (bf16[256,256]{1,0:T(8,128)(2,1)S(1)}, bf16[256,256]{1,0:T(8,128)(2,1)S(1)}, u32[]{:S(2)}, u32[]{:S(2)}) collective-permute-start(bf16[256,256]{1,0:T(8,128)(2,1)S(1)} %copy-done.74), channel_id=1, source_target_pairs={{0,2},{1,3},{2,0},{3,1},{4,6},{5,7},{6,4},{7,5},{8,10},{9,11},{10,... | collective-permute-start | bytes 393224 | tf_op jit(solution)/shard_map/ppermute | solution.py:35
  372.2 30.6 %collective-permute-start.41 = (bf16[256,256]{1,0:T(8,128)(2,1)S(1)}, bf16[256,256]{1,0:T(8,128)(2,1)S(1)}, u32[]{:S(2)}, u32[]{:S(2)}) collective-permute-start(bf16[256,256]{1,0:T(8,128)(2,1)S(1)} %copy-done.73), channel_id=1, source_target_pairs={{0,1},{1,0},{2,3},{3,2},{4,5},{5,4},{6,7},{7,6},{8,9},{9,8},{10,11... | collective-permute-start | bytes 393224 | tf_op jit(solution)/shard_map/ppermute | solution.py:35
  373.8 67.7 %collective-permute-start.74 = (bf16[512,1024]{1,0:T(8,128)(2,1)}, bf16[512,1024]{1,0:T(8,128)(2,1)}, u32[]{:S(2)}, u32[]{:S(2)}) collective-permute-start(bf16[512,1024]{1,0:T(8,128)(2,1)} %pad_maximum_fusion.10), channel_id=1, source_target_pairs={{0,8},{8,0},{16,24},{24,16},{1,9},{9,1},{17,25},{25,17},{2,10},{10... | collective-permute-start | bytes 3145736 | tf_op jit(solution)/shard_map/ppermute | solution.py:35
  373.8 63.0 %collective-permute-start.67 = (bf16[512,1024]{1,0:T(8,128)(2,1)}, bf16[512,1024]{1,0:T(8,128)(2,1)}, u32[]{:S(2)}, u32[]{:S(2)}) collective-permute-start(bf16[512,1024]{1,0:T(8,128)(2,1)} %pad_maximum_fusion.7), channel_id=1, source_target_pairs={{0,8},{8,0},{16,24},{24,16},{1,9},{9,1},{17,25},{25,17},{2,10},{10... | collective-permute-start | bytes 3145736 | tf_op jit(solution)/shard_map/ppermute | solution.py:35
  402.2 59.9 %collective-permute-start.73 = (bf16[512,1024]{1,0:T(8,128)(2,1)}, bf16[512,1024]{1,0:T(8,128)(2,1)}, u32[]{:S(2)}, u32[]{:S(2)}) collective-permute-start(bf16[512,1024]{1,0:T(8,128)(2,1)} %pad_maximum_fusion.9), channel_id=1, source_target_pairs={{0,8},{8,0},{16,24},{24,16},{1,9},{9,1},{17,25},{25,17},{2,10},{10... | collective-permute-start | bytes 3145736 | tf_op jit(solution)/shard_map/ppermute | solution.py:35
  402.4 53.8 %collective-permute-start.66 = (bf16[512,1024]{1,0:T(8,128)(2,1)S(1)}, bf16[512,1024]{1,0:T(8,128)(2,1)}, u32[]{:S(2)}, u32[]{:S(2)}) collective-permute-start(bf16[512,1024]{1,0:T(8,128)(2,1)S(1)} %pad_maximum_fusion.6), channel_id=1, source_target_pairs={{0,8},{8,0},{16,24},{24,16},{1,9},{9,1},{17,25},{25,17},{2,10},{10... | collective-permute-start | bytes 3145736 | tf_op jit(solution)/shard_map/ppermute | solution.py:35
  438.6 14.2 %collective-permute-start.75 = (bf16[256,1024]{1,0:T(8,128)(2,1)S(1)}, bf16[256,1024]{1,0:T(8,128)(2,1)S(1)}, u32[]{:S(2)}, u32[]{:S(2)}) collective-permute-start(bf16[256,1024]{1,0:T(8,128)(2,1)S(1)} %get-tuple-element.159), channel_id=1, source_target_pairs={{2,0},{4,2},{6,4},{7,6},{5,7},{3,5},{1,3},{0,1},{10,8},{12,10},{14... | collective-permute-start | bytes 1572872 | tf_op jit(solution)/shard_map/ppermute | solution.py:207
  439.1 17.1 %collective-permute-start.68 = (bf16[256,1024]{1,0:T(8,128)(2,1)S(1)}, bf16[256,1024]{1,0:T(8,128)(2,1)S(1)}, u32[]{:S(2)}, u32[]{:S(2)}) collective-permute-start(bf16[256,1024]{1,0:T(8,128)(2,1)S(1)} %get-tuple-element.158), channel_id=1, source_target_pairs={{0,2},{2,4},{4,6},{6,7},{7,5},{5,3},{3,1},{1,0},{8,10},{10,12},{12... | collective-permute-start | bytes 1572872 | tf_op jit(solution)/shard_map/ppermute | solution.py:204
  441.5 40.5 %collective-permute-start.65 = (bf16[512,1024]{1,0:T(8,128)(2,1)}, bf16[512,1024]{1,0:T(8,128)(2,1)S(1)}, u32[]{:S(2)}, u32[]{:S(2)}) collective-permute-start(bf16[512,1024]{1,0:T(8,128)(2,1)} %pad_maximum_fusion.5), channel_id=1, source_target_pairs={{0,8},{8,0},{16,24},{24,16},{1,9},{9,1},{17,25},{25,17},{2,10},{10... | collective-permute-start | bytes 3145736 | tf_op jit(solution)/shard_map/ppermute | solution.py:35
  456.1 24.1 %collective-permute-start.76 = (bf16[512,1024]{1,0:T(8,128)(2,1)S(1)}, bf16[512,1024]{1,0:T(8,128)(2,1)S(1)}, u32[]{:S(2)}, u32[]{:S(2)}) collective-permute-start(bf16[512,1024]{1,0:T(8,128)(2,1)S(1)} %fusion.33), channel_id=1, source_target_pairs={{2,0},{4,2},{6,4},{7,6},{5,7},{3,5},{1,3},{0,1},{10,8},{12,10},{14... | collective-permute-start | bytes 3145736 | tf_op jit(solution)/shard_map/ppermute | solution.py:207
  458.0 25.0 %collective-permute-start.69 = (bf16[512,1024]{1,0:T(8,128)(2,1)S(1)}, bf16[512,1024]{1,0:T(8,128)(2,1)S(1)}, u32[]{:S(2)}, u32[]{:S(2)}) collective-permute-start(bf16[512,1024]{1,0:T(8,128)(2,1)S(1)} %fusion.26), channel_id=1, source_target_pairs={{0,2},{2,4},{4,6},{6,7},{7,5},{5,3},{3,1},{1,0},{8,10},{10,12},{12... | collective-permute-start | bytes 3145736 | tf_op jit(solution)/shard_map/ppermute | solution.py:204
  462.0 55.0 %collective-permute-start.72 = (bf16[512,1024]{1,0:T(8,128)(2,1)S(1)}, bf16[512,1024]{1,0:T(8,128)(2,1)S(1)}, u32[]{:S(2)}, u32[]{:S(2)}) collective-permute-start(bf16[512,1024]{1,0:T(8,128)(2,1)S(1)} %copy-done.49), channel_id=1, source_target_pairs={{0,8},{8,0},{16,24},{24,16},{1,9},{9,1},{17,25},{25,17},{2,10},{10... | collective-permute-start | bytes 3145736 | tf_op jit(solution)/shard_map/ppermute | solution.py:35
  462.2 57.1 %collective-permute-start.64 = (bf16[512,1024]{1,0:T(8,128)(2,1)S(1)}, bf16[512,1024]{1,0:T(8,128)(2,1)S(1)}, u32[]{:S(2)}, u32[]{:S(2)}) collective-permute-start(bf16[512,1024]{1,0:T(8,128)(2,1)S(1)} %copy-done.48), channel_id=1, source_target_pairs={{0,8},{8,0},{16,24},{24,16},{1,9},{9,1},{17,25},{25,17},{2,10},{10... | collective-permute-start | bytes 3145736 | tf_op jit(solution)/shard_map/ppermute | solution.py:35
  483.0 34.2 %collective-permute-start.77 = (bf16[512,1024]{1,0:T(8,128)(2,1)S(1)}, bf16[512,1024]{1,0:T(8,128)(2,1)S(1)}, u32[]{:S(2)}, u32[]{:S(2)}) collective-permute-start(bf16[512,1024]{1,0:T(8,128)(2,1)S(1)} %fusion.31), channel_id=1, source_target_pairs={{2,0},{4,2},{6,4},{7,6},{5,7},{3,5},{1,3},{0,1},{10,8},{12,10},{14... | collective-permute-start | bytes 3145736 | tf_op jit(solution)/shard_map/ppermute | solution.py:207
  488.9 30.4 %collective-permute-start.70 = (bf16[512,1024]{1,0:T(8,128)(2,1)S(1)}, bf16[512,1024]{1,0:T(8,128)(2,1)S(1)}, u32[]{:S(2)}, u32[]{:S(2)}) collective-permute-start(bf16[512,1024]{1,0:T(8,128)(2,1)S(1)} %fusion.24), channel_id=1, source_target_pairs={{0,2},{2,4},{4,6},{6,7},{7,5},{5,3},{3,1},{1,0},{8,10},{10,12},{12... | collective-permute-start | bytes 3145736 | tf_op jit(solution)/shard_map/ppermute | solution.py:204
  494.9 22.2 %collective-permute-start.50 = (f32[32,1024]{1,0:T(8,128)S(1)}, f32[32,1024]{1,0:T(8,128)S(1)}, u32[]{:S(2)}, u32[]{:S(2)}) collective-permute-start(f32[32,1024]{1,0:T(8,128)S(1)} %add.456), channel_id=1, source_target_pairs={{0,1},{1,0},{2,3},{3,2},{4,5},{5,4},{6,7},{7,6},{8,9},{9,8},{10,11... | collective-permute-start | bytes 393224 | tf_op jit(solution)/shard_map/ppermute | solution.py:35
  517.0 19.1 %collective-permute-start.63 = (bf16[512,1024]{1,0:T(8,128)(2,1)}, bf16[512,1024]{1,0:T(8,128)(2,1)}, u32[]{:S(2)}, u32[]{:S(2)}) collective-permute-start(bf16[512,1024]{1,0:T(8,128)(2,1)} %pad_maximum_fusion.3), channel_id=1, source_target_pairs={{0,8},{8,0},{16,24},{24,16},{1,9},{9,1},{17,25},{25,17},{2,10},{10... | collective-permute-start | bytes 3145736 | tf_op jit(solution)/shard_map/ppermute | solution.py:35
  517.2 14.2 %collective-permute-start.53 = (bf16[512,768]{0,1:T(8,128)(2,1)S(1)}, bf16[512,768]{0,1:T(8,128)(2,1)S(1)}, u32[]{:S(2)}, u32[]{:S(2)}) collective-permute-start(bf16[512,768]{0,1:T(8,128)(2,1)S(1)} %dynamic-slice_convert_fusion), channel_id=1, source_target_pairs={{0,8},{8,0},{16,24},{24,16},{1,9},{9,1},{17,25},{25,17},{2,10},{10... | collective-permute-start | bytes 2359304 | tf_op jit(solution)/shard_map/ppermute | solution.py:35
  526.3 26.4 %collective-permute-start.78 = (bf16[512,1024]{1,0:T(8,128)(2,1)}, bf16[512,1024]{1,0:T(8,128)(2,1)}, u32[]{:S(2)}, u32[]{:S(2)}) collective-permute-start(bf16[512,1024]{1,0:T(8,128)(2,1)} %fusion.29), channel_id=1, source_target_pairs={{2,0},{4,2},{6,4},{7,6},{5,7},{3,5},{1,3},{0,1},{10,8},{12,10},{14... | collective-permute-start | bytes 3145736 | tf_op jit(solution)/shard_map/ppermute | solution.py:207
  527.5 26.4 %collective-permute-start.71 = (bf16[512,1024]{1,0:T(8,128)(2,1)}, bf16[512,1024]{1,0:T(8,128)(2,1)}, u32[]{:S(2)}, u32[]{:S(2)}) collective-permute-start(bf16[512,1024]{1,0:T(8,128)(2,1)} %fusion.22), channel_id=1, source_target_pairs={{0,2},{2,4},{4,6},{6,7},{7,5},{5,3},{3,1},{1,0},{8,10},{10,12},{12... | collective-permute-start | bytes 3145736 | tf_op jit(solution)/shard_map/ppermute | solution.py:204
  530.7 44.5 %collective-permute-start.44 = (bf16[128,1024]{1,0:T(8,128)(2,1)}, bf16[128,1024]{1,0:T(8,128)(2,1)}, u32[]{:S(2)}, u32[]{:S(2)}) collective-permute-start(bf16[128,1024]{1,0:T(8,128)(2,1)} %get-tuple-element.114), channel_id=1, source_target_pairs={{0,2},{1,3},{2,0},{3,1},{4,6},{5,7},{6,4},{7,5},{8,10},{9,11},{10,... | collective-permute-start | bytes 786440 | tf_op jit(solution)/shard_map/ppermute | solution.py:35
  531.4 43.8 %collective-permute-start.46 = (bf16[128,1024]{1,0:T(8,128)(2,1)}, bf16[128,1024]{1,0:T(8,128)(2,1)}, u32[]{:S(2)}, u32[]{:S(2)}) collective-permute-start(bf16[128,1024]{1,0:T(8,128)(2,1)} %get-tuple-element.115), channel_id=1, source_target_pairs={{0,1},{1,0},{2,3},{3,2},{4,5},{5,4},{6,7},{7,6},{8,9},{9,8},{10,11... | collective-permute-start | bytes 786440 | tf_op jit(solution)/shard_map/ppermute | solution.py:35
  536.1 70.5 %collective-permute-start.40 = (bf16[256,1024]{1,0:T(8,128)(2,1)}, bf16[256,1024]{1,0:T(8,128)(2,1)S(1)}, u32[]{:S(2)}, u32[]{:S(2)}) collective-permute-start(bf16[256,1024]{1,0:T(8,128)(2,1)} %get-tuple-element.106), channel_id=1, source_target_pairs={{0,2},{1,3},{2,0},{3,1},{4,6},{5,7},{6,4},{7,5},{8,10},{9,11},{10,... | collective-permute-start | bytes 1572872 | tf_op jit(solution)/shard_map/ppermute | solution.py:35
  552.7 32.4 %collective-permute-start.55 = (bf16[512,384]{1,0:T(8,128)(2,1)}, bf16[512,384]{1,0:T(8,128)(2,1)S(1)}, u32[]{:S(2)}, u32[]{:S(2)}) collective-permute-start(bf16[512,384]{1,0:T(8,128)(2,1)} %bitcast.177), channel_id=1, source_target_pairs={{4,0},{0,1},{5,2},{1,3},{6,4},{2,5},{7,6},{3,7},{12,8},{8,9},{13,1... | collective-permute-start | bytes 1179656 | tf_op jit(solution)/shard_map/ppermute | solution.py:419
  554.0 32.3 %collective-permute-start.54 = (bf16[512,384]{1,0:T(8,128)(2,1)}, bf16[512,384]{1,0:T(8,128)(2,1)S(1)}, u32[]{:S(2)}, u32[]{:S(2)}) collective-permute-start(bf16[512,384]{1,0:T(8,128)(2,1)} %bitcast.176), channel_id=1, source_target_pairs={{0,0},{4,1},{1,2},{5,3},{2,4},{6,5},{3,6},{7,7},{8,8},{12,9},{9,10... | collective-permute-start | bytes 1179656 | tf_op jit(solution)/shard_map/ppermute | solution.py:419
  575.2 30.9 %collective-permute-start.79 = (bf16[512,1024]{1,0:T(8,128)(2,1)S(1)}, bf16[512,1024]{1,0:T(8,128)(2,1)S(1)}, u32[]{:S(2)}, u32[]{:S(2)}) collective-permute-start(bf16[512,1024]{1,0:T(8,128)(2,1)S(1)} %fusion.20), channel_id=1, source_target_pairs={{0,16},{8,24},{16,0},{24,8},{1,17},{9,25},{17,1},{25,9},{2,18},{10... | collective-permute-start | bytes 3145736 | tf_op jit(solution)/shard_map/ppermute | solution.py:35
  581.1 26.1 %collective-permute-start.38 = (bf16[256,1024]{1,0:T(8,128)(2,1)S(1)}, bf16[256,1024]{1,0:T(8,128)(2,1)S(1)}, u32[]{:S(2)}, u32[]{:S(2)}) collective-permute-start(bf16[256,1024]{1,0:T(8,128)(2,1)S(1)} %copy-done.51), channel_id=1, source_target_pairs={{0,1},{1,0},{2,3},{3,2},{4,5},{5,4},{6,7},{7,6},{8,9},{9,8},{10,11... | collective-permute-start | bytes 1572872 | tf_op jit(solution)/shard_map/ppermute | solution.py:35
  585.1 22.1 %collective-permute-start.47 = (bf16[256,1024]{1,0:T(8,128)(2,1)S(1)}, bf16[256,1024]{1,0:T(8,128)(2,1)S(1)}, u32[]{:S(2)}, u32[]{:S(2)}) collective-permute-start(bf16[256,1024]{1,0:T(8,128)(2,1)S(1)} %get-tuple-element.108), channel_id=1, source_target_pairs={{0,2},{1,3},{2,0},{3,1},{4,6},{5,7},{6,4},{7,5},{8,10},{9,11},{10,... | collective-permute-start | bytes 1572872 | tf_op jit(solution)/shard_map/ppermute | solution.py:35
  586.3 19.7 %collective-permute-start.56 = (bf16[512,384]{1,0:T(8,128)(2,1)S(1)}, bf16[512,384]{1,0:T(8,128)(2,1)S(1)}, u32[]{:S(2)}, u32[]{:S(2)}) collective-permute-start(bf16[512,384]{1,0:T(8,128)(2,1)S(1)} %add_convert_fusion.6), channel_id=1, source_target_pairs={{0,16},{8,24},{16,0},{24,8},{1,17},{9,25},{17,1},{25,9},{2,18},{10... | collective-permute-start | bytes 1179656 | tf_op jit(solution)/shard_map/ppermute | solution.py:35
  606.1 13.2 %collective-permute-start.57 = (bf16[512,384]{1,0:T(8,128)(2,1)S(1)}, bf16[512,384]{1,0:T(8,128)(2,1)S(1)}, u32[]{:S(2)}, u32[]{:S(2)}) collective-permute-start(bf16[512,384]{1,0:T(8,128)(2,1)S(1)} %add_convert_fusion.5), channel_id=1, source_target_pairs={{0,8},{8,0},{16,24},{24,16},{1,9},{9,1},{17,25},{25,17},{2,10},{10... | collective-permute-start | bytes 1179656 | tf_op jit(solution)/shard_map/ppermute | solution.py:35
  606.6 46.6 %collective-permute-start.80 = (bf16[512,1024]{1,0:T(8,128)(2,1)S(1)}, bf16[512,1024]{1,0:T(8,128)(2,1)}, u32[]{:S(2)}, u32[]{:S(2)}) collective-permute-start(bf16[512,1024]{1,0:T(8,128)(2,1)S(1)} %add_convert_fusion.2), channel_id=1, source_target_pairs={{0,8},{8,0},{16,24},{24,16},{1,9},{9,1},{17,25},{25,17},{2,10},{10... | collective-permute-start | bytes 3145736 | tf_op jit(solution)/shard_map/ppermute | solution.py:35
  (136 other events, 1444.0 us)
Sparse Core Ops, SparseCore 0:
  26.6 58.7 all-gather.1
  351.0 68.3 reduce-scatter.1
  619.7 30.8 all-reduce.9

commit v2 on v1

v2 whole, which is shorter than its diff:
```python
import functools

import jax
import jax.numpy as jnp
from jax import lax
from jax.experimental import pallas as pl
from jax.experimental.pallas import tpu as pltpu
from jax.sharding import PartitionSpec as P

HD = 64
LEN = 1024
EPSILON = 1e-12
SCALE = HD ** (-0.5)
ROWS_DIMS = (((0,), (0,)), ((), ()))
LAST_DIMS = (((1,), (1,)), ((), ()))
BF = jnp.bfloat16
F32 = jnp.float32
PAD = 16
PAIR = 2 * HD
VMEM_BYTES = 48 * 1024 * 1024


def product(left_mat, right_mat):
    return jnp.dot(left_mat, right_mat, preferred_element_type=F32)


def over_rows(left_mat, right_mat):
    return lax.dot_general(left_mat, right_mat, ROWS_DIMS, preferred_element_type=F32)


def against(left_mat, right_mat):
    return lax.dot_general(left_mat, right_mat, LAST_DIMS, preferred_element_type=F32)


def swap(values, axis, bit):
    count = lax.axis_size(axis)
    return lax.ppermute(values, axis, [(i, i ^ bit) for i in range(count)])


def fence(*trees):
    return lax.optimization_barrier(trees)


def whole_block(*shape):
    return pl.BlockSpec(shape, lambda *_: (0,) * len(shape))


def params():
    return pltpu.CompilerParams(vmem_limit_bytes=VMEM_BYTES)


def cost(flops, nbytes, transcendentals=0):
    return pl.CostEstimate(flops=flops, bytes_accessed=nbytes, transcendentals=transcendentals)


def assemble_kernel(groups, local, half, at_ref, *refs):
    mines, others = refs[:groups], refs[groups : 2 * groups]
    w_ref, b_ref = refs[2 * groups :]
    for i in range(groups):
        for k in range(groups):

            @pl.when(at_ref[1 + i] == k)
            def _(i=i, k=k):
                for a in range(3):
                    source = pl.ds(a * local, local)
                    lane = (3 * (i * local // PAIR) + a) * PAIR + i * local % PAIR
                    target = pl.ds(lane, local)
                    top = pl.multiple_of(at_ref[0] * half, half)
                    low = pl.multiple_of((1 - at_ref[0]) * half, half)
                    w_ref[pl.ds(top, half), target] = mines[k][pl.ds(0, half), source]
                    w_ref[pl.ds(low, half), target] = others[k][:, source]
                    b_ref[:, target] = mines[k][pl.ds(half, PAD), source][0:1].astype(F32)


def assemble(at, mines, others, local):
    groups = len(mines)
    half, width3 = others[0].shape
    return pl.pallas_call(
        functools.partial(assemble_kernel, groups, local, half),
        out_shape=(
            jax.ShapeDtypeStruct((2 * half, groups * width3), BF),
            jax.ShapeDtypeStruct((1, groups * width3), F32),
        ),
        grid_spec=pltpu.PrefetchScalarGridSpec(
            num_scalar_prefetch=1,
            grid=(1,),
            in_specs=[whole_block(*m.shape) for m in (*mines, *others)],
            out_specs=(whole_block(2 * half, groups * width3), whole_block(1, groups * width3)),
        ),
        compiler_params=params(),
        cost_estimate=cost(0, 8 * half * groups * width3),
        name="assemble",
    )(at, *mines, *others)


def project_kernel(parts, at_ref, *refs):
    pieces = refs[: parts + 1]
    w_ref, b_ref, joint_ref, mine_ref, other_ref, x_ref = refs[parts + 1 :]
    step = pl.program_id(0)
    for j in range(parts - 1):

        @pl.when(step == j)
        def _(j=j):
            x_ref[...] = pieces[j][...]

    @pl.when(step == parts - 1)
    def _():
        rows = pieces[-1].shape[0]
        x_ref[pl.ds(0, rows), :] = pieces[-2][...]
        x_ref[pl.ds(rows, rows), :] = pieces[-1][...]

    joint_ref[...] = (product(x_ref[...], w_ref[...]) + b_ref[...]).astype(BF)
    half = mine_ref.shape[1]
    mine_ref[...] = x_ref[:, pl.ds(pl.multiple_of(at_ref[0] * half, half), half)]
    other_ref[...] = x_ref[:, pl.ds(pl.multiple_of((1 - at_ref[0]) * half, half), half)]


def project(at, pieces, w_seq, b_seq):
    parts = len(pieces) - 1
    rows, width = pieces[0].shape
    joint_width = w_seq.shape[1]
    half = jax.ShapeDtypeStruct((parts * rows, width // 2), BF)
    half_block = pl.BlockSpec((rows, width // 2), lambda i, s: (i, 0))
    return pl.pallas_call(
        functools.partial(project_kernel, parts),
        out_shape=(jax.ShapeDtypeStruct((parts * rows, joint_width), BF), half, half),
        grid_spec=pltpu.PrefetchScalarGridSpec(
            num_scalar_prefetch=1,
            grid=(parts,),
            in_specs=[whole_block(*p.shape) for p in pieces]
            + [whole_block(*w_seq.shape), whole_block(*b_seq.shape)],
            out_specs=(pl.BlockSpec((rows, joint_width), lambda i, s: (i, 0)), half_block, half_block),
            scratch_shapes=[pltpu.VMEM((rows, width), BF)],
        ),
        compiler_params=params(),
        cost_estimate=cost(2 * parts * rows * width * joint_width, 12 * parts * rows * width),
        name="project",
    )(at, *pieces, w_seq, b_seq)


def attn_forward_kernel(q_ref, k_ref, v_ref, *outs):
    mixed = []
    for head in range(2):
        lanes = pl.ds(head * HD, HD)
        scores = against(q_ref[:, lanes], k_ref[:, lanes])
        top = jnp.max(scores, axis=-1, keepdims=True)
        weights = jnp.exp((scores - top) * SCALE)
        total = jnp.sum(weights, axis=-1, keepdims=True)
        mixed.append(product(weights.astype(BF), v_ref[:, lanes]) / total)
    value = jnp.concatenate(mixed, axis=1).astype(BF)
    for j, out in enumerate(outs):

        @pl.when(pl.program_id(1) == j)
        def _(out=out):
            out[...] = value


def attn_forward(joint, parts):
    rows = joint.shape[0] // parts
    pairs = joint.shape[1] // (3 * PAIR)
    shape = jax.ShapeDtypeStruct((rows, pairs * PAIR), BF)
    return pl.pallas_call(
        attn_forward_kernel,
        out_shape=(shape,) * parts,
        grid=(pairs, parts),
        in_specs=[
            pl.BlockSpec((rows, PAIR), lambda g, i: (i, 3 * g)),
            pl.BlockSpec((parts * rows, PAIR), lambda g, i: (0, 3 * g + 1)),
            pl.BlockSpec((parts * rows, PAIR), lambda g, i: (0, 3 * g + 2)),
        ],
        out_specs=(pl.BlockSpec((rows, PAIR), lambda g, i: (0, g)),) * parts,
        compiler_params=params(),
        cost_estimate=cost(
            16 * joint.shape[0] ** 2 * pairs * PAIR, 3 * joint.size, 2 * pairs * joint.shape[0] ** 2
        ),
        name="attn_forward",
    )(joint, joint, joint)


def attn_backward_kernel(parts, q_ref, k_ref, v_ref, *refs):
    pieces = refs[:parts]
    d_ref, g_ref, kt_ref, dk_acc, dv_acc = refs[-5:]
    step = pl.program_id(0)
    rows = q_ref.shape[0]
    for j, piece in enumerate(pieces):

        @pl.when(step == j)
        def _(piece=piece):
            g_ref[...] = piece[...]

    @pl.when(step == 0)
    def _():
        kt_ref[...] = k_ref[...].T
        dk_acc[...] = jnp.zeros_like(dk_acc)
        dv_acc[...] = jnp.zeros_like(dv_acc)

    dq_parts = []
    for head in range(2):
        lanes = pl.ds(head * HD, HD)
        queries = q_ref[:, lanes]
        grads = g_ref[:, lanes]
        scores = against(k_ref[:, lanes], queries)
        top = jnp.max(scores, axis=0, keepdims=True)
        weights = jnp.exp((scores - top) * SCALE)
        probs = weights * (1.0 / jnp.sum(weights, axis=0, keepdims=True))
        d_probs = against(v_ref[:, lanes], grads)
        row_dot = jnp.sum(probs * d_probs, axis=0, keepdims=True)
        d_scores = (probs * (d_probs - row_dot)).astype(BF)
        dv_acc[:, lanes] += product(probs.astype(BF), grads)
        dk_acc[:, lanes] += product(d_scores, queries)
        dq_parts.append(product(kt_ref[lanes, :], d_scores))
    d_ref[pl.ds(step * rows, rows), pl.ds(0, PAIR)] = (
        jnp.concatenate(dq_parts, axis=0).T * SCALE
    ).astype(BF)

    @pl.when(step == parts - 1)
    def _():
        d_ref[:, pl.ds(PAIR, PAIR)] = (dk_acc[...] * SCALE).astype(BF)
        d_ref[:, pl.ds(2 * PAIR, PAIR)] = dv_acc[...].astype(BF)


def attn_backward(joint, pieces, step, pair, kept):
    parts = len(pieces)
    rows = joint.shape[0] // parts
    return pl.pallas_call(
        functools.partial(attn_backward_kernel, parts),
        out_shape=jax.ShapeDtypeStruct(joint.shape, BF),
        grid=(parts,),
        in_specs=[
            pl.BlockSpec((rows, PAIR), lambda i: (i, 3 * pair)),
            pl.BlockSpec((parts * rows, PAIR), lambda i: (0, 3 * pair + 1)),
            pl.BlockSpec((parts * rows, PAIR), lambda i: (0, 3 * pair + 2)),
        ]
        + [pl.BlockSpec((rows, PAIR), lambda i: (step, pair))] * parts
        + [pl.BlockSpec(memory_space=pl.ANY)] * len(kept),
        out_specs=pl.BlockSpec((parts * rows, 3 * PAIR), lambda i: (0, pair)),
        scratch_shapes=[
            pltpu.VMEM((rows, PAIR), BF),
            pltpu.VMEM((PAIR, parts * rows), BF),
            pltpu.VMEM((parts * rows, PAIR), F32),
            pltpu.VMEM((parts * rows, PAIR), F32),
        ],
        input_output_aliases={3 + parts + i: i for i in range(len(kept))},
        compiler_params=params(),
        cost_estimate=cost(20 * joint.shape[0] ** 2 * PAIR, 14 * joint.shape[0] * PAIR, 2 * joint.shape[0] ** 2),
        name="attn_backward",
    )(joint, joint, joint, *pieces, *kept)


def normed(values):
    row_mean = jnp.mean(values, axis=-1, keepdims=True)
    centred = values - row_mean
    row_var = jnp.mean(centred * centred, axis=-1, keepdims=True)
    scale = lax.rsqrt(row_var + EPSILON)
    return centred * scale, scale


def norm_backward(norm, scale, gain_vec, grads):
    d_norm = grads * gain_vec
    mean_d = jnp.mean(d_norm, axis=-1, keepdims=True)
    mean_dn = jnp.mean(d_norm * norm, axis=-1, keepdims=True)
    return (d_norm - mean_d - norm * mean_dn) * scale


def column_sums(sums_ref, *values):
    @pl.when(pl.program_id(0) == 0)
    def _():
        sums_ref[...] = jnp.zeros_like(sums_ref)

    for index, value in enumerate(values):
        sums_ref[pl.ds(index, 1), :] += jnp.sum(value, axis=0, keepdims=True)


def attend_kernel(micros, parts, at_ref, *refs):
    pieces, placed = refs[: micros * parts], refs[micros * parts : micros * (parts + 1)]
    mine_ref, other_ref, vec_ref, heads_ref, norm_ref, scale_ref, first_ref, low_ref, w_ref = refs[
        micros * (parts + 1) :
    ]

    @pl.when(pl.program_id(0) == 0)
    def _():
        shards_, rows = mine_ref.shape[:2]
        for shard in range(shards_):
            for half, core in ((mine_ref, at_ref[parts]), (other_ref, 1 - at_ref[parts])):
                row = pl.multiple_of((2 * shard + core) * rows, rows)
                w_ref[pl.ds(row, rows), :] = half[shard]

    for m in range(micros):

        @pl.when(pl.program_id(0) == m)
        def _(m=m):
            total = placed[m][...].astype(F32) + vec_ref[0:1, :]
            for j in range(parts):
                piece = pieces[m * parts + j][...]
                cols = piece.shape[1]
                at = pl.multiple_of(at_ref[j] * cols, cols)
                total = total + product(piece, w_ref[pl.ds(at, cols), :])
                heads_ref[:, pl.ds(at, cols)] = piece
            norm, scale = normed(total)
            first = norm * vec_ref[1:2, :] + vec_ref[2:3, :]
            norm_ref[...] = norm
            scale_ref[...] = jnp.broadcast_to(scale, scale_ref.shape)
            first_ref[...] = first + vec_ref[3:4, :]
            low_ref[...] = first.astype(BF)


def attend(at, pieces, placed, w_mine, w_other, vectors):
    micros, parts = len(pieces), len(pieces[0])
    rows, width = placed[0].shape
    flat = [p for group in pieces for p in group]

    def out(cols, dtype):
        return jax.ShapeDtypeStruct((micros * rows, cols), dtype)

    return pl.pallas_call(
        functools.partial(attend_kernel, micros, parts),
        out_shape=(
            out(width, BF),
            out(width, F32),
            out(128, F32),
            out(width, F32),
            out(width, BF),
            jax.ShapeDtypeStruct((width, width), BF),
        ),
        grid_spec=pltpu.PrefetchScalarGridSpec(
            num_scalar_prefetch=1,
            grid=(micros,),
            in_specs=[whole_block(*a.shape) for a in (*flat, *placed, w_mine, w_other, vectors)],
            out_specs=tuple(
                pl.BlockSpec((rows, cols), lambda i, s: (i, 0)) for cols in (width, width, 128, width, width)
            )
            + (whole_block(width, width),),
        ),
        compiler_params=params(),
        cost_estimate=cost(2 * micros * rows * width * width, 20 * micros * rows * width),
        name="attend",
    )(at, *flat, *placed, w_mine, w_other, vectors)


def second_norm_kernel(pre_ref, cot_ref, vec_ref, out_ref, d_ref, low_ref, sums_ref):
    norm, scale = normed(pre_ref[...])
    cot = cot_ref[...]
    out_ref[...] = (norm * vec_ref[0:1, :] + vec_ref[1:2, :]).astype(BF)
    d_pre = norm_backward(norm, scale, vec_ref[0:1, :], cot)
    d_ref[...] = d_pre
    low_ref[...] = d_pre.astype(BF)
    column_sums(sums_ref, d_pre, cot * norm, cot)


def second_norm(pre, cot, vectors):
    rows, width = pre.shape
    block = pl.BlockSpec((128, width), lambda i: (i, 0))
    return pl.pallas_call(
        second_norm_kernel,
        out_shape=(
            jax.ShapeDtypeStruct((rows, width), BF),
            jax.ShapeDtypeStruct((rows, width), F32),
            jax.ShapeDtypeStruct((rows, width), BF),
            jax.ShapeDtypeStruct((8, width), F32),
        ),
        grid=(rows // 128,),
        in_specs=[block, block, whole_block(*vectors.shape)],
        out_specs=(block, block, block, whole_block(8, width)),
        compiler_params=params(),
        cost_estimate=cost(30 * rows * width, 16 * rows * width),
        name="second_norm",
    )(pre, cot, vectors)


def attend_back_kernel(parts, at_ref, d_first_ref, norm_ref, scale_ref, vec_ref, w_ref, *refs):
    d_ref, low_ref, sums_ref = refs[:3]
    outs, low_all = refs[3:-1], refs[-1]
    d_first, norm = d_first_ref[...], norm_ref[...]
    d_pre = norm_backward(norm, scale_ref[:, 0:1], vec_ref[1:2, :], d_first)
    low = d_pre.astype(BF)
    d_ref[...] = d_pre
    low_ref[...] = low
    column_sums(sums_ref, d_pre, d_first * norm, d_first)
    rows = low.shape[0]
    step = pl.program_id(0)
    low_all[pl.ds(pl.multiple_of(step * rows, rows), rows), :] = low

    @pl.when(step == pl.num_programs(0) - 1)
    def _():
        for j in range(parts):
            cols = outs[j].shape[1]
            at = pl.multiple_of(at_ref[j] * cols, cols)
            outs[j][...] = against(low_all[...], w_ref[pl.ds(at, cols), :]).astype(BF)


def attend_back(at, d_first, norm, scale, vectors, w_out, parts):
    rows, width = d_first.shape
    split = 4
    block = pl.BlockSpec((rows // split, width), lambda i, s: (i, 0))
    piece = (rows, width // parts)
    return pl.pallas_call(
        functools.partial(attend_back_kernel, parts),
        out_shape=(
            jax.ShapeDtypeStruct((rows, width), F32),
            jax.ShapeDtypeStruct((rows, width), BF),
            jax.ShapeDtypeStruct((8, width), F32),
        )
        + (jax.ShapeDtypeStruct(piece, BF),) * parts,
        grid_spec=pltpu.PrefetchScalarGridSpec(
            num_scalar_prefetch=1,
            grid=(split,),
            in_specs=[
                block,
                block,
                pl.BlockSpec((rows // split, 128), lambda i, s: (i, 0)),
                whole_block(*vectors.shape),
                whole_block(*w_out.shape),
            ],
            out_specs=(block, block, whole_block(8, width)) + (whole_block(*piece),) * parts,
            scratch_shapes=[pltpu.VMEM((rows, width), BF)],
        ),
        compiler_params=params(),
        cost_estimate=cost(2 * rows * width * width, 20 * rows * width),
        name="attend_back",
    )(at, d_first, norm, scale, vectors, w_out)


def next_blocks(blocks, buf, sem):
    step = pl.program_id(0)

    def start(index, slot):
        for h in range(2):
            pltpu.make_async_copy(blocks[2 * index + h], buf.at[slot, h], sem.at[slot, h]).start()

    @pl.when(step == 0)
    def _():
        start(0, 0)

    for index in range(1, len(blocks) // 2):

        @pl.when(step + 1 == index)
        def _(index=index):
            start(index, index % 2)

    slot = step % 2
    for h in range(2):
        pltpu.make_async_copy(blocks[0], buf.at[slot, h], sem.at[slot, h]).wait()
    return [buf.at[slot, h] for h in range(2)]


def upper_tail(size, falling):
    t = 1.0 / (1.0 + (0.3275911 * 0.5**0.5) * size)
    series = 0.5 * 1.061405429 * t - 0.5 * 1.453152027
    series = series * t + 0.5 * 1.421413741
    series = series * t - 0.5 * 0.284496736
    series = series * t + 0.5 * 0.254829592
    return series * t * falling


def ff_forward_kernel(ff_half, count, first_ref, init_ref, *refs):
    sum_ref, hidden_ref, slope_ref, buf, sem = refs[-5:]
    cut = ff_half + PAD

    @pl.when(pl.program_id(0) == 0)
    def _():
        sum_ref[...] = init_ref[...]

    total = 0.0
    for h, block in enumerate(next_blocks(refs[:count], buf, sem)):
        bias = block[pl.ds(ff_half, PAD), pl.ds(0, ff_half)][0:1].astype(F32)
        upper = against(first_ref[...], block[pl.ds(0, ff_half), :]) + bias
        falling = jnp.exp(-0.5 * upper * upper)
        tail = upper_tail(jnp.abs(upper), falling)
        big_phi = jnp.where(upper > 0.0, 1.0 - tail, tail)
        hidden = (upper * big_phi).astype(BF)
        lanes = pl.ds(h * ff_half, ff_half)
        hidden_ref[:, lanes] = hidden
        slope_ref[:, lanes] = big_phi + upper * (falling * 0.3989422804014327)
        total = total + product(hidden, block[pl.ds(cut, ff_half), :])
    sum_ref[...] += total


def ff_forward(first_low, init, blocks, kept, base, ff_half, total):
    rows, width = first_low.shape
    count = len(blocks)
    column = pl.BlockSpec((rows, 2 * ff_half), lambda i: (0, base // 2 + i))
    anywhere = pl.BlockSpec(memory_space=pl.ANY)
    kept = list(kept)
    return pl.pallas_call(
        functools.partial(ff_forward_kernel, ff_half, count),
        out_shape=(
            jax.ShapeDtypeStruct((rows, width), F32),
            jax.ShapeDtypeStruct((rows, total), BF),
            jax.ShapeDtypeStruct((rows, total), F32),
        ),
        grid=(count // 2,),
        in_specs=[whole_block(rows, width)] * 2 + [anywhere] * (count + len(kept)),
        out_specs=(whole_block(rows, width), column, column),
        scratch_shapes=[
            pltpu.VMEM((2, 2) + blocks[0].shape, BF),
            pltpu.SemaphoreType.DMA((2, 2)),
        ],
        input_output_aliases={2 + count + i: 1 + i for i in range(len(kept))},
        compiler_params=params(),
        cost_estimate=cost(
            8 * rows * width * ff_half * count,
            10 * rows * width + count * ff_half * (4 * width + 6 * rows),
            2 * rows * ff_half * count,
        ),
        name="ff_forward",
    )(first_low, init, *blocks, *kept)


def ff_backward_kernel(ff_half, count, d_fed_ref, init_ref, slope_ref, *refs):
    d_upper_ref, d_first_ref, column_ref, buf, sem = refs[count:]
    cut = ff_half + PAD

    @pl.when(pl.program_id(0) == 0)
    def _():
        d_first_ref[...] = init_ref[...]

    total = 0.0
    for h, block in enumerate(next_blocks(refs[:count], buf, sem)):
        lanes = pl.ds(h * ff_half, ff_half)
        d_hidden = against(d_fed_ref[...], block[pl.ds(cut, ff_half), :])
        d_upper = (d_hidden * slope_ref[:, lanes]).astype(BF)
        d_upper_ref[:, lanes] = d_upper
        column_ref[0, :, lanes] = jnp.sum(d_upper.astype(F32), axis=0, keepdims=True)
        total = total + product(d_upper, block[pl.ds(0, ff_half), :])
    d_first_ref[...] += total


def ff_backward(d_fed, init, slope, blocks, ff_half):
    rows, width = d_fed.shape
    count = len(blocks)
    column = pl.BlockSpec((rows, 2 * ff_half), lambda i: (0, i))
    return pl.pallas_call(
        functools.partial(ff_backward_kernel, ff_half, count),
        out_shape=(
            jax.ShapeDtypeStruct((rows, count * ff_half), BF),
            jax.ShapeDtypeStruct((rows, width), F32),
            jax.ShapeDtypeStruct((count // 2, 1, 2 * ff_half), F32),
        ),
        grid=(count // 2,),
        in_specs=[whole_block(rows, width)] * 2 + [column] + [pl.BlockSpec(memory_space=pl.ANY)] * count,
        out_specs=(column, whole_block(rows, width), pl.BlockSpec((1, 1, 2 * ff_half), lambda i: (i, 0, 0))),
        scratch_shapes=[
            pltpu.VMEM((2, 2) + blocks[0].shape, BF),
            pltpu.SemaphoreType.DMA((2, 2)),
        ],
        compiler_params=params(),
        cost_estimate=cost(
            4 * rows * width * ff_half * count,
            10 * rows * width + count * ff_half * (4 * width + 6 * rows),
        ),
        name="ff_backward",
    )(d_fed, init, slope, *blocks)


def ff_grad_kernel(ff_half, spans, splits, joined, index_ref, first_ref, fed_ref, *refs):
    count = len(spans)
    total = splits[-1]
    ups, hiddens, outs = (refs[i * count : (i + 1) * count] for i in range(3))
    adds = list(refs[3 * count : 3 * count + sum(map(len, spans))])
    results = refs[3 * count + len(adds) :]
    pieces = len(splits) - 1
    for index in range(count):
        mine = [adds.pop(0) for _ in spans[index]]
        values = (
            (0, ff_half, lambda: over_rows(ups[index][...], first_ref[...])),
            (ff_half, 2 * ff_half, lambda: over_rows(hiddens[index][...], fed_ref[...])),
            (2 * ff_half, total, lambda: outs[index][...].astype(F32)),
        )
        for low, high, value in values:
            share = value()
            for (start, stop), add in zip(spans[index], mine):
                if start <= low and high <= stop:
                    share = share + add[pl.ds(low - start, high - low), :].astype(F32)
            for piece in range(pieces):
                if splits[piece] <= low and high <= splits[piece + 1]:
                    target = results[0 if joined else index * pieces + piece]
                    row = low - splits[piece] + joined * index * total
                    target[pl.ds(row, high - low), :] = share.astype(BF)


def ff_grad(d_upper, hidden, first_low, d_fed, d_out, items, out_index, ff_half, out_half, cuts=(), joined=False):
    rows, width = first_low.shape
    cols = width // 2
    count = len(items)
    total = 2 * ff_half + out_half
    splits = (0, *cuts, total)
    lanes = pl.BlockSpec((rows, cols), lambda i, s: (0, i))
    adds = [add for _, arrived in items for add in arrived]
    spans = tuple(tuple((start, start + height) for start, height, _, _ in arrived) for _, arrived in items)

    def column(block):
        return pl.BlockSpec((rows, ff_half), lambda i, s: (0, block))

    def out_rows(j):
        return pl.BlockSpec((out_half, cols), lambda i, s: (s[j], i))

    def lane_block(height, at=0):
        return pl.BlockSpec((height, cols), lambda i, s: (at, i))

    columns = [column(block) for block, _ in items]
    heights = [count * total] if joined else [b - a for a, b in zip(splits, splits[1:])] * count
    return pl.pallas_call(
        functools.partial(ff_grad_kernel, ff_half, spans, splits, int(joined)),
        out_shape=tuple(jax.ShapeDtypeStruct((height, width), BF) for height in heights),
        grid_spec=pltpu.PrefetchScalarGridSpec(
            num_scalar_prefetch=1,
            grid=(2,),
            in_specs=[lanes, lanes]
            + columns
            + columns
            + [out_rows(j) for j in range(count)]
            + [lane_block(height, at) for _, height, _, at in adds],
            out_specs=tuple(lane_block(height) for height in heights),
        ),
        compiler_params=params(),
        cost_estimate=cost(
            4 * rows * width * ff_half * count,
            4 * rows * width + count * 4 * rows * ff_half + (count + len(adds)) * 2 * total * width,
        ),
        name="ff_grad",
    )(
        out_index, first_low, d_fed, *[d_upper] * count, *[hidden] * count, *[d_out] * count,
        *[array for _, _, array, _ in adds],
    )


def shards(
    embedded,
    token_table,
    masked_pos,
    replace_ids,
    w_query,
    b_query,
    w_key,
    w_value,
    b_value,
    w_out,
    b_out,
    ln1_gain,
    ln1_bias,
    w_up,
    b_up,
    w_down,
    b_down,
    ln2_gain,
    ln2_bias,
    grad_masked,
):
    rank = lax.axis_index("tensor")
    count = lax.axis_size("tensor")
    dp_count = lax.axis_size("dp")
    core = lax.axis_index("dp") % 2
    micro_count, row_count, width = embedded.shape
    local_width = w_query.shape[1]
    ff_local = w_up.shape[1]
    vocab_count = token_table.shape[0]
    parts = LEN // row_count
    groups = count // parts
    part = rank % parts
    group = rank // parts
    part_width = width // parts
    pairs = part_width // PAIR
    half_count = row_count // 2
    half_rows = width // 2
    ff_half = ff_local // 2
    out_half = local_width // 2
    cut = ff_half + PAD
    own_first = core == 0
    micros = range(micro_count)

    def by_core(mine, other, axis=0):
        return jnp.where(
            own_first,
            jnp.concatenate([mine, other], axis=axis),
            jnp.concatenate([other, mine], axis=axis),
        )

    order = list(range(0, count, 2)) + list(range(count - 1, 0, -2))
    ring_fw = [(order[i], order[(i + 1) % count]) for i in range(count)]
    ring_bw = [(b, a) for a, b in ring_fw]
    far = count // 2
    ring_pos = jnp.where(rank % 2 == 0, rank // 2, count - 1 - rank // 2)
    offsets = [0] + [sign * s for s in range(1, far) for sign in (-1, 1)] + [far]
    slots = {o: index for index, o in enumerate(offsets)}

    def forward(values):
        return lax.ppermute(values, "tensor", ring_fw)

    def backward(values):
        return lax.ppermute(values, "tensor", ring_bw)

    part_order = jnp.stack([part ^ j for j in range(parts)]).astype(jnp.int32)

    slot_pos = lax.dynamic_index_in_dim(masked_pos, group, 1, keepdims=False)
    slot_ids = lax.dynamic_index_in_dim(replace_ids, group, 1, keepdims=False)
    slot_grads = lax.dynamic_index_in_dim(grad_masked, group, 1, keepdims=False)
    vocab_iota = jnp.arange(vocab_count, dtype=jnp.int32)

    def replacement(positions, step):
        matches = positions[:, None] == slot_pos[step][None, :]
        replaced = jnp.any(matches, axis=1)
        row_ids = jnp.sum(jnp.where(matches, slot_ids[step][None, :], 0), axis=1)
        hot = (row_ids[:, None] == vocab_iota[None, :]) & replaced[:, None]
        return matches, replaced, hot

    row_iota = jnp.arange(row_count, dtype=jnp.int32)
    placed, replaced_list, hots, cots, seq_hots = [], [], [], [], []
    for step in micros:
        matches, replaced, hot = replacement(part * row_count + row_iota, step)
        inserted = product(hot.astype(BF), token_table)
        placed.append(jnp.where(replaced[:, None], inserted, embedded[step].astype(F32)).astype(BF))
        replaced_list.append(replaced)
        hots.append(hot.astype(F32))
        cots.append(product(matches.astype(BF), slot_grads[step]))
        seq_pos = jnp.concatenate([(part ^ j) * row_count + row_iota for j in range(parts)])
        seq_hots.append(replacement(seq_pos, step)[2].astype(BF))

    joint_half = jnp.concatenate(
        [
            lax.dynamic_slice_in_dim(
                jnp.concatenate([w_query, w_key, w_value], axis=1), core * half_rows, half_rows, 0
            ),
            jnp.pad(
                jnp.concatenate([b_query, jnp.zeros_like(b_query), b_value])[None, :],
                ((0, PAD - 1), (0, 0)),
            ),
        ],
        axis=0,
    )
    spread = [
        [(groups * p + i, p + parts * ((i + k) % groups)) for p in range(parts) for i in range(groups)]
        for k in range(groups)
    ]
    piece = jnp.concatenate(
        [
            lax.dynamic_slice_in_dim(w_up.T, core * ff_half, ff_half, 0),
            jnp.pad(
                lax.dynamic_slice_in_dim(b_up, core * ff_half, ff_half, 0)[None, :],
                ((0, PAD - 1), (0, width - ff_half)),
            ),
            lax.dynamic_slice_in_dim(w_down, core * ff_half, ff_half, 0),
        ],
        axis=0,
    )

    w_mine = [lax.ppermute(joint_half, "tensor", spread[k]) for k in range(groups)]
    ones = [swap(placed[0], "tensor", 1)]
    twos = [swap(placed[0], "tensor", 2)]
    ones, twos, w_mine, placed, piece, cots, w_out = fence(ones, twos, w_mine, placed, piece, cots, w_out)
    w_out_half = lax.all_gather(
        lax.dynamic_slice_in_dim(w_out, core * out_half, out_half, 0), "tensor", axis=0
    )
    w_other = [swap(w[:half_rows], "dp", 1) for w in w_mine]
    w_seq, b_seq = assemble(
        jnp.stack([core] + [(group - i) % groups for i in range(groups)]).astype(jnp.int32),
        w_mine,
        w_other,
        local_width,
    )

    joints, x_mine, x_other, heads = [], [], [], []
    near = [piece[:cut], piece[cut:]]
    arrived = []
    at_core = core[None].astype(jnp.int32)
    for step in micros:
        threes = (swap(ones[step][:half_count], "tensor", 2), swap(twos[step][half_count:], "tensor", 1))
        rows = [placed[step], ones[step], twos[step], *threes]
        if step + 1 < micro_count:
            ones.append(swap(placed[step + 1], "tensor", 1))
            twos.append(swap(placed[step + 1], "tensor", 2))
        moved = (forward(near[step]), backward(near[step]))
        joint, mine, other = project(at_core, rows, w_seq, b_seq)
        pieces = attn_forward(joint, parts)
        joints.append(joint)
        x_mine.append(mine)
        x_other.append(other)
        ones, twos, moved, pieces, near = fence(ones, twos, moved, pieces, near)
        arrived.append(moved)
        heads.append([pieces[0]] + [swap(pieces[j], "tensor", j) for j in range(1, parts)])
    fw, bw = (jnp.concatenate([arrived[0][d], arrived[1][d]], axis=0) for d in range(2))
    heads, fw, bw, w_out_half = fence(heads, fw, bw, w_out_half)
    w_out_other = swap(w_out_half, "dp", 1)
    blocks = [piece, swap(piece, "dp", 1), fw, swap(fw, "dp", 1), bw, swap(bw, "dp", 1)]

    vectors_one = jnp.stack([b_out, ln1_gain, ln1_bias, b_down] + [b_out] * 4).astype(F32)
    heads_out, norm_one, scale_one, pre_two, first_low, w_out_all = attend(
        jnp.concatenate([part_order, at_core]), heads, placed, w_out_half, w_out_other, vectors_one
    )

    kept = ()

    def work_on(s):
        at = 0 if s == 0 else 4 * s - 2
        return ff_forward(
            first_low, pre_two, blocks[at : at + (2 if s in (0, far) else 4)], kept, at, ff_half,
            2 * count * ff_half,
        )

    for s in range(2, far + 1):
        if s < far:
            moved = [forward(fw), backward(bw)]
        else:
            moved = [jnp.concatenate([forward(fw[:cut]), backward(bw[cut:])], axis=0)]
        for t in (0, 1) if s == 2 else (s - 1,):
            pre_two, *kept = work_on(t)
        if s < far:
            moved, pre_two, kept = fence(moved, pre_two, kept)
            fw, bw = moved
        for block in moved:
            blocks += [block, swap(block, "dp", 1)]
    pre_two, *kept = work_on(far)
    hidden_low, slope = kept

    vectors_two = jnp.stack([ln2_gain, ln2_bias] + [ln2_bias] * 6).astype(F32)
    layer_out, d_pre_two, d_fed, sums_two = second_norm(pre_two, jnp.concatenate(cots, axis=0), vectors_two)
    d_upper, d_first, rel_b_up = ff_backward(d_fed, d_pre_two, slope, blocks, ff_half)
    d_pre_one, d_attended, sums_one, *d_heads = attend_back(
        part_order, d_first, norm_one, scale_one, vectors_one, w_out_all, parts
    )
    d_out = over_rows(heads_out, d_attended).astype(BF)
    seq_grads = [d_heads[0]] + [swap(d_heads[j], "tensor", j) for j in range(1, parts)]

    order_array = jnp.array(order, jnp.int32)

    total = 2 * ff_half + out_half

    def ff_blocks(items, other, cuts=()):
        index = [2 * order_array[(ring_pos + o) % count] + (1 - core if other else core) for o, _ in items]
        result = ff_grad(
            d_upper, hidden_low, first_low, d_fed, d_out,
            [(2 * slots[o] + other, arrived) for o, arrived in items],
            jnp.stack(index).astype(jnp.int32), ff_half, out_half, cuts, bool(other),
        )
        return result[0] if other else result

    d_joints = [() for _ in micros]
    work = [(m, g) for m in micros for g in range(pairs)]

    def row_share(step, j, low=0, high=row_count):
        rows = d_joints[step][0][j * row_count + low : j * row_count + high]
        return against(rows, w_seq)

    def diagonal(step):
        share = row_share(step, 3).astype(BF)
        return (swap(share[:half_count], "tensor", 2), swap(share[half_count:], "tensor", 1))

    def sides(step, arrived):
        to_two, to_one = (a.astype(F32) for a in arrived)
        via_one = row_share(step, 1) + jnp.pad(to_two, ((0, half_count), (0, 0)))
        via_two = row_share(step, 2) + jnp.pad(to_one, ((half_count, 0), (0, 0)))
        return (swap(via_one.astype(BF), "tensor", 1), swap(via_two.astype(BF), "tensor", 2))

    def input_grad(step, arrived):
        mine = slice(step * row_count, (step + 1) * row_count)
        total = d_pre_one[mine] + row_share(step, 0) + arrived[0].astype(F32) + arrived[1].astype(F32)
        return jnp.where(replaced_list[step][:, None], 0.0, total)

    others = swap(ff_blocks([(far, [])], 1), "dp", 1)
    next_others = ff_blocks([(far - 1, []), (1 - far, [])], 1)
    parcel = ff_blocks([(far, [(0, total, others, 0)])], 0, (ff_half,))
    seq_grads, parcel, next_others = fence(seq_grads, parcel, next_others)
    partial = [() for _ in micros]
    for index, s in enumerate(range(far, 0, -1)):
        joints, d_joints, d_upper, parcel = fence(joints, d_joints, d_upper, parcel)
        moved = [forward(parcel[0]), backward(parcel[1])]
        others = swap(next_others, "dp", 1)
        for m in micros:
            if index == pairs * (m + 1):
                partial[m] = diagonal(m)
            elif index == pairs * (m + 1) + 1:
                partial[m] = sides(m, partial[m])
        next_others = ()
        if s > 1:
            next_others = ff_blocks([(s - 2, []), (2 - s, [])] if s > 2 else [(0, [])], 1)
        if work:
            m, g = work.pop(0)
            d_joints[m] = (attn_backward(joints[m], seq_grads, m, g, d_joints[m]),)
        moved, others, next_others, d_joints, partial = fence(moved, others, next_others, d_joints, partial)
        if s > 1:
            heights = (ff_half, total - ff_half) if s == far else (total, total)
            starts = (0, ff_half) if s == far else (0, 0)
            parcel = ff_blocks(
                [
                    (s - 1, [(0, total, others, 0), (starts[0], heights[0], moved[0], 0)]),
                    (1 - s, [(0, total, others, 1), (starts[1], heights[1], moved[1], 0)]),
                ],
                0,
            )
    ff_sum = ff_blocks([(0, [(0, total, others, 0), (0, total, moved[0], 0), (0, total, moved[1], 0)])], 0)[0]

    def over_dp(values):
        bit = 2
        while bit < dp_count:
            values = (values.astype(F32) + swap(values, "dp", bit).astype(F32)).astype(BF)
            bit *= 2
        return values

    def over_bits(values, axis, low, high):
        while low < high:
            if 2 * low < high:
                near, side, both = (swap(values, axis, bit) for bit in (low, 2 * low, 3 * low))
                values = (values + near) + (side + both)
            else:
                values = values + swap(values, axis, low)
            low *= 4
        return values

    rel_b_up = rel_b_up.reshape(count, 2, ff_half)
    rel_b_up = jnp.where(own_first, rel_b_up, rel_b_up[:, ::-1]).reshape(count, ff_local)
    slot_of = [0] * count
    for o, slot in slots.items():
        slot_of[o % count] = slot
    place = jnp.array([order.index(s) for s in range(count)], jnp.int32)
    wanted = jnp.array(slot_of, jnp.int32)[(place - ring_pos) % count]
    all_b_up = rel_b_up[wanted].reshape(-1, width)
    b_rows = all_b_up.shape[0]
    table = jnp.zeros((vocab_count, width), F32)
    for step in micros:
        table = table + lax.dot_general(
            hots[step],
            d_pre_one[step * row_count : (step + 1) * row_count],
            ROWS_DIMS,
            precision=lax.Precision.HIGHEST,
            preferred_element_type=F32,
        )
    hot_sum = sum(over_rows(seq_hots[m], d_joints[m][0]) for m in micros)
    table = table + lax.dot_general(
        hot_sum,
        w_seq.astype(F32),
        LAST_DIMS,
        precision=lax.Precision.HIGHEST,
        preferred_element_type=F32,
    )
    d_b_seq = sum(jnp.sum(d_joints[m][0].astype(F32), axis=0) for m in micros)
    empty = jnp.zeros((width,), F32)
    d_b_query, d_b_value = (
        lax.dynamic_update_slice_in_dim(
            empty,
            jnp.concatenate([d_b_seq[(3 * g + a) * PAIR : (3 * g + a + 1) * PAIR] for g in range(pairs)]),
            part * part_width,
            0,
        )
        for a in (0, 2)
    )
    small = jnp.concatenate(
        [table, d_b_query[None], d_b_value[None], sums_one[:3], sums_two[:3], all_b_up], axis=0
    )

    last = micro_count - 1
    other_half = sum(over_rows(x_other[m], d_joints[m][0]) for m in micros).astype(BF)
    other_half = swap(other_half, "dp", 1)
    if far < 2 + pairs * micro_count:
        partial[last] = diagonal(last)
    small = over_bits(small, "dp", 1, dp_count)
    my_half = sum(over_rows(x_mine[m], d_joints[m][0]) for m in micros)
    my_half = (my_half + other_half.astype(F32)).astype(BF)
    my_half, ff_sum, partial, small = fence(my_half, ff_sum, partial, small)

    if local_width != PAIR:
        columns = [
            jnp.concatenate(
                [my_half[:, (3 * g + a) * PAIR : (3 * g + a + 1) * PAIR] for g in range(pairs)], axis=1
            )
            for a in range(3)
        ]
        my_half = jnp.concatenate(
            [c[:, i * local_width : (i + 1) * local_width] for i in range(groups) for c in columns], axis=1
        )
    joint_sum = sum(
        lax.ppermute(
            lax.dynamic_slice_in_dim(
                my_half, (group - k) % groups * 3 * local_width, 3 * local_width, 1
            ),
            "tensor",
            [(b, a) for a, b in spread[k]],
        ).astype(F32)
        for k in range(groups)
    ).astype(BF)
    if far < 2 + pairs * micro_count:
        partial[last] = sides(last, partial[last])
    ff_sum = over_dp(ff_sum)
    small = over_bits(small, "tensor", 1, min(4, count))
    joint_sum, ff_sum, partial, small = fence(joint_sum, ff_sum, partial, small)

    ff_other = swap(ff_sum, "dp", 1)
    joint_sum = over_dp(joint_sum)
    small = over_bits(small, "tensor", 4, count)
    joint_sum, small, ff_other = fence(joint_sum, small, ff_other)
    grad_joint = by_core(joint_sum, swap(joint_sum, "dp", 1)).astype(F32)
    grad_w_up = by_core(ff_sum[:ff_half], ff_other[:ff_half]).astype(F32).T
    grad_w_down = by_core(ff_sum[ff_half : 2 * ff_half], ff_other[ff_half : 2 * ff_half]).astype(F32)
    grad_w_out = by_core(ff_sum[2 * ff_half :], ff_other[2 * ff_half :]).astype(F32)
    grad_list = [input_grad(m, partial[m]) for m in micros]
    grad_b_query, grad_b_value = (
        lax.dynamic_slice_in_dim(small[vocab_count + i], rank * local_width, local_width, 0) for i in range(2)
    )
    grad_b_out, grad_gone, grad_bone, grad_b_down, grad_gtwo, grad_btwo = (
        small[vocab_count + 2 + i] for i in range(6)
    )
    grad_b_up = lax.dynamic_slice_in_dim(small[vocab_count + 8 :].reshape(-1), rank * ff_local, ff_local, 0)

    return (
        layer_out.reshape(micro_count, row_count, width),
        jnp.stack(grad_list),
        small[:vocab_count],
        grad_joint[:, :local_width],
        grad_b_query,
        grad_joint[:, local_width : 2 * local_width],
        grad_joint[:, 2 * local_width :],
        grad_b_value,
        grad_w_out,
        grad_b_out,
        grad_gone,
        grad_bone,
        grad_w_up,
        grad_b_up,
        grad_w_down,
        grad_b_down,
        grad_gtwo,
        grad_btwo,
    )


def solution(mesh):
    return jax.shard_map(
        shards,
        mesh=mesh,
        in_specs=(
            P(None, ("dp", "tensor"), None),
            P(),
            P(None, "dp", None),
            P(None, "dp", None),
            P(None, "tensor"),
            P("tensor"),
            P(None, "tensor"),
            P(None, "tensor"),
            P("tensor"),
            P("tensor", None),
            P(),
            P(),
            P(),
            P(None, "tensor"),
            P("tensor"),
            P("tensor", None),
            P(),
            P(),
            P(),
            P(None, "dp", None, None),
        ),
        out_specs=(
            P(None, ("dp", "tensor"), None),
            P(None, ("dp", "tensor"), None),
            P(),
            P(None, "tensor"),
            P("tensor"),
            P(None, "tensor"),
            P(None, "tensor"),
            P("tensor"),
            P("tensor", None),
            P(),
            P(),
            P(),
            P(None, "tensor"),
            P("tensor"),
            P("tensor", None),
            P(),
            P(),
            P(),
        ),
        check_vma=False,
    )
```

time: 678 us -> 532 us (0.78)
  Pallas kernels: 66.8 us -> 192 us
  waiting for transfers between devices: 223 us -> 99.4 us
  matrix products: 127 us -> 29.6 us
  other arithmetic: 57.6 us -> 15.8 us
  local copies, waits for them, and re-layouts: 100 us -> 66.4 us
  starting transfers between devices: 76.4 us -> 96.8 us
    pallas_call x4 -> x28, Pallas kernels: 66.8 us -> 192 us  [the longest x4 45.1 us: attn_backward(): pl.pallas_call(functools.partial(attn_backward_kernel, parts), out_shape=...]
    ppermute x8 -> x9, waiting for transfers between devices: 54.2 us -> 2.86 us  [backward(): return lax.ppermute(values, 'tensor', ring_bw)]
    ppermute x61 -> x53, waiting for transfers between devices: 116 us -> 66.5 us  [swap(): return lax.ppermute(values, axis, [(i, i ^ bit) for i in range(count)])]
    dot_general x37 -> x7, matrix products: 52.6 us -> 7.68 us  [over_rows(): lax.dot_general(left_mat, right_mat, ROWS_DIMS, preferred_element_type=F32)]
    dot_general x5 -> x8, matrix products: 42.6 us -> 10.5 us  [against(): lax.dot_general(left_mat, right_mat, LAST_DIMS, preferred_element_type=F32)]
    psum x1 -> x0, waiting for transfers between devices: 29.9 us -> none  [shards(): lax.psum(lax.psum_scatter(over_rows(heads_out, d_attended).astype(BF), 't...]
    dot_general x9 -> x4, matrix products: 29.3 us -> 6.42 us  [product(): return jnp.dot(left_mat, right_mat, preferred_element_type=F32)]
    ppermute x61 -> x53, starting transfers between devices: 53.1 us -> 69.7 us  [swap(): return lax.ppermute(values, axis, [(i, i ^ bit) for i in range(count)])]
  transfers between devices with their start and end apart: 84 -> 76, of which waited for: 27 -> 23; matrix products, arithmetic and copies ran while one was open for 24% -> 11% of each run, Pallas kernels for 10% -> 28%
where the time goes in v2:
time: 532 us; the launch traced here: 521 us
  Pallas kernels  192 us (36%)
  waiting for transfers between devices  99.4 us (19%)
  starting transfers between devices  96.8 us (18%)
  local copies, waits for them, and re-layouts  66.4 us (12%)
  matrix products  29.6 us (6%)
  between operations  21.4 us (4%)
  other arithmetic  15.8 us (3%)
    ppermute x53, starting transfers between devices, swap(): return lax.ppermute(values, axis, [(i, i ^ bit) for i in range(count)])  69.7 us
    ppermute x53, waiting for transfers between devices, swap(): return lax.ppermute(values, axis, [(i, i ^ bit) for i in range(count)])  66.5 us
    pallas_call x4, Pallas kernels, attn_backward(): pl.pallas_call(functools.partial(attn_backward_kernel, parts), out_shape=...  45.1 us
    pallas_call x10, Pallas kernels, ff_grad(): pl.pallas_call(functools.partial(ff_grad_kernel, ff_half, spans, splits,...  42.3 us
    unnamed x242, local copies, waits for them, and re-layouts  41.8 us
    pallas_call x5, Pallas kernels, ff_forward(): pl.pallas_call(functools.partial(ff_forward_kernel, ff_half, count), out_...  37.6 us
    ppermute x9, waiting for transfers between devices, forward(): return lax.ppermute(values, 'tensor', ring_fw)  29.1 us
    pallas_call x2, Pallas kernels, attn_forward(): pl.pallas_call(attn_forward_kernel, out_shape=(shape,) * parts, grid=(pai...  22.1 us
  transfers between devices with their start and end apart: 76, of which 23 were waited for; matrix products, arithmetic and copies ran while one was open for 11% of the time, Pallas kernels for 28%

profile of v2, /device:TPU:0, one launch (start us, length us, event | category | flops | bytes accessed | tf_op | source)
XLA Modules:
  0.0 521.4 jit_solution(14887690665402467874)
XLA Ops:
  10.1 3.0 collective-permute-start
  18.9 2.9 collective-permute-start.3
  21.9 4.0 constant_dynamic-slice_fusion.8
  27.4 2.2 fusion.15.refs_0_.refs_9_
  38.2 6.9 %collective-permute-start.8 = (bf16[128,1024]{1,0:T(8,128)(2,1)}, bf16[128,1024]{1,0:T(8,128)(2,1)}, u32[]{:S(2)}, u32[]{:S(2)}) collective-permute-start(bf16[128,1024]{1,0:T(8,128)(2,1)} %slice.192), channel_id=1, source_target_pairs={{0,2},{1,3},{2,0},{3,1},{4,6},{5,7},{6,4},{7,5},{8,10},{9,11},{10,... | collective-permute-start | bytes 786440 | tf_op jit(solution)/shard_map/ppermute | solution.py:37
  47.7 2.1 collective-permute-start.7
  49.9 2.0 collective-permute-start.4
  56.3 4.5 project.2
  61.8 11.1 %attn_forward.2 = (bf16[256,256]{1,0:T(8,128)(2,1)S(1)}, bf16[256,256]{1,0:T(8,128)(2,1)S(1)}, bf16[256,256]{1,0:T(8,128)(2,1)S(1)}, bf16[256,256]{1,0:T(8,128)(2,1)S(1)}) custom-call(bf16[1024,768]{1,0:T(8,128)(2,1)S(1)} %get-tuple-element.304.q_ref.k_ref.v_ref, bf16[1024,768]{1,0:T(8,128)(2,1)S(1)} %get-tuple-element.304.q_ref.k_ref.v_ref, ...), custom_call_target="tpu_custom_call" | custom-call | flops 4294967296 | bytes 2359296 | tf_op jit(solution)/shard_map/attn_forward/pallas_call | solution.py:162
  73.6 9.6 %collective-permute-done.4.refs_1_ = bf16[256,1024]{1,0:T(8,128)(2,1)S(1)} collective-permute-done((bf16[256,1024]{1,0:T(8,128)(2,1)}, bf16[256,1024]{1,0:T(8,128)(2,1)S(1)}, u32[]{:S(2)}, u32[]{:S(2)}) %collective-permute-start.4) | collective-permute-done | bytes 524320 | tf_op jit(solution)/shard_map/ppermute | solution.py:37
  83.2 2.1 collective-permute-start.17
  85.4 2.0 collective-permute-start.16
  87.4 2.0 collective-permute-start.12
  89.4 5.5 %collective-permute-done.17.refs_3_ = bf16[128,1024]{1,0:T(8,128)(2,1)S(1)} collective-permute-done((bf16[128,1024]{1,0:T(8,128)(2,1)S(1)}, bf16[128,1024]{1,0:T(8,128)(2,1)S(1)}, u32[]{:S(2)}, u32[]{:S(2)}) %collective-permute-start.17) | collective-permute-done | bytes 262176 | tf_op jit(solution)/shard_map/ppermute | solution.py:37
  94.9 2.1 collective-permute-start.13
  97.6 4.1 project.3
  102.7 11.1 %attn_forward.3 = (bf16[256,256]{1,0:T(8,128)(2,1)S(1)}, bf16[256,256]{1,0:T(8,128)(2,1)S(1)}, bf16[256,256]{1,0:T(8,128)(2,1)S(1)}, bf16[256,256]{1,0:T(8,128)(2,1)S(1)}) custom-call(bf16[1024,768]{1,0:T(8,128)(2,1)S(1)} %get-tuple-element.334.q_ref.k_ref.v_ref, bf16[1024,768]{1,0:T(8,128)(2,1)S(1)} %get-tuple-element.334.q_ref.k_ref.v_ref, ...), custom_call_target="tpu_custom_call" | custom-call | flops 4294967296 | bytes 2359296 | tf_op jit(solution)/shard_map/attn_forward/pallas_call | solution.py:162
  114.8 2.0 collective-permute-start.20
  120.4 3.1 collective-permute-done.21.refs_7_
  125.2 2.0 collective-permute-done.22.refs_11_
  137.2 6.4 %attend.1 = (bf16[512,1024]{1,0:T(8,128)(2,1)S(1)}, f32[512,1024]{1,0:T(8,128)}, f32[512,128]{1,0:T(8,128)S(1)}, f32[512,1024]{1,0:T(8,128)}, bf16[512,1024]{1,0:T(8,128)(2,1)S(1)}, /*index=5*/bf16[1024,1024]{1,0:T(8,128)(2,1)}) custom-call(s32[5]{0:T(128)S(1)} %concatenate.65.at_ref, bf16[256,256]{1,0:T(8,128)(2,1)S(1)} %copy-done.40, ...), custom_call_target="tpu_custom_call" | custom-call | flops 1073741824 | bytes 10485760 | tf_op jit(solution)/shard_map/attend/pallas_call | solution.py:315
  144.6 5.9 %ff_forward.5 = (f32[512,1024]{1,0:T(8,128)S(1)}, bf16[512,4096]{1,0:T(8,128)(2,1)}, f32[512,4096]{1,0:T(8,128)}) custom-call(bf16[512,1024]{1,0:T(8,128)(2,1)S(1)} %get-tuple-element.238.first_ref, f32[512,1024]{1,0:T(8,128)} %get-tuple-element.241.init_ref, bf16[528,1024]{1,0:T(8,128)(2,1)S(1)} %copy-done.30, bf16[528,1024]{1,0:T(8,128)(2,1)} %collective-permute-done.25.refs_1_), custom_call_target="tpu_custom_call" | custom-call | flops 2147483648 | bytes 8912896 | tf_op jit(solution)/shard_map/ff_forward/pallas_call | solution.py:484
  151.8 8.5 %ff_forward.6 = (f32[512,1024]{1,0:T(8,128)}, bf16[512,4096]{1,0:T(8,128)(2,1)}, f32[512,4096]{1,0:T(8,128)}) custom-call(bf16[512,1024]{1,0:T(8,128)(2,1)S(1)} %get-tuple-element.238.first_ref, f32[512,1024]{1,0:T(8,128)} %copy-done.33, bf16[528,1024]{1,0:T(8,128)(2,1)S(1)} %pad_maximum_fusion.2.refs_0_.refs_2_, ...), custom_call_target="tpu_custom_call", output_to_operand_aliasing={{1}: (6, {}), {2}: (7, {})} | custom-call | flops 4294967296 | bytes 12582912 | tf_op jit(solution)/shard_map/ff_forward/pallas_call | solution.py:484
  161.0 1.9 collective-permute-start.28
  164.9 8.6 %ff_forward.7 = (f32[512,1024]{1,0:T(8,128)}, bf16[512,4096]{1,0:T(8,128)(2,1)}, f32[512,4096]{1,0:T(8,128)}) custom-call(bf16[512,1024]{1,0:T(8,128)(2,1)S(1)} %get-tuple-element.238.first_ref, f32[512,1024]{1,0:T(8,128)} %get-tuple-element.250.init_ref, ...), custom_call_target="tpu_custom_call", output_to_operand_aliasing={{1}: (6, {}), {2}: (7, {})} | custom-call | flops 4294967296 | bytes 12582912 | tf_op jit(solution)/shard_map/ff_forward/pallas_call | solution.py:484
  173.6 13.5 %collective-permute-done.28.refs_0_.refs_10_ = bf16[528,1024]{1,0:T(8,128)(2,1)S(1)} collective-permute-done((bf16[528,1024]{1,0:T(8,128)(2,1)}, bf16[528,1024]{1,0:T(8,128)(2,1)S(1)}, u32[]{:S(2)}, u32[]{:S(2)}) %collective-permute-start.28) | collective-permute-done | bytes 1081376 | tf_op jit(solution)/shard_map/ppermute | solution.py:687
  190.3 2.2 collective-permute-start.35
  193.0 9.4 %collective-permute-done.34 = bf16[272,1024]{1,0:T(8,128)(2,1)S(1)} collective-permute-done((bf16[272,1024]{1,0:T(8,128)(2,1)S(1)}, bf16[272,1024]{1,0:T(8,128)(2,1)S(1)}, u32[]{:S(2)}, u32[]{:S(2)}) %collective-permute-start.34) | collective-permute-done | bytes 557088 | tf_op jit(solution)/shard_map/ppermute | solution.py:687
  207.2 3.2 pad_maximum_fusion.cot_ref
  210.4 8.5 %ff_forward.8 = (f32[512,1024]{1,0:T(8,128)}, bf16[512,4096]{1,0:T(8,128)(2,1)}, f32[512,4096]{1,0:T(8,128)}) custom-call(bf16[512,1024]{1,0:T(8,128)(2,1)S(1)} %get-tuple-element.238.first_ref, f32[512,1024]{1,0:T(8,128)} %get-tuple-element.256.init_ref, ...), custom_call_target="tpu_custom_call", output_to_operand_aliasing={{1}: (6, {}), {2}: (7, {})} | custom-call | flops 4294967296 | bytes 12582912 | tf_op jit(solution)/shard_map/ff_forward/pallas_call | solution.py:484
  218.9 6.1 %ff_forward.9 = (f32[512,1024]{1,0:T(8,128)S(1)}, bf16[512,4096]{1,0:T(8,128)(2,1)}, f32[512,4096]{1,0:T(8,128)}) custom-call(bf16[512,1024]{1,0:T(8,128)(2,1)S(1)} %get-tuple-element.238.first_ref, f32[512,1024]{1,0:T(8,128)} %get-tuple-element.261.init_ref, ...), custom_call_target="tpu_custom_call", output_to_operand_aliasing={{1}: (4, {}), {2}: (5, {})} | custom-call | flops 2147483648 | bytes 8912896 | tf_op jit(solution)/shard_map/ff_forward/pallas_call | solution.py:484
  225.0 4.6 second_norm.1
  231.5 18.0 %ff_backward.1 = (bf16[512,4096]{1,0:T(8,128)(2,1)}, f32[512,1024]{1,0:T(8,128)}, f32[8,1,512]{2,1,0:T(1,128)S(1)}) custom-call(bf16[512,1024]{1,0:T(8,128)(2,1)S(1)} %get-tuple-element.268.d_fed_ref.fed_ref, f32[512,1024]{1,0:T(8,128)} %copy-done.57, f32[512,4096]{1,0:T(8,128)} %get-tuple-element.270.slope_ref, bf16[528,1024]{1,0:T(8,128)(2,1)S(1)} %copy-done.31, ...), custom_call_target="tpu_custom_call" | custom-call | flops 8589934592 | bytes 34603008 | tf_op jit(solution)/shard_map/ff_backward/pallas_call | solution.py:532
  249.5 6.4 %attend_back.1 = (f32[512,1024]{1,0:T(8,128)S(1)}, bf16[512,1024]{1,0:T(8,128)(2,1)S(1)}, f32[8,1024]{1,0:T(8,128)S(1)}, bf16[512,256]{1,0:T(8,128)(2,1)S(1)}, b...) custom-call(s32[4]{0:T(128)S(1)} %pad_add_fusion.2.at_ref, ...), custom_call_target="tpu_custom_call" | custom-call | flops 1073741824 | bytes 10485760 | tf_op jit(solution)/shard_map/attend_back/pallas_call | solution.py:396
  257.6 3.3 ff_grad.10
  267.6 4.5 ff_grad.12
  272.1 3.2 ff_grad.11
  283.5 4.6 ff_grad.13
  288.1 11.2 %attn_backward.4.refs_4_ = bf16[1024,768]{1,0:T(8,128)(2,1)S(1)} custom-call(bf16[1024,768]{1,0:T(8,128)(2,1)S(1)} %copy-done.83, bf16[1024,768]{1,0:T(8,128)(2,1)S(1)} %copy-done.83, bf16[1024,768]{1,0:T(8,128)(2,1)S(1)} %copy-done.83, bf16[512,256]{1,0:T(8,128)(2,1)S(1)} %copy-done.61, bf16[512,256]{1,0:T(8,128)(2,1)S(1)} %copy-done.63, ...), custom_call_target="tpu_custom_call" | custom-call | flops 2684354560 | bytes 1835008 | tf_op jit(solution)/shard_map/attn_backward/pallas_call | solution.py:225
  301.9 5.1 ff_grad.14
  312.2 4.9 ff_grad.15
  317.1 11.2 %attn_backward.5 = bf16[1024,768]{1,0:T(8,128)(2,1)S(1)} custom-call(bf16[1024,768]{1,0:T(8,128)(2,1)S(1)} %copy-done.84, bf16[1024,768]{1,0:T(8,128)(2,1)S(1)} %copy-done.84, bf16[1024,768]{1,0:T(8,128)(2,1)S(1)} %copy-done.84, bf16[512,256]{1,0:T(8,128)(2,1)S(1)} %copy-done.61, bf16[512,256]{1,0:T(8,128)(2,1)S(1)} %copy-done.64, ...), custom_call_target="tpu_custom_call", output_to_operand_aliasing={{}: (7, {})} | custom-call | flops 2684354560 | bytes 1835008 | tf_op jit(solution)/shard_map/attn_backward/pallas_call | solution.py:225
  329.5 6.2 %collective-permute-done.44.refs_7_ = bf16[576,1024]{1,0:T(8,128)(2,1)} collective-permute-done((bf16[576,1024]{1,0:T(8,128)(2,1)}, bf16[576,1024]{1,0:T(8,128)(2,1)}, u32[]{:S(2)}, u32[]{:S(2)}) %collective-permute-start.44) | collective-permute-done | bytes 1179680 | tf_op jit(solution)/shard_map/ppermute | solution.py:687
  337.8 5.3 %ff_grad.16 = (bf16[576,1024]{1,0:T(8,128)(2,1)}, bf16[576,1024]{1,0:T(8,128)(2,1)}) custom-call(s32[2]{0:T(128)S(1)} %get-tuple-element.472.index_ref, bf16[512,1024]{1,0:T(8,128)(2,1)S(1)} %get-tuple-element.238.first_ref, bf16[512,1024]{1,0:T(8,128)(2,1)S(1)} %copy-done.11, bf16[512,4096]{1,0:T(8,128)(2,1)} %get-tuple-element.344.refs_0_.refs_1_, ...), custom_call_target="tpu_custom_call" | custom-call | flops 1073741824 | bytes 10223616 | tf_op jit(solution)/shard_map/ff_grad/pallas_call | solution.py:602
  347.5 2.3 convolution_convert_fusion.2
  349.8 1.8 collective-permute-start.50
  352.3 3.1 ff_grad.17
  355.5 11.2 %attn_backward.6.refs_4_ = bf16[1024,768]{1,0:T(8,128)(2,1)S(1)} custom-call(bf16[1024,768]{1,0:T(8,128)(2,1)S(1)} %copy-done.80, bf16[1024,768]{1,0:T(8,128)(2,1)S(1)} %copy-done.80, bf16[1024,768]{1,0:T(8,128)(2,1)S(1)} %copy-done.80, bf16[512,256]{1,0:T(8,128)(2,1)S(1)} %copy-done.61, bf16[512,256]{1,0:T(8,128)(2,1)S(1)} %copy-done.65, ...), custom_call_target="tpu_custom_call" | custom-call | flops 2684354560 | bytes 1835008 | tf_op jit(solution)/shard_map/attn_backward/pallas_call | solution.py:225
  367.9 11.2 %collective-permute-done.50 = bf16[128,1024]{1,0:T(8,128)(2,1)S(1)} collective-permute-done((bf16[128,1024]{1,0:T(8,128)(2,1)S(1)}, bf16[128,1024]{1,0:T(8,128)(2,1)S(1)}, u32[]{:S(2)}, u32[]{:S(2)}) %collective-permute-start.50) | collective-permute-done | bytes 262176 | tf_op jit(solution)/shard_map/ppermute | solution.py:37
  379.0 5.4 %ff_grad.18 = (bf16[576,1024]{1,0:T(8,128)(2,1)}, bf16[576,1024]{1,0:T(8,128)(2,1)}) custom-call(s32[2]{0:T(128)S(1)} %pad_add_fusion.8.index_ref, bf16[512,1024]{1,0:T(8,128)(2,1)S(1)} %get-tuple-element.238.first_ref, bf16[512,1024]{1,0:T(8,128)(2,1)S(1)} %copy-done.12, bf16[512,4096]{1,0:T(8,128)(2,1)} %get-tuple-element.344.refs_0_.refs_1_, ...), custom_call_target="tpu_custom_call" | custom-call | flops 1073741824 | bytes 10223616 | tf_op jit(solution)/shard_map/ff_grad/pallas_call | solution.py:602
  384.5 1.9 collective-permute-start.53
  397.8 11.4 %attn_backward.7 = bf16[1024,768]{1,0:T(8,128)(2,1)S(1)} custom-call(bf16[1024,768]{1,0:T(8,128)(2,1)S(1)} %copy-done.81, bf16[1024,768]{1,0:T(8,128)(2,1)S(1)} %copy-done.81, bf16[1024,768]{1,0:T(8,128)(2,1)S(1)} %copy-done.81, bf16[512,256]{1,0:T(8,128)(2,1)S(1)} %copy-done.61, bf16[512,256]{1,0:T(8,128)(2,1)S(1)} %copy-done.65, ...), custom_call_target="tpu_custom_call", output_to_operand_aliasing={{}: (7, {})} | custom-call | flops 2684354560 | bytes 1835008 | tf_op jit(solution)/shard_map/attn_backward/pallas_call | solution.py:225
  409.2 14.2 %collective-permute-done.56 = bf16[256,1024]{1,0:T(8,128)(2,1)} collective-permute-done((bf16[256,1024]{1,0:T(8,128)(2,1)}, bf16[256,1024]{1,0:T(8,128)(2,1)}, u32[]{:S(2)}, u32[]{:S(2)}) %collective-permute-start.56) | collective-permute-done | bytes 524320 | tf_op jit(solution)/shard_map/ppermute | solution.py:37
  432.8 1.9 add_convert_fusion.2
  437.3 2.9 ff_grad.19
  442.2 6.7 %collective-permute-done.59 = bf16[128,1024]{1,0:T(8,128)(2,1)S(1)} collective-permute-done((bf16[128,1024]{1,0:T(8,128)(2,1)S(1)}, bf16[128,1024]{1,0:T(8,128)(2,1)S(1)}, u32[]{:S(2)}, u32[]{:S(2)}) %collective-permute-start.59) | collective-permute-done | bytes 262176 | tf_op jit(solution)/shard_map/ppermute | solution.py:37
  455.8 4.3 collective-permute-start.64
  462.4 18.5 %collective-permute-start.66 = (bf16[256,1024]{1,0:T(8,128)(2,1)S(1)}, bf16[256,1024]{1,0:T(8,128)(2,1)S(1)}, u32[]{:S(2)}, u32[]{:S(2)}) collective-permute-start(bf16[256,1024]{1,0:T(8,128)(2,1)S(1)} %fusion.12), channel_id=1, source_target_pairs={{0,1},{1,0},{2,3},{3,2},{4,5},{5,4},{6,7},{7,6},{8,9},{9,8},{10,11... | collective-permute-start | bytes 1572872 | tf_op jit(solution)/shard_map/ppermute | solution.py:37
  481.6 7.4 %collective-permute-done.67 = bf16[256,1024]{1,0:T(8,128)(2,1)S(1)} collective-permute-done((bf16[256,1024]{1,0:T(8,128)(2,1)S(1)}, bf16[256,1024]{1,0:T(8,128)(2,1)S(1)}, u32[]{:S(2)}, u32[]{:S(2)}) %collective-permute-start.67) | collective-permute-done | bytes 524320 | tf_op jit(solution)/shard_map/ppermute | solution.py:37
  489.8 2.3 collective-permute-start.72
  492.1 3.1 collective-permute-start.71
  495.2 1.9 fusion.9
  504.1 1.8 copy.58
  508.9 2.0 fusion.46
  (484 shorter events, 137.9 us)
Async XLA Ops:
  7.2 117.0 %all-gather.3.cloned.1.call-start = ((), (), s32[]{:S(2)}) async-start(), calls=%async_computation | async-start | bytes 1179648 | tf_op jit(solution)/shard_map/all_gather | solution.py:750
  10.1 24.3 %collective-permute-start = (bf16[256,1024]{1,0:T(8,128)(2,1)S(1)}, bf16[256,1024]{1,0:T(8,128)(2,1)}, u32[]{:S(2)}, u32[]{:S(2)}) collective-permute-start(bf16[256,1024]{1,0:T(8,128)(2,1)S(1)} %fusion.14.refs_0_.refs_8_), channel_id=1, source_target_pairs={{0,1},{1,0},{2,3},{3,2},{4,5},{5,4},{6,7},{7,6},{8,9},{9,8},{10,11... | collective-permute-start | bytes 1572872 | tf_op jit(solution)/shard_map/ppermute | solution.py:37
  13.1 21.3 %collective-permute-start.1 = (bf16[256,1024]{1,0:T(8,128)(2,1)S(1)}, bf16[256,1024]{1,0:T(8,128)(2,1)}, u32[]{:S(2)}, u32[]{:S(2)}) collective-permute-start(bf16[256,1024]{1,0:T(8,128)(2,1)S(1)} %fusion.14.refs_0_.refs_8_), channel_id=1, source_target_pairs={{0,2},{1,3},{2,0},{3,1},{4,6},{5,7},{6,4},{7,5},{8,10},{9,11},{10,... | collective-permute-start | bytes 1572872 | tf_op jit(solution)/shard_map/ppermute | solution.py:37
  17.3 16.3 %collective-permute-start.2 = (bf16[528,384]{1,0:T(8,128)(2,1)}, bf16[528,384]{1,0:T(8,128)(2,1)S(1)}, u32[]{:S(2)}, u32[]{:S(2)}) collective-permute-start(bf16[528,384]{1,0:T(8,128)(2,1)} %fusion.33), channel_id=1, source_target_pairs={{0,0},{1,4},{2,1},{3,5},{4,2},{5,6},{6,3},{7,7},{8,8},{9,12},{10,9... | collective-permute-start | bytes 1216520 | tf_op jit(solution)/shard_map/ppermute | solution.py:746
  18.9 15.5 %collective-permute-start.3 = (bf16[528,384]{1,0:T(8,128)(2,1)}, bf16[528,384]{1,0:T(8,128)(2,1)S(1)}, u32[]{:S(2)}, u32[]{:S(2)}) collective-permute-start(bf16[528,384]{1,0:T(8,128)(2,1)} %fusion.33), channel_id=1, source_target_pairs={{0,4},{1,0},{2,5},{3,1},{4,6},{5,2},{6,7},{7,3},{8,12},{9,8},{10,1... | collective-permute-start | bytes 1216520 | tf_op jit(solution)/shard_map/ppermute | solution.py:746
  35.2 12.4 %collective-permute-start.10 = (bf16[512,384]{1,0:T(8,128)(2,1)}, bf16[512,384]{1,0:T(8,128)(2,1)S(1)}, u32[]{:S(2)}, u32[]{:S(2)}) collective-permute-start(bf16[512,384]{1,0:T(8,128)(2,1)} %slice.194), channel_id=1, source_target_pairs={{0,8},{8,0},{16,24},{24,16},{1,9},{9,1},{17,25},{25,17},{2,10},{10... | collective-permute-start | bytes 1179656 | tf_op jit(solution)/shard_map/ppermute | solution.py:37
  36.0 13.8 %collective-permute-start.11 = (bf16[512,384]{1,0:T(8,128)(2,1)}, bf16[512,384]{1,0:T(8,128)(2,1)S(1)}, u32[]{:S(2)}, u32[]{:S(2)}) collective-permute-start(bf16[512,384]{1,0:T(8,128)(2,1)} %slice.195), channel_id=1, source_target_pairs={{0,8},{8,0},{16,24},{24,16},{1,9},{9,1},{17,25},{25,17},{2,10},{10... | collective-permute-start | bytes 1179656 | tf_op jit(solution)/shard_map/ppermute | solution.py:37
  38.2 15.7 %collective-permute-start.8 = (bf16[128,1024]{1,0:T(8,128)(2,1)}, bf16[128,1024]{1,0:T(8,128)(2,1)}, u32[]{:S(2)}, u32[]{:S(2)}) collective-permute-start(bf16[128,1024]{1,0:T(8,128)(2,1)} %slice.192), channel_id=1, source_target_pairs={{0,2},{1,3},{2,0},{3,1},{4,6},{5,7},{6,4},{7,5},{8,10},{9,11},{10,... | collective-permute-start | bytes 786440 | tf_op jit(solution)/shard_map/ppermute | solution.py:37
  46.8 9.5 %collective-permute-start.9 = (bf16[128,1024]{1,0:T(8,128)(2,1)}, bf16[128,1024]{1,0:T(8,128)(2,1)}, u32[]{:S(2)}, u32[]{:S(2)}) collective-permute-start(bf16[128,1024]{1,0:T(8,128)(2,1)} %slice.193), channel_id=1, source_target_pairs={{0,1},{1,0},{2,3},{3,2},{4,5},{5,4},{6,7},{7,6},{8,9},{9,8},{10,11... | collective-permute-start | bytes 786440 | tf_op jit(solution)/shard_map/ppermute | solution.py:37
  47.6 35.6 %collective-permute-start.6 = (bf16[272,1024]{1,0:T(8,128)(2,1)S(1)}, bf16[272,1024]{1,0:T(8,128)(2,1)S(1)}, u32[]{:S(2)}, u32[]{:S(2)}) collective-permute-start(bf16[272,1024]{1,0:T(8,128)(2,1)S(1)} %slice.191), channel_id=1, source_target_pairs={{0,2},{2,4},{4,6},{6,7},{7,5},{5,3},{3,1},{1,0},{8,10},{10,12},{12... | collective-permute-start | bytes 1671176 | tf_op jit(solution)/shard_map/ppermute | solution.py:687
  47.7 35.5 %collective-permute-start.7 = (bf16[272,1024]{1,0:T(8,128)(2,1)S(1)}, bf16[272,1024]{1,0:T(8,128)(2,1)S(1)}, u32[]{:S(2)}, u32[]{:S(2)}) collective-permute-start(bf16[272,1024]{1,0:T(8,128)(2,1)S(1)} %slice.191), channel_id=1, source_target_pairs={{2,0},{4,2},{6,4},{7,6},{5,7},{3,5},{1,3},{0,1},{10,8},{12,10},{14... | collective-permute-start | bytes 1671176 | tf_op jit(solution)/shard_map/ppermute | solution.py:690
  49.9 33.3 %collective-permute-start.4 = (bf16[256,1024]{1,0:T(8,128)(2,1)}, bf16[256,1024]{1,0:T(8,128)(2,1)S(1)}, u32[]{:S(2)}, u32[]{:S(2)}) collective-permute-start(bf16[256,1024]{1,0:T(8,128)(2,1)} %fusion.15.refs_0_.refs_9_), channel_id=1, source_target_pairs={{0,1},{1,0},{2,3},{3,2},{4,5},{5,4},{6,7},{7,6},{8,9},{9,8},{10,11... | collective-permute-start | bytes 1572872 | tf_op jit(solution)/shard_map/ppermute | solution.py:37
  53.9 29.2 %collective-permute-start.5 = (bf16[256,1024]{1,0:T(8,128)(2,1)}, bf16[256,1024]{1,0:T(8,128)(2,1)S(1)}, u32[]{:S(2)}, u32[]{:S(2)}) collective-permute-start(bf16[256,1024]{1,0:T(8,128)(2,1)} %fusion.15.refs_0_.refs_9_), channel_id=1, source_target_pairs={{0,2},{1,3},{2,0},{3,1},{4,6},{5,7},{6,4},{7,5},{8,10},{9,11},{10,... | collective-permute-start | bytes 1572872 | tf_op jit(solution)/shard_map/ppermute | solution.py:37
  83.2 11.7 %collective-permute-start.17 = (bf16[128,1024]{1,0:T(8,128)(2,1)S(1)}, bf16[128,1024]{1,0:T(8,128)(2,1)S(1)}, u32[]{:S(2)}, u32[]{:S(2)}) collective-permute-start(bf16[128,1024]{1,0:T(8,128)(2,1)S(1)} %slice.197), channel_id=1, source_target_pairs={{0,2},{1,3},{2,0},{3,1},{4,6},{5,7},{6,4},{7,5},{8,10},{9,11},{10,... | collective-permute-start | bytes 786440 | tf_op jit(solution)/shard_map/ppermute | solution.py:37
  85.3 11.7 %collective-permute-start.18 = (bf16[128,1024]{1,0:T(8,128)(2,1)S(1)}, bf16[128,1024]{1,0:T(8,128)(2,1)S(1)}, u32[]{:S(2)}, u32[]{:S(2)}) collective-permute-start(bf16[128,1024]{1,0:T(8,128)(2,1)S(1)} %slice.198), channel_id=1, source_target_pairs={{0,1},{1,0},{2,3},{3,2},{4,5},{5,4},{6,7},{7,6},{8,9},{9,8},{10,11... | collective-permute-start | bytes 786440 | tf_op jit(solution)/shard_map/ppermute | solution.py:37
  85.4 28.5 %collective-permute-start.15 = (bf16[256,1024]{1,0:T(8,128)(2,1)S(1)}, bf16[256,1024]{1,0:T(8,128)(2,1)S(1)}, u32[]{:S(2)}, u32[]{:S(2)}) collective-permute-start(bf16[256,1024]{1,0:T(8,128)(2,1)S(1)} %slice.196), channel_id=1, source_target_pairs={{0,2},{2,4},{4,6},{6,7},{7,5},{5,3},{3,1},{1,0},{8,10},{10,12},{12... | collective-permute-start | bytes 1572872 | tf_op jit(solution)/shard_map/ppermute | solution.py:687
  85.4 28.4 %collective-permute-start.16 = (bf16[256,1024]{1,0:T(8,128)(2,1)S(1)}, bf16[256,1024]{1,0:T(8,128)(2,1)S(1)}, u32[]{:S(2)}, u32[]{:S(2)}) collective-permute-start(bf16[256,1024]{1,0:T(8,128)(2,1)S(1)} %slice.196), channel_id=1, source_target_pairs={{2,0},{4,2},{6,4},{7,6},{5,7},{3,5},{1,3},{0,1},{10,8},{12,10},{14... | collective-permute-start | bytes 1572872 | tf_op jit(solution)/shard_map/ppermute | solution.py:690
  87.4 29.5 %collective-permute-start.12 = (bf16[256,256]{1,0:T(8,128)(2,1)S(1)}, bf16[256,256]{1,0:T(8,128)(2,1)S(1)}, u32[]{:S(2)}, u32[]{:S(2)}) collective-permute-start(bf16[256,256]{1,0:T(8,128)(2,1)S(1)} %get-tuple-element.209), channel_id=1, source_target_pairs={{0,1},{1,0},{2,3},{3,2},{4,5},{5,4},{6,7},{7,6},{8,9},{9,8},{10,11... | collective-permute-start | bytes 393224 | tf_op jit(solution)/shard_map/ppermute | solution.py:37
  94.9 23.5 %collective-permute-start.13 = (bf16[256,256]{1,0:T(8,128)(2,1)S(1)}, bf16[256,256]{1,0:T(8,128)(2,1)S(1)}, u32[]{:S(2)}, u32[]{:S(2)}) collective-permute-start(bf16[256,256]{1,0:T(8,128)(2,1)S(1)} %get-tuple-element.210), channel_id=1, source_target_pairs={{0,2},{1,3},{2,0},{3,1},{4,6},{5,7},{6,4},{7,5},{8,10},{9,11},{10,... | collective-permute-start | bytes 393224 | tf_op jit(solution)/shard_map/ppermute | solution.py:37
  97.0 22.0 %collective-permute-start.14 = (bf16[256,256]{1,0:T(8,128)(2,1)S(1)}, bf16[256,256]{1,0:T(8,128)(2,1)S(1)}, u32[]{:S(2)}, u32[]{:S(2)}) collective-permute-start(bf16[256,256]{1,0:T(8,128)(2,1)S(1)} %get-tuple-element.211), channel_id=1, source_target_pairs={{0,3},{1,2},{2,1},{3,0},{4,7},{5,6},{6,5},{7,4},{8,11},{9,10},{10,... | collective-permute-start | bytes 393224 | tf_op jit(solution)/shard_map/ppermute | solution.py:37
  124.2 20.4 %collective-permute-start.25 = (bf16[528,1024]{1,0:T(8,128)(2,1)}, bf16[528,1024]{1,0:T(8,128)(2,1)}, u32[]{:S(2)}, u32[]{:S(2)}) collective-permute-start(bf16[528,1024]{1,0:T(8,128)(2,1)} %copy-done.29), channel_id=1, source_target_pairs={{0,8},{8,0},{16,24},{24,16},{1,9},{9,1},{17,25},{25,17},{2,10},{10... | collective-permute-start | bytes 3244040 | tf_op jit(solution)/shard_map/ppermute | solution.py:37
  124.7 27.1 %collective-permute-start.26 = (bf16[528,1024]{1,0:T(8,128)(2,1)S(1)}, bf16[528,1024]{1,0:T(8,128)(2,1)}, u32[]{:S(2)}, u32[]{:S(2)}) collective-permute-start(bf16[528,1024]{1,0:T(8,128)(2,1)S(1)} %pad_maximum_fusion.2.refs_0_.refs_2_), channel_id=1, source_target_pairs={{0,8},{8,0},{16,24},{24,16},{1,9},{9,1},{17,25},{25,17},{2,10},{10... | collective-permute-start | bytes 3244040 | tf_op jit(solution)/shard_map/ppermute | solution.py:37
  124.7 27.1 %collective-permute-start.27 = (bf16[528,1024]{1,0:T(8,128)(2,1)S(1)}, bf16[528,1024]{1,0:T(8,128)(2,1)}, u32[]{:S(2)}, u32[]{:S(2)}) collective-permute-start(bf16[528,1024]{1,0:T(8,128)(2,1)S(1)} %pad_maximum_fusion.3.refs_2_.refs_4_), channel_id=1, source_target_pairs={{0,8},{8,0},{16,24},{24,16},{1,9},{9,1},{17,25},{25,17},{2,10},{10... | collective-permute-start | bytes 3244040 | tf_op jit(solution)/shard_map/ppermute | solution.py:37
  125.2 35.2 %collective-permute-start.23 = (bf16[528,1024]{1,0:T(8,128)(2,1)S(1)}, bf16[528,1024]{1,0:T(8,128)(2,1)}, u32[]{:S(2)}, u32[]{:S(2)}) collective-permute-start(bf16[528,1024]{1,0:T(8,128)(2,1)S(1)} %pad_maximum_fusion.2.refs_0_.refs_2_), channel_id=1, source_target_pairs={{0,2},{2,4},{4,6},{6,7},{7,5},{5,3},{3,1},{1,0},{8,10},{10,12},{12... | collective-permute-start | bytes 3244040 | tf_op jit(solution)/shard_map/ppermute | solution.py:687
  127.2 33.2 %collective-permute-start.24 = (bf16[528,1024]{1,0:T(8,128)(2,1)S(1)}, bf16[528,1024]{1,0:T(8,128)(2,1)}, u32[]{:S(2)}, u32[]{:S(2)}) collective-permute-start(bf16[528,1024]{1,0:T(8,128)(2,1)S(1)} %pad_maximum_fusion.3.refs_2_.refs_4_), channel_id=1, source_target_pairs={{2,0},{4,2},{6,4},{7,6},{5,7},{3,5},{1,3},{0,1},{10,8},{12,10},{14... | collective-permute-start | bytes 3244040 | tf_op jit(solution)/shard_map/ppermute | solution.py:690
  161.0 26.1 %collective-permute-start.28 = (bf16[528,1024]{1,0:T(8,128)(2,1)}, bf16[528,1024]{1,0:T(8,128)(2,1)S(1)}, u32[]{:S(2)}, u32[]{:S(2)}) collective-permute-start(bf16[528,1024]{1,0:T(8,128)(2,1)} %collective-permute-done.23.refs_0_.refs_6_), channel_id=1, source_target_pairs={{0,2},{2,4},{4,6},{6,7},{7,5},{5,3},{3,1},{1,0},{8,10},{10,12},{12... | collective-permute-start | bytes 3244040 | tf_op jit(solution)/shard_map/ppermute | solution.py:687
  162.9 25.9 %collective-permute-start.29 = (bf16[528,1024]{1,0:T(8,128)(2,1)}, bf16[528,1024]{1,0:T(8,128)(2,1)}, u32[]{:S(2)}, u32[]{:S(2)}) collective-permute-start(bf16[528,1024]{1,0:T(8,128)(2,1)} %collective-permute-done.24.refs_2_.refs_8_), channel_id=1, source_target_pairs={{2,0},{4,2},{6,4},{7,6},{5,7},{3,5},{1,3},{0,1},{10,8},{12,10},{14... | collective-permute-start | bytes 3244040 | tf_op jit(solution)/shard_map/ppermute | solution.py:690
  188.9 13.5 %collective-permute-start.34 = (bf16[272,1024]{1,0:T(8,128)(2,1)S(1)}, bf16[272,1024]{1,0:T(8,128)(2,1)S(1)}, u32[]{:S(2)}, u32[]{:S(2)}) collective-permute-start(bf16[272,1024]{1,0:T(8,128)(2,1)S(1)} %slice.199), channel_id=1, source_target_pairs={{0,2},{2,4},{4,6},{6,7},{7,5},{5,3},{3,1},{1,0},{8,10},{10,12},{12... | collective-permute-start | bytes 1671176 | tf_op jit(solution)/shard_map/ppermute | solution.py:687
  190.3 13.2 %collective-permute-start.35 = (bf16[256,1024]{1,0:T(8,128)(2,1)S(1)}, bf16[256,1024]{1,0:T(8,128)(2,1)S(1)}, u32[]{:S(2)}, u32[]{:S(2)}) collective-permute-start(bf16[256,1024]{1,0:T(8,128)(2,1)S(1)} %slice.200), channel_id=1, source_target_pairs={{2,0},{4,2},{6,4},{7,6},{5,7},{3,5},{1,3},{0,1},{10,8},{12,10},{14... | collective-permute-start | bytes 1572872 | tf_op jit(solution)/shard_map/ppermute | solution.py:690
  192.5 17.9 %collective-permute-start.32 = (bf16[528,1024]{1,0:T(8,128)(2,1)S(1)}, bf16[528,1024]{1,0:T(8,128)(2,1)}, u32[]{:S(2)}, u32[]{:S(2)}) collective-permute-start(bf16[528,1024]{1,0:T(8,128)(2,1)S(1)} %collective-permute-done.28.refs_0_.refs_10_), channel_id=1, source_target_pairs={{0,8},{8,0},{16,24},{24,16},{1,9},{9,1},{17,25},{25,17},{2,10},{10... | collective-permute-start | bytes 3244040 | tf_op jit(solution)/shard_map/ppermute | solution.py:37
  192.5 17.9 %collective-permute-start.33 = (bf16[528,1024]{1,0:T(8,128)(2,1)}, bf16[528,1024]{1,0:T(8,128)(2,1)}, u32[]{:S(2)}, u32[]{:S(2)}) collective-permute-start(bf16[528,1024]{1,0:T(8,128)(2,1)} %collective-permute-done.29.refs_2_.refs_12_), channel_id=1, source_target_pairs={{0,8},{8,0},{16,24},{24,16},{1,9},{9,1},{17,25},{25,17},{2,10},{10... | collective-permute-start | bytes 3244040 | tf_op jit(solution)/shard_map/ppermute | solution.py:37
  204.4 14.5 %collective-permute-start.36 = (bf16[528,1024]{1,0:T(8,128)(2,1)}, bf16[528,1024]{1,0:T(8,128)(2,1)}, u32[]{:S(2)}, u32[]{:S(2)}) collective-permute-start(bf16[528,1024]{1,0:T(8,128)(2,1)} %constant_dynamic-update-slice_fusion.2.refs_0_.refs_14_), channel_id=1, source_target_pairs={{0,8},{8,0},{16,24},{24,16},{1,9},{9,1},{17,25},{25,17},{2,10},{10... | collective-permute-start | bytes 3244040 | tf_op jit(solution)/shard_map/ppermute | solution.py:37
  260.9 11.1 %collective-permute-start.40 = (bf16[576,1024]{1,0:T(8,128)(2,1)}, bf16[576,1024]{1,0:T(8,128)(2,1)}, u32[]{:S(2)}, u32[]{:S(2)}) collective-permute-start(bf16[576,1024]{1,0:T(8,128)(2,1)} %ff_grad.10), channel_id=1, source_target_pairs={{0,8},{8,0},{16,24},{24,16},{1,9},{9,1},{17,25},{25,17},{2,10},{10... | collective-permute-start | bytes 3538952 | tf_op jit(solution)/shard_map/ppermute | solution.py:37
  262.7 12.6 %collective-permute-start.37 = (bf16[512,256]{1,0:T(8,128)(2,1)}, bf16[512,256]{1,0:T(8,128)(2,1)S(1)}, u32[]{:S(2)}, u32[]{:S(2)}) collective-permute-start(bf16[512,256]{1,0:T(8,128)(2,1)} %copy-done.78), channel_id=1, source_target_pairs={{0,1},{1,0},{2,3},{3,2},{4,5},{5,4},{6,7},{7,6},{8,9},{9,8},{10,11... | collective-permute-start | bytes 786440 | tf_op jit(solution)/shard_map/ppermute | solution.py:37
  264.2 11.8 %collective-permute-start.38 = (bf16[512,256]{1,0:T(8,128)(2,1)}, bf16[512,256]{1,0:T(8,128)(2,1)S(1)}, u32[]{:S(2)}, u32[]{:S(2)}) collective-permute-start(bf16[512,256]{1,0:T(8,128)(2,1)} %copy-done.77), channel_id=1, source_target_pairs={{0,2},{1,3},{2,0},{3,1},{4,6},{5,7},{6,4},{7,5},{8,10},{9,11},{10,... | collective-permute-start | bytes 786440 | tf_op jit(solution)/shard_map/ppermute | solution.py:37
  264.7 13.3 %collective-permute-start.39 = (bf16[512,256]{1,0:T(8,128)(2,1)}, bf16[512,256]{1,0:T(8,128)(2,1)S(1)}, u32[]{:S(2)}, u32[]{:S(2)}) collective-permute-start(bf16[512,256]{1,0:T(8,128)(2,1)} %copy-done.76), channel_id=1, source_target_pairs={{0,3},{1,2},{2,1},{3,0},{4,7},{5,6},{6,5},{7,4},{8,11},{9,10},{10,... | collective-permute-start | bytes 786440 | tf_op jit(solution)/shard_map/ppermute | solution.py:37
  278.7 21.7 %collective-permute-start.43 = (bf16[1152,1024]{1,0:T(8,128)(2,1)}, bf16[1152,1024]{1,0:T(8,128)(2,1)}, u32[]{:S(2)}, u32[]{:S(2)}) collective-permute-start(bf16[1152,1024]{1,0:T(8,128)(2,1)} %ff_grad.12), channel_id=1, source_target_pairs={{0,8},{8,0},{16,24},{24,16},{1,9},{9,1},{17,25},{25,17},{2,10},{10... | collective-permute-start | bytes 7077896 | tf_op jit(solution)/shard_map/ppermute | solution.py:37
  278.7 21.7 %collective-permute-start.42 = (bf16[320,1024]{1,0:T(8,128)(2,1)}, bf16[320,1024]{1,0:T(8,128)(2,1)}, u32[]{:S(2)}, u32[]{:S(2)}) collective-permute-start(bf16[320,1024]{1,0:T(8,128)(2,1)} %get-tuple-element.291), channel_id=1, source_target_pairs={{2,0},{4,2},{6,4},{7,6},{5,7},{3,5},{1,3},{0,1},{10,8},{12,10},{14... | collective-permute-start | bytes 1966088 | tf_op jit(solution)/shard_map/ppermute | solution.py:690
  280.2 20.3 %collective-permute-start.41 = (bf16[256,1024]{1,0:T(8,128)(2,1)}, bf16[256,1024]{1,0:T(8,128)(2,1)}, u32[]{:S(2)}, u32[]{:S(2)}) collective-permute-start(bf16[256,1024]{1,0:T(8,128)(2,1)} %get-tuple-element.290), channel_id=1, source_target_pairs={{0,2},{2,4},{4,6},{6,7},{7,5},{5,3},{3,1},{1,0},{8,10},{10,12},{12... | collective-permute-start | bytes 1572872 | tf_op jit(solution)/shard_map/ppermute | solution.py:687
  300.5 36.0 %collective-permute-start.46 = (bf16[1152,1024]{1,0:T(8,128)(2,1)}, bf16[1152,1024]{1,0:T(8,128)(2,1)}, u32[]{:S(2)}, u32[]{:S(2)}) collective-permute-start(bf16[1152,1024]{1,0:T(8,128)(2,1)} %ff_grad.13), channel_id=1, source_target_pairs={{0,8},{8,0},{16,24},{24,16},{1,9},{9,1},{17,25},{25,17},{2,10},{10... | collective-permute-start | bytes 7077896 | tf_op jit(solution)/shard_map/ppermute | solution.py:37
  307.0 28.7 %collective-permute-start.44 = (bf16[576,1024]{1,0:T(8,128)(2,1)}, bf16[576,1024]{1,0:T(8,128)(2,1)}, u32[]{:S(2)}, u32[]{:S(2)}) collective-permute-start(bf16[576,1024]{1,0:T(8,128)(2,1)} %get-tuple-element.306), channel_id=1, source_target_pairs={{0,2},{2,4},{4,6},{6,7},{7,5},{5,3},{3,1},{1,0},{8,10},{10,12},{12... | collective-permute-start | bytes 3538952 | tf_op jit(solution)/shard_map/ppermute | solution.py:687
  308.1 28.4 %collective-permute-start.45 = (bf16[576,1024]{1,0:T(8,128)(2,1)}, bf16[576,1024]{1,0:T(8,128)(2,1)}, u32[]{:S(2)}, u32[]{:S(2)}) collective-permute-start(bf16[576,1024]{1,0:T(8,128)(2,1)} %get-tuple-element.307), channel_id=1, source_target_pairs={{2,0},{4,2},{6,4},{7,6},{5,7},{3,5},{1,3},{0,1},{10,8},{12,10},{14... | collective-permute-start | bytes 3538952 | tf_op jit(solution)/shard_map/ppermute | solution.py:690
  336.5 42.6 %collective-permute-start.49 = (bf16[1152,1024]{1,0:T(8,128)(2,1)}, bf16[1152,1024]{1,0:T(8,128)(2,1)}, u32[]{:S(2)}, u32[]{:S(2)}) collective-permute-start(bf16[1152,1024]{1,0:T(8,128)(2,1)} %ff_grad.15), channel_id=1, source_target_pairs={{0,8},{8,0},{16,24},{24,16},{1,9},{9,1},{17,25},{25,17},{2,10},{10... | collective-permute-start | bytes 7077896 | tf_op jit(solution)/shard_map/ppermute | solution.py:37
  343.2 35.9 %collective-permute-start.47 = (bf16[576,1024]{1,0:T(8,128)(2,1)}, bf16[576,1024]{1,0:T(8,128)(2,1)}, u32[]{:S(2)}, u32[]{:S(2)}) collective-permute-start(bf16[576,1024]{1,0:T(8,128)(2,1)} %get-tuple-element.318), channel_id=1, source_target_pairs={{0,2},{2,4},{4,6},{6,7},{7,5},{5,3},{3,1},{1,0},{8,10},{10,12},{12... | collective-permute-start | bytes 3538952 | tf_op jit(solution)/shard_map/ppermute | solution.py:687
  344.9 34.1 %collective-permute-start.48 = (bf16[576,1024]{1,0:T(8,128)(2,1)}, bf16[576,1024]{1,0:T(8,128)(2,1)}, u32[]{:S(2)}, u32[]{:S(2)}) collective-permute-start(bf16[576,1024]{1,0:T(8,128)(2,1)} %get-tuple-element.319), channel_id=1, source_target_pairs={{2,0},{4,2},{6,4},{7,6},{5,7},{3,5},{1,3},{0,1},{10,8},{12,10},{14... | collective-permute-start | bytes 3538952 | tf_op jit(solution)/shard_map/ppermute | solution.py:690
  349.8 29.2 %collective-permute-start.50 = (bf16[128,1024]{1,0:T(8,128)(2,1)S(1)}, bf16[128,1024]{1,0:T(8,128)(2,1)S(1)}, u32[]{:S(2)}, u32[]{:S(2)}) collective-permute-start(bf16[128,1024]{1,0:T(8,128)(2,1)S(1)} %get-tuple-element.446), channel_id=1, source_target_pairs={{0,2},{1,3},{2,0},{3,1},{4,6},{5,7},{6,4},{7,5},{8,10},{9,11},{10,... | collective-permute-start | bytes 786440 | tf_op jit(solution)/shard_map/ppermute | solution.py:37
  351.6 27.4 %collective-permute-start.51 = (bf16[128,1024]{1,0:T(8,128)(2,1)S(1)}, bf16[128,1024]{1,0:T(8,128)(2,1)S(1)}, u32[]{:S(2)}, u32[]{:S(2)}) collective-permute-start(bf16[128,1024]{1,0:T(8,128)(2,1)S(1)} %get-tuple-element.445), channel_id=1, source_target_pairs={{0,1},{1,0},{2,3},{3,2},{4,5},{5,4},{6,7},{7,6},{8,9},{9,8},{10,11... | collective-permute-start | bytes 786440 | tf_op jit(solution)/shard_map/ppermute | solution.py:37
  384.4 39.0 %collective-permute-start.52 = (bf16[576,1024]{1,0:T(8,128)(2,1)}, bf16[576,1024]{1,0:T(8,128)(2,1)}, u32[]{:S(2)}, u32[]{:S(2)}) collective-permute-start(bf16[576,1024]{1,0:T(8,128)(2,1)} %get-tuple-element.330), channel_id=1, source_target_pairs={{0,2},{2,4},{4,6},{6,7},{7,5},{5,3},{3,1},{1,0},{8,10},{10,12},{12... | collective-permute-start | bytes 3538952 | tf_op jit(solution)/shard_map/ppermute | solution.py:687
  384.5 38.9 %collective-permute-start.53 = (bf16[576,1024]{1,0:T(8,128)(2,1)}, bf16[576,1024]{1,0:T(8,128)(2,1)}, u32[]{:S(2)}, u32[]{:S(2)}) collective-permute-start(bf16[576,1024]{1,0:T(8,128)(2,1)} %get-tuple-element.331), channel_id=1, source_target_pairs={{2,0},{4,2},{6,4},{7,6},{5,7},{3,5},{1,3},{0,1},{10,8},{12,10},{14... | collective-permute-start | bytes 3538952 | tf_op jit(solution)/shard_map/ppermute | solution.py:690
  386.5 36.9 %collective-permute-start.54 = (bf16[576,1024]{1,0:T(8,128)(2,1)}, bf16[576,1024]{1,0:T(8,128)(2,1)}, u32[]{:S(2)}, u32[]{:S(2)}) collective-permute-start(bf16[576,1024]{1,0:T(8,128)(2,1)} %ff_grad.17), channel_id=1, source_target_pairs={{0,8},{8,0},{16,24},{24,16},{1,9},{9,1},{17,25},{25,17},{2,10},{10... | collective-permute-start | bytes 3538952 | tf_op jit(solution)/shard_map/ppermute | solution.py:37
  387.9 35.5 %collective-permute-start.56 = (bf16[256,1024]{1,0:T(8,128)(2,1)}, bf16[256,1024]{1,0:T(8,128)(2,1)}, u32[]{:S(2)}, u32[]{:S(2)}) collective-permute-start(bf16[256,1024]{1,0:T(8,128)(2,1)} %fusion.11), channel_id=1, source_target_pairs={{0,2},{1,3},{2,0},{3,1},{4,6},{5,7},{6,4},{7,5},{8,10},{9,11},{10,... | collective-permute-start | bytes 1572872 | tf_op jit(solution)/shard_map/ppermute | solution.py:37
  389.4 34.0 %collective-permute-start.55 = (bf16[256,1024]{1,0:T(8,128)(2,1)}, bf16[256,1024]{1,0:T(8,128)(2,1)}, u32[]{:S(2)}, u32[]{:S(2)}) collective-permute-start(bf16[256,1024]{1,0:T(8,128)(2,1)} %fusion.10), channel_id=1, source_target_pairs={{0,1},{1,0},{2,3},{3,2},{4,5},{5,4},{6,7},{7,6},{8,9},{9,8},{10,11... | collective-permute-start | bytes 1572872 | tf_op jit(solution)/shard_map/ppermute | solution.py:37
  427.2 13.0 %collective-permute-start.60 = (f32[42,1024]{1,0:T(8,128)S(1)}, f32[42,1024]{1,0:T(8,128)S(1)}, u32[]{:S(2)}, u32[]{:S(2)}) collective-permute-start(f32[42,1024]{1,0:T(8,128)S(1)} %concatenate.77), channel_id=1, source_target_pairs={{0,8},{8,0},{16,24},{24,16},{1,9},{9,1},{17,25},{25,17},{2,10},{10... | collective-permute-start | bytes 516104 | tf_op jit(solution)/shard_map/ppermute | solution.py:37
  427.3 14.6 %collective-permute-start.61 = (f32[42,1024]{1,0:T(8,128)S(1)}, f32[42,1024]{1,0:T(8,128)S(1)}, u32[]{:S(2)}, u32[]{:S(2)}) collective-permute-start(f32[42,1024]{1,0:T(8,128)S(1)} %concatenate.77), channel_id=1, source_target_pairs={{0,16},{8,24},{16,0},{24,8},{1,17},{9,25},{17,1},{25,9},{2,18},{10... | collective-permute-start | bytes 516104 | tf_op jit(solution)/shard_map/ppermute | solution.py:37
  428.9 13.0 %collective-permute-start.62 = (f32[42,1024]{1,0:T(8,128)S(1)}, f32[42,1024]{1,0:T(8,128)S(1)}, u32[]{:S(2)}, u32[]{:S(2)}) collective-permute-start(f32[42,1024]{1,0:T(8,128)S(1)} %concatenate.77), channel_id=1, source_target_pairs={{0,24},{8,16},{16,8},{24,0},{1,25},{9,17},{17,9},{25,1},{2,26},{10... | collective-permute-start | bytes 516104 | tf_op jit(solution)/shard_map/ppermute | solution.py:37
  430.8 11.5 %collective-permute-start.58 = (bf16[128,1024]{1,0:T(8,128)(2,1)S(1)}, bf16[128,1024]{1,0:T(8,128)(2,1)S(1)}, u32[]{:S(2)}, u32[]{:S(2)}) collective-permute-start(bf16[128,1024]{1,0:T(8,128)(2,1)S(1)} %get-tuple-element.444), channel_id=1, source_target_pairs={{0,2},{1,3},{2,0},{3,1},{4,6},{5,7},{6,4},{7,5},{8,10},{9,11},{10,... | collective-permute-start | bytes 786440 | tf_op jit(solution)/shard_map/ppermute | solution.py:37
  450.5 10.2 %collective-permute-start.69 = (f32[42,1024]{1,0:T(8,128)S(1)}, f32[42,1024]{1,0:T(8,128)S(1)}, u32[]{:S(2)}, u32[]{:S(2)}) collective-permute-start(f32[42,1024]{1,0:T(8,128)S(1)} %add_add_fusion.1), channel_id=1, source_target_pairs={{0,2},{1,3},{2,0},{3,1},{4,6},{5,7},{6,4},{7,5},{8,10},{9,11},{10,... | collective-permute-start | bytes 516104 | tf_op jit(solution)/shard_map/ppermute | solution.py:37
  452.3 10.2 %collective-permute-start.70 = (f32[42,1024]{1,0:T(8,128)S(1)}, f32[42,1024]{1,0:T(8,128)S(1)}, u32[]{:S(2)}, u32[]{:S(2)}) collective-permute-start(f32[42,1024]{1,0:T(8,128)S(1)} %add_add_fusion.1), channel_id=1, source_target_pairs={{0,3},{1,2},{2,1},{3,0},{4,7},{5,6},{6,5},{7,4},{8,11},{9,10},{10,... | collective-permute-start | bytes 516104 | tf_op jit(solution)/shard_map/ppermute | solution.py:37
  452.4 28.7 %collective-permute-start.65 = (bf16[576,1024]{1,0:T(8,128)(2,1)S(1)}, bf16[576,1024]{1,0:T(8,128)(2,1)S(1)}, u32[]{:S(2)}, u32[]{:S(2)}) collective-permute-start(bf16[576,1024]{1,0:T(8,128)(2,1)S(1)} %ff_grad.19), channel_id=1, source_target_pairs={{0,16},{8,24},{16,0},{24,8},{1,17},{9,25},{17,1},{25,9},{2,18},{10... | collective-permute-start | bytes 3538952 | tf_op jit(solution)/shard_map/ppermute | solution.py:37
  454.0 27.0 %collective-permute-start.63 = (bf16[512,384]{1,0:T(8,128)(2,1)S(1)}, bf16[512,384]{1,0:T(8,128)(2,1)S(1)}, u32[]{:S(2)}, u32[]{:S(2)}) collective-permute-start(bf16[512,384]{1,0:T(8,128)(2,1)S(1)} %get-tuple-element.441), channel_id=1, source_target_pairs={{0,0},{4,1},{1,2},{5,3},{2,4},{6,5},{3,6},{7,7},{8,8},{12,9},{9,10... | collective-permute-start | bytes 1179656 | tf_op jit(solution)/shard_map/ppermute | solution.py:970
  455.8 25.2 %collective-permute-start.64 = (bf16[512,384]{1,0:T(8,128)(2,1)S(1)}, bf16[512,384]{1,0:T(8,128)(2,1)S(1)}, u32[]{:S(2)}, u32[]{:S(2)}) collective-permute-start(bf16[512,384]{1,0:T(8,128)(2,1)S(1)} %get-tuple-element.442), channel_id=1, source_target_pairs={{4,0},{0,1},{5,2},{1,3},{6,4},{2,5},{7,6},{3,7},{12,8},{8,9},{13,1... | collective-permute-start | bytes 1179656 | tf_op jit(solution)/shard_map/ppermute | solution.py:970
  460.7 28.3 %collective-permute-start.67 = (bf16[256,1024]{1,0:T(8,128)(2,1)S(1)}, bf16[256,1024]{1,0:T(8,128)(2,1)S(1)}, u32[]{:S(2)}, u32[]{:S(2)}) collective-permute-start(bf16[256,1024]{1,0:T(8,128)(2,1)S(1)} %fusion.13), channel_id=1, source_target_pairs={{0,2},{1,3},{2,0},{3,1},{4,6},{5,7},{6,4},{7,5},{8,10},{9,11},{10,... | collective-permute-start | bytes 1572872 | tf_op jit(solution)/shard_map/ppermute | solution.py:37
  462.4 27.4 %collective-permute-start.66 = (bf16[256,1024]{1,0:T(8,128)(2,1)S(1)}, bf16[256,1024]{1,0:T(8,128)(2,1)S(1)}, u32[]{:S(2)}, u32[]{:S(2)}) collective-permute-start(bf16[256,1024]{1,0:T(8,128)(2,1)S(1)} %fusion.12), channel_id=1, source_target_pairs={{0,1},{1,0},{2,3},{3,2},{4,5},{5,4},{6,7},{7,6},{8,9},{9,8},{10,11... | collective-permute-start | bytes 1572872 | tf_op jit(solution)/shard_map/ppermute | solution.py:37
  489.8 11.1 %collective-permute-start.72 = (f32[42,1024]{1,0:T(8,128)S(1)}, f32[42,1024]{1,0:T(8,128)S(1)}, u32[]{:S(2)}, u32[]{:S(2)}) collective-permute-start(f32[42,1024]{1,0:T(8,128)S(1)} %add_add_fusion), channel_id=1, source_target_pairs={{0,4},{1,5},{2,6},{3,7},{4,0},{5,1},{6,2},{7,3},{8,12},{9,13},{10,... | collective-permute-start | bytes 516104 | tf_op jit(solution)/shard_map/ppermute | solution.py:37
  (130 other events, 843.2 us)
Sparse Core Ops, SparseCore 0:
  47.6 44.2 all-gather.2

commit v3 on v2

--- a/solution.py
+++ b/solution.py
@@ -17,7 +17,7 @@
 F32 = jnp.float32
 PAD = 16
 PAIR = 2 * HD
-VMEM_BYTES = 48 * 1024 * 1024
+LOG2E = 1.4426950408889634
 
 
 def product(left_mat, right_mat):
@@ -45,8 +45,8 @@
     return pl.BlockSpec(shape, lambda *_: (0,) * len(shape))
 
 
-def params():
-    return pltpu.CompilerParams(vmem_limit_bytes=VMEM_BYTES)
+def params(megabytes=24):
+    return pltpu.CompilerParams(vmem_limit_bytes=megabytes * 1024 * 1024)
 
 
 def cost(flops, nbytes, transcendentals=0):
@@ -68,13 +68,13 @@
                     top = pl.multiple_of(at_ref[0] * half, half)
                     low = pl.multiple_of((1 - at_ref[0]) * half, half)
                     w_ref[pl.ds(top, half), target] = mines[k][pl.ds(0, half), source]
-                    w_ref[pl.ds(low, half), target] = others[k][:, source]
+                    w_ref[pl.ds(low, half), target] = others[k][pl.ds(0, half), source]
                     b_ref[:, target] = mines[k][pl.ds(half, PAD), source][0:1].astype(F32)
 
 
 def assemble(at, mines, others, local):
     groups = len(mines)
-    half, width3 = others[0].shape
+    half, width3 = others[0].shape[0] - PAD, others[0].shape[1]
     return pl.pallas_call(
         functools.partial(assemble_kernel, groups, local, half),
         out_shape=(
@@ -138,16 +138,33 @@
     )(at, *pieces, w_seq, b_seq)
 
 
-def attn_forward_kernel(q_ref, k_ref, v_ref, *outs):
-    mixed = []
+def first_head(rows):
+    return lax.broadcasted_iota(jnp.int32, (rows, PAIR), 1) < HD
+
+
+def one_head(values, head, fill=0.0):
+    first = first_head(values.shape[0])
+    filled = jnp.full(values.shape, fill, values.dtype)
+    return jnp.where(first, filled, values) if head else jnp.where(first, values, filled)
+
+
+def attn_forward_kernel(q_ref, k_ref, v_ref, *refs):
+    outs, log_ref = refs[:-1], refs[-1]
+    rows = q_ref.shape[0]
+    mixed, log_sums = [], []
     for head in range(2):
-        lanes = pl.ds(head * HD, HD)
-        scores = against(q_ref[:, lanes], k_ref[:, lanes])
-        top = jnp.max(scores, axis=-1, keepdims=True)
-        weights = jnp.exp((scores - top) * SCALE)
-        total = jnp.sum(weights, axis=-1, keepdims=True)
-        mixed.append(product(weights.astype(BF), v_ref[:, lanes]) / total)
-    value = jnp.concatenate(mixed, axis=1).astype(BF)
+        scores = against(one_head(q_ref[...], head), k_ref[...])
+        top = jnp.max(scores, axis=-1, keepdims=True) * (SCALE * LOG2E)
+        weights = jnp.exp2(scores * (SCALE * LOG2E) - top).astype(BF)
+        both = product(weights, one_head(v_ref[...], head, 1.0))
+        total = pltpu.roll(both, HD, 1)
+        mixed.append(both / total)
+        log_sums.append(top + jnp.log(total) * LOG2E)
+    first = first_head(rows)
+    value = jnp.where(first, mixed[0], mixed[1]).astype(BF)
+    turned = jnp.where(first, log_sums[0], log_sums[1]).T
+    log_ref[0, 0:1, :] = turned[0:1]
+    log_ref[0, 1:2, :] = turned[HD : HD + 1]
     for j, out in enumerate(outs):
 
         @pl.when(pl.program_id(1) == j)
@@ -159,34 +176,37 @@
     rows = joint.shape[0] // parts
     pairs = joint.shape[1] // (3 * PAIR)
     shape = jax.ShapeDtypeStruct((rows, pairs * PAIR), BF)
-    return pl.pallas_call(
+    result = pl.pallas_call(
         attn_forward_kernel,
-        out_shape=(shape,) * parts,
+        out_shape=(shape,) * parts + (jax.ShapeDtypeStruct((pairs, 8, parts * rows), F32),),
         grid=(pairs, parts),
         in_specs=[
             pl.BlockSpec((rows, PAIR), lambda g, i: (i, 3 * g)),
             pl.BlockSpec((parts * rows, PAIR), lambda g, i: (0, 3 * g + 1)),
             pl.BlockSpec((parts * rows, PAIR), lambda g, i: (0, 3 * g + 2)),
         ],
-        out_specs=(pl.BlockSpec((rows, PAIR), lambda g, i: (0, g)),) * parts,
+        out_specs=(pl.BlockSpec((rows, PAIR), lambda g, i: (0, g)),) * parts
+        + (pl.BlockSpec((1, 8, rows), lambda g, i: (g, 0, i)),),
         compiler_params=params(),
         cost_estimate=cost(
             16 * joint.shape[0] ** 2 * pairs * PAIR, 3 * joint.size, 2 * pairs * joint.shape[0] ** 2
         ),
         name="attn_forward",
     )(joint, joint, joint)
-
-
-def attn_backward_kernel(parts, q_ref, k_ref, v_ref, *refs):
-    pieces = refs[:parts]
-    d_ref, g_ref, kt_ref, dk_acc, dv_acc = refs[-5:]
+    return result[:parts], result[parts]
+
+
+def attn_backward_kernel(parts, q_ref, k_ref, v_ref, log_ref, *refs):
+    pieces, heads = refs[:parts], refs[parts : 2 * parts]
+    d_ref, g_ref, o_ref, kt_ref, dk_acc, dv_acc = refs[-6:]
     step = pl.program_id(0)
     rows = q_ref.shape[0]
-    for j, piece in enumerate(pieces):
+    for j in range(parts):
 
         @pl.when(step == j)
-        def _(piece=piece):
-            g_ref[...] = piece[...]
+        def _(j=j):
+            g_ref[...] = pieces[j][...]
+            o_ref[...] = heads[j][...]
 
     @pl.when(step == 0)
     def _():
@@ -194,21 +214,20 @@
         dk_acc[...] = jnp.zeros_like(dk_acc)
         dv_acc[...] = jnp.zeros_like(dv_acc)
 
+    row_dots = (g_ref[...].astype(F32) * o_ref[...].astype(F32)).T
     dq_parts = []
     for head in range(2):
-        lanes = pl.ds(head * HD, HD)
-        queries = q_ref[:, lanes]
-        grads = g_ref[:, lanes]
-        scores = against(k_ref[:, lanes], queries)
-        top = jnp.max(scores, axis=0, keepdims=True)
-        weights = jnp.exp((scores - top) * SCALE)
-        probs = weights * (1.0 / jnp.sum(weights, axis=0, keepdims=True))
-        d_probs = against(v_ref[:, lanes], grads)
-        row_dot = jnp.sum(probs * d_probs, axis=0, keepdims=True)
+        queries = one_head(q_ref[...], head)
+        grads = one_head(g_ref[...], head)
+        row_dot = jnp.sum(row_dots[head * HD : (head + 1) * HD], axis=0, keepdims=True)
+        log_sum = log_ref[0, pl.ds(head, 1), :]
+        scores = against(k_ref[...], queries)
+        probs = jnp.exp2(scores * (SCALE * LOG2E) - log_sum)
+        d_probs = against(v_ref[...], grads)
         d_scores = (probs * (d_probs - row_dot)).astype(BF)
-        dv_acc[:, lanes] += product(probs.astype(BF), grads)
-        dk_acc[:, lanes] += product(d_scores, queries)
-        dq_parts.append(product(kt_ref[lanes, :], d_scores))
+        dv_acc[...] += product(probs.astype(BF), grads)
+        dk_acc[...] += product(d_scores, queries)
+        dq_parts.append(product(kt_ref[pl.ds(head * HD, HD), :], d_scores))
     d_ref[pl.ds(step * rows, rows), pl.ds(0, PAIR)] = (
         jnp.concatenate(dq_parts, axis=0).T * SCALE
     ).astype(BF)
@@ -219,7 +238,7 @@
         d_ref[:, pl.ds(2 * PAIR, PAIR)] = dv_acc[...].astype(BF)
 
 
-def attn_backward(joint, pieces, step, pair, kept):
+def attn_backward(joint, log_sums, pieces, heads, step, pair, kept):
     parts = len(pieces)
     rows = joint.shape[0] // parts
     return pl.pallas_call(
@@ -230,21 +249,24 @@
             pl.BlockSpec((rows, PAIR), lambda i: (i, 3 * pair)),
             pl.BlockSpec((parts * rows, PAIR), lambda i: (0, 3 * pair + 1)),
             pl.BlockSpec((parts * rows, PAIR), lambda i: (0, 3 * pair + 2)),
+            pl.BlockSpec((1, 8, rows), lambda i: (pair, 0, i)),
         ]
         + [pl.BlockSpec((rows, PAIR), lambda i: (step, pair))] * parts
+        + [pl.BlockSpec((rows, PAIR), lambda i: (0, pair))] * parts
         + [pl.BlockSpec(memory_space=pl.ANY)] * len(kept),
         out_specs=pl.BlockSpec((parts * rows, 3 * PAIR), lambda i: (0, pair)),
         scratch_shapes=[
+            pltpu.VMEM((rows, PAIR), BF),
             pltpu.VMEM((rows, PAIR), BF),
             pltpu.VMEM((PAIR, parts * rows), BF),
             pltpu.VMEM((parts * rows, PAIR), F32),
             pltpu.VMEM((parts * rows, PAIR), F32),
         ],
-        input_output_aliases={3 + parts + i: i for i in range(len(kept))},
-        compiler_params=params(),
-        cost_estimate=cost(20 * joint.shape[0] ** 2 * PAIR, 14 * joint.shape[0] * PAIR, 2 * joint.shape[0] ** 2),
+        input_output_aliases={4 + 2 * parts + i: i for i in range(len(kept))},
+        compiler_params=params(60),
+        cost_estimate=cost(1, 1),
         name="attn_backward",
-    )(joint, joint, joint, *pieces, *kept)
+    )(joint, joint, joint, log_sums, *pieces, *heads, *kept)
 
 
 def normed(values):
@@ -331,7 +353,7 @@
             )
             + (whole_block(width, width),),
         ),
-        compiler_params=params(),
+        compiler_params=params(60),
         cost_estimate=cost(2 * micros * rows * width * width, 20 * micros * rows * width),
         name="attend",
     )(at, *flat, *placed, w_mine, w_other, vectors)
@@ -475,27 +497,24 @@
     sum_ref[...] += total
 
 
-def ff_forward(first_low, init, blocks, kept, base, ff_half, total):
+def ff_forward(first_low, init, blocks, ff_half):
     rows, width = first_low.shape
     count = len(blocks)
-    column = pl.BlockSpec((rows, 2 * ff_half), lambda i: (0, base // 2 + i))
-    anywhere = pl.BlockSpec(memory_space=pl.ANY)
-    kept = list(kept)
+    column = pl.BlockSpec((rows, 2 * ff_half), lambda i: (0, i))
     return pl.pallas_call(
         functools.partial(ff_forward_kernel, ff_half, count),
         out_shape=(
             jax.ShapeDtypeStruct((rows, width), F32),
-            jax.ShapeDtypeStruct((rows, total), BF),
-            jax.ShapeDtypeStruct((rows, total), F32),
+            jax.ShapeDtypeStruct((rows, count * ff_half), BF),
+            jax.ShapeDtypeStruct((rows, count * ff_half), F32),
         ),
         grid=(count // 2,),
-        in_specs=[whole_block(rows, width)] * 2 + [anywhere] * (count + len(kept)),
+        in_specs=[whole_block(rows, width)] * 2 + [pl.BlockSpec(memory_space=pl.ANY)] * count,
         out_specs=(whole_block(rows, width), column, column),
         scratch_shapes=[
             pltpu.VMEM((2, 2) + blocks[0].shape, BF),
             pltpu.SemaphoreType.DMA((2, 2)),
         ],
-        input_output_aliases={2 + count + i: 1 + i for i in range(len(kept))},
         compiler_params=params(),
         cost_estimate=cost(
             8 * rows * width * ff_half * count,
@@ -503,11 +522,11 @@
             2 * rows * ff_half * count,
         ),
         name="ff_forward",
-    )(first_low, init, *blocks, *kept)
+    )(first_low, init, *blocks)
 
 
 def ff_backward_kernel(ff_half, count, d_fed_ref, init_ref, slope_ref, *refs):
-    d_upper_ref, d_first_ref, column_ref, buf, sem = refs[count:]
+    d_upper_ref, d_first_ref, column_ref, buf, sem = refs[-5:]
     cut = ff_half + PAD
 
     @pl.when(pl.program_id(0) == 0)
@@ -532,7 +551,7 @@
     return pl.pallas_call(
         functools.partial(ff_backward_kernel, ff_half, count),
         out_shape=(
-            jax.ShapeDtypeStruct((rows, count * ff_half), BF),
+            jax.ShapeDtypeStruct(slope.shape, BF),
             jax.ShapeDtypeStruct((rows, width), F32),
             jax.ShapeDtypeStruct((count // 2, 1, 2 * ff_half), F32),
         ),
@@ -552,22 +571,18 @@
     )(d_fed, init, slope, *blocks)
 
 
-def ff_grad_kernel(ff_half, spans, splits, joined, index_ref, first_ref, fed_ref, *refs):
+def ff_grad_kernel(ff_half, spans, splits, joined, first_ref, fed_ref, up_ref, hidden_ref, *refs):
     count = len(spans)
     total = splits[-1]
-    ups, hiddens, outs = (refs[i * count : (i + 1) * count] for i in range(3))
-    adds = list(refs[3 * count : 3 * count + sum(map(len, spans))])
-    results = refs[3 * count + len(adds) :]
+    adds = list(refs[: sum(map(len, spans))])
+    results = refs[len(adds) :]
     pieces = len(splits) - 1
+    ups = over_rows(up_ref[...], first_ref[...])
+    hiddens = over_rows(hidden_ref[...], fed_ref[...])
     for index in range(count):
         mine = [adds.pop(0) for _ in spans[index]]
-        values = (
-            (0, ff_half, lambda: over_rows(ups[index][...], first_ref[...])),
-            (ff_half, 2 * ff_half, lambda: over_rows(hiddens[index][...], fed_ref[...])),
-            (2 * ff_half, total, lambda: outs[index][...].astype(F32)),
-        )
-        for low, high, value in values:
-            share = value()
+        at = slice(index * ff_half, (index + 1) * ff_half)
+        for low, high, share in ((0, ff_half, ups[at]), (ff_half, total, hiddens[at])):
             for (start, stop), add in zip(spans[index], mine):
                 if start <= low and high <= stop:
                     share = share + add[pl.ds(low - start, high - low), :].astype(F32)
@@ -578,50 +593,147 @@
                     target[pl.ds(row, high - low), :] = share.astype(BF)
 
 
-def ff_grad(d_upper, hidden, first_low, d_fed, d_out, items, out_index, ff_half, out_half, cuts=(), joined=False):
+def ff_grad(d_upper, hidden, first_low, d_fed, place, adds, ff_half, cuts=(), joined=False, megabytes=24):
     rows, width = first_low.shape
     cols = width // 2
-    count = len(items)
-    total = 2 * ff_half + out_half
+    count = len(adds)
+    total = 2 * ff_half
     splits = (0, *cuts, total)
-    lanes = pl.BlockSpec((rows, cols), lambda i, s: (0, i))
-    adds = [add for _, arrived in items for add in arrived]
-    spans = tuple(tuple((start, start + height) for start, height, _, _ in arrived) for _, arrived in items)
-
-    def column(block):
-        return pl.BlockSpec((rows, ff_half), lambda i, s: (0, block))
-
-    def out_rows(j):
-        return pl.BlockSpec((out_half, cols), lambda i, s: (s[j], i))
+    lanes = pl.BlockSpec((rows, cols), lambda i: (0, i))
+    column = pl.BlockSpec((rows, count * ff_half), lambda i: (0, place))
+    spans = tuple(tuple((start, start + height) for start, height, _, _ in arrived) for arrived in adds)
+    flat = [add for arrived in adds for add in arrived]
 
     def lane_block(height, at=0):
-        return pl.BlockSpec((height, cols), lambda i, s: (at, i))
-
-    columns = [column(block) for block, _ in items]
+        return pl.BlockSpec((height, cols), lambda i: (at, i))
+
     heights = [count * total] if joined else [b - a for a, b in zip(splits, splits[1:])] * count
     return pl.pallas_call(
         functools.partial(ff_grad_kernel, ff_half, spans, splits, int(joined)),
         out_shape=tuple(jax.ShapeDtypeStruct((height, width), BF) for height in heights),
-        grid_spec=pltpu.PrefetchScalarGridSpec(
-            num_scalar_prefetch=1,
-            grid=(2,),
-            in_specs=[lanes, lanes]
-            + columns
-            + columns
-            + [out_rows(j) for j in range(count)]
-            + [lane_block(height, at) for _, height, _, at in adds],
-            out_specs=tuple(lane_block(height) for height in heights),
-        ),
+        grid=(2,),
+        in_specs=[lanes, lanes, column, column] + [lane_block(height, at) for _, height, _, at in flat],
+        out_specs=tuple(lane_block(height) for height in heights),
+        compiler_params=params(megabytes),
+        cost_estimate=cost(1, 1),
+        name="ff_grad",
+    )(first_low, d_fed, d_upper, hidden, *[array for _, _, array, _ in flat])
+
+
+def combine_kernel(spans, *refs):
+    arrays = list(refs[: sum(map(len, spans))])
+    step = pl.program_id(0)
+    for result, terms in zip(refs[len(arrays) :], spans):
+        total = 0.0
+        for low, high in terms:
+            term = arrays.pop(0)[...].astype(F32)
+            total = total + (term if (low, high) == terms[0] else jnp.where((low <= step) & (step < high), term, 0.0))
+        result[...] = total.astype(BF)
+
+
+def combine(*sums):
+    height, width = sums[0][0][1].shape
+    split = 4
+    rows = height // split
+    spans = tuple(tuple((low // rows, (low + array.shape[0]) // rows) for low, array in terms) for terms in sums)
+
+    def row_block(low, high):
+        return pl.BlockSpec((rows, width), lambda i: (jnp.clip(i - low, 0, high - low - 1), 0))
+
+    return pl.pallas_call(
+        functools.partial(combine_kernel, spans),
+        out_shape=tuple(jax.ShapeDtypeStruct((height, width), BF) for _ in sums),
+        grid=(split,),
+        in_specs=[row_block(*span) for terms in spans for span in terms],
+        out_specs=tuple(row_block(0, split) for _ in sums),
+        compiler_params=params(60),
+        cost_estimate=cost(1, 1),
+        name="combine",
+    )(*[array for terms in sums for _, array in terms])
+
+
+def diagonal_kernel(d_ref, w_ref, two_ref, one_ref):
+    share = against(d_ref[...], w_ref[...]).astype(BF)
+    half = two_ref.shape[0]
+    two_ref[...] = share[:half]
+    one_ref[...] = share[half:]
+
+
+def diagonal_share(d_joint, w_seq, parts):
+    rows, joint_width = d_joint.shape[0] // parts, d_joint.shape[1]
+    width = w_seq.shape[0]
+    half = (rows // 2, width)
+    return pl.pallas_call(
+        diagonal_kernel,
+        out_shape=(jax.ShapeDtypeStruct(half, BF),) * 2,
+        grid=(1,),
+        in_specs=[pl.BlockSpec((rows, joint_width), lambda i: (parts - 1, 0)), whole_block(*w_seq.shape)],
+        out_specs=(whole_block(*half),) * 2,
         compiler_params=params(),
-        cost_estimate=cost(
-            4 * rows * width * ff_half * count,
-            4 * rows * width + count * 4 * rows * ff_half + (count + len(adds)) * 2 * total * width,
-        ),
-        name="ff_grad",
-    )(
-        out_index, first_low, d_fed, *[d_upper] * count, *[hidden] * count, *[d_out] * count,
-        *[array for _, _, array, _ in adds],
-    )
+        cost_estimate=cost(1, 1),
+        name="diagonal_share",
+    )(d_joint, w_seq)
+
+
+def side_kernel(one_ref, two_ref, w_ref, to_two_ref, to_one_ref, via_one_ref, via_two_ref):
+    half = to_two_ref.shape[0]
+    share = against(one_ref[...], w_ref[...])
+    via_one_ref[pl.ds(0, half), :] = (share[:half] + to_two_ref[...].astype(F32)).astype(BF)
+    via_one_ref[pl.ds(half, half), :] = share[half:].astype(BF)
+    share = against(two_ref[...], w_ref[...])
+    via_two_ref[pl.ds(0, half), :] = share[:half].astype(BF)
+    via_two_ref[pl.ds(half, half), :] = (share[half:] + to_one_ref[...].astype(F32)).astype(BF)
+
+
+def side_shares(d_joint, w_seq, to_two, to_one, parts):
+    rows, joint_width = d_joint.shape[0] // parts, d_joint.shape[1]
+    width = w_seq.shape[0]
+    return pl.pallas_call(
+        side_kernel,
+        out_shape=(jax.ShapeDtypeStruct((rows, width), BF),) * 2,
+        grid=(1,),
+        in_specs=[
+            pl.BlockSpec((rows, joint_width), lambda i: (1, 0)),
+            pl.BlockSpec((rows, joint_width), lambda i: (2, 0)),
+            whole_block(*w_seq.shape),
+            whole_block(*to_two.shape),
+            whole_block(*to_one.shape),
+        ],
+        out_specs=(whole_block(rows, width),) * 2,
+        compiler_params=params(),
+        cost_estimate=cost(1, 1),
+        name="side_shares",
+    )(d_joint, d_joint, w_seq, to_two, to_one)
+
+
+def row_grad_kernel(micros, keep_ref, d_pre_ref, w_ref, *refs):
+    joints, arrived, out_ref = refs[:micros], refs[micros:-1], refs[-1]
+    for m in range(micros):
+
+        @pl.when(pl.program_id(0) == m)
+        def _(m=m):
+            total = d_pre_ref[...] + against(joints[m][...], w_ref[...])
+            total = total + arrived[2 * m][...].astype(F32) + arrived[2 * m + 1][...].astype(F32)
+            out_ref[...] = jnp.where(keep_ref[:, 0:1] > 0.0, total, 0.0)
+
+
+def row_grad(keep, d_pre, w_seq, d_joints, arrived, parts):
+    micros = len(d_joints)
+    rows, joint_width = d_joints[0].shape[0] // parts, d_joints[0].shape[1]
+    width = w_seq.shape[0]
+    block = pl.BlockSpec((rows, width), lambda i: (i, 0))
+    return pl.pallas_call(
+        functools.partial(row_grad_kernel, micros),
+        out_shape=jax.ShapeDtypeStruct(d_pre.shape, F32),
+        grid=(micros,),
+        in_specs=[pl.BlockSpec((rows, 128), lambda i: (i, 0)), block, whole_block(*w_seq.shape)]
+        + [whole_block(rows, joint_width)] * micros
+        + [whole_block(rows, width)] * (2 * micros),
+        out_specs=block,
+        compiler_params=params(60),
+        cost_estimate=cost(1, 1),
+        name="row_grad",
+    )(keep, d_pre, w_seq, *d_joints, *[a for pair in arrived for a in pair])
 
 
 def shards(
@@ -681,7 +793,6 @@
     far = count // 2
     ring_pos = jnp.where(rank % 2 == 0, rank // 2, count - 1 - rank // 2)
     offsets = [0] + [sign * s for s in range(1, far) for sign in (-1, 1)] + [far]
-    slots = {o: index for index, o in enumerate(offsets)}
 
     def forward(values):
         return lax.ppermute(values, "tensor", ring_fw)
@@ -713,7 +824,8 @@
         hots.append(hot.astype(F32))
         cots.append(product(matches.astype(BF), slot_grads[step]))
         seq_pos = jnp.concatenate([(part ^ j) * row_count + row_iota for j in range(parts)])
-        seq_hots.append(replacement(seq_pos, step)[2].astype(BF))
+        seq_hot = replacement(seq_pos, step)[2].astype(BF)
+        seq_hots.append(jnp.concatenate([seq_hot, jnp.ones_like(seq_hot[:, :2])], axis=1))
 
     joint_half = jnp.concatenate(
         [
@@ -750,7 +862,7 @@
     w_out_half = lax.all_gather(
         lax.dynamic_slice_in_dim(w_out, core * out_half, out_half, 0), "tensor", axis=0
     )
-    w_other = [swap(w[:half_rows], "dp", 1) for w in w_mine]
+    w_other = [swap(w, "dp", 1) for w in w_mine]
     w_seq, b_seq = assemble(
         jnp.stack([core] + [(group - i) % groups for i in range(groups)]).astype(jnp.int32),
         w_mine,
@@ -758,7 +870,7 @@
         local_width,
     )
 
-    joints, x_mine, x_other, heads = [], [], [], []
+    joints, x_mine, x_other, heads, log_sums, own_heads = [], [], [], [], [], []
     near = [piece[:cut], piece[cut:]]
     arrived = []
     at_core = core[None].astype(jnp.int32)
@@ -770,8 +882,10 @@
             twos.append(swap(placed[step + 1], "tensor", 2))
         moved = (forward(near[step]), backward(near[step]))
         joint, mine, other = project(at_core, rows, w_seq, b_seq)
-        pieces = attn_forward(joint, parts)
+        pieces, sums = attn_forward(joint, parts)
         joints.append(joint)
+        log_sums.append(sums)
+        own_heads.append(pieces)
         x_mine.append(mine)
         x_other.append(other)
         ones, twos, moved, pieces, near = fence(ones, twos, moved, pieces, near)
@@ -780,113 +894,85 @@
     fw, bw = (jnp.concatenate([arrived[0][d], arrived[1][d]], axis=0) for d in range(2))
     heads, fw, bw, w_out_half = fence(heads, fw, bw, w_out_half)
     w_out_other = swap(w_out_half, "dp", 1)
-    blocks = [piece, swap(piece, "dp", 1), fw, swap(fw, "dp", 1), bw, swap(bw, "dp", 1)]
+    blocks = [piece, swap(piece, "dp", 1), fw, bw, swap(fw, "dp", 1), swap(bw, "dp", 1)]
 
     vectors_one = jnp.stack([b_out, ln1_gain, ln1_bias, b_down] + [b_out] * 4).astype(F32)
     heads_out, norm_one, scale_one, pre_two, first_low, w_out_all = attend(
         jnp.concatenate([part_order, at_core]), heads, placed, w_out_half, w_out_other, vectors_one
     )
 
-    kept = ()
-
-    def work_on(s):
-        at = 0 if s == 0 else 4 * s - 2
-        return ff_forward(
-            first_low, pre_two, blocks[at : at + (2 if s in (0, far) else 4)], kept, at, ff_half,
-            2 * count * ff_half,
-        )
-
+    step_blocks = [blocks[:2], blocks[2:6]]
+    hidden_low, slopes = [None] * (far + 1), [None] * (far + 1)
     for s in range(2, far + 1):
         if s < far:
             moved = [forward(fw), backward(bw)]
         else:
             moved = [jnp.concatenate([forward(fw[:cut]), backward(bw[cut:])], axis=0)]
         for t in (0, 1) if s == 2 else (s - 1,):
-            pre_two, *kept = work_on(t)
+            pre_two, hidden_low[t], slopes[t] = ff_forward(first_low, pre_two, step_blocks[t], ff_half)
         if s < far:
-            moved, pre_two, kept = fence(moved, pre_two, kept)
+            if s < far - 1:
+                moved, pre_two = fence(moved, pre_two)
             fw, bw = moved
-        for block in moved:
-            blocks += [block, swap(block, "dp", 1)]
-    pre_two, *kept = work_on(far)
-    hidden_low, slope = kept
+        step_blocks.append(moved + [swap(block, "dp", 1) for block in moved])
+    pre_two, hidden_low[far], slopes[far] = ff_forward(first_low, pre_two, step_blocks[far], ff_half)
 
     vectors_two = jnp.stack([ln2_gain, ln2_bias] + [ln2_bias] * 6).astype(F32)
     layer_out, d_pre_two, d_fed, sums_two = second_norm(pre_two, jnp.concatenate(cots, axis=0), vectors_two)
-    d_upper, d_first, rel_b_up = ff_backward(d_fed, d_pre_two, slope, blocks, ff_half)
+    total = 2 * ff_half
+
+    def ff_blocks(offsets_, other, adds=None, cuts=(), megabytes=24):
+        s = abs(offsets_[0])
+        result = ff_grad(
+            d_uppers[s], hidden_low[s], first_low, d_fed, other, adds or [[] for _ in offsets_], ff_half, cuts,
+            bool(other), megabytes,
+        )
+        return result[0] if other else result
+
+    def both(s):
+        return [-s, s] if s else [0]
+
+    def summed(s, others, megabytes=24):
+        return ff_blocks(both(s), 0, [[(0, total, others, i)] for i in range(len(both(s)))], (), megabytes)
+
+    d_uppers, column_sums_ = [None] * (far + 1), [None] * (far + 1)
+
+    def back(s, d_first):
+        d_uppers[s], d_first, sums = ff_backward(d_fed, d_first, slopes[s], step_blocks[s], ff_half)
+        column_sums_[s] = sums.reshape(2, -1, ff_half)
+        return d_first
+
+    d_first = back(far, d_pre_two)
+    others = ff_blocks([far], 1)
+    others, d_uppers[far], d_first = fence(others, d_uppers[far], d_first)
+    others = swap(others, "dp", 1)
+    d_first = back(far - 1, d_first)
+    others, d_uppers[far], d_first = fence(others, d_uppers[far], d_first)
+    parcel = ff_blocks([far], 0, [[(0, total, others, 0)]], (ff_half,))
+    next_others = ff_blocks(both(far - 1), 1)
+    parcel, next_others, d_uppers[far - 1], d_first = fence(parcel, next_others, d_uppers[far - 1], d_first)
+    moved = [forward(parcel[0]), backward(parcel[1])]
+    others = swap(next_others, "dp", 1)
+    for s in range(far - 2, -1, -1):
+        d_first = back(s, d_first)
+    rel_b_up = jnp.concatenate(column_sums_, axis=1)
     d_pre_one, d_attended, sums_one, *d_heads = attend_back(
         part_order, d_first, norm_one, scale_one, vectors_one, w_out_all, parts
     )
-    d_out = over_rows(heads_out, d_attended).astype(BF)
+    others, d_uppers[far - 1], d_heads = fence(others, d_uppers[far - 1], d_heads)
     seq_grads = [d_heads[0]] + [swap(d_heads[j], "tensor", j) for j in range(1, parts)]
-
-    order_array = jnp.array(order, jnp.int32)
-
-    total = 2 * ff_half + out_half
-
-    def ff_blocks(items, other, cuts=()):
-        index = [2 * order_array[(ring_pos + o) % count] + (1 - core if other else core) for o, _ in items]
-        result = ff_grad(
-            d_upper, hidden_low, first_low, d_fed, d_out,
-            [(2 * slots[o] + other, arrived) for o, arrived in items],
-            jnp.stack(index).astype(jnp.int32), ff_half, out_half, cuts, bool(other),
-        )
-        return result[0] if other else result
-
-    d_joints = [() for _ in micros]
+    share = summed(far - 1, others)
+    next_others = ff_blocks(both(far - 2), 1)
+
+    d_out = over_rows(heads_out, d_attended).astype(BF).reshape(count, 2, out_half, width)
+    out_other = lax.dynamic_index_in_dim(d_out, 1 - core, 1, keepdims=False).reshape(-1, width)
+    out_mine = lax.dynamic_index_in_dim(d_out, core, 1, keepdims=False).reshape(-1, width)
+    moved, share, seq_grads, next_others, out_other = fence(moved, share, seq_grads, next_others, out_other)
+    parcel = combine([(0, share[0]), (ff_half, moved[1])], [(0, share[1]), (0, moved[0])])
+    parcel, next_others, seq_grads, out_other = fence(parcel, next_others, seq_grads, out_other)
+
+    d_joints = [jnp.zeros((), BF) for _ in micros]
     work = [(m, g) for m in micros for g in range(pairs)]
-
-    def row_share(step, j, low=0, high=row_count):
-        rows = d_joints[step][0][j * row_count + low : j * row_count + high]
-        return against(rows, w_seq)
-
-    def diagonal(step):
-        share = row_share(step, 3).astype(BF)
-        return (swap(share[:half_count], "tensor", 2), swap(share[half_count:], "tensor", 1))
-
-    def sides(step, arrived):
-        to_two, to_one = (a.astype(F32) for a in arrived)
-        via_one = row_share(step, 1) + jnp.pad(to_two, ((0, half_count), (0, 0)))
-        via_two = row_share(step, 2) + jnp.pad(to_one, ((half_count, 0), (0, 0)))
-        return (swap(via_one.astype(BF), "tensor", 1), swap(via_two.astype(BF), "tensor", 2))
-
-    def input_grad(step, arrived):
-        mine = slice(step * row_count, (step + 1) * row_count)
-        total = d_pre_one[mine] + row_share(step, 0) + arrived[0].astype(F32) + arrived[1].astype(F32)
-        return jnp.where(replaced_list[step][:, None], 0.0, total)
-
-    others = swap(ff_blocks([(far, [])], 1), "dp", 1)
-    next_others = ff_blocks([(far - 1, []), (1 - far, [])], 1)
-    parcel = ff_blocks([(far, [(0, total, others, 0)])], 0, (ff_half,))
-    seq_grads, parcel, next_others = fence(seq_grads, parcel, next_others)
-    partial = [() for _ in micros]
-    for index, s in enumerate(range(far, 0, -1)):
-        joints, d_joints, d_upper, parcel = fence(joints, d_joints, d_upper, parcel)
-        moved = [forward(parcel[0]), backward(parcel[1])]
-        others = swap(next_others, "dp", 1)
-        for m in micros:
-            if index == pairs * (m + 1):
-                partial[m] = diagonal(m)
-            elif index == pairs * (m + 1) + 1:
-                partial[m] = sides(m, partial[m])
-        next_others = ()
-        if s > 1:
-            next_others = ff_blocks([(s - 2, []), (2 - s, [])] if s > 2 else [(0, [])], 1)
-        if work:
-            m, g = work.pop(0)
-            d_joints[m] = (attn_backward(joints[m], seq_grads, m, g, d_joints[m]),)
-        moved, others, next_others, d_joints, partial = fence(moved, others, next_others, d_joints, partial)
-        if s > 1:
-            heights = (ff_half, total - ff_half) if s == far else (total, total)
-            starts = (0, ff_half) if s == far else (0, 0)
-            parcel = ff_blocks(
-                [
-                    (s - 1, [(0, total, others, 0), (starts[0], heights[0], moved[0], 0)]),
-                    (1 - s, [(0, total, others, 1), (starts[1], heights[1], moved[1], 0)]),
-                ],
-                0,
-            )
-    ff_sum = ff_blocks([(0, [(0, total, others, 0), (0, total, moved[0], 0), (0, total, moved[1], 0)])], 0)[0]
 
     def over_dp(values):
         bit = 2
@@ -895,43 +981,105 @@
             bit *= 2
         return values
 
+    def diagonal(step):
+        to_two, to_one = diagonal_share(d_joints[step], w_seq, parts)
+        return (swap(to_two, "tensor", 2), swap(to_one, "tensor", 1))
+
+    def side_parcels(step, arrived):
+        return side_shares(d_joints[step], w_seq, *arrived, parts)
+
+    def sides(parcels):
+        return (swap(parcels[0], "tensor", 1), swap(parcels[1], "tensor", 2))
+
+    def own_table(d_rows):
+        return lax.dot_general(
+            jnp.concatenate(hots, axis=0),
+            d_rows,
+            ROWS_DIMS,
+            precision=lax.Precision.HIGHEST,
+            preferred_element_type=F32,
+        )
+
+    partial, stage = [() for _ in micros], [0 for _ in micros]
+    d_w = []
+    table = own_table(d_pre_one)
+    plan = [[pair] for pair in work[:-pairs]] + [work[-pairs:]]
+    for index in range(far - 1):
+        s = far - 1 - index
+        if index:
+            parcel = combine([(0, share[0]), (0, moved[1])], [(0, share[1]), (0, moved[0])])
+        joints, d_joints, d_fed, parcel, next_others = fence(joints, d_joints, d_fed, parcel, next_others)
+        moved = [forward(parcel[1]), backward(parcel[0])]
+        others = swap(next_others, "dp", 1)
+        if index == 0:
+            out_mine = (out_mine.astype(F32) + swap(out_other, "dp", 1).astype(F32)).astype(BF)
+            out_sum = lax.psum_scatter(out_mine, "tensor", scatter_dimension=0, tiled=True)
+        for m in micros:
+            ready = max(i for i, pairs_ in enumerate(plan) if (m, pairs - 1) in pairs_) + 1
+            if index == ready:
+                partial[m], stage[m] = diagonal(m), 1
+            elif index == ready + 1:
+                partial[m], stage[m] = side_parcels(m, partial[m]), 2
+        if index == len(plan) - 1:
+            d_w = [(over_rows(x_other[m], d_joints[m]), over_rows(x_mine[m], d_joints[m])) for m in micros[:-1]]
+        next_others = ()
+        if s > 1:
+            next_others = ff_blocks(both(s - 2), 1, megabytes=60)
+        for m, g in plan[index] if index < len(plan) else ():
+            d_joints[m] = attn_backward(
+                joints[m], log_sums[m], seq_grads, own_heads[m], m, g, (d_joints[m],) if g else ()
+            )
+        share = summed(s - 1, others, 60)
+        moved, share, next_others, d_joints, partial, table, d_w = fence(
+            moved, share, next_others, d_joints, partial, table, d_w
+        )
+
+    last = micro_count - 1
+    parcel = combine([(0, share[0]), (0, moved[0]), (0, moved[1])])[0]
+    ff_up, ff_down = parcel[:ff_half], parcel[ff_half:]
+    for m in micros:
+        if stage[m] == 1:
+            partial[m], stage[m] = side_parcels(m, partial[m]), 2
+    d_w.append((over_rows(x_other[last], d_joints[last]), None))
+    other_half = sum(other for other, _ in d_w).astype(BF)
+    other_half, d_joints, partial, ff_up, ff_down = fence(other_half, d_joints, partial, ff_up, ff_down)
+    other_half = swap(other_half, "dp", 1)
+    ff_up = over_dp(ff_up)
+    for m in micros:
+        if stage[m] == 2:
+            partial[m], stage[m] = sides(partial[m]), 4
+        else:
+            partial[m] = diagonal(m)
+
     def over_bits(values, axis, low, high):
         while low < high:
-            if 2 * low < high:
-                near, side, both = (swap(values, axis, bit) for bit in (low, 2 * low, 3 * low))
-                values = (values + near) + (side + both)
-            else:
-                values = values + swap(values, axis, low)
+            bits = (low, 2 * low, 3 * low) if 2 * low < high else (low,)
+            sent = values.astype(BF)
+            terms = [sent.astype(F32)] + [swap(sent, axis, bit).astype(F32) for bit in bits]
+            while len(terms) > 1:
+                terms = [a + b for a, b in zip(terms[::2], terms[1::2])]
+            values = terms[0]
             low *= 4
         return values
 
-    rel_b_up = rel_b_up.reshape(count, 2, ff_half)
+    rel_b_up = jnp.swapaxes(rel_b_up, 0, 1)
     rel_b_up = jnp.where(own_first, rel_b_up, rel_b_up[:, ::-1]).reshape(count, ff_local)
     slot_of = [0] * count
-    for o, slot in slots.items():
+    for slot, o in enumerate(offsets):
         slot_of[o % count] = slot
     place = jnp.array([order.index(s) for s in range(count)], jnp.int32)
     wanted = jnp.array(slot_of, jnp.int32)[(place - ring_pos) % count]
     all_b_up = rel_b_up[wanted].reshape(-1, width)
     b_rows = all_b_up.shape[0]
-    table = jnp.zeros((vocab_count, width), F32)
-    for step in micros:
-        table = table + lax.dot_general(
-            hots[step],
-            d_pre_one[step * row_count : (step + 1) * row_count],
-            ROWS_DIMS,
-            precision=lax.Precision.HIGHEST,
-            preferred_element_type=F32,
-        )
-    hot_sum = sum(over_rows(seq_hots[m], d_joints[m][0]) for m in micros)
-    table = table + lax.dot_general(
-        hot_sum,
-        w_seq.astype(F32),
-        LAST_DIMS,
-        precision=lax.Precision.HIGHEST,
-        preferred_element_type=F32,
-    )
-    d_b_seq = sum(jnp.sum(d_joints[m][0].astype(F32), axis=0) for m in micros)
+    hot_sum = sum(over_rows(seq_hots[m], d_joints[m]) for m in micros)
+    d_b_seq = hot_sum[vocab_count]
+    rest, thirds = hot_sum, []
+    for _ in range(3):
+        thirds.append(rest.astype(BF))
+        rest = rest - thirds[-1].astype(F32)
+    table_rows = hot_sum.shape[0]
+    shares = against(jnp.concatenate(thirds, axis=0), w_seq).reshape(3, table_rows, width)
+    table = jnp.pad(table, ((0, table_rows - vocab_count), (0, 0))) + ((shares[2] + shares[1]) + shares[0])
     empty = jnp.zeros((width,), F32)
     d_b_query, d_b_value = (
         lax.dynamic_update_slice_in_dim(
@@ -942,19 +1090,15 @@
         )
         for a in (0, 2)
     )
-    small = jnp.concatenate(
-        [table, d_b_query[None], d_b_value[None], sums_one[:3], sums_two[:3], all_b_up], axis=0
-    )
-
-    last = micro_count - 1
-    other_half = sum(over_rows(x_other[m], d_joints[m][0]) for m in micros).astype(BF)
-    other_half = swap(other_half, "dp", 1)
-    if far < 2 + pairs * micro_count:
-        partial[last] = diagonal(last)
-    small = over_bits(small, "dp", 1, dp_count)
-    my_half = sum(over_rows(x_mine[m], d_joints[m][0]) for m in micros)
+    place_row = lax.broadcasted_iota(jnp.int32, table.shape, 0)
+    table = jnp.where(place_row == vocab_count, d_b_query[None], table)
+    table = jnp.where(place_row == vocab_count + 1, d_b_value[None], table)
+    small = jnp.concatenate([table, sums_one, sums_two, jnp.pad(all_b_up, ((0, -b_rows % 8), (0, 0)))], axis=0)
+
+    my_half = sum(mine for _, mine in d_w[: len(d_w)] if mine is not None)
+    my_half = my_half + sum(over_rows(x_mine[m], d_joints[m]) for m in micros if d_w[m][1] is None)
     my_half = (my_half + other_half.astype(F32)).astype(BF)
-    my_half, ff_sum, partial, small = fence(my_half, ff_sum, partial, small)
+    my_half, small, partial, ff_up, ff_down = fence(my_half, small, partial, ff_up, ff_down)
 
     if local_width != PAIR:
         columns = [
@@ -976,32 +1120,46 @@
         ).astype(F32)
         for k in range(groups)
     ).astype(BF)
-    if far < 2 + pairs * micro_count:
-        partial[last] = sides(last, partial[last])
-    ff_sum = over_dp(ff_sum)
+    small = over_bits(small, "dp", 1, dp_count)
+    ff_down = over_dp(ff_down)
+    out_sum = over_dp(out_sum)
+    if stage[last] < 4:
+        partial[last] = side_parcels(last, partial[last])
+    joint_sum, small, ff_up, ff_down, out_sum, partial = fence(
+        joint_sum, small, ff_up, ff_down, out_sum, partial
+    )
+
+    joint_sum = over_dp(joint_sum)
+    ff_other = swap(jnp.concatenate([ff_up, ff_down, out_sum], axis=0), "dp", 1)
+    if stage[last] < 4:
+        partial[last] = sides(partial[last])
     small = over_bits(small, "tensor", 1, min(4, count))
-    joint_sum, ff_sum, partial, small = fence(joint_sum, ff_sum, partial, small)
-
-    ff_other = swap(ff_sum, "dp", 1)
-    joint_sum = over_dp(joint_sum)
+    grad_w_up = by_core(ff_up, ff_other[:ff_half]).astype(F32).T
+    grad_w_down = by_core(ff_down, ff_other[ff_half : 2 * ff_half]).astype(F32)
+    grad_w_out = by_core(out_sum, ff_other[2 * ff_half :]).astype(F32)
+    joint_sum, small, partial, grad_w_up, grad_w_down, grad_w_out = fence(
+        joint_sum, small, partial, grad_w_up, grad_w_down, grad_w_out
+    )
+    joint_other = swap(joint_sum, "dp", 1)
     small = over_bits(small, "tensor", 4, count)
-    joint_sum, small, ff_other = fence(joint_sum, small, ff_other)
-    grad_joint = by_core(joint_sum, swap(joint_sum, "dp", 1)).astype(F32)
-    grad_w_up = by_core(ff_sum[:ff_half], ff_other[:ff_half]).astype(F32).T
-    grad_w_down = by_core(ff_sum[ff_half : 2 * ff_half], ff_other[ff_half : 2 * ff_half]).astype(F32)
-    grad_w_out = by_core(ff_sum[2 * ff_half :], ff_other[2 * ff_half :]).astype(F32)
-    grad_list = [input_grad(m, partial[m]) for m in micros]
+    keep = 1.0 - jnp.concatenate(replaced_list).astype(F32)
+    grad_rows = row_grad(
+        jnp.broadcast_to(keep[:, None], (keep.shape[0], 128)), d_pre_one, w_seq, d_joints, partial, parts
+    )
+    grad_joint = by_core(joint_sum, joint_other).astype(F32)
     grad_b_query, grad_b_value = (
         lax.dynamic_slice_in_dim(small[vocab_count + i], rank * local_width, local_width, 0) for i in range(2)
     )
+    sums_at = (table_rows, table_rows + 8)
     grad_b_out, grad_gone, grad_bone, grad_b_down, grad_gtwo, grad_btwo = (
-        small[vocab_count + 2 + i] for i in range(6)
-    )
-    grad_b_up = lax.dynamic_slice_in_dim(small[vocab_count + 8 :].reshape(-1), rank * ff_local, ff_local, 0)
+        small[at + i] for at in sums_at for i in range(3)
+    )
+    all_b_up = small[table_rows + 16 : table_rows + 16 + b_rows]
+    grad_b_up = lax.dynamic_slice_in_dim(all_b_up.reshape(-1), rank * ff_local, ff_local, 0)
 
     return (
         layer_out.reshape(micro_count, row_count, width),
-        jnp.stack(grad_list),
+        grad_rows.reshape(micro_count, row_count, width),
         small[:vocab_count],
         grad_joint[:, :local_width],
         grad_b_query,

time: 532 us -> 500 us (0.940)
  waiting for transfers between devices: 99.4 us -> 126 us
  starting transfers between devices: 96.8 us -> 77.3 us
  Pallas kernels: 192 us -> 177 us
  local copies, waits for them, and re-layouts: 66.4 us -> 53.3 us
  matrix products: 29.6 us -> 19 us
  other arithmetic: 15.8 us -> 21.7 us
    pallas_call x2 -> x11, Pallas kernels: 22.1 us -> 47.3 us  [the longest x2 21.6 us: attn_forward(): pl.pallas_call(attn_forward_kernel, out_shape=(shape,) * parts + (jax.Sha...]
    ppermute x53 -> x56, starting transfers between devices: 69.7 us -> 48.8 us  [swap(): return lax.ppermute(values, axis, [(i, i ^ bit) for i in range(count)])]
    ppermute x9, waiting for transfers between devices: 29.1 us -> 48.3 us  [forward(): return lax.ppermute(values, 'tensor', ring_fw)]
    ppermute x2, waiting for transfers between devices: 0.01 us -> 15.9 us  [shards(): lax.ppermute(lax.dynamic_slice_in_dim(my_half, (group - k) % groups * 3 *...]
    pallas_call x5, Pallas kernels: 37.6 us -> 23.3 us  [ff_forward(): pl.pallas_call(functools.partial(ff_forward_kernel, ff_half, count), out_...]
    unnamed x242 -> x215, local copies, waits for them, and re-layouts: 41.8 us -> 28.5 us
    pallas_call x10, Pallas kernels: 42.3 us -> 30.4 us  [ff_grad(): pl.pallas_call(functools.partial(ff_grad_kernel, ff_half, spans, splits,...]
    ppermute x53 -> x56, waiting for transfers between devices: 66.5 us -> 55.1 us  [swap(): return lax.ppermute(values, axis, [(i, i ^ bit) for i in range(count)])]
  transfers between devices with their start and end apart: 76 -> 80, of which waited for: 23 -> 23; matrix products, arithmetic and copies ran while one was open for 11% -> 13% of each run, Pallas kernels for 28% -> 33%
where the time goes in v3:
time: 500 us; the launch traced here: 491 us
  Pallas kernels  177 us (35%)
  waiting for transfers between devices  126 us (25%)
  starting transfers between devices  77.3 us (15%)
  local copies, waits for them, and re-layouts  53.3 us (11%)
  other arithmetic  21.7 us (4%)
  matrix products  19 us (4%)
  between operations  16.4 us (3%)
    ppermute x56, waiting for transfers between devices, swap(): return lax.ppermute(values, axis, [(i, i ^ bit) for i in range(count)])  55.1 us
    ppermute x56, starting transfers between devices, swap(): return lax.ppermute(values, axis, [(i, i ^ bit) for i in range(count)])  48.8 us
    ppermute x9, waiting for transfers between devices, forward(): return lax.ppermute(values, 'tensor', ring_fw)  48.3 us
    pallas_call x4, Pallas kernels, attn_backward(): pl.pallas_call(functools.partial(attn_backward_kernel, parts), out_shape=...  34.4 us
    pallas_call x10, Pallas kernels, ff_grad(): pl.pallas_call(functools.partial(ff_grad_kernel, ff_half, spans, splits,...  30.4 us
    unnamed x215, local copies, waits for them, and re-layouts  28.5 us
    pallas_call x5, Pallas kernels, ff_forward(): pl.pallas_call(functools.partial(ff_forward_kernel, ff_half, count), out_...  23.3 us
    pallas_call x2, Pallas kernels, attn_forward(): pl.pallas_call(attn_forward_kernel, out_shape=(shape,) * parts + (jax.Sha...  21.6 us
  transfers between devices with their start and end apart: 80, of which 23 were waited for; matrix products, arithmetic and copies ran while one was open for 13% of the time, Pallas kernels for 33%

profile of v3, /device:TPU:0, one launch (start us, length us, event | category | flops | bytes accessed | tf_op | source)
XLA Modules:
  0.0 490.5 jit_solution(6120966445663561397)
XLA Ops:
  9.9 3.0 collective-permute-start
  18.7 2.9 collective-permute-start.3
  21.6 4.0 constant_dynamic-slice_fusion.10
  28.5 2.1 constant_dynamic-slice_fusion.11
  36.4 7.0 %collective-permute-start.8 = (bf16[128,1024]{1,0:T(8,128)(2,1)}, bf16[128,1024]{1,0:T(8,128)(2,1)S(1)}, u32[]{:S(2)}, u32[]{:S(2)}) collective-permute-start(bf16[128,1024]{1,0:T(8,128)(2,1)} %slice.162), channel_id=1, source_target_pairs={{0,2},{1,3},{2,0},{3,1},{4,6},{5,7},{6,4},{7,5},{8,10},{9,11},{10,... | collective-permute-start | bytes 786440 | tf_op jit(solution)/shard_map/ppermute | solution.py:37
  46.9 2.1 collective-permute-start.7
  49.1 2.0 collective-permute-start.4
  51.1 2.0 assemble.1
  54.6 3.9 project.2
  58.5 10.8 %attn_forward.2 = (bf16[256,256]{1,0:T(8,128)(2,1)S(1)}, bf16[256,256]{1,0:T(8,128)(2,1)S(1)}, bf16[256,256]{1,0:T(8,128)(2,1)S(1)}, bf16[256,256]{1,0:T(8,128)(2,1)S(1)}, f32[2,8,1024]{2,1,0:T(8,128)S(1)}) custom-call(bf16[1024,768]{1,0:T(8,128)(2,1)S(1)} %get-tuple-element.401.q_ref.k_ref.v_ref, ...), custom_call_target="tpu_custom_call" | custom-call | flops 4294967296 | bytes 2359296 | tf_op jit(solution)/shard_map/attn_forward/pallas_call | solution.py:179
  69.4 11.2 %collective-permute-done.4.refs_1_ = bf16[256,1024]{1,0:T(8,128)(2,1)S(1)} collective-permute-done((bf16[256,1024]{1,0:T(8,128)(2,1)S(1)}, bf16[256,1024]{1,0:T(8,128)(2,1)S(1)}, u32[]{:S(2)}, u32[]{:S(2)}) %collective-permute-start.4) | collective-permute-done | bytes 524320 | tf_op jit(solution)/shard_map/ppermute | solution.py:37
  80.6 2.3 collective-permute-start.17
  84.8 2.0 collective-permute-start.16
  87.1 6.2 %collective-permute-done.17.refs_3_ = bf16[128,1024]{1,0:T(8,128)(2,1)S(1)} collective-permute-done((bf16[128,1024]{1,0:T(8,128)(2,1)S(1)}, bf16[128,1024]{1,0:T(8,128)(2,1)S(1)}, u32[]{:S(2)}, u32[]{:S(2)}) %collective-permute-start.17) | collective-permute-done | bytes 262176 | tf_op jit(solution)/shard_map/ppermute | solution.py:37
  96.5 2.6 project.3
  99.1 10.8 %attn_forward.3 = (bf16[256,256]{1,0:T(8,128)(2,1)S(1)}, bf16[256,256]{1,0:T(8,128)(2,1)S(1)}, bf16[256,256]{1,0:T(8,128)(2,1)S(1)}, bf16[256,256]{1,0:T(8,128)(2,1)S(1)}, f32[2,8,1024]{2,1,0:T(8,128)S(1)}) custom-call(bf16[1024,768]{1,0:T(8,128)(2,1)S(1)} %get-tuple-element.426.q_ref.k_ref.v_ref, ...), custom_call_target="tpu_custom_call" | custom-call | flops 4294967296 | bytes 2359296 | tf_op jit(solution)/shard_map/attn_forward/pallas_call | solution.py:179
  115.9 3.0 collective-permute-done.21.refs_7_
  120.5 2.3 collective-permute-done.22.refs_11_
  125.8 7.8 %attend.1 = (bf16[512,1024]{1,0:T(8,128)(2,1)}, f32[512,1024]{1,0:T(8,128)}, f32[512,128]{1,0:T(8,128)}, f32[512,1024]{1,0:T(8,128)}, bf16[512,1024]{1,0:T(8,128)(2,1)}, /*index=5*/bf16[1024,1024]{1,0:T(8,128)(2,1)}) custom-call(s32[5]{0:T(128)} %concatenate.97.at_ref, bf16[256,256]{1,0:T(8,128)(2,1)} %copy-done.36, bf16[256,256]{1,0:T(8,128)(2,1)} %copy-done.89, ...), custom_call_target="tpu_custom_call" | custom-call | flops 1073741824 | bytes 10485760 | tf_op jit(solution)/shard_map/attend/pallas_call | solution.py:337
  138.7 2.3 ff_forward.5
  142.7 5.6 %ff_forward.6 = (f32[512,1024]{1,0:T(8,128)S(1)}, bf16[512,1024]{1,0:T(8,128)(2,1)S(1)}, f32[512,1024]{1,0:T(8,128)S(1)}) custom-call(bf16[512,1024]{1,0:T(8,128)(2,1)S(1)} %copy-done.4, f32[512,1024]{1,0:T(8,128)S(1)} %get-tuple-element.303.init_ref, bf16[528,1024]{1,0:T(8,128)(2,1)} %pad_maximum_fusion.2.refs_0_, ...), custom_call_target="tpu_custom_call" | custom-call | flops 4294967296 | bytes 12582912 | tf_op jit(solution)/shard_map/ff_forward/pallas_call | solution.py:504
  151.7 23.9 %collective-permute-done.30.refs_0_ = bf16[528,1024]{1,0:T(8,128)(2,1)} collective-permute-done((bf16[528,1024]{1,0:T(8,128)(2,1)}, bf16[528,1024]{1,0:T(8,128)(2,1)}, u32[]{:S(2)}, u32[]{:S(2)}) %collective-permute-start.30) | collective-permute-done | bytes 1081376 | tf_op jit(solution)/shard_map/ppermute | solution.py:798
  180.9 9.4 %collective-permute-done.34 = bf16[272,1024]{1,0:T(8,128)(2,1)S(1)} collective-permute-done((bf16[272,1024]{1,0:T(8,128)(2,1)S(1)}, bf16[272,1024]{1,0:T(8,128)(2,1)S(1)}, u32[]{:S(2)}, u32[]{:S(2)}) %collective-permute-start.34) | collective-permute-done | bytes 557088 | tf_op jit(solution)/shard_map/ppermute | solution.py:798
  191.2 2.1 collective-permute-done.35
  196.2 5.6 %ff_forward.7 = (f32[512,1024]{1,0:T(8,128)S(1)}, bf16[512,1024]{1,0:T(8,128)(2,1)S(1)}, f32[512,1024]{1,0:T(8,128)S(1)}) custom-call(bf16[512,1024]{1,0:T(8,128)(2,1)S(1)} %copy-done.4, f32[512,1024]{1,0:T(8,128)S(1)} %copy-done.68, bf16[528,1024]{1,0:T(8,128)(2,1)} %collective-permute-done.23.refs_0_, bf16[528,1024]{1,0:T(8,128)(2,1)} %collective-permute-done.24.refs_1_, ...), custom_call_target="tpu_custom_call" | custom-call | flops 4294967296 | bytes 12582912 | tf_op jit(solution)/shard_map/ff_forward/pallas_call | solution.py:504
  203.1 6.0 %ff_forward.8 = (f32[512,1024]{1,0:T(8,128)S(1)}, bf16[512,1024]{1,0:T(8,128)(2,1)S(1)}, f32[512,1024]{1,0:T(8,128)S(1)}) custom-call(bf16[512,1024]{1,0:T(8,128)(2,1)S(1)} %copy-done.4, f32[512,1024]{1,0:T(8,128)S(1)} %get-tuple-element.308.init_ref, bf16[528,1024]{1,0:T(8,128)(2,1)} %collective-permute-done.30.refs_0_, ...), custom_call_target="tpu_custom_call" | custom-call | flops 4294967296 | bytes 12582912 | tf_op jit(solution)/shard_map/ff_forward/pallas_call | solution.py:504
  209.1 3.9 ff_forward.9
  213.0 3.0 second_norm.1
  216.0 3.3 ff_backward.5
  221.1 4.4 ff_backward.6
  225.6 2.8 ff_grad.12
  236.8 4.6 ff_backward.7
  241.4 4.9 %ff_backward.8 = (bf16[512,1024]{1,0:T(8,128)(2,1)S(1)}, f32[512,1024]{1,0:T(8,128)S(1)}, f32[2,1,512]{2,1,0:T(1,128)S(1)}) custom-call(bf16[512,1024]{1,0:T(8,128)(2,1)S(1)} %get-tuple-element.423.d_fed_ref.fed_ref, f32[512,1024]{1,0:T(8,128)S(1)} %get-tuple-element.334.init_ref, f32[512,1024]{1,0:T(8,128)S(1)} %copy-done.28, ...), custom_call_target="tpu_custom_call" | custom-call | flops 2147483648 | bytes 12582912 | tf_op jit(solution)/shard_map/ff_backward/pallas_call | solution.py:551
  249.9 3.7 attend_back.1
  258.5 1.9 ff_grad.14
  263.6 2.9 ff_grad.13
  269.8 4.2 combine.4
  277.9 4.0 ff_grad.16
  281.9 8.6 %attn_backward.4.refs_8_ = bf16[1024,768]{1,0:T(8,128)(2,1)} custom-call(bf16[1024,768]{1,0:T(8,128)(2,1)} %copy-done.11, bf16[1024,768]{1,0:T(8,128)(2,1)} %copy-done.11, bf16[1024,768]{1,0:T(8,128)(2,1)} %copy-done.11, f32[2,8,1024]{2,1,0:T(8,128)} %copy-done.54, bf16[512,256]{1,0:T(8,128)(2,1)} %copy-done.14, bf16[512,256]{1,0:T(8,128)(2,1)} %copy-done.71, ...), custom_call_target="tpu_custom_call" | custom-call | flops 1 | bytes 1 | tf_op jit(solution)/shard_map/attn_backward/pallas_call | solution.py:244
  290.5 4.8 ff_grad.15
  295.2 4.7 collective-permute-done.44.refs_3_
  301.1 4.2 combine.5
  305.4 2.6 fusion.2
  313.3 8.6 %attn_backward.5.d_ref.one_ref.two_ref.refs_0_ = bf16[1024,768]{1,0:T(8,128)(2,1)} custom-call(bf16[1024,768]{1,0:T(8,128)(2,1)} %copy-done.11, bf16[1024,768]{1,0:T(8,128)(2,1)} %copy-done.11, bf16[1024,768]{1,0:T(8,128)(2,1)} %copy-done.11, f32[2,8,1024]{2,1,0:T(8,128)} %copy-done.54, ...), custom_call_target="tpu_custom_call", output_to_operand_aliasing={{}: (12, {})} | custom-call | flops 1 | bytes 1 | tf_op jit(solution)/shard_map/attn_backward/pallas_call | solution.py:244
  321.9 3.1 ff_grad.18
  326.4 4.9 %ff_grad.17 = (bf16[512,1024]{1,0:T(8,128)(2,1)}, bf16[512,1024]{1,0:T(8,128)(2,1)}) custom-call(bf16[512,1024]{1,0:T(8,128)(2,1)} %get-tuple-element.299.first_ref, bf16[512,1024]{1,0:T(8,128)(2,1)} %copy-done.2, bf16[512,1024]{1,0:T(8,128)(2,1)} %copy-done.16, bf16[512,1024]{1,0:T(8,128)(2,1)} %copy-done.15, bf16[1024,1024]{1,0:T(8,128)(2,1)} %copy-done.70, ...), custom_call_target="tpu_custom_call" | custom-call | flops 1 | bytes 1 | tf_op jit(solution)/shard_map/ff_grad/pallas_call | solution.py:611
  331.3 10.3 %collective-permute-done.47.refs_3_ = bf16[512,1024]{1,0:T(8,128)(2,1)S(1)} collective-permute-done((bf16[512,1024]{1,0:T(8,128)(2,1)}, bf16[512,1024]{1,0:T(8,128)(2,1)S(1)}, u32[]{:S(2)}, u32[]{:S(2)}) %collective-permute-start.47) | collective-permute-done | bytes 1048608 | tf_op jit(solution)/shard_map/ppermute | solution.py:798
  341.6 2.2 collective-permute-done.48.refs_1_
  343.8 4.4 combine.6
  354.3 8.6 %attn_backward.6.refs_8_ = bf16[1024,768]{1,0:T(8,128)(2,1)} custom-call(bf16[1024,768]{1,0:T(8,128)(2,1)} %copy-done.10, bf16[1024,768]{1,0:T(8,128)(2,1)} %copy-done.10, bf16[1024,768]{1,0:T(8,128)(2,1)} %copy-done.10, f32[2,8,1024]{2,1,0:T(8,128)} %copy-done.53, bf16[512,256]{1,0:T(8,128)(2,1)} %copy-done.14, bf16[512,256]{1,0:T(8,128)(2,1)} %copy-done.71, ...), custom_call_target="tpu_custom_call" | custom-call | flops 1 | bytes 1 | tf_op jit(solution)/shard_map/attn_backward/pallas_call | solution.py:244
  362.9 8.6 %attn_backward.7.d_ref.one_ref.two_ref.refs_1_ = bf16[1024,768]{1,0:T(8,128)(2,1)} custom-call(bf16[1024,768]{1,0:T(8,128)(2,1)} %copy-done.10, bf16[1024,768]{1,0:T(8,128)(2,1)} %copy-done.10, bf16[1024,768]{1,0:T(8,128)(2,1)} %copy-done.10, f32[2,8,1024]{2,1,0:T(8,128)} %copy-done.53, ...), custom_call_target="tpu_custom_call", output_to_operand_aliasing={{}: (12, {})} | custom-call | flops 1 | bytes 1 | tf_op jit(solution)/shard_map/attn_backward/pallas_call | solution.py:244
  371.5 3.5 fusion.63
  375.0 2.2 fusion.62
  378.7 3.4 ff_grad.19.refs_0_
  382.1 3.3 collective-permute-done.53.to_two_ref
  386.1 3.9 combine.7
  391.7 2.4 fusion.64
  403.0 6.8 %collective-permute-done.60 = bf16[256,1024]{1,0:T(8,128)(2,1)S(1)} collective-permute-done((bf16[256,1024]{1,0:T(8,128)(2,1)S(1)}, bf16[256,1024]{1,0:T(8,128)(2,1)S(1)}, u32[]{:S(2)}, u32[]{:S(2)}) %collective-permute-start.60) | collective-permute-done | bytes 524320 | tf_op jit(solution)/shard_map/ppermute | solution.py:37
  411.3 8.9 %collective-permute-done.59.to_one_ref = bf16[128,1024]{1,0:T(8,128)(2,1)S(1)} collective-permute-done((bf16[128,1024]{1,0:T(8,128)(2,1)S(1)}, bf16[128,1024]{1,0:T(8,128)(2,1)S(1)}, u32[]{:S(2)}, u32[]{:S(2)}) %collective-permute-start.59) | collective-permute-done | bytes 262176 | tf_op jit(solution)/shard_map/ppermute | solution.py:37
  420.2 1.9 collective-permute-done.57.refs_3_
  426.3 3.5 collective-permute-start.62
  430.9 15.9 %collective-permute-done.62 = bf16[512,384]{1,0:T(8,128)(2,1)S(1)} collective-permute-done((bf16[512,384]{1,0:T(8,128)(2,1)S(1)}, bf16[512,384]{1,0:T(8,128)(2,1)S(1)}, u32[]{:S(2)}, u32[]{:S(2)}) %collective-permute-start.62) | collective-permute-done | bytes 393248 | tf_op jit(solution)/shard_map/ppermute | solution.py:1114
  462.1 5.6 %collective-permute-done.73.refs_4_ = bf16[256,1024]{1,0:T(8,128)(2,1)S(1)} collective-permute-done((bf16[256,1024]{1,0:T(8,128)(2,1)S(1)}, bf16[256,1024]{1,0:T(8,128)(2,1)S(1)}, u32[]{:S(2)}, u32[]{:S(2)}) %collective-permute-start.73) | collective-permute-done | bytes 524320 | tf_op jit(solution)/shard_map/ppermute | solution.py:37
  469.8 5.0 %row_grad.1 = f32[512,1024]{1,0:T(8,128)} custom-call(f32[512,128]{1,0:T(8,128)} %broadcast_in_dim.122.keep_ref, f32[512,1024]{1,0:T(8,128)} %copy-done.12, bf16[1024,768]{1,0:T(8,128)(2,1)} %copy-done.7, bf16[1024,768]{1,0:T(8,128)(2,1)} %attn_backward.5.d_ref.one_ref.two_ref.refs_0_, bf16[1024,768]{1,0:T(8,128)(2,1)} %attn_backward.7.d_ref.one_ref.two_ref.refs_1_, ...), custom_call_target="tpu_custom_call" | custom-call | flops 1 | bytes 1 | tf_op jit(solution)/shard_map/row_grad/pallas_call | solution.py:725
  (469 shorter events, 145.8 us)
Async XLA Ops:
  7.2 111.8 %all-gather.3.cloned.1.call-start = ((), (), s32[]{:S(2)}) async-start(), calls=%async_computation.2 | async-start | bytes 1179648 | tf_op jit(solution)/shard_map/all_gather | solution.py:862
  9.9 24.3 %collective-permute-start = (bf16[256,1024]{1,0:T(8,128)(2,1)S(1)}, bf16[256,1024]{1,0:T(8,128)(2,1)}, u32[]{:S(2)}, u32[]{:S(2)}) collective-permute-start(bf16[256,1024]{1,0:T(8,128)(2,1)S(1)} %fusion.3.refs_0_.refs_8_), channel_id=1, source_target_pairs={{0,1},{1,0},{2,3},{3,2},{4,5},{5,4},{6,7},{7,6},{8,9},{9,8},{10,11... | collective-permute-start | bytes 1572872 | tf_op jit(solution)/shard_map/ppermute | solution.py:37
  12.9 21.3 %collective-permute-start.1 = (bf16[256,1024]{1,0:T(8,128)(2,1)S(1)}, bf16[256,1024]{1,0:T(8,128)(2,1)}, u32[]{:S(2)}, u32[]{:S(2)}) collective-permute-start(bf16[256,1024]{1,0:T(8,128)(2,1)S(1)} %fusion.3.refs_0_.refs_8_), channel_id=1, source_target_pairs={{0,2},{1,3},{2,0},{3,1},{4,6},{5,7},{6,4},{7,5},{8,10},{9,11},{10,... | collective-permute-start | bytes 1572872 | tf_op jit(solution)/shard_map/ppermute | solution.py:37
  17.1 16.5 %collective-permute-start.2 = (bf16[528,384]{1,0:T(8,128)(2,1)}, bf16[528,384]{1,0:T(8,128)(2,1)S(1)}, u32[]{:S(2)}, u32[]{:S(2)}) collective-permute-start(bf16[528,384]{1,0:T(8,128)(2,1)} %fusion.19), channel_id=1, source_target_pairs={{0,0},{1,4},{2,1},{3,5},{4,2},{5,6},{6,3},{7,7},{8,8},{9,12},{10,9... | collective-permute-start | bytes 1216520 | tf_op jit(solution)/shard_map/ppermute | solution.py:858
  18.7 15.5 %collective-permute-start.3 = (bf16[528,384]{1,0:T(8,128)(2,1)}, bf16[528,384]{1,0:T(8,128)(2,1)}, u32[]{:S(2)}, u32[]{:S(2)}) collective-permute-start(bf16[528,384]{1,0:T(8,128)(2,1)} %fusion.19), channel_id=1, source_target_pairs={{0,4},{1,0},{2,5},{3,1},{4,6},{5,2},{6,7},{7,3},{8,12},{9,8},{10,1... | collective-permute-start | bytes 1216520 | tf_op jit(solution)/shard_map/ppermute | solution.py:858
  34.2 12.7 %collective-permute-start.10 = (bf16[528,384]{1,0:T(8,128)(2,1)S(1)}, bf16[528,384]{1,0:T(8,128)(2,1)S(1)}, u32[]{:S(2)}, u32[]{:S(2)}) collective-permute-start(bf16[528,384]{1,0:T(8,128)(2,1)S(1)} %collective-permute-done.2.refs_0_), channel_id=1, source_target_pairs={{0,8},{8,0},{16,24},{24,16},{1,9},{9,1},{17,25},{25,17},{2,10},{10... | collective-permute-start | bytes 1216520 | tf_op jit(solution)/shard_map/ppermute | solution.py:37
  34.2 14.9 %collective-permute-start.11 = (bf16[528,384]{1,0:T(8,128)(2,1)}, bf16[528,384]{1,0:T(8,128)(2,1)}, u32[]{:S(2)}, u32[]{:S(2)}) collective-permute-start(bf16[528,384]{1,0:T(8,128)(2,1)} %collective-permute-done.3.refs_1_), channel_id=1, source_target_pairs={{0,8},{8,0},{16,24},{24,16},{1,9},{9,1},{17,25},{25,17},{2,10},{10... | collective-permute-start | bytes 1216520 | tf_op jit(solution)/shard_map/ppermute | solution.py:37
  36.4 16.7 %collective-permute-start.8 = (bf16[128,1024]{1,0:T(8,128)(2,1)}, bf16[128,1024]{1,0:T(8,128)(2,1)S(1)}, u32[]{:S(2)}, u32[]{:S(2)}) collective-permute-start(bf16[128,1024]{1,0:T(8,128)(2,1)} %slice.162), channel_id=1, source_target_pairs={{0,2},{1,3},{2,0},{3,1},{4,6},{5,7},{6,4},{7,5},{8,10},{9,11},{10,... | collective-permute-start | bytes 786440 | tf_op jit(solution)/shard_map/ppermute | solution.py:37
  46.7 330.4 %reduce-scatter.2.cloned.1.call-start = ((), (), s32[]{:S(2)}) async-start(), calls=%async_computation.1 | async-start | bytes 1179648 | tf_op jit(solution)/shard_map/reduce_scatter | solution.py:1016
  46.8 33.8 %collective-permute-start.6 = (bf16[272,1024]{1,0:T(8,128)(2,1)S(1)}, bf16[272,1024]{1,0:T(8,128)(2,1)S(1)}, u32[]{:S(2)}, u32[]{:S(2)}) collective-permute-start(bf16[272,1024]{1,0:T(8,128)(2,1)S(1)} %slice.161), channel_id=1, source_target_pairs={{0,2},{2,4},{4,6},{6,7},{7,5},{5,3},{3,1},{1,0},{8,10},{10,12},{12... | collective-permute-start | bytes 1671176 | tf_op jit(solution)/shard_map/ppermute | solution.py:798
  46.9 33.7 %collective-permute-start.7 = (bf16[272,1024]{1,0:T(8,128)(2,1)S(1)}, bf16[272,1024]{1,0:T(8,128)(2,1)S(1)}, u32[]{:S(2)}, u32[]{:S(2)}) collective-permute-start(bf16[272,1024]{1,0:T(8,128)(2,1)S(1)} %slice.161), channel_id=1, source_target_pairs={{2,0},{4,2},{6,4},{7,6},{5,7},{3,5},{1,3},{0,1},{10,8},{12,10},{14... | collective-permute-start | bytes 1671176 | tf_op jit(solution)/shard_map/ppermute | solution.py:801
  49.1 31.5 %collective-permute-start.4 = (bf16[256,1024]{1,0:T(8,128)(2,1)S(1)}, bf16[256,1024]{1,0:T(8,128)(2,1)S(1)}, u32[]{:S(2)}, u32[]{:S(2)}) collective-permute-start(bf16[256,1024]{1,0:T(8,128)(2,1)S(1)} %fusion.4.refs_0_.refs_9_), channel_id=1, source_target_pairs={{0,1},{1,0},{2,3},{3,2},{4,5},{5,4},{6,7},{7,6},{8,9},{9,8},{10,11... | collective-permute-start | bytes 1572872 | tf_op jit(solution)/shard_map/ppermute | solution.py:37
  53.1 27.5 %collective-permute-start.5 = (bf16[256,1024]{1,0:T(8,128)(2,1)S(1)}, bf16[256,1024]{1,0:T(8,128)(2,1)S(1)}, u32[]{:S(2)}, u32[]{:S(2)}) collective-permute-start(bf16[256,1024]{1,0:T(8,128)(2,1)S(1)} %fusion.4.refs_0_.refs_9_), channel_id=1, source_target_pairs={{0,2},{1,3},{2,0},{3,1},{4,6},{5,7},{6,4},{7,5},{8,10},{9,11},{10,... | collective-permute-start | bytes 1572872 | tf_op jit(solution)/shard_map/ppermute | solution.py:37
  80.6 12.7 %collective-permute-start.17 = (bf16[128,1024]{1,0:T(8,128)(2,1)S(1)}, bf16[128,1024]{1,0:T(8,128)(2,1)S(1)}, u32[]{:S(2)}, u32[]{:S(2)}) collective-permute-start(bf16[128,1024]{1,0:T(8,128)(2,1)S(1)} %slice.165), channel_id=1, source_target_pairs={{0,2},{1,3},{2,0},{3,1},{4,6},{5,7},{6,4},{7,5},{8,10},{9,11},{10,... | collective-permute-start | bytes 786440 | tf_op jit(solution)/shard_map/ppermute | solution.py:37
  82.9 11.9 %collective-permute-start.18 = (bf16[128,1024]{1,0:T(8,128)(2,1)S(1)}, bf16[128,1024]{1,0:T(8,128)(2,1)S(1)}, u32[]{:S(2)}, u32[]{:S(2)}) collective-permute-start(bf16[128,1024]{1,0:T(8,128)(2,1)S(1)} %slice.166), channel_id=1, source_target_pairs={{0,1},{1,0},{2,3},{3,2},{4,5},{5,4},{6,7},{7,6},{8,9},{9,8},{10,11... | collective-permute-start | bytes 786440 | tf_op jit(solution)/shard_map/ppermute | solution.py:37
  84.8 25.3 %collective-permute-start.15 = (bf16[256,1024]{1,0:T(8,128)(2,1)S(1)}, bf16[256,1024]{1,0:T(8,128)(2,1)S(1)}, u32[]{:S(2)}, u32[]{:S(2)}) collective-permute-start(bf16[256,1024]{1,0:T(8,128)(2,1)S(1)} %slice.164), channel_id=1, source_target_pairs={{0,2},{2,4},{4,6},{6,7},{7,5},{5,3},{3,1},{1,0},{8,10},{10,12},{12... | collective-permute-start | bytes 1572872 | tf_op jit(solution)/shard_map/ppermute | solution.py:798
  84.8 25.2 %collective-permute-start.16 = (bf16[256,1024]{1,0:T(8,128)(2,1)S(1)}, bf16[256,1024]{1,0:T(8,128)(2,1)S(1)}, u32[]{:S(2)}, u32[]{:S(2)}) collective-permute-start(bf16[256,1024]{1,0:T(8,128)(2,1)S(1)} %slice.164), channel_id=1, source_target_pairs={{2,0},{4,2},{6,4},{7,6},{5,7},{3,5},{1,3},{0,1},{10,8},{12,10},{14... | collective-permute-start | bytes 1572872 | tf_op jit(solution)/shard_map/ppermute | solution.py:801
  86.8 26.2 %collective-permute-start.12 = (bf16[256,256]{1,0:T(8,128)(2,1)S(1)}, bf16[256,256]{1,0:T(8,128)(2,1)S(1)}, u32[]{:S(2)}, u32[]{:S(2)}) collective-permute-start(bf16[256,256]{1,0:T(8,128)(2,1)S(1)} %get-tuple-element.270.refs_5_), channel_id=1, source_target_pairs={{0,1},{1,0},{2,3},{3,2},{4,5},{5,4},{6,7},{7,6},{8,9},{9,8},{10,11... | collective-permute-start | bytes 393224 | tf_op jit(solution)/shard_map/ppermute | solution.py:37
  93.3 22.5 %collective-permute-start.13 = (bf16[256,256]{1,0:T(8,128)(2,1)S(1)}, bf16[256,256]{1,0:T(8,128)(2,1)S(1)}, u32[]{:S(2)}, u32[]{:S(2)}) collective-permute-start(bf16[256,256]{1,0:T(8,128)(2,1)S(1)} %get-tuple-element.271.refs_6_), channel_id=1, source_target_pairs={{0,2},{1,3},{2,0},{3,1},{4,6},{5,7},{6,4},{7,5},{8,10},{9,11},{10,... | collective-permute-start | bytes 393224 | tf_op jit(solution)/shard_map/ppermute | solution.py:37
  94.8 21.0 %collective-permute-start.14 = (bf16[256,256]{1,0:T(8,128)(2,1)S(1)}, bf16[256,256]{1,0:T(8,128)(2,1)S(1)}, u32[]{:S(2)}, u32[]{:S(2)}) collective-permute-start(bf16[256,256]{1,0:T(8,128)(2,1)S(1)} %get-tuple-element.272.refs_7_), channel_id=1, source_target_pairs={{0,3},{1,2},{2,1},{3,0},{4,7},{5,6},{6,5},{7,4},{8,11},{9,10},{10,... | collective-permute-start | bytes 393224 | tf_op jit(solution)/shard_map/ppermute | solution.py:37
  119.0 14.6 %collective-permute-start.25 = (bf16[528,1024]{1,0:T(8,128)(2,1)S(1)}, bf16[528,1024]{1,0:T(8,128)(2,1)S(1)}, u32[]{:S(2)}, u32[]{:S(2)}) collective-permute-start(bf16[528,1024]{1,0:T(8,128)(2,1)S(1)} %fusion.6.refs_0_), channel_id=1, source_target_pairs={{0,8},{8,0},{16,24},{24,16},{1,9},{9,1},{17,25},{25,17},{2,10},{10... | collective-permute-start | bytes 3244040 | tf_op jit(solution)/shard_map/ppermute | solution.py:37
  119.5 23.2 %collective-permute-start.26 = (bf16[528,1024]{1,0:T(8,128)(2,1)}, bf16[528,1024]{1,0:T(8,128)(2,1)}, u32[]{:S(2)}, u32[]{:S(2)}) collective-permute-start(bf16[528,1024]{1,0:T(8,128)(2,1)} %pad_maximum_fusion.2.refs_0_), channel_id=1, source_target_pairs={{0,8},{8,0},{16,24},{24,16},{1,9},{9,1},{17,25},{25,17},{2,10},{10... | collective-permute-start | bytes 3244040 | tf_op jit(solution)/shard_map/ppermute | solution.py:37
  119.5 23.1 %collective-permute-start.27 = (bf16[528,1024]{1,0:T(8,128)(2,1)}, bf16[528,1024]{1,0:T(8,128)(2,1)}, u32[]{:S(2)}, u32[]{:S(2)}) collective-permute-start(bf16[528,1024]{1,0:T(8,128)(2,1)} %pad_maximum_fusion.3.refs_1_), channel_id=1, source_target_pairs={{0,8},{8,0},{16,24},{24,16},{1,9},{9,1},{17,25},{25,17},{2,10},{10... | collective-permute-start | bytes 3244040 | tf_op jit(solution)/shard_map/ppermute | solution.py:37
  120.0 29.6 %collective-permute-start.23 = (bf16[528,1024]{1,0:T(8,128)(2,1)}, bf16[528,1024]{1,0:T(8,128)(2,1)}, u32[]{:S(2)}, u32[]{:S(2)}) collective-permute-start(bf16[528,1024]{1,0:T(8,128)(2,1)} %pad_maximum_fusion.2.refs_0_), channel_id=1, source_target_pairs={{0,2},{2,4},{4,6},{6,7},{7,5},{5,3},{3,1},{1,0},{8,10},{10,12},{12... | collective-permute-start | bytes 3244040 | tf_op jit(solution)/shard_map/ppermute | solution.py:798
  122.8 26.8 %collective-permute-start.24 = (bf16[528,1024]{1,0:T(8,128)(2,1)}, bf16[528,1024]{1,0:T(8,128)(2,1)}, u32[]{:S(2)}, u32[]{:S(2)}) collective-permute-start(bf16[528,1024]{1,0:T(8,128)(2,1)} %pad_maximum_fusion.3.refs_1_), channel_id=1, source_target_pairs={{2,0},{4,2},{6,4},{7,6},{5,7},{3,5},{1,3},{0,1},{10,8},{12,10},{14... | collective-permute-start | bytes 3244040 | tf_op jit(solution)/shard_map/ppermute | solution.py:801
  149.7 26.0 %collective-permute-start.30 = (bf16[528,1024]{1,0:T(8,128)(2,1)}, bf16[528,1024]{1,0:T(8,128)(2,1)}, u32[]{:S(2)}, u32[]{:S(2)}) collective-permute-start(bf16[528,1024]{1,0:T(8,128)(2,1)} %collective-permute-done.23.refs_0_), channel_id=1, source_target_pairs={{0,2},{2,4},{4,6},{6,7},{7,5},{5,3},{3,1},{1,0},{8,10},{10,12},{12... | collective-permute-start | bytes 3244040 | tf_op jit(solution)/shard_map/ppermute | solution.py:798
  150.4 27.5 %collective-permute-start.31 = (bf16[528,1024]{1,0:T(8,128)(2,1)}, bf16[528,1024]{1,0:T(8,128)(2,1)}, u32[]{:S(2)}, u32[]{:S(2)}) collective-permute-start(bf16[528,1024]{1,0:T(8,128)(2,1)} %collective-permute-done.24.refs_1_), channel_id=1, source_target_pairs={{2,0},{4,2},{6,4},{7,6},{5,7},{3,5},{1,3},{0,1},{10,8},{12,10},{14... | collective-permute-start | bytes 3244040 | tf_op jit(solution)/shard_map/ppermute | solution.py:801
  176.8 13.6 %collective-permute-start.34 = (bf16[272,1024]{1,0:T(8,128)(2,1)S(1)}, bf16[272,1024]{1,0:T(8,128)(2,1)S(1)}, u32[]{:S(2)}, u32[]{:S(2)}) collective-permute-start(bf16[272,1024]{1,0:T(8,128)(2,1)S(1)} %slice.202), channel_id=1, source_target_pairs={{0,2},{2,4},{4,6},{6,7},{7,5},{5,3},{3,1},{1,0},{8,10},{10,12},{12... | collective-permute-start | bytes 1671176 | tf_op jit(solution)/shard_map/ppermute | solution.py:798
  177.4 18.4 %collective-permute-start.28 = (bf16[528,1024]{1,0:T(8,128)(2,1)}, bf16[528,1024]{1,0:T(8,128)(2,1)}, u32[]{:S(2)}, u32[]{:S(2)}) collective-permute-start(bf16[528,1024]{1,0:T(8,128)(2,1)} %collective-permute-done.23.refs_0_), channel_id=1, source_target_pairs={{0,8},{8,0},{16,24},{24,16},{1,9},{9,1},{17,25},{25,17},{2,10},{10... | collective-permute-start | bytes 3244040 | tf_op jit(solution)/shard_map/ppermute | solution.py:37
  177.4 18.4 %collective-permute-start.29 = (bf16[528,1024]{1,0:T(8,128)(2,1)}, bf16[528,1024]{1,0:T(8,128)(2,1)}, u32[]{:S(2)}, u32[]{:S(2)}) collective-permute-start(bf16[528,1024]{1,0:T(8,128)(2,1)} %collective-permute-done.24.refs_1_), channel_id=1, source_target_pairs={{0,8},{8,0},{16,24},{24,16},{1,9},{9,1},{17,25},{25,17},{2,10},{10... | collective-permute-start | bytes 3244040 | tf_op jit(solution)/shard_map/ppermute | solution.py:37
  179.0 14.3 %collective-permute-start.35 = (bf16[256,1024]{1,0:T(8,128)(2,1)S(1)}, bf16[256,1024]{1,0:T(8,128)(2,1)S(1)}, u32[]{:S(2)}, u32[]{:S(2)}) collective-permute-start(bf16[256,1024]{1,0:T(8,128)(2,1)S(1)} %slice.203), channel_id=1, source_target_pairs={{2,0},{4,2},{6,4},{7,6},{5,7},{3,5},{1,3},{0,1},{10,8},{12,10},{14... | collective-permute-start | bytes 1572872 | tf_op jit(solution)/shard_map/ppermute | solution.py:801
  180.9 22.2 %collective-permute-start.32 = (bf16[528,1024]{1,0:T(8,128)(2,1)}, bf16[528,1024]{1,0:T(8,128)(2,1)}, u32[]{:S(2)}, u32[]{:S(2)}) collective-permute-start(bf16[528,1024]{1,0:T(8,128)(2,1)} %collective-permute-done.30.refs_0_), channel_id=1, source_target_pairs={{0,8},{8,0},{16,24},{24,16},{1,9},{9,1},{17,25},{25,17},{2,10},{10... | collective-permute-start | bytes 3244040 | tf_op jit(solution)/shard_map/ppermute | solution.py:37
  190.3 12.8 %collective-permute-start.33 = (bf16[528,1024]{1,0:T(8,128)(2,1)}, bf16[528,1024]{1,0:T(8,128)(2,1)}, u32[]{:S(2)}, u32[]{:S(2)}) collective-permute-start(bf16[528,1024]{1,0:T(8,128)(2,1)} %collective-permute-done.31.refs_1_), channel_id=1, source_target_pairs={{0,8},{8,0},{16,24},{24,16},{1,9},{9,1},{17,25},{25,17},{2,10},{10... | collective-permute-start | bytes 3244040 | tf_op jit(solution)/shard_map/ppermute | solution.py:37
  194.2 14.9 %collective-permute-start.36 = (bf16[528,1024]{1,0:T(8,128)(2,1)}, bf16[528,1024]{1,0:T(8,128)(2,1)}, u32[]{:S(2)}, u32[]{:S(2)}) collective-permute-start(bf16[528,1024]{1,0:T(8,128)(2,1)} %constant_dynamic-update-slice_fusion.refs_0_), channel_id=1, source_target_pairs={{0,8},{8,0},{16,24},{24,16},{1,9},{9,1},{17,25},{25,17},{2,10},{10... | collective-permute-start | bytes 3244040 | tf_op jit(solution)/shard_map/ppermute | solution.py:37
  231.3 22.3 %collective-permute-start.40 = (bf16[1024,1024]{1,0:T(8,128)(2,1)}, bf16[1024,1024]{1,0:T(8,128)(2,1)}, u32[]{:S(2)}, u32[]{:S(2)}) collective-permute-start(bf16[1024,1024]{1,0:T(8,128)(2,1)} %ff_grad.12), channel_id=1, source_target_pairs={{0,8},{8,0},{16,24},{24,16},{1,9},{9,1},{17,25},{25,17},{2,10},{10... | collective-permute-start | bytes 6291464 | tf_op jit(solution)/shard_map/ppermute | solution.py:37
  231.4 37.1 %collective-permute-start.38 = (bf16[256,1024]{1,0:T(8,128)(2,1)}, bf16[256,1024]{1,0:T(8,128)(2,1)S(1)}, u32[]{:S(2)}, u32[]{:S(2)}) collective-permute-start(bf16[256,1024]{1,0:T(8,128)(2,1)} %copy-done.60), channel_id=1, source_target_pairs={{0,2},{2,4},{4,6},{6,7},{7,5},{5,3},{3,1},{1,0},{8,10},{10,12},{12... | collective-permute-start | bytes 1572872 | tf_op jit(solution)/shard_map/ppermute | solution.py:798
  232.7 35.8 %collective-permute-start.39 = (bf16[256,1024]{1,0:T(8,128)(2,1)}, bf16[256,1024]{1,0:T(8,128)(2,1)S(1)}, u32[]{:S(2)}, u32[]{:S(2)}) collective-permute-start(bf16[256,1024]{1,0:T(8,128)(2,1)} %copy-done.59), channel_id=1, source_target_pairs={{2,0},{4,2},{6,4},{7,6},{5,7},{3,5},{1,3},{0,1},{10,8},{12,10},{14... | collective-permute-start | bytes 1572872 | tf_op jit(solution)/shard_map/ppermute | solution.py:801
  253.6 15.0 %collective-permute-start.41 = (bf16[512,256]{1,0:T(8,128)(2,1)S(1)}, bf16[512,256]{1,0:T(8,128)(2,1)S(1)}, u32[]{:S(2)}, u32[]{:S(2)}) collective-permute-start(bf16[512,256]{1,0:T(8,128)(2,1)S(1)} %get-tuple-element.356), channel_id=1, source_target_pairs={{0,1},{1,0},{2,3},{3,2},{4,5},{5,4},{6,7},{7,6},{8,9},{9,8},{10,11... | collective-permute-start | bytes 786440 | tf_op jit(solution)/shard_map/ppermute | solution.py:37
  255.1 13.5 %collective-permute-start.42 = (bf16[512,256]{1,0:T(8,128)(2,1)S(1)}, bf16[512,256]{1,0:T(8,128)(2,1)S(1)}, u32[]{:S(2)}, u32[]{:S(2)}) collective-permute-start(bf16[512,256]{1,0:T(8,128)(2,1)S(1)} %get-tuple-element.357), channel_id=1, source_target_pairs={{0,2},{1,3},{2,0},{3,1},{4,6},{5,7},{6,4},{7,5},{8,10},{9,11},{10,... | collective-permute-start | bytes 786440 | tf_op jit(solution)/shard_map/ppermute | solution.py:37
  255.9 12.7 %collective-permute-start.43 = (bf16[512,256]{1,0:T(8,128)(2,1)S(1)}, bf16[512,256]{1,0:T(8,128)(2,1)S(1)}, u32[]{:S(2)}, u32[]{:S(2)}) collective-permute-start(bf16[512,256]{1,0:T(8,128)(2,1)S(1)} %get-tuple-element.358), channel_id=1, source_target_pairs={{0,3},{1,2},{2,1},{3,0},{4,7},{5,6},{6,5},{7,4},{8,11},{9,10},{10,... | collective-permute-start | bytes 786440 | tf_op jit(solution)/shard_map/ppermute | solution.py:37
  274.0 16.5 %collective-permute-start.46 = (bf16[1024,1024]{1,0:T(8,128)(2,1)}, bf16[1024,1024]{1,0:T(8,128)(2,1)}, u32[]{:S(2)}, u32[]{:S(2)}) collective-permute-start(bf16[1024,1024]{1,0:T(8,128)(2,1)} %copy-done.24), channel_id=1, source_target_pairs={{0,8},{8,0},{16,24},{24,16},{1,9},{9,1},{17,25},{25,17},{2,10},{10... | collective-permute-start | bytes 6291464 | tf_op jit(solution)/shard_map/ppermute | solution.py:37
  274.0 25.9 %collective-permute-start.44 = (bf16[512,1024]{1,0:T(8,128)(2,1)}, bf16[512,1024]{1,0:T(8,128)(2,1)}, u32[]{:S(2)}, u32[]{:S(2)}) collective-permute-start(bf16[512,1024]{1,0:T(8,128)(2,1)} %get-tuple-element.380), channel_id=1, source_target_pairs={{0,2},{2,4},{4,6},{6,7},{7,5},{5,3},{3,1},{1,0},{8,10},{10,12},{12... | collective-permute-start | bytes 3145736 | tf_op jit(solution)/shard_map/ppermute | solution.py:798
  275.4 25.8 %collective-permute-start.45 = (bf16[512,1024]{1,0:T(8,128)(2,1)}, bf16[512,1024]{1,0:T(8,128)(2,1)}, u32[]{:S(2)}, u32[]{:S(2)}) collective-permute-start(bf16[512,1024]{1,0:T(8,128)(2,1)} %get-tuple-element.381), channel_id=1, source_target_pairs={{2,0},{4,2},{6,4},{7,6},{5,7},{3,5},{1,3},{0,1},{10,8},{12,10},{14... | collective-permute-start | bytes 3145736 | tf_op jit(solution)/shard_map/ppermute | solution.py:801
  276.3 29.1 %collective-permute-start.67 = (bf16[512,1024]{1,0:T(8,128)(2,1)}, bf16[512,1024]{1,0:T(8,128)(2,1)}, u32[]{:S(2)}, u32[]{:S(2)}) collective-permute-start(bf16[512,1024]{1,0:T(8,128)(2,1)} %bitcast.92), channel_id=1, source_target_pairs={{0,8},{8,0},{16,24},{24,16},{1,9},{9,1},{17,25},{25,17},{2,10},{10... | collective-permute-start | bytes 3145736 | tf_op jit(solution)/shard_map/ppermute | solution.py:37
  305.3 19.7 %collective-permute-start.49 = (bf16[1024,1024]{1,0:T(8,128)(2,1)}, bf16[1024,1024]{1,0:T(8,128)(2,1)S(1)}, u32[]{:S(2)}, u32[]{:S(2)}) collective-permute-start(bf16[1024,1024]{1,0:T(8,128)(2,1)} %ff_grad.16), channel_id=1, source_target_pairs={{0,8},{8,0},{16,24},{24,16},{1,9},{9,1},{17,25},{25,17},{2,10},{10... | collective-permute-start | bytes 6291464 | tf_op jit(solution)/shard_map/ppermute | solution.py:37
  308.0 33.6 %collective-permute-start.47 = (bf16[512,1024]{1,0:T(8,128)(2,1)}, bf16[512,1024]{1,0:T(8,128)(2,1)S(1)}, u32[]{:S(2)}, u32[]{:S(2)}) collective-permute-start(bf16[512,1024]{1,0:T(8,128)(2,1)} %get-tuple-element.403), channel_id=1, source_target_pairs={{0,2},{2,4},{4,6},{6,7},{7,5},{5,3},{3,1},{1,0},{8,10},{10,12},{12... | collective-permute-start | bytes 3145736 | tf_op jit(solution)/shard_map/ppermute | solution.py:798
  309.8 34.0 %collective-permute-start.48 = (bf16[512,1024]{1,0:T(8,128)(2,1)}, bf16[512,1024]{1,0:T(8,128)(2,1)}, u32[]{:S(2)}, u32[]{:S(2)}) collective-permute-start(bf16[512,1024]{1,0:T(8,128)(2,1)} %get-tuple-element.404), channel_id=1, source_target_pairs={{2,0},{4,2},{6,4},{7,6},{5,7},{3,5},{1,3},{0,1},{10,8},{12,10},{14... | collective-permute-start | bytes 3145736 | tf_op jit(solution)/shard_map/ppermute | solution.py:801
  348.2 28.9 %collective-permute-start.52 = (bf16[512,1024]{1,0:T(8,128)(2,1)}, bf16[512,1024]{1,0:T(8,128)(2,1)}, u32[]{:S(2)}, u32[]{:S(2)}) collective-permute-start(bf16[512,1024]{1,0:T(8,128)(2,1)} %ff_grad.18), channel_id=1, source_target_pairs={{0,8},{8,0},{16,24},{24,16},{1,9},{9,1},{17,25},{25,17},{2,10},{10... | collective-permute-start | bytes 3145736 | tf_op jit(solution)/shard_map/ppermute | solution.py:37
  348.2 37.9 %collective-permute-start.50 = (bf16[512,1024]{1,0:T(8,128)(2,1)}, bf16[512,1024]{1,0:T(8,128)(2,1)}, u32[]{:S(2)}, u32[]{:S(2)}) collective-permute-start(bf16[512,1024]{1,0:T(8,128)(2,1)} %get-tuple-element.421), channel_id=1, source_target_pairs={{0,2},{2,4},{4,6},{6,7},{7,5},{5,3},{3,1},{1,0},{8,10},{10,12},{12... | collective-permute-start | bytes 3145736 | tf_op jit(solution)/shard_map/ppermute | solution.py:798
  349.9 36.2 %collective-permute-start.51 = (bf16[512,1024]{1,0:T(8,128)(2,1)}, bf16[512,1024]{1,0:T(8,128)(2,1)}, u32[]{:S(2)}, u32[]{:S(2)}) collective-permute-start(bf16[512,1024]{1,0:T(8,128)(2,1)} %get-tuple-element.422), channel_id=1, source_target_pairs={{2,0},{4,2},{6,4},{7,6},{5,7},{3,5},{1,3},{0,1},{10,8},{12,10},{14... | collective-permute-start | bytes 3145736 | tf_op jit(solution)/shard_map/ppermute | solution.py:801
  352.7 32.7 %collective-permute-start.53 = (bf16[128,1024]{1,0:T(8,128)(2,1)}, bf16[128,1024]{1,0:T(8,128)(2,1)S(1)}, u32[]{:S(2)}, u32[]{:S(2)}) collective-permute-start(bf16[128,1024]{1,0:T(8,128)(2,1)} %get-tuple-element.428), channel_id=1, source_target_pairs={{0,2},{1,3},{2,0},{3,1},{4,6},{5,7},{6,4},{7,5},{8,10},{9,11},{10,... | collective-permute-start | bytes 786440 | tf_op jit(solution)/shard_map/ppermute | solution.py:37
  362.9 22.5 %collective-permute-start.54 = (bf16[128,1024]{1,0:T(8,128)(2,1)}, bf16[128,1024]{1,0:T(8,128)(2,1)S(1)}, u32[]{:S(2)}, u32[]{:S(2)}) collective-permute-start(bf16[128,1024]{1,0:T(8,128)(2,1)} %get-tuple-element.429), channel_id=1, source_target_pairs={{0,1},{1,0},{2,3},{3,2},{4,5},{5,4},{6,7},{7,6},{8,9},{9,8},{10,11... | collective-permute-start | bytes 786440 | tf_op jit(solution)/shard_map/ppermute | solution.py:37
  377.1 48.4 %collective-permute-start.68 = (bf16[64,1024]{1,0:T(8,128)(2,1)}, bf16[64,1024]{1,0:T(8,128)(2,1)S(1)}, u32[]{:S(2)}, u32[]{:S(2)}) collective-permute-start(bf16[64,1024]{1,0:T(8,128)(2,1)} %reduce-scatter.2.cloned.1.call-done), channel_id=1, source_target_pairs={{0,16},{8,24},{16,0},{24,8},{1,17},{9,25},{17,1},{25,9},{2,18},{10... | collective-permute-start | bytes 393224 | tf_op jit(solution)/shard_map/ppermute | solution.py:37
  396.6 13.2 %collective-permute-start.60 = (bf16[256,1024]{1,0:T(8,128)(2,1)S(1)}, bf16[256,1024]{1,0:T(8,128)(2,1)S(1)}, u32[]{:S(2)}, u32[]{:S(2)}) collective-permute-start(bf16[256,1024]{1,0:T(8,128)(2,1)S(1)} %get-tuple-element.461), channel_id=1, source_target_pairs={{0,16},{8,24},{16,0},{24,8},{1,17},{9,25},{17,1},{25,9},{2,18},{10... | collective-permute-start | bytes 1572872 | tf_op jit(solution)/shard_map/ppermute | solution.py:37
  398.8 12.5 %collective-permute-start.58 = (bf16[128,1024]{1,0:T(8,128)(2,1)S(1)}, bf16[128,1024]{1,0:T(8,128)(2,1)S(1)}, u32[]{:S(2)}, u32[]{:S(2)}) collective-permute-start(bf16[128,1024]{1,0:T(8,128)(2,1)S(1)} %get-tuple-element.459), channel_id=1, source_target_pairs={{0,2},{1,3},{2,0},{3,1},{4,6},{5,7},{6,4},{7,5},{8,10},{9,11},{10,... | collective-permute-start | bytes 786440 | tf_op jit(solution)/shard_map/ppermute | solution.py:37
  400.2 20.0 %collective-permute-start.56 = (bf16[256,1024]{1,0:T(8,128)(2,1)S(1)}, bf16[256,1024]{1,0:T(8,128)(2,1)S(1)}, u32[]{:S(2)}, u32[]{:S(2)}) collective-permute-start(bf16[256,1024]{1,0:T(8,128)(2,1)S(1)} %get-tuple-element.457), channel_id=1, source_target_pairs={{0,1},{1,0},{2,3},{3,2},{4,5},{5,4},{6,7},{7,6},{8,9},{9,8},{10,11... | collective-permute-start | bytes 1572872 | tf_op jit(solution)/shard_map/ppermute | solution.py:37
  409.8 12.3 %collective-permute-start.57 = (bf16[256,1024]{1,0:T(8,128)(2,1)S(1)}, bf16[256,1024]{1,0:T(8,128)(2,1)S(1)}, u32[]{:S(2)}, u32[]{:S(2)}) collective-permute-start(bf16[256,1024]{1,0:T(8,128)(2,1)S(1)} %get-tuple-element.458), channel_id=1, source_target_pairs={{0,2},{1,3},{2,0},{3,1},{4,6},{5,7},{6,4},{7,5},{8,10},{9,11},{10,... | collective-permute-start | bytes 1572872 | tf_op jit(solution)/shard_map/ppermute | solution.py:37
  423.9 23.0 %collective-permute-start.66 = (bf16[256,1024]{1,0:T(8,128)(2,1)S(1)}, bf16[256,1024]{1,0:T(8,128)(2,1)S(1)}, u32[]{:S(2)}, u32[]{:S(2)}) collective-permute-start(bf16[256,1024]{1,0:T(8,128)(2,1)S(1)} %get-tuple-element.466), channel_id=1, source_target_pairs={{0,16},{8,24},{16,0},{24,8},{1,17},{9,25},{17,1},{25,9},{2,18},{10... | collective-permute-start | bytes 1572872 | tf_op jit(solution)/shard_map/ppermute | solution.py:37
  426.3 20.6 %collective-permute-start.62 = (bf16[512,384]{1,0:T(8,128)(2,1)S(1)}, bf16[512,384]{1,0:T(8,128)(2,1)S(1)}, u32[]{:S(2)}, u32[]{:S(2)}) collective-permute-start(bf16[512,384]{1,0:T(8,128)(2,1)S(1)} %get-tuple-element.584), channel_id=1, source_target_pairs={{4,0},{0,1},{5,2},{1,3},{6,4},{2,5},{7,6},{3,7},{12,8},{8,9},{13,1... | collective-permute-start | bytes 1179656 | tf_op jit(solution)/shard_map/ppermute | solution.py:1114
  447.3 11.7 %collective-permute-start.75 = (bf16[576,1024]{1,0:T(8,128)(2,1)S(1)}, bf16[576,1024]{1,0:T(8,128)(2,1)S(1)}, u32[]{:S(2)}, u32[]{:S(2)}) collective-permute-start(bf16[576,1024]{1,0:T(8,128)(2,1)S(1)} %pad_maximum_fusion.1), channel_id=1, source_target_pairs={{0,8},{8,0},{16,24},{24,16},{1,9},{9,1},{17,25},{25,17},{2,10},{10... | collective-permute-start | bytes 3538952 | tf_op jit(solution)/shard_map/ppermute | solution.py:37
  447.3 11.5 %collective-permute-start.69 = (bf16[512,384]{1,0:T(8,128)(2,1)S(1)}, bf16[512,384]{1,0:T(8,128)(2,1)S(1)}, u32[]{:S(2)}, u32[]{:S(2)}) collective-permute-start(bf16[512,384]{1,0:T(8,128)(2,1)S(1)} %add_convert_fusion.5), channel_id=1, source_target_pairs={{0,16},{8,24},{16,0},{24,8},{1,17},{9,25},{17,1},{25,9},{2,18},{10... | collective-permute-start | bytes 1179656 | tf_op jit(solution)/shard_map/ppermute | solution.py:37
  452.9 14.9 %collective-permute-start.73 = (bf16[256,1024]{1,0:T(8,128)(2,1)S(1)}, bf16[256,1024]{1,0:T(8,128)(2,1)S(1)}, u32[]{:S(2)}, u32[]{:S(2)}) collective-permute-start(bf16[256,1024]{1,0:T(8,128)(2,1)S(1)} %get-tuple-element.478), channel_id=1, source_target_pairs={{0,1},{1,0},{2,3},{3,2},{4,5},{5,4},{6,7},{7,6},{8,9},{9,8},{10,11... | collective-permute-start | bytes 1572872 | tf_op jit(solution)/shard_map/ppermute | solution.py:37
  454.9 12.9 %collective-permute-start.74 = (bf16[256,1024]{1,0:T(8,128)(2,1)S(1)}, bf16[256,1024]{1,0:T(8,128)(2,1)S(1)}, u32[]{:S(2)}, u32[]{:S(2)}) collective-permute-start(bf16[256,1024]{1,0:T(8,128)(2,1)S(1)} %get-tuple-element.479), channel_id=1, source_target_pairs={{0,2},{1,3},{2,0},{3,1},{4,6},{5,7},{6,4},{7,5},{8,10},{9,11},{10,... | collective-permute-start | bytes 1572872 | tf_op jit(solution)/shard_map/ppermute | solution.py:37
  469.0 11.7 %collective-permute-start.77 = (bf16[512,384]{1,0:T(8,128)(2,1)S(1)}, bf16[512,384]{1,0:T(8,128)(2,1)}, u32[]{:S(2)}, u32[]{:S(2)}) collective-permute-start(bf16[512,384]{1,0:T(8,128)(2,1)S(1)} %add_convert_fusion.4), channel_id=1, source_target_pairs={{0,8},{8,0},{16,24},{24,16},{1,9},{9,1},{17,25},{25,17},{2,10},{10... | collective-permute-start | bytes 1179656 | tf_op jit(solution)/shard_map/ppermute | solution.py:37
  (121 other events, 1046.7 us)
Sparse Core Ops, SparseCore 0:
  46.8 44.0 all-gather.2
  308.2 67.1 reduce-scatter.1

commit v4 on v3

--- a/solution.py
+++ b/solution.py
@@ -149,22 +149,23 @@
 
 
 def attn_forward_kernel(q_ref, k_ref, v_ref, *refs):
-    outs, log_ref = refs[:-1], refs[-1]
+    outs, all_ref, log_ref = refs[:-2], refs[-2], refs[-1]
     rows = q_ref.shape[0]
     mixed, log_sums = [], []
+    scores = [against(one_head(q_ref[...], head), k_ref[...]) for head in range(2)]
+    tops = [jnp.max(score, axis=-1, keepdims=True) * (SCALE * LOG2E) for score in scores]
+    weights = [jnp.exp2(score * (SCALE * LOG2E) - top).astype(BF) for score, top in zip(scores, tops)]
     for head in range(2):
-        scores = against(one_head(q_ref[...], head), k_ref[...])
-        top = jnp.max(scores, axis=-1, keepdims=True) * (SCALE * LOG2E)
-        weights = jnp.exp2(scores * (SCALE * LOG2E) - top).astype(BF)
-        both = product(weights, one_head(v_ref[...], head, 1.0))
+        both = product(weights[head], one_head(v_ref[...], head, 1.0))
         total = pltpu.roll(both, HD, 1)
         mixed.append(both / total)
-        log_sums.append(top + jnp.log(total) * LOG2E)
+        log_sums.append(tops[head] + jnp.log(total) * LOG2E)
     first = first_head(rows)
     value = jnp.where(first, mixed[0], mixed[1]).astype(BF)
     turned = jnp.where(first, log_sums[0], log_sums[1]).T
     log_ref[0, 0:1, :] = turned[0:1]
     log_ref[0, 1:2, :] = turned[HD : HD + 1]
+    all_ref[...] = value
     for j, out in enumerate(outs):
 
         @pl.when(pl.program_id(1) == j)
@@ -178,7 +179,11 @@
     shape = jax.ShapeDtypeStruct((rows, pairs * PAIR), BF)
     result = pl.pallas_call(
         attn_forward_kernel,
-        out_shape=(shape,) * parts + (jax.ShapeDtypeStruct((pairs, 8, parts * rows), F32),),
+        out_shape=(shape,) * parts
+        + (
+            jax.ShapeDtypeStruct((parts * rows, pairs * PAIR), BF),
+            jax.ShapeDtypeStruct((pairs, 8, parts * rows), F32),
+        ),
         grid=(pairs, parts),
         in_specs=[
             pl.BlockSpec((rows, PAIR), lambda g, i: (i, 3 * g)),
@@ -186,27 +191,20 @@
             pl.BlockSpec((parts * rows, PAIR), lambda g, i: (0, 3 * g + 2)),
         ],
         out_specs=(pl.BlockSpec((rows, PAIR), lambda g, i: (0, g)),) * parts
-        + (pl.BlockSpec((1, 8, rows), lambda g, i: (g, 0, i)),),
+        + (pl.BlockSpec((rows, PAIR), lambda g, i: (i, g)), pl.BlockSpec((1, 8, rows), lambda g, i: (g, 0, i))),
         compiler_params=params(),
         cost_estimate=cost(
             16 * joint.shape[0] ** 2 * pairs * PAIR, 3 * joint.size, 2 * pairs * joint.shape[0] ** 2
         ),
         name="attn_forward",
     )(joint, joint, joint)
-    return result[:parts], result[parts]
-
-
-def attn_backward_kernel(parts, q_ref, k_ref, v_ref, log_ref, *refs):
-    pieces, heads = refs[:parts], refs[parts : 2 * parts]
-    d_ref, g_ref, o_ref, kt_ref, dk_acc, dv_acc = refs[-6:]
+    return result[:parts], result[parts], result[parts + 1]
+
+
+def attn_backward_kernel(parts, q_ref, k_ref, v_ref, log_ref, g_ref, o_ref, *refs):
+    d_ref, kt_ref, dk_acc, dv_acc = refs[-4:]
     step = pl.program_id(0)
     rows = q_ref.shape[0]
-    for j in range(parts):
-
-        @pl.when(step == j)
-        def _(j=j):
-            g_ref[...] = pieces[j][...]
-            o_ref[...] = heads[j][...]
 
     @pl.when(step == 0)
     def _():
@@ -238,8 +236,7 @@
         d_ref[:, pl.ds(2 * PAIR, PAIR)] = dv_acc[...].astype(BF)
 
 
-def attn_backward(joint, log_sums, pieces, heads, step, pair, kept):
-    parts = len(pieces)
+def attn_backward(joint, log_sums, grads, heads, parts, step, micros, pair, kept):
     rows = joint.shape[0] // parts
     return pl.pallas_call(
         functools.partial(attn_backward_kernel, parts),
@@ -250,23 +247,21 @@
             pl.BlockSpec((parts * rows, PAIR), lambda i: (0, 3 * pair + 1)),
             pl.BlockSpec((parts * rows, PAIR), lambda i: (0, 3 * pair + 2)),
             pl.BlockSpec((1, 8, rows), lambda i: (pair, 0, i)),
+            pl.BlockSpec((rows, PAIR), lambda i: (i * micros + step, pair)),
+            pl.BlockSpec((rows, PAIR), lambda i: (i, pair)),
         ]
-        + [pl.BlockSpec((rows, PAIR), lambda i: (step, pair))] * parts
-        + [pl.BlockSpec((rows, PAIR), lambda i: (0, pair))] * parts
         + [pl.BlockSpec(memory_space=pl.ANY)] * len(kept),
         out_specs=pl.BlockSpec((parts * rows, 3 * PAIR), lambda i: (0, pair)),
         scratch_shapes=[
-            pltpu.VMEM((rows, PAIR), BF),
-            pltpu.VMEM((rows, PAIR), BF),
             pltpu.VMEM((PAIR, parts * rows), BF),
             pltpu.VMEM((parts * rows, PAIR), F32),
             pltpu.VMEM((parts * rows, PAIR), F32),
         ],
-        input_output_aliases={4 + 2 * parts + i: i for i in range(len(kept))},
-        compiler_params=params(60),
+        input_output_aliases={6 + i: i for i in range(len(kept))},
+        compiler_params=params(),
         cost_estimate=cost(1, 1),
         name="attn_backward",
-    )(joint, joint, joint, log_sums, *pieces, *heads, *kept)
+    )(joint, joint, joint, log_sums, grads, heads, *kept)
 
 
 def normed(values):
@@ -516,22 +511,19 @@
             pltpu.SemaphoreType.DMA((2, 2)),
         ],
         compiler_params=params(),
-        cost_estimate=cost(
-            8 * rows * width * ff_half * count,
-            10 * rows * width + count * ff_half * (4 * width + 6 * rows),
-            2 * rows * ff_half * count,
-        ),
+        cost_estimate=cost(1, 1),
         name="ff_forward",
     )(first_low, init, *blocks)
 
 
-def ff_backward_kernel(ff_half, count, d_fed_ref, init_ref, slope_ref, *refs):
+def ff_backward_kernel(ff_half, count, base, d_fed_ref, init_ref, slope_ref, *refs):
     d_upper_ref, d_first_ref, column_ref, buf, sem = refs[-5:]
     cut = ff_half + PAD
 
     @pl.when(pl.program_id(0) == 0)
     def _():
         d_first_ref[...] = init_ref[...]
+        column_ref[...] = refs[count][...]
 
     total = 0.0
     for h, block in enumerate(next_blocks(refs[:count], buf, sem)):
@@ -539,25 +531,28 @@
         d_hidden = against(d_fed_ref[...], block[pl.ds(cut, ff_half), :])
         d_upper = (d_hidden * slope_ref[:, lanes]).astype(BF)
         d_upper_ref[:, lanes] = d_upper
-        column_ref[0, :, lanes] = jnp.sum(d_upper.astype(F32), axis=0, keepdims=True)
+        row = base + 2 * pl.program_id(0) + h
+        column_ref[pl.ds(row, 1), :] = jnp.sum(d_upper.astype(F32), axis=0, keepdims=True)
         total = total + product(d_upper, block[pl.ds(0, ff_half), :])
     d_first_ref[...] += total
 
 
-def ff_backward(d_fed, init, slope, blocks, ff_half):
+def ff_backward(d_fed, init, slope, blocks, columns, base, ff_half):
     rows, width = d_fed.shape
     count = len(blocks)
     column = pl.BlockSpec((rows, 2 * ff_half), lambda i: (0, i))
     return pl.pallas_call(
-        functools.partial(ff_backward_kernel, ff_half, count),
+        functools.partial(ff_backward_kernel, ff_half, count, base),
         out_shape=(
             jax.ShapeDtypeStruct(slope.shape, BF),
             jax.ShapeDtypeStruct((rows, width), F32),
-            jax.ShapeDtypeStruct((count // 2, 1, 2 * ff_half), F32),
+            jax.ShapeDtypeStruct(columns.shape, F32),
         ),
         grid=(count // 2,),
-        in_specs=[whole_block(rows, width)] * 2 + [column] + [pl.BlockSpec(memory_space=pl.ANY)] * count,
-        out_specs=(column, whole_block(rows, width), pl.BlockSpec((1, 1, 2 * ff_half), lambda i: (i, 0, 0))),
+        in_specs=[whole_block(rows, width)] * 2 + [column]
+        + [pl.BlockSpec(memory_space=pl.ANY)] * count
+        + [whole_block(*columns.shape)],
+        out_specs=(column, whole_block(rows, width), whole_block(*columns.shape)),
         scratch_shapes=[
             pltpu.VMEM((2, 2) + blocks[0].shape, BF),
             pltpu.SemaphoreType.DMA((2, 2)),
@@ -568,7 +563,7 @@
             10 * rows * width + count * ff_half * (4 * width + 6 * rows),
         ),
         name="ff_backward",
-    )(d_fed, init, slope, *blocks)
+    )(d_fed, init, slope, *blocks, columns)
 
 
 def ff_grad_kernel(ff_half, spans, splits, joined, first_ref, fed_ref, up_ref, hidden_ref, *refs):
@@ -646,7 +641,7 @@
         grid=(split,),
         in_specs=[row_block(*span) for terms in spans for span in terms],
         out_specs=tuple(row_block(0, split) for _ in sums),
-        compiler_params=params(60),
+        compiler_params=params(),
         cost_estimate=cost(1, 1),
         name="combine",
     )(*[array for terms in sums for _, array in terms])
@@ -706,34 +701,36 @@
     )(d_joint, d_joint, w_seq, to_two, to_one)
 
 
-def row_grad_kernel(micros, keep_ref, d_pre_ref, w_ref, *refs):
+def row_grad_kernel(micros, d_pre_ref, w_ref, *refs):
     joints, arrived, out_ref = refs[:micros], refs[micros:-1], refs[-1]
     for m in range(micros):
 
         @pl.when(pl.program_id(0) == m)
         def _(m=m):
             total = d_pre_ref[...] + against(joints[m][...], w_ref[...])
-            total = total + arrived[2 * m][...].astype(F32) + arrived[2 * m + 1][...].astype(F32)
-            out_ref[...] = jnp.where(keep_ref[:, 0:1] > 0.0, total, 0.0)
-
-
-def row_grad(keep, d_pre, w_seq, d_joints, arrived, parts):
+            for term in arrived[2 * m : 2 * m + 2]:
+                total = total + term[...].astype(F32)
+            out_ref[...] = total
+
+
+def row_grad(d_pre, w_seq, d_joints, arrived, parts):
     micros = len(d_joints)
     rows, joint_width = d_joints[0].shape[0] // parts, d_joints[0].shape[1]
     width = w_seq.shape[0]
     block = pl.BlockSpec((rows, width), lambda i: (i, 0))
+    flat = [a for pair in arrived for a in pair]
     return pl.pallas_call(
         functools.partial(row_grad_kernel, micros),
         out_shape=jax.ShapeDtypeStruct(d_pre.shape, F32),
         grid=(micros,),
-        in_specs=[pl.BlockSpec((rows, 128), lambda i: (i, 0)), block, whole_block(*w_seq.shape)]
+        in_specs=[block, whole_block(*w_seq.shape)]
         + [whole_block(rows, joint_width)] * micros
-        + [whole_block(rows, width)] * (2 * micros),
+        + [whole_block(rows, width)] * len(flat),
         out_specs=block,
-        compiler_params=params(60),
+        compiler_params=params(),
         cost_estimate=cost(1, 1),
         name="row_grad",
-    )(keep, d_pre, w_seq, *d_joints, *[a for pair in arrived for a in pair])
+    )(d_pre, w_seq, *d_joints, *flat)
 
 
 def shards(
@@ -762,6 +759,7 @@
     count = lax.axis_size("tensor")
     dp_count = lax.axis_size("dp")
     core = lax.axis_index("dp") % 2
+    row_part = lax.axis_index("dp") // 2 % 2
     micro_count, row_count, width = embedded.shape
     local_width = w_query.shape[1]
     ff_local = w_up.shape[1]
@@ -780,9 +778,9 @@
     own_first = core == 0
     micros = range(micro_count)
 
-    def by_core(mine, other, axis=0):
+    def by_core(mine, other, axis=0, first=None):
         return jnp.where(
-            own_first,
+            own_first if first is None else first,
             jnp.concatenate([mine, other], axis=axis),
             jnp.concatenate([other, mine], axis=axis),
         )
@@ -858,7 +856,9 @@
     w_mine = [lax.ppermute(joint_half, "tensor", spread[k]) for k in range(groups)]
     ones = [swap(placed[0], "tensor", 1)]
     twos = [swap(placed[0], "tensor", 2)]
-    ones, twos, w_mine, placed, piece, cots, w_out = fence(ones, twos, w_mine, placed, piece, cots, w_out)
+    ones, twos, w_mine, placed, piece, cots, w_out, hots, seq_hots, replaced_list = fence(
+        ones, twos, w_mine, placed, piece, cots, w_out, hots, seq_hots, replaced_list
+    )
     w_out_half = lax.all_gather(
         lax.dynamic_slice_in_dim(w_out, core * out_half, out_half, 0), "tensor", axis=0
     )
@@ -882,10 +882,10 @@
             twos.append(swap(placed[step + 1], "tensor", 2))
         moved = (forward(near[step]), backward(near[step]))
         joint, mine, other = project(at_core, rows, w_seq, b_seq)
-        pieces, sums = attn_forward(joint, parts)
+        pieces, whole, sums = attn_forward(joint, parts)
         joints.append(joint)
         log_sums.append(sums)
-        own_heads.append(pieces)
+        own_heads.append(whole)
         x_mine.append(mine)
         x_other.append(other)
         ones, twos, moved, pieces, near = fence(ones, twos, moved, pieces, near)
@@ -907,12 +907,13 @@
         if s < far:
             moved = [forward(fw), backward(bw)]
         else:
-            moved = [jnp.concatenate([forward(fw[:cut]), backward(bw[cut:])], axis=0)]
+            moved = [forward(fw[:cut]), backward(bw[cut:])]
         for t in (0, 1) if s == 2 else (s - 1,):
             pre_two, hidden_low[t], slopes[t] = ff_forward(first_low, pre_two, step_blocks[t], ff_half)
-        if s < far:
-            if s < far - 1:
-                moved, pre_two = fence(moved, pre_two)
+        moved, pre_two = fence(moved, pre_two)
+        if s == far:
+            moved = [jnp.concatenate(moved, axis=0)]
+        else:
             fw, bw = moved
         step_blocks.append(moved + [swap(block, "dp", 1) for block in moved])
     pre_two, hidden_low[far], slopes[far] = ff_forward(first_low, pre_two, step_blocks[far], ff_half)
@@ -935,11 +936,15 @@
     def summed(s, others, megabytes=24):
         return ff_blocks(both(s), 0, [[(0, total, others, i)] for i in range(len(both(s)))], (), megabytes)
 
-    d_uppers, column_sums_ = [None] * (far + 1), [None] * (far + 1)
+    d_uppers = [None] * (far + 1)
+    rel_b_up = jnp.zeros((2 * count, ff_half), F32)
 
     def back(s, d_first):
-        d_uppers[s], d_first, sums = ff_backward(d_fed, d_first, slopes[s], step_blocks[s], ff_half)
-        column_sums_[s] = sums.reshape(2, -1, ff_half)
+        nonlocal rel_b_up
+        base = 4 * s - 2 if s else 0
+        d_uppers[s], d_first, rel_b_up = ff_backward(
+            d_fed, d_first, slopes[s], step_blocks[s], rel_b_up, base, ff_half
+        )
         return d_first
 
     d_first = back(far, d_pre_two)
@@ -953,29 +958,36 @@
     parcel, next_others, d_uppers[far - 1], d_first = fence(parcel, next_others, d_uppers[far - 1], d_first)
     moved = [forward(parcel[0]), backward(parcel[1])]
     others = swap(next_others, "dp", 1)
-    for s in range(far - 2, -1, -1):
+    for s in range(far - 2, far // 2 - 1, -1):
         d_first = back(s, d_first)
-    rel_b_up = jnp.concatenate(column_sums_, axis=1)
+    others, d_uppers[far - 1], d_first = fence(others, d_uppers[far - 1], d_first)
+    share = summed(far - 1, others)
+    next_others = ff_blocks(both(far - 2), 1)
+    moved, share, next_others, d_first = fence(moved, share, next_others, d_first)
+    parcel = combine([(0, share[0]), (ff_half, moved[1])], [(0, share[1]), (0, moved[0])])
+    parcel, next_others, d_first = fence(parcel, next_others, d_first)
+    moved = [forward(parcel[1]), backward(parcel[0])]
+    others = swap(next_others, "dp", 1)
+    for s in range(far // 2 - 1, -1, -1):
+        d_first = back(s, d_first)
     d_pre_one, d_attended, sums_one, *d_heads = attend_back(
         part_order, d_first, norm_one, scale_one, vectors_one, w_out_all, parts
     )
-    others, d_uppers[far - 1], d_heads = fence(others, d_uppers[far - 1], d_heads)
+    others, d_uppers[far - 2], d_heads = fence(others, d_uppers[far - 2], d_heads)
     seq_grads = [d_heads[0]] + [swap(d_heads[j], "tensor", j) for j in range(1, parts)]
-    share = summed(far - 1, others)
-    next_others = ff_blocks(both(far - 2), 1)
+    share = summed(far - 2, others)
+    next_others = ff_blocks(both(far - 3), 1)
 
     d_out = over_rows(heads_out, d_attended).astype(BF).reshape(count, 2, out_half, width)
     out_other = lax.dynamic_index_in_dim(d_out, 1 - core, 1, keepdims=False).reshape(-1, width)
     out_mine = lax.dynamic_index_in_dim(d_out, core, 1, keepdims=False).reshape(-1, width)
     moved, share, seq_grads, next_others, out_other = fence(moved, share, seq_grads, next_others, out_other)
-    parcel = combine([(0, share[0]), (ff_half, moved[1])], [(0, share[1]), (0, moved[0])])
-    parcel, next_others, seq_grads, out_other = fence(parcel, next_others, seq_grads, out_other)
+    seq_grads = jnp.concatenate(seq_grads, axis=0)
 
     d_joints = [jnp.zeros((), BF) for _ in micros]
     work = [(m, g) for m in micros for g in range(pairs)]
 
-    def over_dp(values):
-        bit = 2
+    def over_dp(values, bit=2):
         while bit < dp_count:
             values = (values.astype(F32) + swap(values, "dp", bit).astype(F32)).astype(BF)
             bit *= 2
@@ -1003,53 +1015,60 @@
     partial, stage = [() for _ in micros], [0 for _ in micros]
     d_w = []
     table = own_table(d_pre_one)
-    plan = [[pair] for pair in work[:-pairs]] + [work[-pairs:]]
-    for index in range(far - 1):
-        s = far - 1 - index
-        if index:
+    plan = [work[:pairs], work[pairs:-1], work[-1:]]
+    for index in range(max(far - 1, len(plan))):
+        s = far - 2 - index
+        if s > 0:
             parcel = combine([(0, share[0]), (0, moved[1])], [(0, share[1]), (0, moved[0])])
-        joints, d_joints, d_fed, parcel, next_others = fence(joints, d_joints, d_fed, parcel, next_others)
-        moved = [forward(parcel[1]), backward(parcel[0])]
-        others = swap(next_others, "dp", 1)
+            joints, d_joints, d_fed, parcel, next_others = fence(joints, d_joints, d_fed, parcel, next_others)
+            moved = [forward(parcel[1]), backward(parcel[0])]
+            others = swap(next_others, "dp", 1)
+        elif s == 0:
+            parcel = combine([(0, share[0]), (0, moved[0]), (0, moved[1])])[0]
+            ff_up, ff_down = parcel[:ff_half], parcel[ff_half:]
+            joints, d_joints, ff_up, ff_down = fence(joints, d_joints, ff_up, ff_down)
+            ff_up = over_dp(ff_up)
         if index == 0:
             out_mine = (out_mine.astype(F32) + swap(out_other, "dp", 1).astype(F32)).astype(BF)
+            out_mine = out_mine.reshape(count, 2, out_half // 2, width)
+            out_other = lax.dynamic_index_in_dim(out_mine, 1 - row_part, 1, keepdims=False).reshape(-1, width)
+            out_mine = lax.dynamic_index_in_dim(out_mine, row_part, 1, keepdims=False).reshape(-1, width)
+            out_mine = (out_mine.astype(F32) + swap(out_other, "dp", 2).astype(F32)).astype(BF)
+        elif index == 1:
             out_sum = lax.psum_scatter(out_mine, "tensor", scatter_dimension=0, tiled=True)
         for m in micros:
             ready = max(i for i, pairs_ in enumerate(plan) if (m, pairs - 1) in pairs_) + 1
             if index == ready:
                 partial[m], stage[m] = diagonal(m), 1
             elif index == ready + 1:
-                partial[m], stage[m] = side_parcels(m, partial[m]), 2
+                partial[m], stage[m] = sides(side_parcels(m, partial[m])), 2
         if index == len(plan) - 1:
             d_w = [(over_rows(x_other[m], d_joints[m]), over_rows(x_mine[m], d_joints[m])) for m in micros[:-1]]
         next_others = ()
         if s > 1:
-            next_others = ff_blocks(both(s - 2), 1, megabytes=60)
+            next_others = ff_blocks(both(s - 2), 1)
         for m, g in plan[index] if index < len(plan) else ():
             d_joints[m] = attn_backward(
-                joints[m], log_sums[m], seq_grads, own_heads[m], m, g, (d_joints[m],) if g else ()
+                joints[m], log_sums[m], seq_grads, own_heads[m], parts, m, micro_count, g, (d_joints[m],) if g else ()
             )
-        share = summed(s - 1, others, 60)
-        moved, share, next_others, d_joints, partial, table, d_w = fence(
-            moved, share, next_others, d_joints, partial, table, d_w
-        )
+        if s > 0:
+            share = summed(s - 1, others)
+            moved, share, next_others, d_joints, partial, table, d_w, out_mine = fence(
+                moved, share, next_others, d_joints, partial, table, d_w, out_mine
+            )
+        elif s == 0:
+            ff_up, d_joints, partial, table, d_w = fence(ff_up, d_joints, partial, table, d_w)
 
     last = micro_count - 1
-    parcel = combine([(0, share[0]), (0, moved[0]), (0, moved[1])])[0]
-    ff_up, ff_down = parcel[:ff_half], parcel[ff_half:]
-    for m in micros:
-        if stage[m] == 1:
-            partial[m], stage[m] = side_parcels(m, partial[m]), 2
     d_w.append((over_rows(x_other[last], d_joints[last]), None))
     other_half = sum(other for other, _ in d_w).astype(BF)
     other_half, d_joints, partial, ff_up, ff_down = fence(other_half, d_joints, partial, ff_up, ff_down)
     other_half = swap(other_half, "dp", 1)
-    ff_up = over_dp(ff_up)
     for m in micros:
-        if stage[m] == 2:
-            partial[m], stage[m] = sides(partial[m]), 4
-        else:
+        if stage[m] == 0:
             partial[m] = diagonal(m)
+        elif stage[m] == 1:
+            partial[m] = sides(side_parcels(m, partial[m]))
 
     def over_bits(values, axis, low, high):
         while low < high:
@@ -1062,15 +1081,20 @@
             low *= 4
         return values
 
-    rel_b_up = jnp.swapaxes(rel_b_up, 0, 1)
-    rel_b_up = jnp.where(own_first, rel_b_up, rel_b_up[:, ::-1]).reshape(count, ff_local)
-    slot_of = [0] * count
-    for slot, o in enumerate(offsets):
-        slot_of[o % count] = slot
-    place = jnp.array([order.index(s) for s in range(count)], jnp.int32)
-    wanted = jnp.array(slot_of, jnp.int32)[(place - ring_pos) % count]
-    all_b_up = rel_b_up[wanted].reshape(-1, width)
-    b_rows = all_b_up.shape[0]
+    row_offset, row_other = [0, 0], [0, 1]
+    for s in range(1, far):
+        row_offset += [-s % count, s, -s % count, s]
+        row_other += [0, 0, 1, 1]
+    row_offset, row_other = jnp.array(row_offset + [far, far]), jnp.array(row_other + [0, 1])
+    place = jnp.repeat(jnp.array([order.index(i) for i in range(count)]), 2)
+    half_of = jnp.tile(jnp.arange(2), count)
+    chosen = (((place - ring_pos) % count)[:, None] == row_offset[None, :]) & (
+        (half_of != core)[:, None] == (row_other[None, :] == 1)
+    )
+    all_b_up = jnp.dot(
+        chosen.astype(F32), rel_b_up, precision=lax.Precision.HIGHEST, preferred_element_type=F32
+    )
+    all_b_up = jnp.pad(all_b_up, ((0, 0), (0, width - ff_half)))
     hot_sum = sum(over_rows(seq_hots[m], d_joints[m]) for m in micros)
     d_b_seq = hot_sum[vocab_count]
     rest, thirds = hot_sum, []
@@ -1093,12 +1117,12 @@
     place_row = lax.broadcasted_iota(jnp.int32, table.shape, 0)
     table = jnp.where(place_row == vocab_count, d_b_query[None], table)
     table = jnp.where(place_row == vocab_count + 1, d_b_value[None], table)
-    small = jnp.concatenate([table, sums_one, sums_two, jnp.pad(all_b_up, ((0, -b_rows % 8), (0, 0)))], axis=0)
+    small = jnp.concatenate([table, sums_one, sums_two, all_b_up], axis=0)
 
     my_half = sum(mine for _, mine in d_w[: len(d_w)] if mine is not None)
     my_half = my_half + sum(over_rows(x_mine[m], d_joints[m]) for m in micros if d_w[m][1] is None)
     my_half = (my_half + other_half.astype(F32)).astype(BF)
-    my_half, small, partial, ff_up, ff_down = fence(my_half, small, partial, ff_up, ff_down)
+    my_half, small, ff_up, ff_down, partial = fence(my_half, small, ff_up, ff_down, partial)
 
     if local_width != PAIR:
         columns = [
@@ -1122,30 +1146,33 @@
     ).astype(BF)
     small = over_bits(small, "dp", 1, dp_count)
     ff_down = over_dp(ff_down)
-    out_sum = over_dp(out_sum)
-    if stage[last] < 4:
+    ff_up = ff_up.T
+    up_other = swap(ff_up, "dp", 1)
+    if stage[last] == 0:
         partial[last] = side_parcels(last, partial[last])
-    joint_sum, small, ff_up, ff_down, out_sum, partial = fence(
-        joint_sum, small, ff_up, ff_down, out_sum, partial
+    grad_rows = row_grad(d_pre_one, w_seq, d_joints, partial[:last], parts)
+    joint_sum, small, ff_up, ff_down, up_other, out_sum, partial[last], grad_rows = fence(
+        joint_sum, small, ff_up, ff_down, up_other, out_sum, partial[last], grad_rows
     )
 
     joint_sum = over_dp(joint_sum)
-    ff_other = swap(jnp.concatenate([ff_up, ff_down, out_sum], axis=0), "dp", 1)
-    if stage[last] < 4:
+    out_sum = over_dp(out_sum, 4)
+    out_sum = by_core(out_sum, swap(out_sum, "dp", 2), 0, row_part == 0)
+    down_other = swap(ff_down, "dp", 1)
+    if stage[last] == 0:
         partial[last] = sides(partial[last])
     small = over_bits(small, "tensor", 1, min(4, count))
-    grad_w_up = by_core(ff_up, ff_other[:ff_half]).astype(F32).T
-    grad_w_down = by_core(ff_down, ff_other[ff_half : 2 * ff_half]).astype(F32)
-    grad_w_out = by_core(out_sum, ff_other[2 * ff_half :]).astype(F32)
-    joint_sum, small, partial, grad_w_up, grad_w_down, grad_w_out = fence(
-        joint_sum, small, partial, grad_w_up, grad_w_down, grad_w_out
-    )
+    grad_w_up = by_core(ff_up, up_other, 1).astype(F32)
+    grad_w_down = by_core(ff_down, down_other).astype(F32)
+    joint_sum, out_sum, grad_w_up, grad_w_down = fence(joint_sum, out_sum, grad_w_up, grad_w_down)
+    out_other = swap(out_sum, "dp", 1)
+    grad_w_out = by_core(out_sum, out_other).astype(F32)
     joint_other = swap(joint_sum, "dp", 1)
     small = over_bits(small, "tensor", 4, count)
-    keep = 1.0 - jnp.concatenate(replaced_list).astype(F32)
-    grad_rows = row_grad(
-        jnp.broadcast_to(keep[:, None], (keep.shape[0], 128)), d_pre_one, w_seq, d_joints, partial, parts
-    )
+    late = jnp.concatenate([partial[last][0], partial[last][1]], axis=1).astype(F32)
+    late = late[:, :width] + late[:, width:]
+    late = jnp.concatenate([jnp.zeros((row_count * last, width), F32), late], axis=0)
+    grad_rows = jnp.where(jnp.concatenate(replaced_list)[:, None], 0.0, grad_rows + late)
     grad_joint = by_core(joint_sum, joint_other).astype(F32)
     grad_b_query, grad_b_value = (
         lax.dynamic_slice_in_dim(small[vocab_count + i], rank * local_width, local_width, 0) for i in range(2)
@@ -1154,8 +1181,7 @@
     grad_b_out, grad_gone, grad_bone, grad_b_down, grad_gtwo, grad_btwo = (
         small[at + i] for at in sums_at for i in range(3)
     )
-    all_b_up = small[table_rows + 16 : table_rows + 16 + b_rows]
-    grad_b_up = lax.dynamic_slice_in_dim(all_b_up.reshape(-1), rank * ff_local, ff_local, 0)
+    grad_b_up = lax.dynamic_slice_in_dim(small, table_rows + 16 + 2 * rank, 2, 0)[:, :ff_half].reshape(-1)
 
     return (
         layer_out.reshape(micro_count, row_count, width),

time: 500 us -> 454 us (0.908)
  Pallas kernels: 177 us -> 147 us
  waiting for transfers between devices: 126 us -> 98.4 us
  other arithmetic: 21.7 us -> 32 us
  starting transfers between devices: 77.3 us -> 82.3 us
    ppermute x9, waiting for transfers between devices: 48.3 us -> 17 us  [forward(): return lax.ppermute(values, 'tensor', ring_fw)]
    ppermute x56 -> x59, waiting for transfers between devices: 55.1 us -> 64.9 us  [swap(): return lax.ppermute(values, axis, [(i, i ^ bit) for i in range(count)])]
    pallas_call x10, Pallas kernels: 30.4 us -> 22.1 us  [ff_grad(): pl.pallas_call(functools.partial(ff_grad_kernel, ff_half, spans, splits,...]
    pallas_call x4, Pallas kernels: 34.4 us -> 26.6 us  [attn_backward(): pl.pallas_call(functools.partial(attn_backward_kernel, parts), out_shape=...]
    unnamed x215 -> x258, local copies, waits for them, and re-layouts: 28.5 us -> 35.4 us
    convert_element_type x2 -> x8, other arithmetic: 2.61 us -> 9.46 us  [the longest x1 3.31 us: shards(): grad_w_up = by_core(ff_up, up_other, 1).astype(F32)]
    ppermute x2, waiting for transfers between devices: 15.9 us -> 9.16 us  [shards(): lax.ppermute(lax.dynamic_slice_in_dim(my_half, (group - k) % groups * 3 *...]
    dot_general x7, matrix products: 11.2 us -> 6.14 us  [over_rows(): lax.dot_general(left_mat, right_mat, ROWS_DIMS, preferred_element_type=F32)]
  transfers between devices with their start and end apart: 80 -> 83, of which waited for: 23 -> 29; matrix products, arithmetic and copies ran while one was open for 13% -> 14% of each run, Pallas kernels for 33% -> 29%
where the time goes in v4:
time: 454 us; the launch traced here: 446 us
  Pallas kernels  147 us (32%)
  waiting for transfers between devices  98.4 us (22%)
  starting transfers between devices  82.3 us (18%)
  local copies, waits for them, and re-layouts  53.6 us (12%)
  other arithmetic  32 us (7%)
  between operations  16.3 us (4%)
  matrix products  15.7 us (3%)
    ppermute x59, waiting for transfers between devices, swap(): return lax.ppermute(values, axis, [(i, i ^ bit) for i in range(count)])  64.9 us
    ppermute x59, starting transfers between devices, swap(): return lax.ppermute(values, axis, [(i, i ^ bit) for i in range(count)])  53.2 us
    unnamed x258, local copies, waits for them, and re-layouts  35.4 us
    pallas_call x4, Pallas kernels, attn_backward(): pl.pallas_call(functools.partial(attn_backward_kernel, parts), out_shape=...  26.6 us
    pallas_call x10, Pallas kernels, ff_grad(): pl.pallas_call(functools.partial(ff_grad_kernel, ff_half, spans, splits,...  22.1 us
    pallas_call x5, Pallas kernels, ff_forward(): pl.pallas_call(functools.partial(ff_forward_kernel, ff_half, count), out_...  22 us
    pallas_call x2, Pallas kernels, attn_forward(): pl.pallas_call(attn_forward_kernel, out_shape=(shape,) * parts + (jax.Sha...  17.9 us
    pallas_call x5, Pallas kernels, ff_backward(): pl.pallas_call(functools.partial(ff_backward_kernel, ff_half, count, base...  17.4 us
  transfers between devices with their start and end apart: 83, of which 29 were waited for; matrix products, arithmetic and copies ran while one was open for 14% of the time, Pallas kernels for 29%

profile of v4, /device:TPU:0, one launch (start us, length us, event | category | flops | bytes accessed | tf_op | source)
XLA Modules:
  0.0 445.8 jit_solution(1173924322445036344)
XLA Ops:
  10.0 3.0 collective-permute-start
  18.8 2.9 collective-permute-start.3
  25.2 2.6 constant_dynamic-slice_fusion.13
  36.5 7.0 %collective-permute-start.8 = (bf16[128,1024]{1,0:T(8,128)(2,1)}, bf16[128,1024]{1,0:T(8,128)(2,1)S(1)}, u32[]{:S(2)}, u32[]{:S(2)}) collective-permute-start(bf16[128,1024]{1,0:T(8,128)(2,1)} %slice.159), channel_id=1, source_target_pairs={{0,2},{1,3},{2,0},{3,1},{4,6},{5,7},{6,4},{7,5},{8,10},{9,11},{10,... | collective-permute-start | bytes 786440 | tf_op jit(solution)/shard_map/ppermute | solution.py:37
  47.1 2.0 collective-permute-start.7
  49.2 2.0 collective-permute-start.4
  51.3 2.0 assemble.1
  54.7 3.9 project.2
  58.7 8.9 %attn_forward.2 = (bf16[256,256]{1,0:T(8,128)(2,1)S(1)}, bf16[256,256]{1,0:T(8,128)(2,1)S(1)}, bf16[256,256]{1,0:T(8,128)(2,1)S(1)}, bf16[256,256]{1,0:T(8,128)(...) custom-call(bf16[1024,768]{1,0:T(8,128)(2,1)S(1)} %get-tuple-element.412.q_ref.k_ref.v_ref, ...), custom_call_target="tpu_custom_call" | custom-call | flops 4294967296 | bytes 2359296 | tf_op jit(solution)/shard_map/attn_forward/pallas_call | solution.py:180
  67.7 13.1 %collective-permute-done.4.refs_1_ = bf16[256,1024]{1,0:T(8,128)(2,1)S(1)} collective-permute-done((bf16[256,1024]{1,0:T(8,128)(2,1)S(1)}, bf16[256,1024]{1,0:T(8,128)(2,1)S(1)}, u32[]{:S(2)}, u32[]{:S(2)}) %collective-permute-start.4) | collective-permute-done | bytes 524320 | tf_op jit(solution)/shard_map/ppermute | solution.py:37
  80.8 2.3 collective-permute-start.17
  84.9 2.2 collective-permute-start.16
  87.4 6.1 %collective-permute-done.17.refs_3_ = bf16[128,1024]{1,0:T(8,128)(2,1)S(1)} collective-permute-done((bf16[128,1024]{1,0:T(8,128)(2,1)S(1)}, bf16[128,1024]{1,0:T(8,128)(2,1)S(1)}, u32[]{:S(2)}, u32[]{:S(2)}) %collective-permute-start.17) | collective-permute-done | bytes 262176 | tf_op jit(solution)/shard_map/ppermute | solution.py:37
  96.7 2.6 project.3
  99.3 8.9 %attn_forward.3 = (bf16[256,256]{1,0:T(8,128)(2,1)S(1)}, bf16[256,256]{1,0:T(8,128)(2,1)S(1)}, bf16[256,256]{1,0:T(8,128)(2,1)S(1)}, bf16[256,256]{1,0:T(8,128)(...) custom-call(bf16[1024,768]{1,0:T(8,128)(2,1)S(1)} %get-tuple-element.459.q_ref.k_ref.v_ref, ...), custom_call_target="tpu_custom_call" | custom-call | flops 4294967296 | bytes 2359296 | tf_op jit(solution)/shard_map/attn_forward/pallas_call | solution.py:180
  114.9 2.4 collective-permute-done.21.refs_7_
  118.8 2.4 collective-permute-done.22.refs_11_
  123.9 7.8 %attend.1 = (bf16[512,1024]{1,0:T(8,128)(2,1)}, f32[512,1024]{1,0:T(8,128)}, f32[512,128]{1,0:T(8,128)}, f32[512,1024]{1,0:T(8,128)}, bf16[512,1024]{1,0:T(8,128)(2,1)}, /*index=5*/bf16[1024,1024]{1,0:T(8,128)(2,1)}) custom-call(s32[5]{0:T(128)} %concatenate.99.at_ref, bf16[256,256]{1,0:T(8,128)(2,1)} %copy-done.76, bf16[256,256]{1,0:T(8,128)(2,1)} %copy-done.100, ...), custom_call_target="tpu_custom_call" | custom-call | flops 1073741824 | bytes 10485760 | tf_op jit(solution)/shard_map/attend/pallas_call | solution.py:332
  136.7 2.3 ff_forward.5
  140.8 5.6 %ff_forward.6 = (f32[512,1024]{1,0:T(8,128)S(1)}, bf16[512,1024]{1,0:T(8,128)(2,1)S(1)}, f32[512,1024]{1,0:T(8,128)S(1)}) custom-call(bf16[512,1024]{1,0:T(8,128)(2,1)S(1)} %copy-done.3, f32[512,1024]{1,0:T(8,128)S(1)} %get-tuple-element.315.init_ref, bf16[528,1024]{1,0:T(8,128)(2,1)} %pad_maximum_fusion.1.refs_0_, ...), custom_call_target="tpu_custom_call" | custom-call | flops 1 | bytes 1 | tf_op jit(solution)/shard_map/ff_forward/pallas_call | solution.py:499
  151.8 6.0 %ff_forward.7 = (f32[512,1024]{1,0:T(8,128)S(1)}, bf16[512,1024]{1,0:T(8,128)(2,1)S(1)}, f32[512,1024]{1,0:T(8,128)S(1)}) custom-call(bf16[512,1024]{1,0:T(8,128)(2,1)S(1)} %copy-done.3, f32[512,1024]{1,0:T(8,128)S(1)} %get-tuple-element.319.init_ref, bf16[528,1024]{1,0:T(8,128)(2,1)} %collective-permute-done.23.refs_0_, ...), custom_call_target="tpu_custom_call" | custom-call | flops 1 | bytes 1 | tf_op jit(solution)/shard_map/ff_forward/pallas_call | solution.py:499
  159.2 14.7 %collective-permute-done.28.refs_0_ = bf16[528,1024]{1,0:T(8,128)(2,1)S(1)} collective-permute-done((bf16[528,1024]{1,0:T(8,128)(2,1)}, bf16[528,1024]{1,0:T(8,128)(2,1)S(1)}, u32[]{:S(2)}, u32[]{:S(2)}) %collective-permute-start.28) | collective-permute-done | bytes 1081376 | tf_op jit(solution)/shard_map/ppermute | solution.py:796
  179.0 4.6 %ff_forward.8 = (f32[512,1024]{1,0:T(8,128)S(1)}, bf16[512,1024]{1,0:T(8,128)(2,1)S(1)}, f32[512,1024]{1,0:T(8,128)S(1)}) custom-call(bf16[512,1024]{1,0:T(8,128)(2,1)S(1)} %copy-done.3, f32[512,1024]{1,0:T(8,128)S(1)} %get-tuple-element.323.init_ref, bf16[528,1024]{1,0:T(8,128)(2,1)S(1)} %collective-permute-done.28.refs_0_, ...), custom_call_target="tpu_custom_call" | custom-call | flops 1 | bytes 1 | tf_op jit(solution)/shard_map/ff_forward/pallas_call | solution.py:499
  187.4 3.5 collective-permute-done.33
  195.7 3.5 ff_forward.9
  199.2 3.0 second_norm.1
  202.2 3.0 ff_backward.5
  207.1 3.5 ff_backward.6
  210.6 1.9 ff_grad.12
  216.5 4.6 %ff_backward.7 = (bf16[512,1024]{1,0:T(8,128)(2,1)S(1)}, f32[512,1024]{1,0:T(8,128)S(1)}, f32[16,256]{1,0:T(8,128)S(1)}) custom-call(bf16[512,1024]{1,0:T(8,128)(2,1)S(1)} %get-tuple-element.443.d_fed_ref.fed_ref, f32[512,1024]{1,0:T(8,128)S(1)} %get-tuple-element.357.init_ref, f32[512,1024]{1,0:T(8,128)S(1)} %copy-done.50, ...), custom_call_target="tpu_custom_call" | custom-call | flops 2147483648 | bytes 12582912 | tf_op jit(solution)/shard_map/ff_backward/pallas_call | solution.py:544
  221.1 2.8 ff_grad.14
  223.9 2.0 ff_grad.13
  226.0 2.3 collective-permute-done.38.refs_3_
  230.1 2.0 combine.4
  237.4 4.6 %ff_backward.8 = (bf16[512,1024]{1,0:T(8,128)(2,1)S(1)}, f32[512,1024]{1,0:T(8,128)S(1)}, f32[16,256]{1,0:T(8,128)S(1)}) custom-call(bf16[512,1024]{1,0:T(8,128)(2,1)S(1)} %get-tuple-element.443.d_fed_ref.fed_ref, f32[512,1024]{1,0:T(8,128)S(1)} %copy-done.52, f32[512,1024]{1,0:T(8,128)S(1)} %copy-done.48, bf16[528,1024]{1,0:T(8,128)(2,1)} %pad_maximum_fusion.1.refs_0_, ...), custom_call_target="tpu_custom_call" | custom-call | flops 2147483648 | bytes 12582912 | tf_op jit(solution)/shard_map/ff_backward/pallas_call | solution.py:544
  244.6 3.6 attend_back.1
  249.1 2.7 collective-permute-start.46
  253.2 2.7 ff_grad.16
  258.2 2.9 ff_grad.15
  261.1 8.0 %collective-permute-done.44 = bf16[512,256]{1,0:T(8,128)(2,1)S(1)} collective-permute-done((bf16[512,256]{1,0:T(8,128)(2,1)S(1)}, bf16[512,256]{1,0:T(8,128)(2,1)S(1)}, u32[]{:S(2)}, u32[]{:S(2)}) %collective-permute-start.44) | collective-permute-done | bytes 262176 | tf_op jit(solution)/shard_map/ppermute | solution.py:37
  269.2 4.0 combine.5
  276.8 1.9 fusion.2
  280.6 6.7 %attn_backward.4.refs_0_ = bf16[1024,768]{1,0:T(8,128)(2,1)S(1)} custom-call(bf16[1024,768]{1,0:T(8,128)(2,1)S(1)} %copy-done.14, bf16[1024,768]{1,0:T(8,128)(2,1)S(1)} %copy-done.14, bf16[1024,768]{1,0:T(8,128)(2,1)S(1)} %copy-done.14, f32[2,8,1024]{2,1,0:T(8,128)S(1)} %get-tuple-element.422.log_ref, ...), custom_call_target="tpu_custom_call" | custom-call | flops 1 | bytes 1 | tf_op jit(solution)/shard_map/attn_backward/pallas_call | solution.py:241
  287.3 2.0 fusion.40
  289.3 6.6 %attn_backward.5.d_ref.one_ref.two_ref.refs_0_ = bf16[1024,768]{1,0:T(8,128)(2,1)S(1)} custom-call(bf16[1024,768]{1,0:T(8,128)(2,1)S(1)} %copy-done.14, bf16[1024,768]{1,0:T(8,128)(2,1)S(1)} %copy-done.14, bf16[1024,768]{1,0:T(8,128)(2,1)S(1)} %copy-done.14, f32[2,8,1024]{2,1,0:T(8,128)S(1)} %get-tuple-element.422.log_ref, ...), custom_call_target="tpu_custom_call", output_to_operand_aliasing={{}: (6, {})} | custom-call | flops 1 | bytes 1 | tf_op jit(solution)/shard_map/attn_backward/pallas_call | solution.py:241
  297.1 2.0 ff_grad.18
  302.6 2.9 ff_grad.17
  305.6 3.8 combine.6
  324.8 6.6 %attn_backward.6.refs_0_ = bf16[1024,768]{1,0:T(8,128)(2,1)S(1)} custom-call(bf16[1024,768]{1,0:T(8,128)(2,1)S(1)} %copy-done.11, bf16[1024,768]{1,0:T(8,128)(2,1)S(1)} %copy-done.11, bf16[1024,768]{1,0:T(8,128)(2,1)S(1)} %copy-done.11, f32[2,8,1024]{2,1,0:T(8,128)S(1)} %get-tuple-element.446.log_ref, ...), custom_call_target="tpu_custom_call" | custom-call | flops 1 | bytes 1 | tf_op jit(solution)/shard_map/attn_backward/pallas_call | solution.py:241
  331.5 2.2 ff_grad.19.refs_0_
  333.7 11.6 %collective-permute-done.55.to_two_ref = bf16[128,1024]{1,0:T(8,128)(2,1)S(1)} collective-permute-done((bf16[128,1024]{1,0:T(8,128)(2,1)}, bf16[128,1024]{1,0:T(8,128)(2,1)S(1)}, u32[]{:S(2)}, u32[]{:S(2)}) %collective-permute-start.55) | collective-permute-done | bytes 262176 | tf_op jit(solution)/shard_map/ppermute | solution.py:37
  345.3 2.6 combine.7
  349.3 2.1 side_shares.2
  351.9 2.1 collective-permute-start.59
  355.4 6.6 %attn_backward.7.d_ref.one_ref.two_ref.refs_1_ = bf16[1024,768]{1,0:T(8,128)(2,1)S(1)} custom-call(bf16[1024,768]{1,0:T(8,128)(2,1)S(1)} %copy-done.12, bf16[1024,768]{1,0:T(8,128)(2,1)S(1)} %copy-done.12, bf16[1024,768]{1,0:T(8,128)(2,1)S(1)} %copy-done.12, f32[2,8,1024]{2,1,0:T(8,128)S(1)} %get-tuple-element.446.log_ref, ...), custom_call_target="tpu_custom_call", output_to_operand_aliasing={{}: (6, {})} | custom-call | flops 1 | bytes 1 | tf_op jit(solution)/shard_map/attn_backward/pallas_call | solution.py:241
  364.3 2.2 collective-permute-done.57
  374.7 1.9 collective-permute-done.61.to_two_ref
  377.6 4.4 collective-permute-start.64
  390.9 9.2 %collective-permute-done.64 = bf16[512,384]{1,0:T(8,128)(2,1)S(1)} collective-permute-done((bf16[512,384]{1,0:T(8,128)(2,1)S(1)}, bf16[512,384]{1,0:T(8,128)(2,1)S(1)}, u32[]{:S(2)}, u32[]{:S(2)}) %collective-permute-start.64) | collective-permute-done | bytes 393248 | tf_op jit(solution)/shard_map/ppermute | solution.py:1138
  403.2 2.8 collective-permute-start.74
  413.2 3.3 fusion.7
  426.3 3.1 collective-permute-done.71
  431.3 2.9 copy.53
  434.2 2.0 fusion.23
  (514 shorter events, 162.1 us)
Async XLA Ops:
  7.2 110.1 %all-gather.3.cloned.1.call-start = ((), (), s32[]{:S(2)}) async-start(), calls=%async_computation.2 | async-start | bytes 1179648 | tf_op jit(solution)/shard_map/all_gather | solution.py:862
  10.0 24.3 %collective-permute-start = (bf16[256,1024]{1,0:T(8,128)(2,1)S(1)}, bf16[256,1024]{1,0:T(8,128)(2,1)}, u32[]{:S(2)}, u32[]{:S(2)}) collective-permute-start(bf16[256,1024]{1,0:T(8,128)(2,1)S(1)} %fusion.3.refs_0_.refs_8_), channel_id=1, source_target_pairs={{0,1},{1,0},{2,3},{3,2},{4,5},{5,4},{6,7},{7,6},{8,9},{9,8},{10,11... | collective-permute-start | bytes 1572872 | tf_op jit(solution)/shard_map/ppermute | solution.py:37
  13.0 21.3 %collective-permute-start.1 = (bf16[256,1024]{1,0:T(8,128)(2,1)S(1)}, bf16[256,1024]{1,0:T(8,128)(2,1)}, u32[]{:S(2)}, u32[]{:S(2)}) collective-permute-start(bf16[256,1024]{1,0:T(8,128)(2,1)S(1)} %fusion.3.refs_0_.refs_8_), channel_id=1, source_target_pairs={{0,2},{1,3},{2,0},{3,1},{4,6},{5,7},{6,4},{7,5},{8,10},{9,11},{10,... | collective-permute-start | bytes 1572872 | tf_op jit(solution)/shard_map/ppermute | solution.py:37
  17.2 17.0 %collective-permute-start.2 = (bf16[528,384]{1,0:T(8,128)(2,1)}, bf16[528,384]{1,0:T(8,128)(2,1)S(1)}, u32[]{:S(2)}, u32[]{:S(2)}) collective-permute-start(bf16[528,384]{1,0:T(8,128)(2,1)} %fusion.18), channel_id=1, source_target_pairs={{0,0},{1,4},{2,1},{3,5},{4,2},{5,6},{6,3},{7,7},{8,8},{9,12},{10,9... | collective-permute-start | bytes 1216520 | tf_op jit(solution)/shard_map/ppermute | solution.py:856
  18.8 15.5 %collective-permute-start.3 = (bf16[528,384]{1,0:T(8,128)(2,1)}, bf16[528,384]{1,0:T(8,128)(2,1)}, u32[]{:S(2)}, u32[]{:S(2)}) collective-permute-start(bf16[528,384]{1,0:T(8,128)(2,1)} %fusion.18), channel_id=1, source_target_pairs={{0,4},{1,0},{2,5},{3,1},{4,6},{5,2},{6,7},{7,3},{8,12},{9,8},{10,1... | collective-permute-start | bytes 1216520 | tf_op jit(solution)/shard_map/ppermute | solution.py:856
  34.4 12.7 %collective-permute-start.10 = (bf16[528,384]{1,0:T(8,128)(2,1)S(1)}, bf16[528,384]{1,0:T(8,128)(2,1)S(1)}, u32[]{:S(2)}, u32[]{:S(2)}) collective-permute-start(bf16[528,384]{1,0:T(8,128)(2,1)S(1)} %collective-permute-done.2.refs_0_), channel_id=1, source_target_pairs={{0,8},{8,0},{16,24},{24,16},{1,9},{9,1},{17,25},{25,17},{2,10},{10... | collective-permute-start | bytes 1216520 | tf_op jit(solution)/shard_map/ppermute | solution.py:37
  34.4 14.9 %collective-permute-start.11 = (bf16[528,384]{1,0:T(8,128)(2,1)}, bf16[528,384]{1,0:T(8,128)(2,1)}, u32[]{:S(2)}, u32[]{:S(2)}) collective-permute-start(bf16[528,384]{1,0:T(8,128)(2,1)} %collective-permute-done.3.refs_1_), channel_id=1, source_target_pairs={{0,8},{8,0},{16,24},{24,16},{1,9},{9,1},{17,25},{25,17},{2,10},{10... | collective-permute-start | bytes 1216520 | tf_op jit(solution)/shard_map/ppermute | solution.py:37
  36.5 16.7 %collective-permute-start.8 = (bf16[128,1024]{1,0:T(8,128)(2,1)}, bf16[128,1024]{1,0:T(8,128)(2,1)S(1)}, u32[]{:S(2)}, u32[]{:S(2)}) collective-permute-start(bf16[128,1024]{1,0:T(8,128)(2,1)} %slice.159), channel_id=1, source_target_pairs={{0,2},{1,3},{2,0},{3,1},{4,6},{5,7},{6,4},{7,5},{8,10},{9,11},{10,... | collective-permute-start | bytes 786440 | tf_op jit(solution)/shard_map/ppermute | solution.py:37
  45.2 9.5 %collective-permute-start.9 = (bf16[128,1024]{1,0:T(8,128)(2,1)}, bf16[128,1024]{1,0:T(8,128)(2,1)}, u32[]{:S(2)}, u32[]{:S(2)}) collective-permute-start(bf16[128,1024]{1,0:T(8,128)(2,1)} %slice.160), channel_id=1, source_target_pairs={{0,1},{1,0},{2,3},{3,2},{4,5},{5,4},{6,7},{7,6},{8,9},{9,8},{10,11... | collective-permute-start | bytes 786440 | tf_op jit(solution)/shard_map/ppermute | solution.py:37
  46.8 355.6 %reduce-scatter.2.cloned.1.call-start = ((), (), s32[]{:S(2)}) async-start(), calls=%async_computation.1 | async-start | bytes 589824 | tf_op jit(solution)/shard_map/reduce_scatter | solution.py:1038
  47.0 33.8 %collective-permute-start.6 = (bf16[272,1024]{1,0:T(8,128)(2,1)S(1)}, bf16[272,1024]{1,0:T(8,128)(2,1)S(1)}, u32[]{:S(2)}, u32[]{:S(2)}) collective-permute-start(bf16[272,1024]{1,0:T(8,128)(2,1)S(1)} %slice.158), channel_id=1, source_target_pairs={{0,2},{2,4},{4,6},{6,7},{7,5},{5,3},{3,1},{1,0},{8,10},{10,12},{12... | collective-permute-start | bytes 1671176 | tf_op jit(solution)/shard_map/ppermute | solution.py:796
  47.1 33.7 %collective-permute-start.7 = (bf16[272,1024]{1,0:T(8,128)(2,1)S(1)}, bf16[272,1024]{1,0:T(8,128)(2,1)S(1)}, u32[]{:S(2)}, u32[]{:S(2)}) collective-permute-start(bf16[272,1024]{1,0:T(8,128)(2,1)S(1)} %slice.158), channel_id=1, source_target_pairs={{2,0},{4,2},{6,4},{7,6},{5,7},{3,5},{1,3},{0,1},{10,8},{12,10},{14... | collective-permute-start | bytes 1671176 | tf_op jit(solution)/shard_map/ppermute | solution.py:799
  49.2 31.5 %collective-permute-start.4 = (bf16[256,1024]{1,0:T(8,128)(2,1)S(1)}, bf16[256,1024]{1,0:T(8,128)(2,1)S(1)}, u32[]{:S(2)}, u32[]{:S(2)}) collective-permute-start(bf16[256,1024]{1,0:T(8,128)(2,1)S(1)} %copy-done.72), channel_id=1, source_target_pairs={{0,1},{1,0},{2,3},{3,2},{4,5},{5,4},{6,7},{7,6},{8,9},{9,8},{10,11... | collective-permute-start | bytes 1572872 | tf_op jit(solution)/shard_map/ppermute | solution.py:37
  53.2 27.5 %collective-permute-start.5 = (bf16[256,1024]{1,0:T(8,128)(2,1)S(1)}, bf16[256,1024]{1,0:T(8,128)(2,1)S(1)}, u32[]{:S(2)}, u32[]{:S(2)}) collective-permute-start(bf16[256,1024]{1,0:T(8,128)(2,1)S(1)} %copy-done.72), channel_id=1, source_target_pairs={{0,2},{1,3},{2,0},{3,1},{4,6},{5,7},{6,4},{7,5},{8,10},{9,11},{10,... | collective-permute-start | bytes 1572872 | tf_op jit(solution)/shard_map/ppermute | solution.py:37
  80.8 12.6 %collective-permute-start.17 = (bf16[128,1024]{1,0:T(8,128)(2,1)S(1)}, bf16[128,1024]{1,0:T(8,128)(2,1)S(1)}, u32[]{:S(2)}, u32[]{:S(2)}) collective-permute-start(bf16[128,1024]{1,0:T(8,128)(2,1)S(1)} %slice.162), channel_id=1, source_target_pairs={{0,2},{1,3},{2,0},{3,1},{4,6},{5,7},{6,4},{7,5},{8,10},{9,11},{10,... | collective-permute-start | bytes 786440 | tf_op jit(solution)/shard_map/ppermute | solution.py:37
  83.1 11.9 %collective-permute-start.18 = (bf16[128,1024]{1,0:T(8,128)(2,1)S(1)}, bf16[128,1024]{1,0:T(8,128)(2,1)S(1)}, u32[]{:S(2)}, u32[]{:S(2)}) collective-permute-start(bf16[128,1024]{1,0:T(8,128)(2,1)S(1)} %slice.163), channel_id=1, source_target_pairs={{0,1},{1,0},{2,3},{3,2},{4,5},{5,4},{6,7},{7,6},{8,9},{9,8},{10,11... | collective-permute-start | bytes 786440 | tf_op jit(solution)/shard_map/ppermute | solution.py:37
  84.9 23.4 %collective-permute-start.15 = (bf16[256,1024]{1,0:T(8,128)(2,1)S(1)}, bf16[256,1024]{1,0:T(8,128)(2,1)S(1)}, u32[]{:S(2)}, u32[]{:S(2)}) collective-permute-start(bf16[256,1024]{1,0:T(8,128)(2,1)S(1)} %slice.161), channel_id=1, source_target_pairs={{0,2},{2,4},{4,6},{6,7},{7,5},{5,3},{3,1},{1,0},{8,10},{10,12},{12... | collective-permute-start | bytes 1572872 | tf_op jit(solution)/shard_map/ppermute | solution.py:796
  84.9 23.4 %collective-permute-start.16 = (bf16[256,1024]{1,0:T(8,128)(2,1)S(1)}, bf16[256,1024]{1,0:T(8,128)(2,1)S(1)}, u32[]{:S(2)}, u32[]{:S(2)}) collective-permute-start(bf16[256,1024]{1,0:T(8,128)(2,1)S(1)} %slice.161), channel_id=1, source_target_pairs={{2,0},{4,2},{6,4},{7,6},{5,7},{3,5},{1,3},{0,1},{10,8},{12,10},{14... | collective-permute-start | bytes 1572872 | tf_op jit(solution)/shard_map/ppermute | solution.py:799
  87.1 24.2 %collective-permute-start.12 = (bf16[256,256]{1,0:T(8,128)(2,1)S(1)}, bf16[256,256]{1,0:T(8,128)(2,1)S(1)}, u32[]{:S(2)}, u32[]{:S(2)}) collective-permute-start(bf16[256,256]{1,0:T(8,128)(2,1)S(1)} %get-tuple-element.282), channel_id=1, source_target_pairs={{0,1},{1,0},{2,3},{3,2},{4,5},{5,4},{6,7},{7,6},{8,9},{9,8},{10,11... | collective-permute-start | bytes 393224 | tf_op jit(solution)/shard_map/ppermute | solution.py:37
  93.4 20.7 %collective-permute-start.13 = (bf16[256,256]{1,0:T(8,128)(2,1)S(1)}, bf16[256,256]{1,0:T(8,128)(2,1)S(1)}, u32[]{:S(2)}, u32[]{:S(2)}) collective-permute-start(bf16[256,256]{1,0:T(8,128)(2,1)S(1)} %get-tuple-element.283), channel_id=1, source_target_pairs={{0,2},{1,3},{2,0},{3,1},{4,6},{5,7},{6,4},{7,5},{8,10},{9,11},{10,... | collective-permute-start | bytes 393224 | tf_op jit(solution)/shard_map/ppermute | solution.py:37
  95.0 19.1 %collective-permute-start.14 = (bf16[256,256]{1,0:T(8,128)(2,1)S(1)}, bf16[256,256]{1,0:T(8,128)(2,1)S(1)}, u32[]{:S(2)}, u32[]{:S(2)}) collective-permute-start(bf16[256,256]{1,0:T(8,128)(2,1)S(1)} %get-tuple-element.284), channel_id=1, source_target_pairs={{0,3},{1,2},{2,1},{3,0},{4,7},{5,6},{6,5},{7,4},{8,11},{9,10},{10,... | collective-permute-start | bytes 393224 | tf_op jit(solution)/shard_map/ppermute | solution.py:37
  117.3 14.4 %collective-permute-start.25 = (bf16[528,1024]{1,0:T(8,128)(2,1)S(1)}, bf16[528,1024]{1,0:T(8,128)(2,1)S(1)}, u32[]{:S(2)}, u32[]{:S(2)}) collective-permute-start(bf16[528,1024]{1,0:T(8,128)(2,1)S(1)} %fusion.6.refs_0_), channel_id=1, source_target_pairs={{0,8},{8,0},{16,24},{24,16},{1,9},{9,1},{17,25},{25,17},{2,10},{10... | collective-permute-start | bytes 3244040 | tf_op jit(solution)/shard_map/ppermute | solution.py:37
  117.8 23.0 %collective-permute-start.26 = (bf16[528,1024]{1,0:T(8,128)(2,1)}, bf16[528,1024]{1,0:T(8,128)(2,1)}, u32[]{:S(2)}, u32[]{:S(2)}) collective-permute-start(bf16[528,1024]{1,0:T(8,128)(2,1)} %pad_maximum_fusion.1.refs_0_), channel_id=1, source_target_pairs={{0,8},{8,0},{16,24},{24,16},{1,9},{9,1},{17,25},{25,17},{2,10},{10... | collective-permute-start | bytes 3244040 | tf_op jit(solution)/shard_map/ppermute | solution.py:37
  117.8 23.0 %collective-permute-start.27 = (bf16[528,1024]{1,0:T(8,128)(2,1)}, bf16[528,1024]{1,0:T(8,128)(2,1)}, u32[]{:S(2)}, u32[]{:S(2)}) collective-permute-start(bf16[528,1024]{1,0:T(8,128)(2,1)} %pad_maximum_fusion.2.refs_1_), channel_id=1, source_target_pairs={{0,8},{8,0},{16,24},{24,16},{1,9},{9,1},{17,25},{25,17},{2,10},{10... | collective-permute-start | bytes 3244040 | tf_op jit(solution)/shard_map/ppermute | solution.py:37
  118.3 28.2 %collective-permute-start.23 = (bf16[528,1024]{1,0:T(8,128)(2,1)}, bf16[528,1024]{1,0:T(8,128)(2,1)}, u32[]{:S(2)}, u32[]{:S(2)}) collective-permute-start(bf16[528,1024]{1,0:T(8,128)(2,1)} %pad_maximum_fusion.1.refs_0_), channel_id=1, source_target_pairs={{0,2},{2,4},{4,6},{6,7},{7,5},{5,3},{3,1},{1,0},{8,10},{10,12},{12... | collective-permute-start | bytes 3244040 | tf_op jit(solution)/shard_map/ppermute | solution.py:796
  121.1 26.2 %collective-permute-start.24 = (bf16[528,1024]{1,0:T(8,128)(2,1)}, bf16[528,1024]{1,0:T(8,128)(2,1)}, u32[]{:S(2)}, u32[]{:S(2)}) collective-permute-start(bf16[528,1024]{1,0:T(8,128)(2,1)} %pad_maximum_fusion.2.refs_1_), channel_id=1, source_target_pairs={{2,0},{4,2},{6,4},{7,6},{5,7},{3,5},{1,3},{0,1},{10,8},{12,10},{14... | collective-permute-start | bytes 3244040 | tf_op jit(solution)/shard_map/ppermute | solution.py:799
  147.9 26.0 %collective-permute-start.28 = (bf16[528,1024]{1,0:T(8,128)(2,1)}, bf16[528,1024]{1,0:T(8,128)(2,1)S(1)}, u32[]{:S(2)}, u32[]{:S(2)}) collective-permute-start(bf16[528,1024]{1,0:T(8,128)(2,1)} %collective-permute-done.23.refs_0_), channel_id=1, source_target_pairs={{0,2},{2,4},{4,6},{6,7},{7,5},{5,3},{3,1},{1,0},{8,10},{10,12},{12... | collective-permute-start | bytes 3244040 | tf_op jit(solution)/shard_map/ppermute | solution.py:796
  149.0 25.7 %collective-permute-start.29 = (bf16[528,1024]{1,0:T(8,128)(2,1)}, bf16[528,1024]{1,0:T(8,128)(2,1)S(1)}, u32[]{:S(2)}, u32[]{:S(2)}) collective-permute-start(bf16[528,1024]{1,0:T(8,128)(2,1)} %collective-permute-done.24.refs_1_), channel_id=1, source_target_pairs={{2,0},{4,2},{6,4},{7,6},{5,7},{3,5},{1,3},{0,1},{10,8},{12,10},{14... | collective-permute-start | bytes 3244040 | tf_op jit(solution)/shard_map/ppermute | solution.py:799
  175.3 15.7 %collective-permute-start.32 = (bf16[272,1024]{1,0:T(8,128)(2,1)S(1)}, bf16[272,1024]{1,0:T(8,128)(2,1)S(1)}, u32[]{:S(2)}, u32[]{:S(2)}) collective-permute-start(bf16[272,1024]{1,0:T(8,128)(2,1)S(1)} %slice.164), channel_id=1, source_target_pairs={{0,2},{2,4},{4,6},{6,7},{7,5},{5,3},{3,1},{1,0},{8,10},{10,12},{12... | collective-permute-start | bytes 1671176 | tf_op jit(solution)/shard_map/ppermute | solution.py:796
  177.1 13.8 %collective-permute-start.33 = (bf16[256,1024]{1,0:T(8,128)(2,1)S(1)}, bf16[256,1024]{1,0:T(8,128)(2,1)S(1)}, u32[]{:S(2)}, u32[]{:S(2)}) collective-permute-start(bf16[256,1024]{1,0:T(8,128)(2,1)S(1)} %slice.165), channel_id=1, source_target_pairs={{2,0},{4,2},{6,4},{7,6},{5,7},{3,5},{1,3},{0,1},{10,8},{12,10},{14... | collective-permute-start | bytes 1572872 | tf_op jit(solution)/shard_map/ppermute | solution.py:799
  213.9 10.0 %collective-permute-start.40 = (bf16[1024,1024]{1,0:T(8,128)(2,1)S(1)}, bf16[1024,1024]{1,0:T(8,128)(2,1)S(1)}, u32[]{:S(2)}, u32[]{:S(2)}) collective-permute-start(bf16[1024,1024]{1,0:T(8,128)(2,1)S(1)} %ff_grad.12), channel_id=1, source_target_pairs={{0,8},{8,0},{16,24},{24,16},{1,9},{9,1},{17,25},{25,17},{2,10},{10... | collective-permute-start | bytes 6291464 | tf_op jit(solution)/shard_map/ppermute | solution.py:37
  214.1 14.2 %collective-permute-start.38 = (bf16[256,1024]{1,0:T(8,128)(2,1)S(1)}, bf16[256,1024]{1,0:T(8,128)(2,1)S(1)}, u32[]{:S(2)}, u32[]{:S(2)}) collective-permute-start(bf16[256,1024]{1,0:T(8,128)(2,1)S(1)} %get-tuple-element.353), channel_id=1, source_target_pairs={{0,2},{2,4},{4,6},{6,7},{7,5},{5,3},{3,1},{1,0},{8,10},{10,12},{12... | collective-permute-start | bytes 1572872 | tf_op jit(solution)/shard_map/ppermute | solution.py:796
  215.8 14.3 %collective-permute-start.39 = (bf16[256,1024]{1,0:T(8,128)(2,1)S(1)}, bf16[256,1024]{1,0:T(8,128)(2,1)S(1)}, u32[]{:S(2)}, u32[]{:S(2)}) collective-permute-start(bf16[256,1024]{1,0:T(8,128)(2,1)S(1)} %get-tuple-element.354), channel_id=1, source_target_pairs={{2,0},{4,2},{6,4},{7,6},{5,7},{3,5},{1,3},{0,1},{10,8},{12,10},{14... | collective-permute-start | bytes 1572872 | tf_op jit(solution)/shard_map/ppermute | solution.py:799
  232.1 16.1 %collective-permute-start.43 = (bf16[1024,1024]{1,0:T(8,128)(2,1)}, bf16[1024,1024]{1,0:T(8,128)(2,1)}, u32[]{:S(2)}, u32[]{:S(2)}) collective-permute-start(bf16[1024,1024]{1,0:T(8,128)(2,1)} %ff_grad.14), channel_id=1, source_target_pairs={{0,8},{8,0},{16,24},{24,16},{1,9},{9,1},{17,25},{25,17},{2,10},{10... | collective-permute-start | bytes 6291464 | tf_op jit(solution)/shard_map/ppermute | solution.py:37
  232.1 29.0 %collective-permute-start.41 = (bf16[512,1024]{1,0:T(8,128)(2,1)}, bf16[512,1024]{1,0:T(8,128)(2,1)}, u32[]{:S(2)}, u32[]{:S(2)}) collective-permute-start(bf16[512,1024]{1,0:T(8,128)(2,1)} %get-tuple-element.376), channel_id=1, source_target_pairs={{0,2},{2,4},{4,6},{6,7},{7,5},{5,3},{3,1},{1,0},{8,10},{10,12},{12... | collective-permute-start | bytes 3145736 | tf_op jit(solution)/shard_map/ppermute | solution.py:796
  232.8 28.3 %collective-permute-start.42 = (bf16[512,1024]{1,0:T(8,128)(2,1)}, bf16[512,1024]{1,0:T(8,128)(2,1)}, u32[]{:S(2)}, u32[]{:S(2)}) collective-permute-start(bf16[512,1024]{1,0:T(8,128)(2,1)} %get-tuple-element.377), channel_id=1, source_target_pairs={{2,0},{4,2},{6,4},{7,6},{5,7},{3,5},{1,3},{0,1},{10,8},{12,10},{14... | collective-permute-start | bytes 3145736 | tf_op jit(solution)/shard_map/ppermute | solution.py:799
  248.2 20.9 %collective-permute-start.44 = (bf16[512,256]{1,0:T(8,128)(2,1)S(1)}, bf16[512,256]{1,0:T(8,128)(2,1)S(1)}, u32[]{:S(2)}, u32[]{:S(2)}) collective-permute-start(bf16[512,256]{1,0:T(8,128)(2,1)S(1)} %get-tuple-element.398), channel_id=1, source_target_pairs={{0,1},{1,0},{2,3},{3,2},{4,5},{5,4},{6,7},{7,6},{8,9},{9,8},{10,11... | collective-permute-start | bytes 786440 | tf_op jit(solution)/shard_map/ppermute | solution.py:37
  248.6 20.5 %collective-permute-start.45 = (bf16[512,256]{1,0:T(8,128)(2,1)S(1)}, bf16[512,256]{1,0:T(8,128)(2,1)S(1)}, u32[]{:S(2)}, u32[]{:S(2)}) collective-permute-start(bf16[512,256]{1,0:T(8,128)(2,1)S(1)} %get-tuple-element.399), channel_id=1, source_target_pairs={{0,2},{1,3},{2,0},{3,1},{4,6},{5,7},{6,4},{7,5},{8,10},{9,11},{10,... | collective-permute-start | bytes 786440 | tf_op jit(solution)/shard_map/ppermute | solution.py:37
  249.1 20.1 %collective-permute-start.46 = (bf16[512,256]{1,0:T(8,128)(2,1)S(1)}, bf16[512,256]{1,0:T(8,128)(2,1)S(1)}, u32[]{:S(2)}, u32[]{:S(2)}) collective-permute-start(bf16[512,256]{1,0:T(8,128)(2,1)S(1)} %get-tuple-element.400), channel_id=1, source_target_pairs={{0,3},{1,2},{2,1},{3,0},{4,7},{5,6},{6,5},{7,4},{8,11},{9,10},{10,... | collective-permute-start | bytes 786440 | tf_op jit(solution)/shard_map/ppermute | solution.py:37
  273.3 26.8 %collective-permute-start.49 = (bf16[1024,1024]{1,0:T(8,128)(2,1)}, bf16[1024,1024]{1,0:T(8,128)(2,1)}, u32[]{:S(2)}, u32[]{:S(2)}) collective-permute-start(bf16[1024,1024]{1,0:T(8,128)(2,1)} %ff_grad.16), channel_id=1, source_target_pairs={{0,8},{8,0},{16,24},{24,16},{1,9},{9,1},{17,25},{25,17},{2,10},{10... | collective-permute-start | bytes 6291464 | tf_op jit(solution)/shard_map/ppermute | solution.py:37
  273.7 31.9 %collective-permute-start.47 = (bf16[512,1024]{1,0:T(8,128)(2,1)}, bf16[512,1024]{1,0:T(8,128)(2,1)}, u32[]{:S(2)}, u32[]{:S(2)}) collective-permute-start(bf16[512,1024]{1,0:T(8,128)(2,1)} %get-tuple-element.414), channel_id=1, source_target_pairs={{0,2},{2,4},{4,6},{6,7},{7,5},{5,3},{3,1},{1,0},{8,10},{10,12},{12... | collective-permute-start | bytes 3145736 | tf_op jit(solution)/shard_map/ppermute | solution.py:796
  275.1 30.4 %collective-permute-start.48 = (bf16[512,1024]{1,0:T(8,128)(2,1)}, bf16[512,1024]{1,0:T(8,128)(2,1)}, u32[]{:S(2)}, u32[]{:S(2)}) collective-permute-start(bf16[512,1024]{1,0:T(8,128)(2,1)} %get-tuple-element.415), channel_id=1, source_target_pairs={{2,0},{4,2},{6,4},{7,6},{5,7},{3,5},{1,3},{0,1},{10,8},{12,10},{14... | collective-permute-start | bytes 3145736 | tf_op jit(solution)/shard_map/ppermute | solution.py:799
  278.9 20.2 %collective-permute-start.51 = (bf16[256,1024]{1,0:T(8,128)(2,1)S(1)}, bf16[256,1024]{1,0:T(8,128)(2,1)S(1)}, u32[]{:S(2)}, u32[]{:S(2)}) collective-permute-start(bf16[256,1024]{1,0:T(8,128)(2,1)S(1)} %bitcast.84), channel_id=1, source_target_pairs={{0,16},{8,24},{16,0},{24,8},{1,17},{9,25},{17,1},{25,9},{2,18},{10... | collective-permute-start | bytes 1572872 | tf_op jit(solution)/shard_map/ppermute | solution.py:37
  309.4 22.1 %collective-permute-start.54 = (bf16[512,1024]{1,0:T(8,128)(2,1)}, bf16[512,1024]{1,0:T(8,128)(2,1)}, u32[]{:S(2)}, u32[]{:S(2)}) collective-permute-start(bf16[512,1024]{1,0:T(8,128)(2,1)} %ff_grad.18), channel_id=1, source_target_pairs={{0,8},{8,0},{16,24},{24,16},{1,9},{9,1},{17,25},{25,17},{2,10},{10... | collective-permute-start | bytes 3145736 | tf_op jit(solution)/shard_map/ppermute | solution.py:37
  309.4 35.9 %collective-permute-start.52 = (bf16[512,1024]{1,0:T(8,128)(2,1)}, bf16[512,1024]{1,0:T(8,128)(2,1)}, u32[]{:S(2)}, u32[]{:S(2)}) collective-permute-start(bf16[512,1024]{1,0:T(8,128)(2,1)} %get-tuple-element.441), channel_id=1, source_target_pairs={{0,2},{2,4},{4,6},{6,7},{7,5},{5,3},{3,1},{1,0},{8,10},{10,12},{12... | collective-permute-start | bytes 3145736 | tf_op jit(solution)/shard_map/ppermute | solution.py:796
  310.8 34.5 %collective-permute-start.53 = (bf16[512,1024]{1,0:T(8,128)(2,1)}, bf16[512,1024]{1,0:T(8,128)(2,1)}, u32[]{:S(2)}, u32[]{:S(2)}) collective-permute-start(bf16[512,1024]{1,0:T(8,128)(2,1)} %get-tuple-element.442), channel_id=1, source_target_pairs={{2,0},{4,2},{6,4},{7,6},{5,7},{3,5},{1,3},{0,1},{10,8},{12,10},{14... | collective-permute-start | bytes 3145736 | tf_op jit(solution)/shard_map/ppermute | solution.py:799
  317.0 28.3 %collective-permute-start.55 = (bf16[128,1024]{1,0:T(8,128)(2,1)}, bf16[128,1024]{1,0:T(8,128)(2,1)S(1)}, u32[]{:S(2)}, u32[]{:S(2)}) collective-permute-start(bf16[128,1024]{1,0:T(8,128)(2,1)} %get-tuple-element.448), channel_id=1, source_target_pairs={{0,2},{1,3},{2,0},{3,1},{4,6},{5,7},{6,4},{7,5},{8,10},{9,11},{10,... | collective-permute-start | bytes 786440 | tf_op jit(solution)/shard_map/ppermute | solution.py:37
  318.4 26.9 %collective-permute-start.56 = (bf16[128,1024]{1,0:T(8,128)(2,1)}, bf16[128,1024]{1,0:T(8,128)(2,1)}, u32[]{:S(2)}, u32[]{:S(2)}) collective-permute-start(bf16[128,1024]{1,0:T(8,128)(2,1)} %get-tuple-element.449), channel_id=1, source_target_pairs={{0,1},{1,0},{2,3},{3,2},{4,5},{5,4},{6,7},{7,6},{8,9},{9,8},{10,11... | collective-permute-start | bytes 786440 | tf_op jit(solution)/shard_map/ppermute | solution.py:37
  351.5 16.0 %collective-permute-start.58 = (bf16[256,1024]{1,0:T(8,128)(2,1)S(1)}, bf16[256,1024]{1,0:T(8,128)(2,1)S(1)}, u32[]{:S(2)}, u32[]{:S(2)}) collective-permute-start(bf16[256,1024]{1,0:T(8,128)(2,1)S(1)} %get-tuple-element.463), channel_id=1, source_target_pairs={{0,1},{1,0},{2,3},{3,2},{4,5},{5,4},{6,7},{7,6},{8,9},{9,8},{10,11... | collective-permute-start | bytes 1572872 | tf_op jit(solution)/shard_map/ppermute | solution.py:37
  351.9 15.6 %collective-permute-start.59 = (bf16[256,1024]{1,0:T(8,128)(2,1)S(1)}, bf16[256,1024]{1,0:T(8,128)(2,1)S(1)}, u32[]{:S(2)}, u32[]{:S(2)}) collective-permute-start(bf16[256,1024]{1,0:T(8,128)(2,1)S(1)} %get-tuple-element.464), channel_id=1, source_target_pairs={{0,2},{1,3},{2,0},{3,1},{4,6},{5,7},{6,4},{7,5},{8,10},{9,11},{10,... | collective-permute-start | bytes 1572872 | tf_op jit(solution)/shard_map/ppermute | solution.py:37
  354.0 12.5 %collective-permute-start.57 = (bf16[256,1024]{1,0:T(8,128)(2,1)S(1)}, bf16[256,1024]{1,0:T(8,128)(2,1)S(1)}, u32[]{:S(2)}, u32[]{:S(2)}) collective-permute-start(bf16[256,1024]{1,0:T(8,128)(2,1)S(1)} %get-tuple-element.457), channel_id=1, source_target_pairs={{0,16},{8,24},{16,0},{24,8},{1,17},{9,25},{17,1},{25,9},{2,18},{10... | collective-permute-start | bytes 1572872 | tf_op jit(solution)/shard_map/ppermute | solution.py:37
  376.9 13.9 %collective-permute-start.63 = (bf16[512,384]{1,0:T(8,128)(2,1)S(1)}, bf16[512,384]{1,0:T(8,128)(2,1)S(1)}, u32[]{:S(2)}, u32[]{:S(2)}) collective-permute-start(bf16[512,384]{1,0:T(8,128)(2,1)S(1)} %get-tuple-element.607), channel_id=1, source_target_pairs={{0,0},{4,1},{1,2},{5,3},{2,4},{6,5},{3,6},{7,7},{8,8},{12,9},{9,10... | collective-permute-start | bytes 1179656 | tf_op jit(solution)/shard_map/ppermute | solution.py:1138
  377.6 22.4 %collective-permute-start.64 = (bf16[512,384]{1,0:T(8,128)(2,1)S(1)}, bf16[512,384]{1,0:T(8,128)(2,1)S(1)}, u32[]{:S(2)}, u32[]{:S(2)}) collective-permute-start(bf16[512,384]{1,0:T(8,128)(2,1)S(1)} %get-tuple-element.608), channel_id=1, source_target_pairs={{4,0},{0,1},{5,2},{1,3},{6,4},{2,5},{7,6},{3,7},{12,8},{8,9},{13,1... | collective-permute-start | bytes 1179656 | tf_op jit(solution)/shard_map/ppermute | solution.py:1138
  383.4 18.0 %collective-permute-start.68 = (bf16[256,1024]{1,0:T(8,128)(2,1)S(1)}, bf16[256,1024]{1,0:T(8,128)(2,1)S(1)}, u32[]{:S(2)}, u32[]{:S(2)}) collective-permute-start(bf16[256,1024]{1,0:T(8,128)(2,1)S(1)} %get-tuple-element.496), channel_id=1, source_target_pairs={{0,16},{8,24},{16,0},{24,8},{1,17},{9,25},{17,1},{25,9},{2,18},{10... | collective-permute-start | bytes 1572872 | tf_op jit(solution)/shard_map/ppermute | solution.py:37
  388.5 14.0 %collective-permute-start.69 = (bf16[1024,256]{0,1:T(8,128)(2,1)}, bf16[1024,256]{0,1:T(8,128)(2,1)}, u32[]{:S(2)}, u32[]{:S(2)}) collective-permute-start(bf16[1024,256]{0,1:T(8,128)(2,1)} %bitcast.28), channel_id=1, source_target_pairs={{0,8},{8,0},{16,24},{24,16},{1,9},{9,1},{17,25},{25,17},{2,10},{10... | collective-permute-start | bytes 1572872 | tf_op jit(solution)/shard_map/ppermute | solution.py:37
  402.8 7.7 %collective-permute-start.73 = (bf16[64,1024]{1,0:T(8,128)(2,1)}, bf16[64,1024]{1,0:T(8,128)(2,1)}, u32[]{:S(2)}, u32[]{:S(2)}) collective-permute-start(bf16[64,1024]{1,0:T(8,128)(2,1)} %add_add_fusion), channel_id=1, source_target_pairs={{0,2},{1,3},{2,0},{3,1},{4,6},{5,7},{6,4},{7,5},{8,10},{9,11},{10,... | collective-permute-start | bytes 393224 | tf_op jit(solution)/shard_map/ppermute | solution.py:37
  403.2 8.2 %collective-permute-start.74 = (bf16[64,1024]{1,0:T(8,128)(2,1)}, bf16[64,1024]{1,0:T(8,128)(2,1)}, u32[]{:S(2)}, u32[]{:S(2)}) collective-permute-start(bf16[64,1024]{1,0:T(8,128)(2,1)} %add_add_fusion), channel_id=1, source_target_pairs={{0,3},{1,2},{2,1},{3,0},{4,7},{5,6},{6,5},{7,4},{8,11},{9,10},{10,... | collective-permute-start | bytes 393224 | tf_op jit(solution)/shard_map/ppermute | solution.py:37
  406.0 18.0 %collective-permute-start.78 = (bf16[256,1024]{1,0:T(8,128)(2,1)}, bf16[256,1024]{1,0:T(8,128)(2,1)S(1)}, u32[]{:S(2)}, u32[]{:S(2)}) collective-permute-start(bf16[256,1024]{1,0:T(8,128)(2,1)} %add_convert_fusion.2), channel_id=1, source_target_pairs={{0,8},{8,0},{16,24},{24,16},{1,9},{9,1},{17,25},{25,17},{2,10},{10... | collective-permute-start | bytes 1572872 | tf_op jit(solution)/shard_map/ppermute | solution.py:37
  406.0 10.5 %collective-permute-start.77 = (bf16[32,1024]{1,0:T(8,128)(2,1)}, bf16[32,1024]{1,0:T(8,128)(2,1)S(1)}, u32[]{:S(2)}, u32[]{:S(2)}) collective-permute-start(bf16[32,1024]{1,0:T(8,128)(2,1)} %reduce-scatter.2.cloned.1.call-done), channel_id=1, source_target_pairs={{0,16},{8,24},{16,0},{24,8},{1,17},{9,25},{17,1},{25,9},{2,18},{10... | collective-permute-start | bytes 196616 | tf_op jit(solution)/shard_map/ppermute | solution.py:37
  409.1 13.7 %collective-permute-start.76 = (bf16[512,384]{1,0:T(8,128)(2,1)S(1)}, bf16[512,384]{1,0:T(8,128)(2,1)S(1)}, u32[]{:S(2)}, u32[]{:S(2)}) collective-permute-start(bf16[512,384]{1,0:T(8,128)(2,1)S(1)} %add_convert_fusion.5), channel_id=1, source_target_pairs={{0,16},{8,24},{16,0},{24,8},{1,17},{9,25},{17,1},{25,9},{2,18},{10... | collective-permute-start | bytes 1179656 | tf_op jit(solution)/shard_map/ppermute | solution.py:37
  410.5 15.8 %collective-permute-start.70 = (bf16[256,1024]{1,0:T(8,128)(2,1)S(1)}, bf16[256,1024]{1,0:T(8,128)(2,1)S(1)}, u32[]{:S(2)}, u32[]{:S(2)}) collective-permute-start(bf16[256,1024]{1,0:T(8,128)(2,1)S(1)} %get-tuple-element.504), channel_id=1, source_target_pairs={{0,1},{1,0},{2,3},{3,2},{4,5},{5,4},{6,7},{7,6},{8,9},{9,8},{10,11... | collective-permute-start | bytes 1572872 | tf_op jit(solution)/shard_map/ppermute | solution.py:37
  416.5 12.9 %collective-permute-start.71 = (bf16[256,1024]{1,0:T(8,128)(2,1)S(1)}, bf16[256,1024]{1,0:T(8,128)(2,1)S(1)}, u32[]{:S(2)}, u32[]{:S(2)}) collective-permute-start(bf16[256,1024]{1,0:T(8,128)(2,1)S(1)} %get-tuple-element.505), channel_id=1, source_target_pairs={{0,2},{1,3},{2,0},{3,1},{4,6},{5,7},{6,4},{7,5},{8,10},{9,11},{10,... | collective-permute-start | bytes 1572872 | tf_op jit(solution)/shard_map/ppermute | solution.py:37
  425.8 8.5 %collective-permute-start.80 = (bf16[64,1024]{1,0:T(8,128)(2,1)}, bf16[64,1024]{1,0:T(8,128)(2,1)}, u32[]{:S(2)}, u32[]{:S(2)}) collective-permute-start(bf16[64,1024]{1,0:T(8,128)(2,1)} %maximum_select_fusion.4), channel_id=1, source_target_pairs={{0,8},{8,0},{16,24},{24,16},{1,9},{9,1},{17,25},{25,17},{2,10},{10... | collective-permute-start | bytes 393224 | tf_op jit(solution)/shard_map/ppermute | solution.py:37
  425.8 10.4 %collective-permute-start.79 = (bf16[512,384]{1,0:T(8,128)(2,1)S(1)}, bf16[512,384]{1,0:T(8,128)(2,1)}, u32[]{:S(2)}, u32[]{:S(2)}) collective-permute-start(bf16[512,384]{1,0:T(8,128)(2,1)S(1)} %add_convert_fusion.4), channel_id=1, source_target_pairs={{0,8},{8,0},{16,24},{24,16},{1,9},{9,1},{17,25},{25,17},{2,10},{10... | collective-permute-start | bytes 1179656 | tf_op jit(solution)/shard_map/ppermute | solution.py:37
  (144 other events, 909.2 us)
Sparse Core Ops, SparseCore 0:
  46.9 44.0 all-gather.2
  322.5 61.5 reduce-scatter.1

commit v5 on v4

--- a/solution.py
+++ b/solution.py
@@ -590,7 +590,7 @@
 
 def ff_grad(d_upper, hidden, first_low, d_fed, place, adds, ff_half, cuts=(), joined=False, megabytes=24):
     rows, width = first_low.shape
-    cols = width // 2
+    cols = width
     count = len(adds)
     total = 2 * ff_half
     splits = (0, *cuts, total)
@@ -606,13 +606,31 @@
     return pl.pallas_call(
         functools.partial(ff_grad_kernel, ff_half, spans, splits, int(joined)),
         out_shape=tuple(jax.ShapeDtypeStruct((height, width), BF) for height in heights),
-        grid=(2,),
+        grid=(1,),
         in_specs=[lanes, lanes, column, column] + [lane_block(height, at) for _, height, _, at in flat],
         out_specs=tuple(lane_block(height) for height in heights),
         compiler_params=params(megabytes),
         cost_estimate=cost(1, 1),
         name="ff_grad",
     )(first_low, d_fed, d_upper, hidden, *[array for _, _, array, _ in flat])
+
+
+def turn_kernel(in_ref, out_ref):
+    out_ref[...] = in_ref[...].T
+
+
+def turned(values):
+    height, width = values.shape
+    return pl.pallas_call(
+        turn_kernel,
+        out_shape=jax.ShapeDtypeStruct((width, height), values.dtype),
+        grid=(1,),
+        in_specs=[whole_block(height, width)],
+        out_specs=whole_block(width, height),
+        compiler_params=params(),
+        cost_estimate=cost(1, 1),
+        name="turned",
+    )(values)
 
 
 def combine_kernel(spans, *refs):
@@ -628,7 +646,7 @@
 
 def combine(*sums):
     height, width = sums[0][0][1].shape
-    split = 4
+    split = 2
     rows = height // split
     spans = tuple(tuple((low // rows, (low + array.shape[0]) // rows) for low, array in terms) for terms in sums)
 
@@ -1146,7 +1164,7 @@
     ).astype(BF)
     small = over_bits(small, "dp", 1, dp_count)
     ff_down = over_dp(ff_down)
-    ff_up = ff_up.T
+    ff_up = turned(ff_up)
     up_other = swap(ff_up, "dp", 1)
     if stage[last] == 0:
         partial[last] = side_parcels(last, partial[last])
@@ -1164,7 +1182,9 @@
     small = over_bits(small, "tensor", 1, min(4, count))
     grad_w_up = by_core(ff_up, up_other, 1).astype(F32)
     grad_w_down = by_core(ff_down, down_other).astype(F32)
-    joint_sum, out_sum, grad_w_up, grad_w_down = fence(joint_sum, out_sum, grad_w_up, grad_w_down)
+    joint_sum, partial[last], out_sum, grad_w_up, grad_w_down = fence(
+        joint_sum, partial[last], out_sum, grad_w_up, grad_w_down
+    )
     out_other = swap(out_sum, "dp", 1)
     grad_w_out = by_core(out_sum, out_other).astype(F32)
     joint_other = swap(joint_sum, "dp", 1)
@@ -1173,7 +1193,10 @@
     late = late[:, :width] + late[:, width:]
     late = jnp.concatenate([jnp.zeros((row_count * last, width), F32), late], axis=0)
     grad_rows = jnp.where(jnp.concatenate(replaced_list)[:, None], 0.0, grad_rows + late)
-    grad_joint = by_core(joint_sum, joint_other).astype(F32)
+    grad_query, grad_key, grad_value = (
+        by_core(joint_sum[:, at : at + local_width], joint_other[:, at : at + local_width]).astype(F32)
+        for at in (0, local_width, 2 * local_width)
+    )
     grad_b_query, grad_b_value = (
         lax.dynamic_slice_in_dim(small[vocab_count + i], rank * local_width, local_width, 0) for i in range(2)
     )
@@ -1187,10 +1210,10 @@
         layer_out.reshape(micro_count, row_count, width),
         grad_rows.reshape(micro_count, row_count, width),
         small[:vocab_count],
-        grad_joint[:, :local_width],
+        grad_query,
         grad_b_query,
-        grad_joint[:, local_width : 2 * local_width],
-        grad_joint[:, 2 * local_width :],
+        grad_key,
+        grad_value,
         grad_b_value,
         grad_w_out,
         grad_b_out,

time: 454 us -> 445 us (0.980)
  Pallas kernels: 147 us -> 141 us
    unnamed x258 -> x255, local copies, waits for them, and re-layouts: 35.4 us -> 32.9 us
  transfers between devices with their start and end apart: 83 -> 83, of which waited for: 29 -> 28; matrix products, arithmetic and copies ran while one was open for 14% -> 13% of each run, Pallas kernels for 29% -> 29%
where the time goes in v5:
time: 445 us; the launch traced here: 437 us
  Pallas kernels  141 us (32%)
  waiting for transfers between devices  102 us (23%)
  starting transfers between devices  81.9 us (18%)
  local copies, waits for them, and re-layouts  50.1 us (11%)
  other arithmetic  29.2 us (7%)
  matrix products  16.7 us (4%)
  between operations  16.4 us (4%)
    ppermute x59, waiting for transfers between devices, swap(): return lax.ppermute(values, axis, [(i, i ^ bit) for i in range(count)])  66.7 us
    ppermute x59, starting transfers between devices, swap(): return lax.ppermute(values, axis, [(i, i ^ bit) for i in range(count)])  52.7 us
    unnamed x255, local copies, waits for them, and re-layouts  32.9 us
    pallas_call x4, Pallas kernels, attn_backward(): pl.pallas_call(functools.partial(attn_backward_kernel, parts), out_shape=...  26.5 us
    pallas_call x5, Pallas kernels, ff_forward(): pl.pallas_call(functools.partial(ff_forward_kernel, ff_half, count), out_...  22 us
    pallas_call x10, Pallas kernels, ff_grad(): pl.pallas_call(functools.partial(ff_grad_kernel, ff_half, spans, splits,...  18.9 us
    pallas_call x2, Pallas kernels, attn_forward(): pl.pallas_call(attn_forward_kernel, out_shape=(shape,) * parts + (jax.Sha...  17.9 us
    ppermute x9, waiting for transfers between devices, forward(): return lax.ppermute(values, 'tensor', ring_fw)  17.8 us
  transfers between devices with their start and end apart: 83, of which 28 were waited for; matrix products, arithmetic and copies ran while one was open for 13% of the time, Pallas kernels for 29%

profile of v5, /device:TPU:0, one launch (start us, length us, event | category | flops | bytes accessed | tf_op | source)
XLA Modules:
  0.0 436.8 jit_solution(23841170486855999)
XLA Ops:
  10.0 3.0 collective-permute-start
  18.8 2.9 collective-permute-start.3
  25.1 2.6 constant_dynamic-slice_fusion.13
  31.8 2.6 fusion.16
  36.6 6.9 %collective-permute-start.8 = (bf16[128,1024]{1,0:T(8,128)(2,1)}, bf16[128,1024]{1,0:T(8,128)(2,1)S(1)}, u32[]{:S(2)}, u32[]{:S(2)}) collective-permute-start(bf16[128,1024]{1,0:T(8,128)(2,1)} %slice.168), channel_id=1, source_target_pairs={{0,2},{1,3},{2,0},{3,1},{4,6},{5,7},{6,4},{7,5},{8,10},{9,11},{10,... | collective-permute-start | bytes 786440 | tf_op jit(solution)/shard_map/ppermute | solution.py:37
  47.0 2.1 collective-permute-start.7
  49.2 2.0 collective-permute-start.4
  51.2 2.0 assemble.1
  54.7 3.9 project.2
  58.6 8.9 %attn_forward.2 = (bf16[256,256]{1,0:T(8,128)(2,1)S(1)}, bf16[256,256]{1,0:T(8,128)(2,1)S(1)}, bf16[256,256]{1,0:T(8,128)(2,1)S(1)}, bf16[256,256]{1,0:T(8,128)(...) custom-call(bf16[1024,768]{1,0:T(8,128)(2,1)S(1)} %get-tuple-element.414.q_ref.k_ref.v_ref, ...), custom_call_target="tpu_custom_call" | custom-call | flops 4294967296 | bytes 2359296 | tf_op jit(solution)/shard_map/attn_forward/pallas_call | solution.py:180
  67.6 13.1 %collective-permute-done.4.refs_1_ = bf16[256,1024]{1,0:T(8,128)(2,1)S(1)} collective-permute-done((bf16[256,1024]{1,0:T(8,128)(2,1)S(1)}, bf16[256,1024]{1,0:T(8,128)(2,1)S(1)}, u32[]{:S(2)}, u32[]{:S(2)}) %collective-permute-start.4) | collective-permute-done | bytes 524320 | tf_op jit(solution)/shard_map/ppermute | solution.py:37
  80.8 2.3 collective-permute-start.17
  83.1 1.8 collective-permute-start.18
  84.9 2.2 collective-permute-start.16
  87.3 6.1 %collective-permute-done.17.refs_3_ = bf16[128,1024]{1,0:T(8,128)(2,1)S(1)} collective-permute-done((bf16[128,1024]{1,0:T(8,128)(2,1)S(1)}, bf16[128,1024]{1,0:T(8,128)(2,1)S(1)}, u32[]{:S(2)}, u32[]{:S(2)}) %collective-permute-start.17) | collective-permute-done | bytes 262176 | tf_op jit(solution)/shard_map/ppermute | solution.py:37
  96.7 2.6 project.3
  99.3 8.9 %attn_forward.3 = (bf16[256,256]{1,0:T(8,128)(2,1)S(1)}, bf16[256,256]{1,0:T(8,128)(2,1)S(1)}, bf16[256,256]{1,0:T(8,128)(2,1)S(1)}, bf16[256,256]{1,0:T(8,128)(...) custom-call(bf16[1024,768]{1,0:T(8,128)(2,1)S(1)} %get-tuple-element.461.q_ref.k_ref.v_ref, ...), custom_call_target="tpu_custom_call" | custom-call | flops 4294967296 | bytes 2359296 | tf_op jit(solution)/shard_map/attn_forward/pallas_call | solution.py:180
  114.8 2.3 collective-permute-done.21.refs_7_
  118.7 2.4 collective-permute-done.22.refs_11_
  123.9 7.8 %attend.1 = (bf16[512,1024]{1,0:T(8,128)(2,1)}, f32[512,1024]{1,0:T(8,128)}, f32[512,128]{1,0:T(8,128)}, f32[512,1024]{1,0:T(8,128)}, bf16[512,1024]{1,0:T(8,128)(2,1)}, /*index=5*/bf16[1024,1024]{1,0:T(8,128)(2,1)}) custom-call(s32[5]{0:T(128)} %concatenate.111.at_ref, bf16[256,256]{1,0:T(8,128)(2,1)} %copy-done.76, bf16[256,256]{1,0:T(8,128)(2,1)} %copy-done.99, ...), custom_call_target="tpu_custom_call" | custom-call | flops 1073741824 | bytes 10485760 | tf_op jit(solution)/shard_map/attend/pallas_call | solution.py:332
  136.7 2.3 ff_forward.5
  140.8 5.6 %ff_forward.6 = (f32[512,1024]{1,0:T(8,128)S(1)}, bf16[512,1024]{1,0:T(8,128)(2,1)S(1)}, f32[512,1024]{1,0:T(8,128)S(1)}) custom-call(bf16[512,1024]{1,0:T(8,128)(2,1)S(1)} %copy-done.3, f32[512,1024]{1,0:T(8,128)S(1)} %get-tuple-element.317.init_ref, bf16[528,1024]{1,0:T(8,128)(2,1)} %pad_maximum_fusion.1.refs_0_, ...), custom_call_target="tpu_custom_call" | custom-call | flops 1 | bytes 1 | tf_op jit(solution)/shard_map/ff_forward/pallas_call | solution.py:499
  151.7 6.0 %ff_forward.7 = (f32[512,1024]{1,0:T(8,128)S(1)}, bf16[512,1024]{1,0:T(8,128)(2,1)S(1)}, f32[512,1024]{1,0:T(8,128)S(1)}) custom-call(bf16[512,1024]{1,0:T(8,128)(2,1)S(1)} %copy-done.3, f32[512,1024]{1,0:T(8,128)S(1)} %get-tuple-element.321.init_ref, bf16[528,1024]{1,0:T(8,128)(2,1)} %collective-permute-done.23.refs_0_, ...), custom_call_target="tpu_custom_call" | custom-call | flops 1 | bytes 1 | tf_op jit(solution)/shard_map/ff_forward/pallas_call | solution.py:499
  159.1 14.7 %collective-permute-done.28.refs_0_ = bf16[528,1024]{1,0:T(8,128)(2,1)S(1)} collective-permute-done((bf16[528,1024]{1,0:T(8,128)(2,1)}, bf16[528,1024]{1,0:T(8,128)(2,1)S(1)}, u32[]{:S(2)}, u32[]{:S(2)}) %collective-permute-start.28) | collective-permute-done | bytes 1081376 | tf_op jit(solution)/shard_map/ppermute | solution.py:814
  175.2 1.8 collective-permute-start.32
  178.9 4.6 %ff_forward.8 = (f32[512,1024]{1,0:T(8,128)S(1)}, bf16[512,1024]{1,0:T(8,128)(2,1)S(1)}, f32[512,1024]{1,0:T(8,128)S(1)}) custom-call(bf16[512,1024]{1,0:T(8,128)(2,1)S(1)} %copy-done.3, f32[512,1024]{1,0:T(8,128)S(1)} %get-tuple-element.325.init_ref, bf16[528,1024]{1,0:T(8,128)(2,1)S(1)} %collective-permute-done.28.refs_0_, ...), custom_call_target="tpu_custom_call" | custom-call | flops 1 | bytes 1 | tf_op jit(solution)/shard_map/ff_forward/pallas_call | solution.py:499
  187.4 3.5 collective-permute-done.33
  195.6 3.5 ff_forward.9
  199.1 3.0 second_norm.1
  202.1 3.0 ff_backward.5
  207.1 3.5 ff_backward.6
  215.3 4.6 %ff_backward.7 = (bf16[512,1024]{1,0:T(8,128)(2,1)S(1)}, f32[512,1024]{1,0:T(8,128)S(1)}, f32[16,256]{1,0:T(8,128)S(1)}) custom-call(bf16[512,1024]{1,0:T(8,128)(2,1)S(1)} %get-tuple-element.445.d_fed_ref.fed_ref, f32[512,1024]{1,0:T(8,128)S(1)} %get-tuple-element.359.init_ref, f32[512,1024]{1,0:T(8,128)S(1)} %copy-done.50, ...), custom_call_target="tpu_custom_call" | custom-call | flops 2147483648 | bytes 12582912 | tf_op jit(solution)/shard_map/ff_backward/pallas_call | solution.py:544
  219.9 2.7 ff_grad.14
  223.9 3.2 collective-permute-done.38.refs_3_
  227.0 1.8 collective-permute-done.39.refs_1_
  235.7 4.6 %ff_backward.8 = (bf16[512,1024]{1,0:T(8,128)(2,1)S(1)}, f32[512,1024]{1,0:T(8,128)S(1)}, f32[16,256]{1,0:T(8,128)S(1)}) custom-call(bf16[512,1024]{1,0:T(8,128)(2,1)S(1)} %get-tuple-element.445.d_fed_ref.fed_ref, f32[512,1024]{1,0:T(8,128)S(1)} %copy-done.52, f32[512,1024]{1,0:T(8,128)S(1)} %copy-done.48, bf16[528,1024]{1,0:T(8,128)(2,1)} %pad_maximum_fusion.1.refs_0_, ...), custom_call_target="tpu_custom_call" | custom-call | flops 2147483648 | bytes 12582912 | tf_op jit(solution)/shard_map/ff_backward/pallas_call | solution.py:544
  242.9 3.6 attend_back.1
  247.3 2.7 collective-permute-start.46
  251.4 2.6 ff_grad.16
  256.3 2.9 ff_grad.15
  259.2 8.1 %collective-permute-done.44 = bf16[512,256]{1,0:T(8,128)(2,1)S(1)} collective-permute-done((bf16[512,256]{1,0:T(8,128)(2,1)S(1)}, bf16[512,256]{1,0:T(8,128)(2,1)S(1)}, u32[]{:S(2)}, u32[]{:S(2)}) %collective-permute-start.44) | collective-permute-done | bytes 262176 | tf_op jit(solution)/shard_map/ppermute | solution.py:37
  267.5 2.9 combine.5
  273.9 2.0 fusion.2
  277.8 6.6 %attn_backward.4.refs_0_ = bf16[1024,768]{1,0:T(8,128)(2,1)S(1)} custom-call(bf16[1024,768]{1,0:T(8,128)(2,1)S(1)} %copy-done.14, bf16[1024,768]{1,0:T(8,128)(2,1)S(1)} %copy-done.14, bf16[1024,768]{1,0:T(8,128)(2,1)S(1)} %copy-done.14, f32[2,8,1024]{2,1,0:T(8,128)S(1)} %get-tuple-element.424.log_ref, ...), custom_call_target="tpu_custom_call" | custom-call | flops 1 | bytes 1 | tf_op jit(solution)/shard_map/attn_backward/pallas_call | solution.py:241
  284.4 2.0 fusion.42
  286.4 6.6 %attn_backward.5.d_ref.one_ref.two_ref.refs_0_ = bf16[1024,768]{1,0:T(8,128)(2,1)S(1)} custom-call(bf16[1024,768]{1,0:T(8,128)(2,1)S(1)} %copy-done.14, bf16[1024,768]{1,0:T(8,128)(2,1)S(1)} %copy-done.14, bf16[1024,768]{1,0:T(8,128)(2,1)S(1)} %copy-done.14, f32[2,8,1024]{2,1,0:T(8,128)S(1)} %get-tuple-element.424.log_ref, ...), custom_call_target="tpu_custom_call", output_to_operand_aliasing={{}: (6, {})} | custom-call | flops 1 | bytes 1 | tf_op jit(solution)/shard_map/attn_backward/pallas_call | solution.py:241
  294.2 1.8 ff_grad.18
  299.5 2.9 ff_grad.17
  302.4 2.7 combine.6
  320.6 6.6 %attn_backward.6.refs_0_ = bf16[1024,768]{1,0:T(8,128)(2,1)S(1)} custom-call(bf16[1024,768]{1,0:T(8,128)(2,1)S(1)} %copy-done.11, bf16[1024,768]{1,0:T(8,128)(2,1)S(1)} %copy-done.11, bf16[1024,768]{1,0:T(8,128)(2,1)S(1)} %copy-done.11, f32[2,8,1024]{2,1,0:T(8,128)S(1)} %get-tuple-element.448.log_ref, ...), custom_call_target="tpu_custom_call" | custom-call | flops 1 | bytes 1 | tf_op jit(solution)/shard_map/attn_backward/pallas_call | solution.py:241
  327.2 2.0 ff_grad.19.refs_0_
  329.2 11.8 %collective-permute-done.55.to_two_ref = bf16[128,1024]{1,0:T(8,128)(2,1)S(1)} collective-permute-done((bf16[128,1024]{1,0:T(8,128)(2,1)}, bf16[128,1024]{1,0:T(8,128)(2,1)S(1)}, u32[]{:S(2)}, u32[]{:S(2)}) %collective-permute-start.55) | collective-permute-done | bytes 262176 | tf_op jit(solution)/shard_map/ppermute | solution.py:37
  341.0 1.9 combine.7
  344.4 2.1 side_shares.2
  346.9 2.2 collective-permute-start.59
  350.3 6.6 %attn_backward.7.d_ref.one_ref.two_ref.refs_1_ = bf16[1024,768]{1,0:T(8,128)(2,1)S(1)} custom-call(bf16[1024,768]{1,0:T(8,128)(2,1)S(1)} %copy-done.12, bf16[1024,768]{1,0:T(8,128)(2,1)S(1)} %copy-done.12, bf16[1024,768]{1,0:T(8,128)(2,1)S(1)} %copy-done.12, f32[2,8,1024]{2,1,0:T(8,128)S(1)} %get-tuple-element.448.log_ref, ...), custom_call_target="tpu_custom_call", output_to_operand_aliasing={{}: (6, {})} | custom-call | flops 1 | bytes 1 | tf_op jit(solution)/shard_map/attn_backward/pallas_call | solution.py:241
  359.2 2.4 collective-permute-done.57
  368.8 2.0 collective-permute-done.61.to_two_ref
  371.9 4.5 %collective-permute-start.64 = (bf16[512,384]{1,0:T(8,128)(2,1)S(1)}, bf16[512,384]{1,0:T(8,128)(2,1)S(1)}, u32[]{:S(2)}, u32[]{:S(2)}) collective-permute-start(bf16[512,384]{1,0:T(8,128)(2,1)S(1)} %get-tuple-element.537), channel_id=1, source_target_pairs={{4,0},{0,1},{5,2},{1,3},{6,4},{2,5},{7,6},{3,7},{12,8},{8,9},{13,1... | collective-permute-start | bytes 1179656 | tf_op jit(solution)/shard_map/ppermute | solution.py:1156
  385.0 9.9 %collective-permute-done.64 = bf16[512,384]{1,0:T(8,128)(2,1)S(1)} collective-permute-done((bf16[512,384]{1,0:T(8,128)(2,1)S(1)}, bf16[512,384]{1,0:T(8,128)(2,1)S(1)}, u32[]{:S(2)}, u32[]{:S(2)}) %collective-permute-start.64) | collective-permute-done | bytes 393248 | tf_op jit(solution)/shard_map/ppermute | solution.py:1156
  397.6 2.6 collective-permute-start.77
  401.7 1.8 collective-permute-done.75
  408.0 2.8 fusion.7
  418.6 5.0 %collective-permute-done.72 = bf16[256,1024]{1,0:T(8,128)(2,1)S(1)} collective-permute-done((bf16[256,1024]{1,0:T(8,128)(2,1)S(1)}, bf16[256,1024]{1,0:T(8,128)(2,1)S(1)}, u32[]{:S(2)}, u32[]{:S(2)}) %collective-permute-start.72) | collective-permute-done | bytes 524320 | tf_op jit(solution)/shard_map/ppermute | solution.py:37
  (515 shorter events, 154.2 us)
Async XLA Ops:
  7.2 110.0 %all-gather.3.cloned.1.call-start = ((), (), s32[]{:S(2)}) async-start(), calls=%async_computation.2 | async-start | bytes 1179648 | tf_op jit(solution)/shard_map/all_gather | solution.py:880
  10.0 24.3 %collective-permute-start = (bf16[256,1024]{1,0:T(8,128)(2,1)S(1)}, bf16[256,1024]{1,0:T(8,128)(2,1)}, u32[]{:S(2)}, u32[]{:S(2)}) collective-permute-start(bf16[256,1024]{1,0:T(8,128)(2,1)S(1)} %fusion.3.refs_0_.refs_8_), channel_id=1, source_target_pairs={{0,1},{1,0},{2,3},{3,2},{4,5},{5,4},{6,7},{7,6},{8,9},{9,8},{10,11... | collective-permute-start | bytes 1572872 | tf_op jit(solution)/shard_map/ppermute | solution.py:37
  13.0 21.4 %collective-permute-start.1 = (bf16[256,1024]{1,0:T(8,128)(2,1)S(1)}, bf16[256,1024]{1,0:T(8,128)(2,1)}, u32[]{:S(2)}, u32[]{:S(2)}) collective-permute-start(bf16[256,1024]{1,0:T(8,128)(2,1)S(1)} %fusion.3.refs_0_.refs_8_), channel_id=1, source_target_pairs={{0,2},{1,3},{2,0},{3,1},{4,6},{5,7},{6,4},{7,5},{8,10},{9,11},{10,... | collective-permute-start | bytes 1572872 | tf_op jit(solution)/shard_map/ppermute | solution.py:37
  17.2 17.2 %collective-permute-start.2 = (bf16[528,384]{1,0:T(8,128)(2,1)}, bf16[528,384]{1,0:T(8,128)(2,1)S(1)}, u32[]{:S(2)}, u32[]{:S(2)}) collective-permute-start(bf16[528,384]{1,0:T(8,128)(2,1)} %fusion.17), channel_id=1, source_target_pairs={{0,0},{1,4},{2,1},{3,5},{4,2},{5,6},{6,3},{7,7},{8,8},{9,12},{10,9... | collective-permute-start | bytes 1216520 | tf_op jit(solution)/shard_map/ppermute | solution.py:874
  18.8 15.5 %collective-permute-start.3 = (bf16[528,384]{1,0:T(8,128)(2,1)}, bf16[528,384]{1,0:T(8,128)(2,1)}, u32[]{:S(2)}, u32[]{:S(2)}) collective-permute-start(bf16[528,384]{1,0:T(8,128)(2,1)} %fusion.17), channel_id=1, source_target_pairs={{0,4},{1,0},{2,5},{3,1},{4,6},{5,2},{6,7},{7,3},{8,12},{9,8},{10,1... | collective-permute-start | bytes 1216520 | tf_op jit(solution)/shard_map/ppermute | solution.py:874
  34.4 12.6 %collective-permute-start.10 = (bf16[528,384]{1,0:T(8,128)(2,1)S(1)}, bf16[528,384]{1,0:T(8,128)(2,1)S(1)}, u32[]{:S(2)}, u32[]{:S(2)}) collective-permute-start(bf16[528,384]{1,0:T(8,128)(2,1)S(1)} %collective-permute-done.2.refs_0_), channel_id=1, source_target_pairs={{0,8},{8,0},{16,24},{24,16},{1,9},{9,1},{17,25},{25,17},{2,10},{10... | collective-permute-start | bytes 1216520 | tf_op jit(solution)/shard_map/ppermute | solution.py:37
  34.4 14.8 %collective-permute-start.11 = (bf16[528,384]{1,0:T(8,128)(2,1)}, bf16[528,384]{1,0:T(8,128)(2,1)}, u32[]{:S(2)}, u32[]{:S(2)}) collective-permute-start(bf16[528,384]{1,0:T(8,128)(2,1)} %collective-permute-done.3.refs_1_), channel_id=1, source_target_pairs={{0,8},{8,0},{16,24},{24,16},{1,9},{9,1},{17,25},{25,17},{2,10},{10... | collective-permute-start | bytes 1216520 | tf_op jit(solution)/shard_map/ppermute | solution.py:37
  36.6 16.6 %collective-permute-start.8 = (bf16[128,1024]{1,0:T(8,128)(2,1)}, bf16[128,1024]{1,0:T(8,128)(2,1)S(1)}, u32[]{:S(2)}, u32[]{:S(2)}) collective-permute-start(bf16[128,1024]{1,0:T(8,128)(2,1)} %slice.168), channel_id=1, source_target_pairs={{0,2},{1,3},{2,0},{3,1},{4,6},{5,7},{6,4},{7,5},{8,10},{9,11},{10,... | collective-permute-start | bytes 786440 | tf_op jit(solution)/shard_map/ppermute | solution.py:37
  45.2 9.5 %collective-permute-start.9 = (bf16[128,1024]{1,0:T(8,128)(2,1)}, bf16[128,1024]{1,0:T(8,128)(2,1)}, u32[]{:S(2)}, u32[]{:S(2)}) collective-permute-start(bf16[128,1024]{1,0:T(8,128)(2,1)} %slice.169), channel_id=1, source_target_pairs={{0,1},{1,0},{2,3},{3,2},{4,5},{5,4},{6,7},{7,6},{8,9},{9,8},{10,11... | collective-permute-start | bytes 786440 | tf_op jit(solution)/shard_map/ppermute | solution.py:37
  46.8 350.0 %reduce-scatter.2.cloned.1.call-start = ((), (), s32[]{:S(2)}) async-start(), calls=%async_computation.1 | async-start | bytes 589824 | tf_op jit(solution)/shard_map/reduce_scatter | solution.py:1056
  46.9 33.8 %collective-permute-start.6 = (bf16[272,1024]{1,0:T(8,128)(2,1)S(1)}, bf16[272,1024]{1,0:T(8,128)(2,1)S(1)}, u32[]{:S(2)}, u32[]{:S(2)}) collective-permute-start(bf16[272,1024]{1,0:T(8,128)(2,1)S(1)} %slice.167), channel_id=1, source_target_pairs={{0,2},{2,4},{4,6},{6,7},{7,5},{5,3},{3,1},{1,0},{8,10},{10,12},{12... | collective-permute-start | bytes 1671176 | tf_op jit(solution)/shard_map/ppermute | solution.py:814
  47.0 33.7 %collective-permute-start.7 = (bf16[272,1024]{1,0:T(8,128)(2,1)S(1)}, bf16[272,1024]{1,0:T(8,128)(2,1)S(1)}, u32[]{:S(2)}, u32[]{:S(2)}) collective-permute-start(bf16[272,1024]{1,0:T(8,128)(2,1)S(1)} %slice.167), channel_id=1, source_target_pairs={{2,0},{4,2},{6,4},{7,6},{5,7},{3,5},{1,3},{0,1},{10,8},{12,10},{14... | collective-permute-start | bytes 1671176 | tf_op jit(solution)/shard_map/ppermute | solution.py:817
  49.2 31.5 %collective-permute-start.4 = (bf16[256,1024]{1,0:T(8,128)(2,1)S(1)}, bf16[256,1024]{1,0:T(8,128)(2,1)S(1)}, u32[]{:S(2)}, u32[]{:S(2)}) collective-permute-start(bf16[256,1024]{1,0:T(8,128)(2,1)S(1)} %copy-done.72), channel_id=1, source_target_pairs={{0,1},{1,0},{2,3},{3,2},{4,5},{5,4},{6,7},{7,6},{8,9},{9,8},{10,11... | collective-permute-start | bytes 1572872 | tf_op jit(solution)/shard_map/ppermute | solution.py:37
  53.2 27.5 %collective-permute-start.5 = (bf16[256,1024]{1,0:T(8,128)(2,1)S(1)}, bf16[256,1024]{1,0:T(8,128)(2,1)S(1)}, u32[]{:S(2)}, u32[]{:S(2)}) collective-permute-start(bf16[256,1024]{1,0:T(8,128)(2,1)S(1)} %copy-done.72), channel_id=1, source_target_pairs={{0,2},{1,3},{2,0},{3,1},{4,6},{5,7},{6,4},{7,5},{8,10},{9,11},{10,... | collective-permute-start | bytes 1572872 | tf_op jit(solution)/shard_map/ppermute | solution.py:37
  80.8 12.6 %collective-permute-start.17 = (bf16[128,1024]{1,0:T(8,128)(2,1)S(1)}, bf16[128,1024]{1,0:T(8,128)(2,1)S(1)}, u32[]{:S(2)}, u32[]{:S(2)}) collective-permute-start(bf16[128,1024]{1,0:T(8,128)(2,1)S(1)} %slice.171), channel_id=1, source_target_pairs={{0,2},{1,3},{2,0},{3,1},{4,6},{5,7},{6,4},{7,5},{8,10},{9,11},{10,... | collective-permute-start | bytes 786440 | tf_op jit(solution)/shard_map/ppermute | solution.py:37
  83.1 11.9 %collective-permute-start.18 = (bf16[128,1024]{1,0:T(8,128)(2,1)S(1)}, bf16[128,1024]{1,0:T(8,128)(2,1)S(1)}, u32[]{:S(2)}, u32[]{:S(2)}) collective-permute-start(bf16[128,1024]{1,0:T(8,128)(2,1)S(1)} %slice.172), channel_id=1, source_target_pairs={{0,1},{1,0},{2,3},{3,2},{4,5},{5,4},{6,7},{7,6},{8,9},{9,8},{10,11... | collective-permute-start | bytes 786440 | tf_op jit(solution)/shard_map/ppermute | solution.py:37
  84.9 23.4 %collective-permute-start.15 = (bf16[256,1024]{1,0:T(8,128)(2,1)S(1)}, bf16[256,1024]{1,0:T(8,128)(2,1)S(1)}, u32[]{:S(2)}, u32[]{:S(2)}) collective-permute-start(bf16[256,1024]{1,0:T(8,128)(2,1)S(1)} %slice.170), channel_id=1, source_target_pairs={{0,2},{2,4},{4,6},{6,7},{7,5},{5,3},{3,1},{1,0},{8,10},{10,12},{12... | collective-permute-start | bytes 1572872 | tf_op jit(solution)/shard_map/ppermute | solution.py:814
  84.9 23.4 %collective-permute-start.16 = (bf16[256,1024]{1,0:T(8,128)(2,1)S(1)}, bf16[256,1024]{1,0:T(8,128)(2,1)S(1)}, u32[]{:S(2)}, u32[]{:S(2)}) collective-permute-start(bf16[256,1024]{1,0:T(8,128)(2,1)S(1)} %slice.170), channel_id=1, source_target_pairs={{2,0},{4,2},{6,4},{7,6},{5,7},{3,5},{1,3},{0,1},{10,8},{12,10},{14... | collective-permute-start | bytes 1572872 | tf_op jit(solution)/shard_map/ppermute | solution.py:817
  87.0 24.3 %collective-permute-start.12 = (bf16[256,256]{1,0:T(8,128)(2,1)S(1)}, bf16[256,256]{1,0:T(8,128)(2,1)S(1)}, u32[]{:S(2)}, u32[]{:S(2)}) collective-permute-start(bf16[256,256]{1,0:T(8,128)(2,1)S(1)} %get-tuple-element.284), channel_id=1, source_target_pairs={{0,1},{1,0},{2,3},{3,2},{4,5},{5,4},{6,7},{7,6},{8,9},{9,8},{10,11... | collective-permute-start | bytes 393224 | tf_op jit(solution)/shard_map/ppermute | solution.py:37
  93.4 20.6 %collective-permute-start.13 = (bf16[256,256]{1,0:T(8,128)(2,1)S(1)}, bf16[256,256]{1,0:T(8,128)(2,1)S(1)}, u32[]{:S(2)}, u32[]{:S(2)}) collective-permute-start(bf16[256,256]{1,0:T(8,128)(2,1)S(1)} %get-tuple-element.285), channel_id=1, source_target_pairs={{0,2},{1,3},{2,0},{3,1},{4,6},{5,7},{6,4},{7,5},{8,10},{9,11},{10,... | collective-permute-start | bytes 393224 | tf_op jit(solution)/shard_map/ppermute | solution.py:37
  94.9 19.1 %collective-permute-start.14 = (bf16[256,256]{1,0:T(8,128)(2,1)S(1)}, bf16[256,256]{1,0:T(8,128)(2,1)S(1)}, u32[]{:S(2)}, u32[]{:S(2)}) collective-permute-start(bf16[256,256]{1,0:T(8,128)(2,1)S(1)} %get-tuple-element.286), channel_id=1, source_target_pairs={{0,3},{1,2},{2,1},{3,0},{4,7},{5,6},{6,5},{7,4},{8,11},{9,10},{10,... | collective-permute-start | bytes 393224 | tf_op jit(solution)/shard_map/ppermute | solution.py:37
  117.2 14.4 %collective-permute-start.25 = (bf16[528,1024]{1,0:T(8,128)(2,1)S(1)}, bf16[528,1024]{1,0:T(8,128)(2,1)S(1)}, u32[]{:S(2)}, u32[]{:S(2)}) collective-permute-start(bf16[528,1024]{1,0:T(8,128)(2,1)S(1)} %fusion.6.refs_0_), channel_id=1, source_target_pairs={{0,8},{8,0},{16,24},{24,16},{1,9},{9,1},{17,25},{25,17},{2,10},{10... | collective-permute-start | bytes 3244040 | tf_op jit(solution)/shard_map/ppermute | solution.py:37
  117.7 23.1 %collective-permute-start.26 = (bf16[528,1024]{1,0:T(8,128)(2,1)}, bf16[528,1024]{1,0:T(8,128)(2,1)}, u32[]{:S(2)}, u32[]{:S(2)}) collective-permute-start(bf16[528,1024]{1,0:T(8,128)(2,1)} %pad_maximum_fusion.1.refs_0_), channel_id=1, source_target_pairs={{0,8},{8,0},{16,24},{24,16},{1,9},{9,1},{17,25},{25,17},{2,10},{10... | collective-permute-start | bytes 3244040 | tf_op jit(solution)/shard_map/ppermute | solution.py:37
  117.8 23.0 %collective-permute-start.27 = (bf16[528,1024]{1,0:T(8,128)(2,1)}, bf16[528,1024]{1,0:T(8,128)(2,1)}, u32[]{:S(2)}, u32[]{:S(2)}) collective-permute-start(bf16[528,1024]{1,0:T(8,128)(2,1)} %pad_maximum_fusion.2.refs_1_), channel_id=1, source_target_pairs={{0,8},{8,0},{16,24},{24,16},{1,9},{9,1},{17,25},{25,17},{2,10},{10... | collective-permute-start | bytes 3244040 | tf_op jit(solution)/shard_map/ppermute | solution.py:37
  118.2 28.2 %collective-permute-start.23 = (bf16[528,1024]{1,0:T(8,128)(2,1)}, bf16[528,1024]{1,0:T(8,128)(2,1)}, u32[]{:S(2)}, u32[]{:S(2)}) collective-permute-start(bf16[528,1024]{1,0:T(8,128)(2,1)} %pad_maximum_fusion.1.refs_0_), channel_id=1, source_target_pairs={{0,2},{2,4},{4,6},{6,7},{7,5},{5,3},{3,1},{1,0},{8,10},{10,12},{12... | collective-permute-start | bytes 3244040 | tf_op jit(solution)/shard_map/ppermute | solution.py:814
  121.1 26.2 %collective-permute-start.24 = (bf16[528,1024]{1,0:T(8,128)(2,1)}, bf16[528,1024]{1,0:T(8,128)(2,1)}, u32[]{:S(2)}, u32[]{:S(2)}) collective-permute-start(bf16[528,1024]{1,0:T(8,128)(2,1)} %pad_maximum_fusion.2.refs_1_), channel_id=1, source_target_pairs={{2,0},{4,2},{6,4},{7,6},{5,7},{3,5},{1,3},{0,1},{10,8},{12,10},{14... | collective-permute-start | bytes 3244040 | tf_op jit(solution)/shard_map/ppermute | solution.py:817
  147.8 26.0 %collective-permute-start.28 = (bf16[528,1024]{1,0:T(8,128)(2,1)}, bf16[528,1024]{1,0:T(8,128)(2,1)S(1)}, u32[]{:S(2)}, u32[]{:S(2)}) collective-permute-start(bf16[528,1024]{1,0:T(8,128)(2,1)} %collective-permute-done.23.refs_0_), channel_id=1, source_target_pairs={{0,2},{2,4},{4,6},{6,7},{7,5},{5,3},{3,1},{1,0},{8,10},{10,12},{12... | collective-permute-start | bytes 3244040 | tf_op jit(solution)/shard_map/ppermute | solution.py:814
  149.0 25.7 %collective-permute-start.29 = (bf16[528,1024]{1,0:T(8,128)(2,1)}, bf16[528,1024]{1,0:T(8,128)(2,1)S(1)}, u32[]{:S(2)}, u32[]{:S(2)}) collective-permute-start(bf16[528,1024]{1,0:T(8,128)(2,1)} %collective-permute-done.24.refs_1_), channel_id=1, source_target_pairs={{2,0},{4,2},{6,4},{7,6},{5,7},{3,5},{1,3},{0,1},{10,8},{12,10},{14... | collective-permute-start | bytes 3244040 | tf_op jit(solution)/shard_map/ppermute | solution.py:817
  175.2 15.7 %collective-permute-start.32 = (bf16[272,1024]{1,0:T(8,128)(2,1)S(1)}, bf16[272,1024]{1,0:T(8,128)(2,1)S(1)}, u32[]{:S(2)}, u32[]{:S(2)}) collective-permute-start(bf16[272,1024]{1,0:T(8,128)(2,1)S(1)} %slice.173), channel_id=1, source_target_pairs={{0,2},{2,4},{4,6},{6,7},{7,5},{5,3},{3,1},{1,0},{8,10},{10,12},{12... | collective-permute-start | bytes 1671176 | tf_op jit(solution)/shard_map/ppermute | solution.py:814
  177.0 13.8 %collective-permute-start.33 = (bf16[256,1024]{1,0:T(8,128)(2,1)S(1)}, bf16[256,1024]{1,0:T(8,128)(2,1)S(1)}, u32[]{:S(2)}, u32[]{:S(2)}) collective-permute-start(bf16[256,1024]{1,0:T(8,128)(2,1)S(1)} %slice.174), channel_id=1, source_target_pairs={{2,0},{4,2},{6,4},{7,6},{5,7},{3,5},{1,3},{0,1},{10,8},{12,10},{14... | collective-permute-start | bytes 1572872 | tf_op jit(solution)/shard_map/ppermute | solution.py:817
  212.6 9.9 %collective-permute-start.40 = (bf16[1024,1024]{1,0:T(8,128)(2,1)S(1)}, bf16[1024,1024]{1,0:T(8,128)(2,1)S(1)}, u32[]{:S(2)}, u32[]{:S(2)}) collective-permute-start(bf16[1024,1024]{1,0:T(8,128)(2,1)S(1)} %ff_grad.12), channel_id=1, source_target_pairs={{0,8},{8,0},{16,24},{24,16},{1,9},{9,1},{17,25},{25,17},{2,10},{10... | collective-permute-start | bytes 6291464 | tf_op jit(solution)/shard_map/ppermute | solution.py:37
  212.8 14.2 %collective-permute-start.38 = (bf16[256,1024]{1,0:T(8,128)(2,1)S(1)}, bf16[256,1024]{1,0:T(8,128)(2,1)S(1)}, u32[]{:S(2)}, u32[]{:S(2)}) collective-permute-start(bf16[256,1024]{1,0:T(8,128)(2,1)S(1)} %get-tuple-element.355), channel_id=1, source_target_pairs={{0,2},{2,4},{4,6},{6,7},{7,5},{5,3},{3,1},{1,0},{8,10},{10,12},{12... | collective-permute-start | bytes 1572872 | tf_op jit(solution)/shard_map/ppermute | solution.py:814
  214.6 14.3 %collective-permute-start.39 = (bf16[256,1024]{1,0:T(8,128)(2,1)S(1)}, bf16[256,1024]{1,0:T(8,128)(2,1)S(1)}, u32[]{:S(2)}, u32[]{:S(2)}) collective-permute-start(bf16[256,1024]{1,0:T(8,128)(2,1)S(1)} %get-tuple-element.356), channel_id=1, source_target_pairs={{2,0},{4,2},{6,4},{7,6},{5,7},{3,5},{1,3},{0,1},{10,8},{12,10},{14... | collective-permute-start | bytes 1572872 | tf_op jit(solution)/shard_map/ppermute | solution.py:817
  230.4 16.1 %collective-permute-start.43 = (bf16[1024,1024]{1,0:T(8,128)(2,1)}, bf16[1024,1024]{1,0:T(8,128)(2,1)}, u32[]{:S(2)}, u32[]{:S(2)}) collective-permute-start(bf16[1024,1024]{1,0:T(8,128)(2,1)} %ff_grad.14), channel_id=1, source_target_pairs={{0,8},{8,0},{16,24},{24,16},{1,9},{9,1},{17,25},{25,17},{2,10},{10... | collective-permute-start | bytes 6291464 | tf_op jit(solution)/shard_map/ppermute | solution.py:37
  230.4 28.9 %collective-permute-start.41 = (bf16[512,1024]{1,0:T(8,128)(2,1)}, bf16[512,1024]{1,0:T(8,128)(2,1)}, u32[]{:S(2)}, u32[]{:S(2)}) collective-permute-start(bf16[512,1024]{1,0:T(8,128)(2,1)} %get-tuple-element.378), channel_id=1, source_target_pairs={{0,2},{2,4},{4,6},{6,7},{7,5},{5,3},{3,1},{1,0},{8,10},{10,12},{12... | collective-permute-start | bytes 3145736 | tf_op jit(solution)/shard_map/ppermute | solution.py:814
  231.0 28.2 %collective-permute-start.42 = (bf16[512,1024]{1,0:T(8,128)(2,1)}, bf16[512,1024]{1,0:T(8,128)(2,1)}, u32[]{:S(2)}, u32[]{:S(2)}) collective-permute-start(bf16[512,1024]{1,0:T(8,128)(2,1)} %get-tuple-element.379), channel_id=1, source_target_pairs={{2,0},{4,2},{6,4},{7,6},{5,7},{3,5},{1,3},{0,1},{10,8},{12,10},{14... | collective-permute-start | bytes 3145736 | tf_op jit(solution)/shard_map/ppermute | solution.py:817
  246.5 20.9 %collective-permute-start.44 = (bf16[512,256]{1,0:T(8,128)(2,1)S(1)}, bf16[512,256]{1,0:T(8,128)(2,1)S(1)}, u32[]{:S(2)}, u32[]{:S(2)}) collective-permute-start(bf16[512,256]{1,0:T(8,128)(2,1)S(1)} %get-tuple-element.400), channel_id=1, source_target_pairs={{0,1},{1,0},{2,3},{3,2},{4,5},{5,4},{6,7},{7,6},{8,9},{9,8},{10,11... | collective-permute-start | bytes 786440 | tf_op jit(solution)/shard_map/ppermute | solution.py:37
  246.9 20.5 %collective-permute-start.45 = (bf16[512,256]{1,0:T(8,128)(2,1)S(1)}, bf16[512,256]{1,0:T(8,128)(2,1)S(1)}, u32[]{:S(2)}, u32[]{:S(2)}) collective-permute-start(bf16[512,256]{1,0:T(8,128)(2,1)S(1)} %get-tuple-element.401), channel_id=1, source_target_pairs={{0,2},{1,3},{2,0},{3,1},{4,6},{5,7},{6,4},{7,5},{8,10},{9,11},{10,... | collective-permute-start | bytes 786440 | tf_op jit(solution)/shard_map/ppermute | solution.py:37
  247.3 20.1 %collective-permute-start.46 = (bf16[512,256]{1,0:T(8,128)(2,1)S(1)}, bf16[512,256]{1,0:T(8,128)(2,1)S(1)}, u32[]{:S(2)}, u32[]{:S(2)}) collective-permute-start(bf16[512,256]{1,0:T(8,128)(2,1)S(1)} %get-tuple-element.402), channel_id=1, source_target_pairs={{0,3},{1,2},{2,1},{3,0},{4,7},{5,6},{6,5},{7,4},{8,11},{9,10},{10,... | collective-permute-start | bytes 786440 | tf_op jit(solution)/shard_map/ppermute | solution.py:37
  270.4 26.6 %collective-permute-start.49 = (bf16[1024,1024]{1,0:T(8,128)(2,1)}, bf16[1024,1024]{1,0:T(8,128)(2,1)}, u32[]{:S(2)}, u32[]{:S(2)}) collective-permute-start(bf16[1024,1024]{1,0:T(8,128)(2,1)} %ff_grad.16), channel_id=1, source_target_pairs={{0,8},{8,0},{16,24},{24,16},{1,9},{9,1},{17,25},{25,17},{2,10},{10... | collective-permute-start | bytes 6291464 | tf_op jit(solution)/shard_map/ppermute | solution.py:37
  270.8 31.6 %collective-permute-start.47 = (bf16[512,1024]{1,0:T(8,128)(2,1)}, bf16[512,1024]{1,0:T(8,128)(2,1)}, u32[]{:S(2)}, u32[]{:S(2)}) collective-permute-start(bf16[512,1024]{1,0:T(8,128)(2,1)} %get-tuple-element.416), channel_id=1, source_target_pairs={{0,2},{2,4},{4,6},{6,7},{7,5},{5,3},{3,1},{1,0},{8,10},{10,12},{12... | collective-permute-start | bytes 3145736 | tf_op jit(solution)/shard_map/ppermute | solution.py:814
  272.2 30.2 %collective-permute-start.48 = (bf16[512,1024]{1,0:T(8,128)(2,1)}, bf16[512,1024]{1,0:T(8,128)(2,1)}, u32[]{:S(2)}, u32[]{:S(2)}) collective-permute-start(bf16[512,1024]{1,0:T(8,128)(2,1)} %get-tuple-element.417), channel_id=1, source_target_pairs={{2,0},{4,2},{6,4},{7,6},{5,7},{3,5},{1,3},{0,1},{10,8},{12,10},{14... | collective-permute-start | bytes 3145736 | tf_op jit(solution)/shard_map/ppermute | solution.py:817
  276.1 19.9 %collective-permute-start.51 = (bf16[256,1024]{1,0:T(8,128)(2,1)S(1)}, bf16[256,1024]{1,0:T(8,128)(2,1)S(1)}, u32[]{:S(2)}, u32[]{:S(2)}) collective-permute-start(bf16[256,1024]{1,0:T(8,128)(2,1)S(1)} %bitcast.83), channel_id=1, source_target_pairs={{0,16},{8,24},{16,0},{24,8},{1,17},{9,25},{17,1},{25,9},{2,18},{10... | collective-permute-start | bytes 1572872 | tf_op jit(solution)/shard_map/ppermute | solution.py:37
  305.1 22.1 %collective-permute-start.54 = (bf16[512,1024]{1,0:T(8,128)(2,1)}, bf16[512,1024]{1,0:T(8,128)(2,1)}, u32[]{:S(2)}, u32[]{:S(2)}) collective-permute-start(bf16[512,1024]{1,0:T(8,128)(2,1)} %ff_grad.18), channel_id=1, source_target_pairs={{0,8},{8,0},{16,24},{24,16},{1,9},{9,1},{17,25},{25,17},{2,10},{10... | collective-permute-start | bytes 3145736 | tf_op jit(solution)/shard_map/ppermute | solution.py:37
  305.1 35.9 %collective-permute-start.52 = (bf16[512,1024]{1,0:T(8,128)(2,1)}, bf16[512,1024]{1,0:T(8,128)(2,1)}, u32[]{:S(2)}, u32[]{:S(2)}) collective-permute-start(bf16[512,1024]{1,0:T(8,128)(2,1)} %get-tuple-element.443), channel_id=1, source_target_pairs={{0,2},{2,4},{4,6},{6,7},{7,5},{5,3},{3,1},{1,0},{8,10},{10,12},{12... | collective-permute-start | bytes 3145736 | tf_op jit(solution)/shard_map/ppermute | solution.py:814
  306.5 34.5 %collective-permute-start.53 = (bf16[512,1024]{1,0:T(8,128)(2,1)}, bf16[512,1024]{1,0:T(8,128)(2,1)}, u32[]{:S(2)}, u32[]{:S(2)}) collective-permute-start(bf16[512,1024]{1,0:T(8,128)(2,1)} %get-tuple-element.444), channel_id=1, source_target_pairs={{2,0},{4,2},{6,4},{7,6},{5,7},{3,5},{1,3},{0,1},{10,8},{12,10},{14... | collective-permute-start | bytes 3145736 | tf_op jit(solution)/shard_map/ppermute | solution.py:817
  312.7 28.3 %collective-permute-start.55 = (bf16[128,1024]{1,0:T(8,128)(2,1)}, bf16[128,1024]{1,0:T(8,128)(2,1)S(1)}, u32[]{:S(2)}, u32[]{:S(2)}) collective-permute-start(bf16[128,1024]{1,0:T(8,128)(2,1)} %get-tuple-element.450), channel_id=1, source_target_pairs={{0,2},{1,3},{2,0},{3,1},{4,6},{5,7},{6,4},{7,5},{8,10},{9,11},{10,... | collective-permute-start | bytes 786440 | tf_op jit(solution)/shard_map/ppermute | solution.py:37
  314.1 26.9 %collective-permute-start.56 = (bf16[128,1024]{1,0:T(8,128)(2,1)}, bf16[128,1024]{1,0:T(8,128)(2,1)}, u32[]{:S(2)}, u32[]{:S(2)}) collective-permute-start(bf16[128,1024]{1,0:T(8,128)(2,1)} %get-tuple-element.451), channel_id=1, source_target_pairs={{0,1},{1,0},{2,3},{3,2},{4,5},{5,4},{6,7},{7,6},{8,9},{9,8},{10,11... | collective-permute-start | bytes 786440 | tf_op jit(solution)/shard_map/ppermute | solution.py:37
  346.5 15.3 %collective-permute-start.58 = (bf16[256,1024]{1,0:T(8,128)(2,1)S(1)}, bf16[256,1024]{1,0:T(8,128)(2,1)S(1)}, u32[]{:S(2)}, u32[]{:S(2)}) collective-permute-start(bf16[256,1024]{1,0:T(8,128)(2,1)S(1)} %get-tuple-element.465), channel_id=1, source_target_pairs={{0,1},{1,0},{2,3},{3,2},{4,5},{5,4},{6,7},{7,6},{8,9},{9,8},{10,11... | collective-permute-start | bytes 1572872 | tf_op jit(solution)/shard_map/ppermute | solution.py:37
  346.9 14.9 %collective-permute-start.59 = (bf16[256,1024]{1,0:T(8,128)(2,1)S(1)}, bf16[256,1024]{1,0:T(8,128)(2,1)S(1)}, u32[]{:S(2)}, u32[]{:S(2)}) collective-permute-start(bf16[256,1024]{1,0:T(8,128)(2,1)S(1)} %get-tuple-element.466), channel_id=1, source_target_pairs={{0,2},{1,3},{2,0},{3,1},{4,6},{5,7},{6,4},{7,5},{8,10},{9,11},{10,... | collective-permute-start | bytes 1572872 | tf_op jit(solution)/shard_map/ppermute | solution.py:37
  349.1 12.5 %collective-permute-start.57 = (bf16[256,1024]{1,0:T(8,128)(2,1)S(1)}, bf16[256,1024]{1,0:T(8,128)(2,1)S(1)}, u32[]{:S(2)}, u32[]{:S(2)}) collective-permute-start(bf16[256,1024]{1,0:T(8,128)(2,1)S(1)} %get-tuple-element.459), channel_id=1, source_target_pairs={{0,16},{8,24},{16,0},{24,8},{1,17},{9,25},{17,1},{25,9},{2,18},{10... | collective-permute-start | bytes 1572872 | tf_op jit(solution)/shard_map/ppermute | solution.py:37
  363.7 7.1 %collective-permute-start.61 = (bf16[128,1024]{1,0:T(8,128)(2,1)S(1)}, bf16[128,1024]{1,0:T(8,128)(2,1)S(1)}, u32[]{:S(2)}, u32[]{:S(2)}) collective-permute-start(bf16[128,1024]{1,0:T(8,128)(2,1)S(1)} %get-tuple-element.493), channel_id=1, source_target_pairs={{0,2},{1,3},{2,0},{3,1},{4,6},{5,7},{6,4},{7,5},{8,10},{9,11},{10,... | collective-permute-start | bytes 786440 | tf_op jit(solution)/shard_map/ppermute | solution.py:37
  364.0 7.1 %collective-permute-start.62 = (bf16[128,1024]{1,0:T(8,128)(2,1)S(1)}, bf16[128,1024]{1,0:T(8,128)(2,1)S(1)}, u32[]{:S(2)}, u32[]{:S(2)}) collective-permute-start(bf16[128,1024]{1,0:T(8,128)(2,1)S(1)} %get-tuple-element.494), channel_id=1, source_target_pairs={{0,1},{1,0},{2,3},{3,2},{4,5},{5,4},{6,7},{7,6},{8,9},{9,8},{10,11... | collective-permute-start | bytes 786440 | tf_op jit(solution)/shard_map/ppermute | solution.py:37
  371.2 13.8 %collective-permute-start.63 = (bf16[512,384]{1,0:T(8,128)(2,1)S(1)}, bf16[512,384]{1,0:T(8,128)(2,1)S(1)}, u32[]{:S(2)}, u32[]{:S(2)}) collective-permute-start(bf16[512,384]{1,0:T(8,128)(2,1)S(1)} %get-tuple-element.536), channel_id=1, source_target_pairs={{0,0},{4,1},{1,2},{5,3},{2,4},{6,5},{3,6},{7,7},{8,8},{12,9},{9,10... | collective-permute-start | bytes 1179656 | tf_op jit(solution)/shard_map/ppermute | solution.py:1156
  371.9 23.0 %collective-permute-start.64 = (bf16[512,384]{1,0:T(8,128)(2,1)S(1)}, bf16[512,384]{1,0:T(8,128)(2,1)S(1)}, u32[]{:S(2)}, u32[]{:S(2)}) collective-permute-start(bf16[512,384]{1,0:T(8,128)(2,1)S(1)} %get-tuple-element.537), channel_id=1, source_target_pairs={{4,0},{0,1},{5,2},{1,3},{6,4},{2,5},{7,6},{3,7},{12,8},{8,9},{13,1... | collective-permute-start | bytes 1179656 | tf_op jit(solution)/shard_map/ppermute | solution.py:1156
  377.7 18.1 %collective-permute-start.68 = (bf16[256,1024]{1,0:T(8,128)(2,1)S(1)}, bf16[256,1024]{1,0:T(8,128)(2,1)S(1)}, u32[]{:S(2)}, u32[]{:S(2)}) collective-permute-start(bf16[256,1024]{1,0:T(8,128)(2,1)S(1)} %get-tuple-element.498), channel_id=1, source_target_pairs={{0,16},{8,24},{16,0},{24,8},{1,17},{9,25},{17,1},{25,9},{2,18},{10... | collective-permute-start | bytes 1572872 | tf_op jit(solution)/shard_map/ppermute | solution.py:37
  382.7 14.0 %collective-permute-start.69 = (bf16[1024,256]{1,0:T(8,128)(2,1)S(1)}, bf16[1024,256]{1,0:T(8,128)(2,1)}, u32[]{:S(2)}, u32[]{:S(2)}) collective-permute-start(bf16[1024,256]{1,0:T(8,128)(2,1)S(1)} %turned.1), channel_id=1, source_target_pairs={{0,8},{8,0},{16,24},{24,16},{1,9},{9,1},{17,25},{25,17},{2,10},{10... | collective-permute-start | bytes 1572872 | tf_op jit(solution)/shard_map/ppermute | solution.py:37
  397.2 7.5 %collective-permute-start.76 = (bf16[64,1024]{1,0:T(8,128)(2,1)}, bf16[64,1024]{1,0:T(8,128)(2,1)}, u32[]{:S(2)}, u32[]{:S(2)}) collective-permute-start(bf16[64,1024]{1,0:T(8,128)(2,1)} %add_add_fusion), channel_id=1, source_target_pairs={{0,2},{1,3},{2,0},{3,1},{4,6},{5,7},{6,4},{7,5},{8,10},{9,11},{10,... | collective-permute-start | bytes 393224 | tf_op jit(solution)/shard_map/ppermute | solution.py:37
  397.6 8.0 %collective-permute-start.77 = (bf16[64,1024]{1,0:T(8,128)(2,1)}, bf16[64,1024]{1,0:T(8,128)(2,1)}, u32[]{:S(2)}, u32[]{:S(2)}) collective-permute-start(bf16[64,1024]{1,0:T(8,128)(2,1)} %add_add_fusion), channel_id=1, source_target_pairs={{0,3},{1,2},{2,1},{3,0},{4,7},{5,6},{6,5},{7,4},{8,11},{9,10},{10,... | collective-permute-start | bytes 393224 | tf_op jit(solution)/shard_map/ppermute | solution.py:37
  400.3 16.6 %collective-permute-start.74 = (bf16[256,1024]{1,0:T(8,128)(2,1)}, bf16[256,1024]{1,0:T(8,128)(2,1)S(1)}, u32[]{:S(2)}, u32[]{:S(2)}) collective-permute-start(bf16[256,1024]{1,0:T(8,128)(2,1)} %add_convert_fusion.2), channel_id=1, source_target_pairs={{0,8},{8,0},{16,24},{24,16},{1,9},{9,1},{17,25},{25,17},{2,10},{10... | collective-permute-start | bytes 1572872 | tf_op jit(solution)/shard_map/ppermute | solution.py:37
  400.4 10.5 %collective-permute-start.73 = (bf16[32,1024]{1,0:T(8,128)(2,1)}, bf16[32,1024]{1,0:T(8,128)(2,1)S(1)}, u32[]{:S(2)}, u32[]{:S(2)}) collective-permute-start(bf16[32,1024]{1,0:T(8,128)(2,1)} %reduce-scatter.2.cloned.1.call-done), channel_id=1, source_target_pairs={{0,16},{8,24},{16,0},{24,8},{1,17},{9,25},{17,1},{25,9},{2,18},{10... | collective-permute-start | bytes 196616 | tf_op jit(solution)/shard_map/ppermute | solution.py:37
  403.5 13.3 %collective-permute-start.70 = (bf16[512,384]{1,0:T(8,128)(2,1)S(1)}, bf16[512,384]{1,0:T(8,128)(2,1)S(1)}, u32[]{:S(2)}, u32[]{:S(2)}) collective-permute-start(bf16[512,384]{1,0:T(8,128)(2,1)S(1)} %add_convert_fusion.5), channel_id=1, source_target_pairs={{0,16},{8,24},{16,0},{24,8},{1,17},{9,25},{17,1},{25,9},{2,18},{10... | collective-permute-start | bytes 1179656 | tf_op jit(solution)/shard_map/ppermute | solution.py:37
  404.7 14.0 %collective-permute-start.71 = (bf16[256,1024]{1,0:T(8,128)(2,1)}, bf16[256,1024]{1,0:T(8,128)(2,1)S(1)}, u32[]{:S(2)}, u32[]{:S(2)}) collective-permute-start(bf16[256,1024]{1,0:T(8,128)(2,1)} %copy-done.78), channel_id=1, source_target_pairs={{0,1},{1,0},{2,3},{3,2},{4,5},{5,4},{6,7},{7,6},{8,9},{9,8},{10,11... | collective-permute-start | bytes 1572872 | tf_op jit(solution)/shard_map/ppermute | solution.py:37
  410.8 12.8 %collective-permute-start.72 = (bf16[256,1024]{1,0:T(8,128)(2,1)S(1)}, bf16[256,1024]{1,0:T(8,128)(2,1)S(1)}, u32[]{:S(2)}, u32[]{:S(2)}) collective-permute-start(bf16[256,1024]{1,0:T(8,128)(2,1)S(1)} %get-tuple-element.508), channel_id=1, source_target_pairs={{0,2},{1,3},{2,0},{3,1},{4,6},{5,7},{6,4},{7,5},{8,10},{9,11},{10,... | collective-permute-start | bytes 1572872 | tf_op jit(solution)/shard_map/ppermute | solution.py:37
  (143 other events, 905.2 us)
Sparse Core Ops, SparseCore 0:
  46.9 44.0 all-gather.2
  318.2 61.3 reduce-scatter.1

commit v6 on v5

--- a/solution.py
+++ b/solution.py
@@ -366,7 +366,7 @@
 
 def second_norm(pre, cot, vectors):
     rows, width = pre.shape
-    block = pl.BlockSpec((128, width), lambda i: (i, 0))
+    block = pl.BlockSpec((rows // 2, width), lambda i: (i, 0))
     return pl.pallas_call(
         second_norm_kernel,
         out_shape=(
@@ -375,7 +375,7 @@
             jax.ShapeDtypeStruct((rows, width), BF),
             jax.ShapeDtypeStruct((8, width), F32),
         ),
-        grid=(rows // 128,),
+        grid=(2,),
         in_specs=[block, block, whole_block(*vectors.shape)],
         out_specs=(block, block, block, whole_block(8, width)),
         compiler_params=params(),
@@ -407,7 +407,7 @@
 
 def attend_back(at, d_first, norm, scale, vectors, w_out, parts):
     rows, width = d_first.shape
-    split = 4
+    split = 2
     block = pl.BlockSpec((rows // split, width), lambda i, s: (i, 0))
     piece = (rows, width // parts)
     return pl.pallas_call(

time: 445 us -> 445 us (level)
  no operation moved by 1% of the time
where the time goes in v6:
time: 445 us; the launch traced here: 436 us
  Pallas kernels  141 us (32%)
  waiting for transfers between devices  102 us (23%)
  starting transfers between devices  81.9 us (18%)
  local copies, waits for them, and re-layouts  50.1 us (11%)
  other arithmetic  29.2 us (7%)
  matrix products  16.7 us (4%)
  between operations  16.4 us (4%)
    ppermute x59, waiting for transfers between devices, swap(): return lax.ppermute(values, axis, [(i, i ^ bit) for i in range(count)])  66.7 us
    ppermute x59, starting transfers between devices, swap(): return lax.ppermute(values, axis, [(i, i ^ bit) for i in range(count)])  52.7 us
    unnamed x255, local copies, waits for them, and re-layouts  32.9 us
    pallas_call x4, Pallas kernels, attn_backward(): pl.pallas_call(functools.partial(attn_backward_kernel, parts), out_shape=...  26.5 us
    pallas_call x5, Pallas kernels, ff_forward(): pl.pallas_call(functools.partial(ff_forward_kernel, ff_half, count), out_...  22 us
    pallas_call x10, Pallas kernels, ff_grad(): pl.pallas_call(functools.partial(ff_grad_kernel, ff_half, spans, splits,...  18.9 us
    ppermute x9, waiting for transfers between devices, forward(): return lax.ppermute(values, 'tensor', ring_fw)  17.9 us
    pallas_call x2, Pallas kernels, attn_forward(): pl.pallas_call(attn_forward_kernel, out_shape=(shape,) * parts + (jax.Sha...  17.9 us
  transfers between devices with their start and end apart: 83, of which 28 were waited for; matrix products, arithmetic and copies ran while one was open for 13% of the time, Pallas kernels for 29%

profile of v6, /device:TPU:0, one launch (start us, length us, event | category | flops | bytes accessed | tf_op | source)
XLA Modules:
  0.0 436.4 jit_solution(6686875296672672118)
XLA Ops:
  10.0 3.0 collective-permute-start
  18.8 2.9 collective-permute-start.3
  25.1 2.6 constant_dynamic-slice_fusion.13
  31.8 2.6 fusion.16
  36.6 6.9 %collective-permute-start.8 = (bf16[128,1024]{1,0:T(8,128)(2,1)}, bf16[128,1024]{1,0:T(8,128)(2,1)S(1)}, u32[]{:S(2)}, u32[]{:S(2)}) collective-permute-start(bf16[128,1024]{1,0:T(8,128)(2,1)} %slice.168), channel_id=1, source_target_pairs={{0,2},{1,3},{2,0},{3,1},{4,6},{5,7},{6,4},{7,5},{8,10},{9,11},{10,... | collective-permute-start | bytes 786440 | tf_op jit(solution)/shard_map/ppermute | solution.py:37
  47.0 2.1 collective-permute-start.7
  49.2 2.0 collective-permute-start.4
  51.2 2.0 assemble.1
  54.7 3.9 project.2
  58.6 8.9 %attn_forward.2 = (bf16[256,256]{1,0:T(8,128)(2,1)S(1)}, bf16[256,256]{1,0:T(8,128)(2,1)S(1)}, bf16[256,256]{1,0:T(8,128)(2,1)S(1)}, bf16[256,256]{1,0:T(8,128)(...) custom-call(bf16[1024,768]{1,0:T(8,128)(2,1)S(1)} %get-tuple-element.414.q_ref.k_ref.v_ref, ...), custom_call_target="tpu_custom_call" | custom-call | flops 4294967296 | bytes 2359296 | tf_op jit(solution)/shard_map/attn_forward/pallas_call | solution.py:180
  67.6 13.1 %collective-permute-done.4.refs_1_ = bf16[256,1024]{1,0:T(8,128)(2,1)S(1)} collective-permute-done((bf16[256,1024]{1,0:T(8,128)(2,1)S(1)}, bf16[256,1024]{1,0:T(8,128)(2,1)S(1)}, u32[]{:S(2)}, u32[]{:S(2)}) %collective-permute-start.4) | collective-permute-done | bytes 524320 | tf_op jit(solution)/shard_map/ppermute | solution.py:37
  80.8 2.3 collective-permute-start.17
  83.1 1.8 collective-permute-start.18
  84.9 2.2 collective-permute-start.16
  87.3 6.1 %collective-permute-done.17.refs_3_ = bf16[128,1024]{1,0:T(8,128)(2,1)S(1)} collective-permute-done((bf16[128,1024]{1,0:T(8,128)(2,1)S(1)}, bf16[128,1024]{1,0:T(8,128)(2,1)S(1)}, u32[]{:S(2)}, u32[]{:S(2)}) %collective-permute-start.17) | collective-permute-done | bytes 262176 | tf_op jit(solution)/shard_map/ppermute | solution.py:37
  96.7 2.6 project.3
  99.3 8.9 %attn_forward.3 = (bf16[256,256]{1,0:T(8,128)(2,1)S(1)}, bf16[256,256]{1,0:T(8,128)(2,1)S(1)}, bf16[256,256]{1,0:T(8,128)(2,1)S(1)}, bf16[256,256]{1,0:T(8,128)(...) custom-call(bf16[1024,768]{1,0:T(8,128)(2,1)S(1)} %get-tuple-element.461.q_ref.k_ref.v_ref, ...), custom_call_target="tpu_custom_call" | custom-call | flops 4294967296 | bytes 2359296 | tf_op jit(solution)/shard_map/attn_forward/pallas_call | solution.py:180
  114.8 2.3 collective-permute-done.21.refs_7_
  118.7 2.4 collective-permute-done.22.refs_11_
  123.9 7.8 %attend.1 = (bf16[512,1024]{1,0:T(8,128)(2,1)}, f32[512,1024]{1,0:T(8,128)}, f32[512,128]{1,0:T(8,128)}, f32[512,1024]{1,0:T(8,128)}, bf16[512,1024]{1,0:T(8,128)(2,1)}, /*index=5*/bf16[1024,1024]{1,0:T(8,128)(2,1)}) custom-call(s32[5]{0:T(128)} %concatenate.111.at_ref, bf16[256,256]{1,0:T(8,128)(2,1)} %copy-done.76, bf16[256,256]{1,0:T(8,128)(2,1)} %copy-done.99, ...), custom_call_target="tpu_custom_call" | custom-call | flops 1073741824 | bytes 10485760 | tf_op jit(solution)/shard_map/attend/pallas_call | solution.py:332
  136.7 2.3 ff_forward.5
  140.8 5.6 %ff_forward.6 = (f32[512,1024]{1,0:T(8,128)S(1)}, bf16[512,1024]{1,0:T(8,128)(2,1)S(1)}, f32[512,1024]{1,0:T(8,128)S(1)}) custom-call(bf16[512,1024]{1,0:T(8,128)(2,1)S(1)} %copy-done.3, f32[512,1024]{1,0:T(8,128)S(1)} %get-tuple-element.317.init_ref, bf16[528,1024]{1,0:T(8,128)(2,1)} %pad_maximum_fusion.1.refs_0_, ...), custom_call_target="tpu_custom_call" | custom-call | flops 1 | bytes 1 | tf_op jit(solution)/shard_map/ff_forward/pallas_call | solution.py:499
  151.7 6.0 %ff_forward.7 = (f32[512,1024]{1,0:T(8,128)S(1)}, bf16[512,1024]{1,0:T(8,128)(2,1)S(1)}, f32[512,1024]{1,0:T(8,128)S(1)}) custom-call(bf16[512,1024]{1,0:T(8,128)(2,1)S(1)} %copy-done.3, f32[512,1024]{1,0:T(8,128)S(1)} %get-tuple-element.321.init_ref, bf16[528,1024]{1,0:T(8,128)(2,1)} %collective-permute-done.23.refs_0_, ...), custom_call_target="tpu_custom_call" | custom-call | flops 1 | bytes 1 | tf_op jit(solution)/shard_map/ff_forward/pallas_call | solution.py:499
  159.1 14.7 %collective-permute-done.28.refs_0_ = bf16[528,1024]{1,0:T(8,128)(2,1)S(1)} collective-permute-done((bf16[528,1024]{1,0:T(8,128)(2,1)}, bf16[528,1024]{1,0:T(8,128)(2,1)S(1)}, u32[]{:S(2)}, u32[]{:S(2)}) %collective-permute-start.28) | collective-permute-done | bytes 1081376 | tf_op jit(solution)/shard_map/ppermute | solution.py:814
  175.2 1.8 collective-permute-start.32
  178.9 4.6 %ff_forward.8 = (f32[512,1024]{1,0:T(8,128)S(1)}, bf16[512,1024]{1,0:T(8,128)(2,1)S(1)}, f32[512,1024]{1,0:T(8,128)S(1)}) custom-call(bf16[512,1024]{1,0:T(8,128)(2,1)S(1)} %copy-done.3, f32[512,1024]{1,0:T(8,128)S(1)} %get-tuple-element.325.init_ref, bf16[528,1024]{1,0:T(8,128)(2,1)S(1)} %collective-permute-done.28.refs_0_, ...), custom_call_target="tpu_custom_call" | custom-call | flops 1 | bytes 1 | tf_op jit(solution)/shard_map/ff_forward/pallas_call | solution.py:499
  187.4 3.5 collective-permute-done.33
  195.6 3.5 ff_forward.9
  199.1 2.7 second_norm.1
  201.8 3.0 ff_backward.5
  206.7 3.5 ff_backward.6
  214.9 4.6 %ff_backward.7 = (bf16[512,1024]{1,0:T(8,128)(2,1)S(1)}, f32[512,1024]{1,0:T(8,128)S(1)}, f32[16,256]{1,0:T(8,128)S(1)}) custom-call(bf16[512,1024]{1,0:T(8,128)(2,1)S(1)} %get-tuple-element.445.d_fed_ref.fed_ref, f32[512,1024]{1,0:T(8,128)S(1)} %get-tuple-element.359.init_ref, f32[512,1024]{1,0:T(8,128)S(1)} %copy-done.50, ...), custom_call_target="tpu_custom_call" | custom-call | flops 2147483648 | bytes 12582912 | tf_op jit(solution)/shard_map/ff_backward/pallas_call | solution.py:544
  219.5 2.7 ff_grad.14
  223.5 3.2 collective-permute-done.38.refs_3_
  226.7 1.8 collective-permute-done.39.refs_1_
  235.3 4.6 %ff_backward.8 = (bf16[512,1024]{1,0:T(8,128)(2,1)S(1)}, f32[512,1024]{1,0:T(8,128)S(1)}, f32[16,256]{1,0:T(8,128)S(1)}) custom-call(bf16[512,1024]{1,0:T(8,128)(2,1)S(1)} %get-tuple-element.445.d_fed_ref.fed_ref, f32[512,1024]{1,0:T(8,128)S(1)} %copy-done.52, f32[512,1024]{1,0:T(8,128)S(1)} %copy-done.48, bf16[528,1024]{1,0:T(8,128)(2,1)} %pad_maximum_fusion.1.refs_0_, ...), custom_call_target="tpu_custom_call" | custom-call | flops 2147483648 | bytes 12582912 | tf_op jit(solution)/shard_map/ff_backward/pallas_call | solution.py:544
  242.5 3.5 attend_back.1
  246.9 2.8 collective-permute-start.46
  251.0 2.6 ff_grad.16
  255.9 2.9 ff_grad.15
  258.8 8.2 %collective-permute-done.44 = bf16[512,256]{1,0:T(8,128)(2,1)S(1)} collective-permute-done((bf16[512,256]{1,0:T(8,128)(2,1)S(1)}, bf16[512,256]{1,0:T(8,128)(2,1)S(1)}, u32[]{:S(2)}, u32[]{:S(2)}) %collective-permute-start.44) | collective-permute-done | bytes 262176 | tf_op jit(solution)/shard_map/ppermute | solution.py:37
  267.1 2.9 combine.5
  273.6 2.0 fusion.2
  277.4 6.6 %attn_backward.4.refs_0_ = bf16[1024,768]{1,0:T(8,128)(2,1)S(1)} custom-call(bf16[1024,768]{1,0:T(8,128)(2,1)S(1)} %copy-done.14, bf16[1024,768]{1,0:T(8,128)(2,1)S(1)} %copy-done.14, bf16[1024,768]{1,0:T(8,128)(2,1)S(1)} %copy-done.14, f32[2,8,1024]{2,1,0:T(8,128)S(1)} %get-tuple-element.424.log_ref, ...), custom_call_target="tpu_custom_call" | custom-call | flops 1 | bytes 1 | tf_op jit(solution)/shard_map/attn_backward/pallas_call | solution.py:241
  284.1 2.0 fusion.42
  286.0 6.6 %attn_backward.5.d_ref.one_ref.two_ref.refs_0_ = bf16[1024,768]{1,0:T(8,128)(2,1)S(1)} custom-call(bf16[1024,768]{1,0:T(8,128)(2,1)S(1)} %copy-done.14, bf16[1024,768]{1,0:T(8,128)(2,1)S(1)} %copy-done.14, bf16[1024,768]{1,0:T(8,128)(2,1)S(1)} %copy-done.14, f32[2,8,1024]{2,1,0:T(8,128)S(1)} %get-tuple-element.424.log_ref, ...), custom_call_target="tpu_custom_call", output_to_operand_aliasing={{}: (6, {})} | custom-call | flops 1 | bytes 1 | tf_op jit(solution)/shard_map/attn_backward/pallas_call | solution.py:241
  293.8 1.8 ff_grad.18
  299.1 2.9 ff_grad.17
  302.0 2.7 combine.6
  320.2 6.6 %attn_backward.6.refs_0_ = bf16[1024,768]{1,0:T(8,128)(2,1)S(1)} custom-call(bf16[1024,768]{1,0:T(8,128)(2,1)S(1)} %copy-done.11, bf16[1024,768]{1,0:T(8,128)(2,1)S(1)} %copy-done.11, bf16[1024,768]{1,0:T(8,128)(2,1)S(1)} %copy-done.11, f32[2,8,1024]{2,1,0:T(8,128)S(1)} %get-tuple-element.448.log_ref, ...), custom_call_target="tpu_custom_call" | custom-call | flops 1 | bytes 1 | tf_op jit(solution)/shard_map/attn_backward/pallas_call | solution.py:241
  326.9 2.0 ff_grad.19.refs_0_
  328.9 11.8 %collective-permute-done.55.to_two_ref = bf16[128,1024]{1,0:T(8,128)(2,1)S(1)} collective-permute-done((bf16[128,1024]{1,0:T(8,128)(2,1)}, bf16[128,1024]{1,0:T(8,128)(2,1)S(1)}, u32[]{:S(2)}, u32[]{:S(2)}) %collective-permute-start.55) | collective-permute-done | bytes 262176 | tf_op jit(solution)/shard_map/ppermute | solution.py:37
  340.7 1.9 combine.7
  344.0 2.1 side_shares.2
  346.6 2.2 collective-permute-start.59
  350.0 6.6 %attn_backward.7.d_ref.one_ref.two_ref.refs_1_ = bf16[1024,768]{1,0:T(8,128)(2,1)S(1)} custom-call(bf16[1024,768]{1,0:T(8,128)(2,1)S(1)} %copy-done.12, bf16[1024,768]{1,0:T(8,128)(2,1)S(1)} %copy-done.12, bf16[1024,768]{1,0:T(8,128)(2,1)S(1)} %copy-done.12, f32[2,8,1024]{2,1,0:T(8,128)S(1)} %get-tuple-element.448.log_ref, ...), custom_call_target="tpu_custom_call", output_to_operand_aliasing={{}: (6, {})} | custom-call | flops 1 | bytes 1 | tf_op jit(solution)/shard_map/attn_backward/pallas_call | solution.py:241
  358.9 2.4 collective-permute-done.57
  368.4 1.9 collective-permute-done.61.to_two_ref
  371.6 4.5 %collective-permute-start.64 = (bf16[512,384]{1,0:T(8,128)(2,1)S(1)}, bf16[512,384]{1,0:T(8,128)(2,1)S(1)}, u32[]{:S(2)}, u32[]{:S(2)}) collective-permute-start(bf16[512,384]{1,0:T(8,128)(2,1)S(1)} %get-tuple-element.537), channel_id=1, source_target_pairs={{4,0},{0,1},{5,2},{1,3},{6,4},{2,5},{7,6},{3,7},{12,8},{8,9},{13,1... | collective-permute-start | bytes 1179656 | tf_op jit(solution)/shard_map/ppermute | solution.py:1156
  384.7 9.9 %collective-permute-done.64 = bf16[512,384]{1,0:T(8,128)(2,1)S(1)} collective-permute-done((bf16[512,384]{1,0:T(8,128)(2,1)S(1)}, bf16[512,384]{1,0:T(8,128)(2,1)S(1)}, u32[]{:S(2)}, u32[]{:S(2)}) %collective-permute-start.64) | collective-permute-done | bytes 393248 | tf_op jit(solution)/shard_map/ppermute | solution.py:1156
  397.4 2.6 collective-permute-start.77
  401.3 1.8 collective-permute-done.75
  407.6 2.8 fusion.7
  418.3 5.0 %collective-permute-done.72 = bf16[256,1024]{1,0:T(8,128)(2,1)S(1)} collective-permute-done((bf16[256,1024]{1,0:T(8,128)(2,1)S(1)}, bf16[256,1024]{1,0:T(8,128)(2,1)S(1)}, u32[]{:S(2)}, u32[]{:S(2)}) %collective-permute-start.72) | collective-permute-done | bytes 524320 | tf_op jit(solution)/shard_map/ppermute | solution.py:37
  (515 shorter events, 154.3 us)
Async XLA Ops:
  7.2 110.0 %all-gather.3.cloned.1.call-start = ((), (), s32[]{:S(2)}) async-start(), calls=%async_computation.2 | async-start | bytes 1179648 | tf_op jit(solution)/shard_map/all_gather | solution.py:880
  10.0 24.3 %collective-permute-start = (bf16[256,1024]{1,0:T(8,128)(2,1)S(1)}, bf16[256,1024]{1,0:T(8,128)(2,1)}, u32[]{:S(2)}, u32[]{:S(2)}) collective-permute-start(bf16[256,1024]{1,0:T(8,128)(2,1)S(1)} %fusion.3.refs_0_.refs_8_), channel_id=1, source_target_pairs={{0,1},{1,0},{2,3},{3,2},{4,5},{5,4},{6,7},{7,6},{8,9},{9,8},{10,11... | collective-permute-start | bytes 1572872 | tf_op jit(solution)/shard_map/ppermute | solution.py:37
  13.0 21.4 %collective-permute-start.1 = (bf16[256,1024]{1,0:T(8,128)(2,1)S(1)}, bf16[256,1024]{1,0:T(8,128)(2,1)}, u32[]{:S(2)}, u32[]{:S(2)}) collective-permute-start(bf16[256,1024]{1,0:T(8,128)(2,1)S(1)} %fusion.3.refs_0_.refs_8_), channel_id=1, source_target_pairs={{0,2},{1,3},{2,0},{3,1},{4,6},{5,7},{6,4},{7,5},{8,10},{9,11},{10,... | collective-permute-start | bytes 1572872 | tf_op jit(solution)/shard_map/ppermute | solution.py:37
  17.2 17.2 %collective-permute-start.2 = (bf16[528,384]{1,0:T(8,128)(2,1)}, bf16[528,384]{1,0:T(8,128)(2,1)S(1)}, u32[]{:S(2)}, u32[]{:S(2)}) collective-permute-start(bf16[528,384]{1,0:T(8,128)(2,1)} %fusion.17), channel_id=1, source_target_pairs={{0,0},{1,4},{2,1},{3,5},{4,2},{5,6},{6,3},{7,7},{8,8},{9,12},{10,9... | collective-permute-start | bytes 1216520 | tf_op jit(solution)/shard_map/ppermute | solution.py:874
  18.8 15.5 %collective-permute-start.3 = (bf16[528,384]{1,0:T(8,128)(2,1)}, bf16[528,384]{1,0:T(8,128)(2,1)}, u32[]{:S(2)}, u32[]{:S(2)}) collective-permute-start(bf16[528,384]{1,0:T(8,128)(2,1)} %fusion.17), channel_id=1, source_target_pairs={{0,4},{1,0},{2,5},{3,1},{4,6},{5,2},{6,7},{7,3},{8,12},{9,8},{10,1... | collective-permute-start | bytes 1216520 | tf_op jit(solution)/shard_map/ppermute | solution.py:874
  34.4 12.6 %collective-permute-start.10 = (bf16[528,384]{1,0:T(8,128)(2,1)S(1)}, bf16[528,384]{1,0:T(8,128)(2,1)S(1)}, u32[]{:S(2)}, u32[]{:S(2)}) collective-permute-start(bf16[528,384]{1,0:T(8,128)(2,1)S(1)} %collective-permute-done.2.refs_0_), channel_id=1, source_target_pairs={{0,8},{8,0},{16,24},{24,16},{1,9},{9,1},{17,25},{25,17},{2,10},{10... | collective-permute-start | bytes 1216520 | tf_op jit(solution)/shard_map/ppermute | solution.py:37
  34.4 14.8 %collective-permute-start.11 = (bf16[528,384]{1,0:T(8,128)(2,1)}, bf16[528,384]{1,0:T(8,128)(2,1)}, u32[]{:S(2)}, u32[]{:S(2)}) collective-permute-start(bf16[528,384]{1,0:T(8,128)(2,1)} %collective-permute-done.3.refs_1_), channel_id=1, source_target_pairs={{0,8},{8,0},{16,24},{24,16},{1,9},{9,1},{17,25},{25,17},{2,10},{10... | collective-permute-start | bytes 1216520 | tf_op jit(solution)/shard_map/ppermute | solution.py:37
  36.6 16.6 %collective-permute-start.8 = (bf16[128,1024]{1,0:T(8,128)(2,1)}, bf16[128,1024]{1,0:T(8,128)(2,1)S(1)}, u32[]{:S(2)}, u32[]{:S(2)}) collective-permute-start(bf16[128,1024]{1,0:T(8,128)(2,1)} %slice.168), channel_id=1, source_target_pairs={{0,2},{1,3},{2,0},{3,1},{4,6},{5,7},{6,4},{7,5},{8,10},{9,11},{10,... | collective-permute-start | bytes 786440 | tf_op jit(solution)/shard_map/ppermute | solution.py:37
  45.2 9.5 %collective-permute-start.9 = (bf16[128,1024]{1,0:T(8,128)(2,1)}, bf16[128,1024]{1,0:T(8,128)(2,1)}, u32[]{:S(2)}, u32[]{:S(2)}) collective-permute-start(bf16[128,1024]{1,0:T(8,128)(2,1)} %slice.169), channel_id=1, source_target_pairs={{0,1},{1,0},{2,3},{3,2},{4,5},{5,4},{6,7},{7,6},{8,9},{9,8},{10,11... | collective-permute-start | bytes 786440 | tf_op jit(solution)/shard_map/ppermute | solution.py:37
  46.8 349.6 %reduce-scatter.2.cloned.1.call-start = ((), (), s32[]{:S(2)}) async-start(), calls=%async_computation.1 | async-start | bytes 589824 | tf_op jit(solution)/shard_map/reduce_scatter | solution.py:1056
  46.9 33.8 %collective-permute-start.6 = (bf16[272,1024]{1,0:T(8,128)(2,1)S(1)}, bf16[272,1024]{1,0:T(8,128)(2,1)S(1)}, u32[]{:S(2)}, u32[]{:S(2)}) collective-permute-start(bf16[272,1024]{1,0:T(8,128)(2,1)S(1)} %slice.167), channel_id=1, source_target_pairs={{0,2},{2,4},{4,6},{6,7},{7,5},{5,3},{3,1},{1,0},{8,10},{10,12},{12... | collective-permute-start | bytes 1671176 | tf_op jit(solution)/shard_map/ppermute | solution.py:814
  47.0 33.7 %collective-permute-start.7 = (bf16[272,1024]{1,0:T(8,128)(2,1)S(1)}, bf16[272,1024]{1,0:T(8,128)(2,1)S(1)}, u32[]{:S(2)}, u32[]{:S(2)}) collective-permute-start(bf16[272,1024]{1,0:T(8,128)(2,1)S(1)} %slice.167), channel_id=1, source_target_pairs={{2,0},{4,2},{6,4},{7,6},{5,7},{3,5},{1,3},{0,1},{10,8},{12,10},{14... | collective-permute-start | bytes 1671176 | tf_op jit(solution)/shard_map/ppermute | solution.py:817
  49.2 31.5 %collective-permute-start.4 = (bf16[256,1024]{1,0:T(8,128)(2,1)S(1)}, bf16[256,1024]{1,0:T(8,128)(2,1)S(1)}, u32[]{:S(2)}, u32[]{:S(2)}) collective-permute-start(bf16[256,1024]{1,0:T(8,128)(2,1)S(1)} %copy-done.72), channel_id=1, source_target_pairs={{0,1},{1,0},{2,3},{3,2},{4,5},{5,4},{6,7},{7,6},{8,9},{9,8},{10,11... | collective-permute-start | bytes 1572872 | tf_op jit(solution)/shard_map/ppermute | solution.py:37
  53.2 27.5 %collective-permute-start.5 = (bf16[256,1024]{1,0:T(8,128)(2,1)S(1)}, bf16[256,1024]{1,0:T(8,128)(2,1)S(1)}, u32[]{:S(2)}, u32[]{:S(2)}) collective-permute-start(bf16[256,1024]{1,0:T(8,128)(2,1)S(1)} %copy-done.72), channel_id=1, source_target_pairs={{0,2},{1,3},{2,0},{3,1},{4,6},{5,7},{6,4},{7,5},{8,10},{9,11},{10,... | collective-permute-start | bytes 1572872 | tf_op jit(solution)/shard_map/ppermute | solution.py:37
  80.8 12.6 %collective-permute-start.17 = (bf16[128,1024]{1,0:T(8,128)(2,1)S(1)}, bf16[128,1024]{1,0:T(8,128)(2,1)S(1)}, u32[]{:S(2)}, u32[]{:S(2)}) collective-permute-start(bf16[128,1024]{1,0:T(8,128)(2,1)S(1)} %slice.171), channel_id=1, source_target_pairs={{0,2},{1,3},{2,0},{3,1},{4,6},{5,7},{6,4},{7,5},{8,10},{9,11},{10,... | collective-permute-start | bytes 786440 | tf_op jit(solution)/shard_map/ppermute | solution.py:37
  83.1 11.9 %collective-permute-start.18 = (bf16[128,1024]{1,0:T(8,128)(2,1)S(1)}, bf16[128,1024]{1,0:T(8,128)(2,1)S(1)}, u32[]{:S(2)}, u32[]{:S(2)}) collective-permute-start(bf16[128,1024]{1,0:T(8,128)(2,1)S(1)} %slice.172), channel_id=1, source_target_pairs={{0,1},{1,0},{2,3},{3,2},{4,5},{5,4},{6,7},{7,6},{8,9},{9,8},{10,11... | collective-permute-start | bytes 786440 | tf_op jit(solution)/shard_map/ppermute | solution.py:37
  84.9 23.4 %collective-permute-start.15 = (bf16[256,1024]{1,0:T(8,128)(2,1)S(1)}, bf16[256,1024]{1,0:T(8,128)(2,1)S(1)}, u32[]{:S(2)}, u32[]{:S(2)}) collective-permute-start(bf16[256,1024]{1,0:T(8,128)(2,1)S(1)} %slice.170), channel_id=1, source_target_pairs={{0,2},{2,4},{4,6},{6,7},{7,5},{5,3},{3,1},{1,0},{8,10},{10,12},{12... | collective-permute-start | bytes 1572872 | tf_op jit(solution)/shard_map/ppermute | solution.py:814
  84.9 23.4 %collective-permute-start.16 = (bf16[256,1024]{1,0:T(8,128)(2,1)S(1)}, bf16[256,1024]{1,0:T(8,128)(2,1)S(1)}, u32[]{:S(2)}, u32[]{:S(2)}) collective-permute-start(bf16[256,1024]{1,0:T(8,128)(2,1)S(1)} %slice.170), channel_id=1, source_target_pairs={{2,0},{4,2},{6,4},{7,6},{5,7},{3,5},{1,3},{0,1},{10,8},{12,10},{14... | collective-permute-start | bytes 1572872 | tf_op jit(solution)/shard_map/ppermute | solution.py:817
  87.0 24.3 %collective-permute-start.12 = (bf16[256,256]{1,0:T(8,128)(2,1)S(1)}, bf16[256,256]{1,0:T(8,128)(2,1)S(1)}, u32[]{:S(2)}, u32[]{:S(2)}) collective-permute-start(bf16[256,256]{1,0:T(8,128)(2,1)S(1)} %get-tuple-element.284), channel_id=1, source_target_pairs={{0,1},{1,0},{2,3},{3,2},{4,5},{5,4},{6,7},{7,6},{8,9},{9,8},{10,11... | collective-permute-start | bytes 393224 | tf_op jit(solution)/shard_map/ppermute | solution.py:37
  93.4 20.6 %collective-permute-start.13 = (bf16[256,256]{1,0:T(8,128)(2,1)S(1)}, bf16[256,256]{1,0:T(8,128)(2,1)S(1)}, u32[]{:S(2)}, u32[]{:S(2)}) collective-permute-start(bf16[256,256]{1,0:T(8,128)(2,1)S(1)} %get-tuple-element.285), channel_id=1, source_target_pairs={{0,2},{1,3},{2,0},{3,1},{4,6},{5,7},{6,4},{7,5},{8,10},{9,11},{10,... | collective-permute-start | bytes 393224 | tf_op jit(solution)/shard_map/ppermute | solution.py:37
  94.9 19.1 %collective-permute-start.14 = (bf16[256,256]{1,0:T(8,128)(2,1)S(1)}, bf16[256,256]{1,0:T(8,128)(2,1)S(1)}, u32[]{:S(2)}, u32[]{:S(2)}) collective-permute-start(bf16[256,256]{1,0:T(8,128)(2,1)S(1)} %get-tuple-element.286), channel_id=1, source_target_pairs={{0,3},{1,2},{2,1},{3,0},{4,7},{5,6},{6,5},{7,4},{8,11},{9,10},{10,... | collective-permute-start | bytes 393224 | tf_op jit(solution)/shard_map/ppermute | solution.py:37
  117.2 14.4 %collective-permute-start.25 = (bf16[528,1024]{1,0:T(8,128)(2,1)S(1)}, bf16[528,1024]{1,0:T(8,128)(2,1)S(1)}, u32[]{:S(2)}, u32[]{:S(2)}) collective-permute-start(bf16[528,1024]{1,0:T(8,128)(2,1)S(1)} %fusion.6.refs_0_), channel_id=1, source_target_pairs={{0,8},{8,0},{16,24},{24,16},{1,9},{9,1},{17,25},{25,17},{2,10},{10... | collective-permute-start | bytes 3244040 | tf_op jit(solution)/shard_map/ppermute | solution.py:37
  117.7 23.1 %collective-permute-start.26 = (bf16[528,1024]{1,0:T(8,128)(2,1)}, bf16[528,1024]{1,0:T(8,128)(2,1)}, u32[]{:S(2)}, u32[]{:S(2)}) collective-permute-start(bf16[528,1024]{1,0:T(8,128)(2,1)} %pad_maximum_fusion.1.refs_0_), channel_id=1, source_target_pairs={{0,8},{8,0},{16,24},{24,16},{1,9},{9,1},{17,25},{25,17},{2,10},{10... | collective-permute-start | bytes 3244040 | tf_op jit(solution)/shard_map/ppermute | solution.py:37
  117.8 23.0 %collective-permute-start.27 = (bf16[528,1024]{1,0:T(8,128)(2,1)}, bf16[528,1024]{1,0:T(8,128)(2,1)}, u32[]{:S(2)}, u32[]{:S(2)}) collective-permute-start(bf16[528,1024]{1,0:T(8,128)(2,1)} %pad_maximum_fusion.2.refs_1_), channel_id=1, source_target_pairs={{0,8},{8,0},{16,24},{24,16},{1,9},{9,1},{17,25},{25,17},{2,10},{10... | collective-permute-start | bytes 3244040 | tf_op jit(solution)/shard_map/ppermute | solution.py:37
  118.2 28.2 %collective-permute-start.23 = (bf16[528,1024]{1,0:T(8,128)(2,1)}, bf16[528,1024]{1,0:T(8,128)(2,1)}, u32[]{:S(2)}, u32[]{:S(2)}) collective-permute-start(bf16[528,1024]{1,0:T(8,128)(2,1)} %pad_maximum_fusion.1.refs_0_), channel_id=1, source_target_pairs={{0,2},{2,4},{4,6},{6,7},{7,5},{5,3},{3,1},{1,0},{8,10},{10,12},{12... | collective-permute-start | bytes 3244040 | tf_op jit(solution)/shard_map/ppermute | solution.py:814
  121.1 26.2 %collective-permute-start.24 = (bf16[528,1024]{1,0:T(8,128)(2,1)}, bf16[528,1024]{1,0:T(8,128)(2,1)}, u32[]{:S(2)}, u32[]{:S(2)}) collective-permute-start(bf16[528,1024]{1,0:T(8,128)(2,1)} %pad_maximum_fusion.2.refs_1_), channel_id=1, source_target_pairs={{2,0},{4,2},{6,4},{7,6},{5,7},{3,5},{1,3},{0,1},{10,8},{12,10},{14... | collective-permute-start | bytes 3244040 | tf_op jit(solution)/shard_map/ppermute | solution.py:817
  147.8 26.0 %collective-permute-start.28 = (bf16[528,1024]{1,0:T(8,128)(2,1)}, bf16[528,1024]{1,0:T(8,128)(2,1)S(1)}, u32[]{:S(2)}, u32[]{:S(2)}) collective-permute-start(bf16[528,1024]{1,0:T(8,128)(2,1)} %collective-permute-done.23.refs_0_), channel_id=1, source_target_pairs={{0,2},{2,4},{4,6},{6,7},{7,5},{5,3},{3,1},{1,0},{8,10},{10,12},{12... | collective-permute-start | bytes 3244040 | tf_op jit(solution)/shard_map/ppermute | solution.py:814
  149.0 25.7 %collective-permute-start.29 = (bf16[528,1024]{1,0:T(8,128)(2,1)}, bf16[528,1024]{1,0:T(8,128)(2,1)S(1)}, u32[]{:S(2)}, u32[]{:S(2)}) collective-permute-start(bf16[528,1024]{1,0:T(8,128)(2,1)} %collective-permute-done.24.refs_1_), channel_id=1, source_target_pairs={{2,0},{4,2},{6,4},{7,6},{5,7},{3,5},{1,3},{0,1},{10,8},{12,10},{14... | collective-permute-start | bytes 3244040 | tf_op jit(solution)/shard_map/ppermute | solution.py:817
  175.2 15.7 %collective-permute-start.32 = (bf16[272,1024]{1,0:T(8,128)(2,1)S(1)}, bf16[272,1024]{1,0:T(8,128)(2,1)S(1)}, u32[]{:S(2)}, u32[]{:S(2)}) collective-permute-start(bf16[272,1024]{1,0:T(8,128)(2,1)S(1)} %slice.173), channel_id=1, source_target_pairs={{0,2},{2,4},{4,6},{6,7},{7,5},{5,3},{3,1},{1,0},{8,10},{10,12},{12... | collective-permute-start | bytes 1671176 | tf_op jit(solution)/shard_map/ppermute | solution.py:814
  177.0 13.8 %collective-permute-start.33 = (bf16[256,1024]{1,0:T(8,128)(2,1)S(1)}, bf16[256,1024]{1,0:T(8,128)(2,1)S(1)}, u32[]{:S(2)}, u32[]{:S(2)}) collective-permute-start(bf16[256,1024]{1,0:T(8,128)(2,1)S(1)} %slice.174), channel_id=1, source_target_pairs={{2,0},{4,2},{6,4},{7,6},{5,7},{3,5},{1,3},{0,1},{10,8},{12,10},{14... | collective-permute-start | bytes 1572872 | tf_op jit(solution)/shard_map/ppermute | solution.py:817
  212.3 9.9 %collective-permute-start.40 = (bf16[1024,1024]{1,0:T(8,128)(2,1)S(1)}, bf16[1024,1024]{1,0:T(8,128)(2,1)S(1)}, u32[]{:S(2)}, u32[]{:S(2)}) collective-permute-start(bf16[1024,1024]{1,0:T(8,128)(2,1)S(1)} %ff_grad.12), channel_id=1, source_target_pairs={{0,8},{8,0},{16,24},{24,16},{1,9},{9,1},{17,25},{25,17},{2,10},{10... | collective-permute-start | bytes 6291464 | tf_op jit(solution)/shard_map/ppermute | solution.py:37
  212.5 14.2 %collective-permute-start.38 = (bf16[256,1024]{1,0:T(8,128)(2,1)S(1)}, bf16[256,1024]{1,0:T(8,128)(2,1)S(1)}, u32[]{:S(2)}, u32[]{:S(2)}) collective-permute-start(bf16[256,1024]{1,0:T(8,128)(2,1)S(1)} %get-tuple-element.355), channel_id=1, source_target_pairs={{0,2},{2,4},{4,6},{6,7},{7,5},{5,3},{3,1},{1,0},{8,10},{10,12},{12... | collective-permute-start | bytes 1572872 | tf_op jit(solution)/shard_map/ppermute | solution.py:814
  214.2 14.3 %collective-permute-start.39 = (bf16[256,1024]{1,0:T(8,128)(2,1)S(1)}, bf16[256,1024]{1,0:T(8,128)(2,1)S(1)}, u32[]{:S(2)}, u32[]{:S(2)}) collective-permute-start(bf16[256,1024]{1,0:T(8,128)(2,1)S(1)} %get-tuple-element.356), channel_id=1, source_target_pairs={{2,0},{4,2},{6,4},{7,6},{5,7},{3,5},{1,3},{0,1},{10,8},{12,10},{14... | collective-permute-start | bytes 1572872 | tf_op jit(solution)/shard_map/ppermute | solution.py:817
  230.0 16.1 %collective-permute-start.43 = (bf16[1024,1024]{1,0:T(8,128)(2,1)}, bf16[1024,1024]{1,0:T(8,128)(2,1)}, u32[]{:S(2)}, u32[]{:S(2)}) collective-permute-start(bf16[1024,1024]{1,0:T(8,128)(2,1)} %ff_grad.14), channel_id=1, source_target_pairs={{0,8},{8,0},{16,24},{24,16},{1,9},{9,1},{17,25},{25,17},{2,10},{10... | collective-permute-start | bytes 6291464 | tf_op jit(solution)/shard_map/ppermute | solution.py:37
  230.0 28.8 %collective-permute-start.41 = (bf16[512,1024]{1,0:T(8,128)(2,1)}, bf16[512,1024]{1,0:T(8,128)(2,1)}, u32[]{:S(2)}, u32[]{:S(2)}) collective-permute-start(bf16[512,1024]{1,0:T(8,128)(2,1)} %get-tuple-element.378), channel_id=1, source_target_pairs={{0,2},{2,4},{4,6},{6,7},{7,5},{5,3},{3,1},{1,0},{8,10},{10,12},{12... | collective-permute-start | bytes 3145736 | tf_op jit(solution)/shard_map/ppermute | solution.py:814
  230.7 28.2 %collective-permute-start.42 = (bf16[512,1024]{1,0:T(8,128)(2,1)}, bf16[512,1024]{1,0:T(8,128)(2,1)}, u32[]{:S(2)}, u32[]{:S(2)}) collective-permute-start(bf16[512,1024]{1,0:T(8,128)(2,1)} %get-tuple-element.379), channel_id=1, source_target_pairs={{2,0},{4,2},{6,4},{7,6},{5,7},{3,5},{1,3},{0,1},{10,8},{12,10},{14... | collective-permute-start | bytes 3145736 | tf_op jit(solution)/shard_map/ppermute | solution.py:817
  246.1 20.9 %collective-permute-start.44 = (bf16[512,256]{1,0:T(8,128)(2,1)S(1)}, bf16[512,256]{1,0:T(8,128)(2,1)S(1)}, u32[]{:S(2)}, u32[]{:S(2)}) collective-permute-start(bf16[512,256]{1,0:T(8,128)(2,1)S(1)} %get-tuple-element.400), channel_id=1, source_target_pairs={{0,1},{1,0},{2,3},{3,2},{4,5},{5,4},{6,7},{7,6},{8,9},{9,8},{10,11... | collective-permute-start | bytes 786440 | tf_op jit(solution)/shard_map/ppermute | solution.py:37
  246.5 20.6 %collective-permute-start.45 = (bf16[512,256]{1,0:T(8,128)(2,1)S(1)}, bf16[512,256]{1,0:T(8,128)(2,1)S(1)}, u32[]{:S(2)}, u32[]{:S(2)}) collective-permute-start(bf16[512,256]{1,0:T(8,128)(2,1)S(1)} %get-tuple-element.401), channel_id=1, source_target_pairs={{0,2},{1,3},{2,0},{3,1},{4,6},{5,7},{6,4},{7,5},{8,10},{9,11},{10,... | collective-permute-start | bytes 786440 | tf_op jit(solution)/shard_map/ppermute | solution.py:37
  246.9 20.2 %collective-permute-start.46 = (bf16[512,256]{1,0:T(8,128)(2,1)S(1)}, bf16[512,256]{1,0:T(8,128)(2,1)S(1)}, u32[]{:S(2)}, u32[]{:S(2)}) collective-permute-start(bf16[512,256]{1,0:T(8,128)(2,1)S(1)} %get-tuple-element.402), channel_id=1, source_target_pairs={{0,3},{1,2},{2,1},{3,0},{4,7},{5,6},{6,5},{7,4},{8,11},{9,10},{10,... | collective-permute-start | bytes 786440 | tf_op jit(solution)/shard_map/ppermute | solution.py:37
  270.0 26.6 %collective-permute-start.49 = (bf16[1024,1024]{1,0:T(8,128)(2,1)}, bf16[1024,1024]{1,0:T(8,128)(2,1)}, u32[]{:S(2)}, u32[]{:S(2)}) collective-permute-start(bf16[1024,1024]{1,0:T(8,128)(2,1)} %ff_grad.16), channel_id=1, source_target_pairs={{0,8},{8,0},{16,24},{24,16},{1,9},{9,1},{17,25},{25,17},{2,10},{10... | collective-permute-start | bytes 6291464 | tf_op jit(solution)/shard_map/ppermute | solution.py:37
  270.4 31.6 %collective-permute-start.47 = (bf16[512,1024]{1,0:T(8,128)(2,1)}, bf16[512,1024]{1,0:T(8,128)(2,1)}, u32[]{:S(2)}, u32[]{:S(2)}) collective-permute-start(bf16[512,1024]{1,0:T(8,128)(2,1)} %get-tuple-element.416), channel_id=1, source_target_pairs={{0,2},{2,4},{4,6},{6,7},{7,5},{5,3},{3,1},{1,0},{8,10},{10,12},{12... | collective-permute-start | bytes 3145736 | tf_op jit(solution)/shard_map/ppermute | solution.py:814
  271.8 30.2 %collective-permute-start.48 = (bf16[512,1024]{1,0:T(8,128)(2,1)}, bf16[512,1024]{1,0:T(8,128)(2,1)}, u32[]{:S(2)}, u32[]{:S(2)}) collective-permute-start(bf16[512,1024]{1,0:T(8,128)(2,1)} %get-tuple-element.417), channel_id=1, source_target_pairs={{2,0},{4,2},{6,4},{7,6},{5,7},{3,5},{1,3},{0,1},{10,8},{12,10},{14... | collective-permute-start | bytes 3145736 | tf_op jit(solution)/shard_map/ppermute | solution.py:817
  275.7 19.9 %collective-permute-start.51 = (bf16[256,1024]{1,0:T(8,128)(2,1)S(1)}, bf16[256,1024]{1,0:T(8,128)(2,1)S(1)}, u32[]{:S(2)}, u32[]{:S(2)}) collective-permute-start(bf16[256,1024]{1,0:T(8,128)(2,1)S(1)} %bitcast.83), channel_id=1, source_target_pairs={{0,16},{8,24},{16,0},{24,8},{1,17},{9,25},{17,1},{25,9},{2,18},{10... | collective-permute-start | bytes 1572872 | tf_op jit(solution)/shard_map/ppermute | solution.py:37
  304.7 22.1 %collective-permute-start.54 = (bf16[512,1024]{1,0:T(8,128)(2,1)}, bf16[512,1024]{1,0:T(8,128)(2,1)}, u32[]{:S(2)}, u32[]{:S(2)}) collective-permute-start(bf16[512,1024]{1,0:T(8,128)(2,1)} %ff_grad.18), channel_id=1, source_target_pairs={{0,8},{8,0},{16,24},{24,16},{1,9},{9,1},{17,25},{25,17},{2,10},{10... | collective-permute-start | bytes 3145736 | tf_op jit(solution)/shard_map/ppermute | solution.py:37
  304.7 35.9 %collective-permute-start.52 = (bf16[512,1024]{1,0:T(8,128)(2,1)}, bf16[512,1024]{1,0:T(8,128)(2,1)}, u32[]{:S(2)}, u32[]{:S(2)}) collective-permute-start(bf16[512,1024]{1,0:T(8,128)(2,1)} %get-tuple-element.443), channel_id=1, source_target_pairs={{0,2},{2,4},{4,6},{6,7},{7,5},{5,3},{3,1},{1,0},{8,10},{10,12},{12... | collective-permute-start | bytes 3145736 | tf_op jit(solution)/shard_map/ppermute | solution.py:814
  306.1 34.5 %collective-permute-start.53 = (bf16[512,1024]{1,0:T(8,128)(2,1)}, bf16[512,1024]{1,0:T(8,128)(2,1)}, u32[]{:S(2)}, u32[]{:S(2)}) collective-permute-start(bf16[512,1024]{1,0:T(8,128)(2,1)} %get-tuple-element.444), channel_id=1, source_target_pairs={{2,0},{4,2},{6,4},{7,6},{5,7},{3,5},{1,3},{0,1},{10,8},{12,10},{14... | collective-permute-start | bytes 3145736 | tf_op jit(solution)/shard_map/ppermute | solution.py:817
  312.3 28.3 %collective-permute-start.55 = (bf16[128,1024]{1,0:T(8,128)(2,1)}, bf16[128,1024]{1,0:T(8,128)(2,1)S(1)}, u32[]{:S(2)}, u32[]{:S(2)}) collective-permute-start(bf16[128,1024]{1,0:T(8,128)(2,1)} %get-tuple-element.450), channel_id=1, source_target_pairs={{0,2},{1,3},{2,0},{3,1},{4,6},{5,7},{6,4},{7,5},{8,10},{9,11},{10,... | collective-permute-start | bytes 786440 | tf_op jit(solution)/shard_map/ppermute | solution.py:37
  313.7 26.9 %collective-permute-start.56 = (bf16[128,1024]{1,0:T(8,128)(2,1)}, bf16[128,1024]{1,0:T(8,128)(2,1)}, u32[]{:S(2)}, u32[]{:S(2)}) collective-permute-start(bf16[128,1024]{1,0:T(8,128)(2,1)} %get-tuple-element.451), channel_id=1, source_target_pairs={{0,1},{1,0},{2,3},{3,2},{4,5},{5,4},{6,7},{7,6},{8,9},{9,8},{10,11... | collective-permute-start | bytes 786440 | tf_op jit(solution)/shard_map/ppermute | solution.py:37
  346.1 15.3 %collective-permute-start.58 = (bf16[256,1024]{1,0:T(8,128)(2,1)S(1)}, bf16[256,1024]{1,0:T(8,128)(2,1)S(1)}, u32[]{:S(2)}, u32[]{:S(2)}) collective-permute-start(bf16[256,1024]{1,0:T(8,128)(2,1)S(1)} %get-tuple-element.465), channel_id=1, source_target_pairs={{0,1},{1,0},{2,3},{3,2},{4,5},{5,4},{6,7},{7,6},{8,9},{9,8},{10,11... | collective-permute-start | bytes 1572872 | tf_op jit(solution)/shard_map/ppermute | solution.py:37
  346.6 14.9 %collective-permute-start.59 = (bf16[256,1024]{1,0:T(8,128)(2,1)S(1)}, bf16[256,1024]{1,0:T(8,128)(2,1)S(1)}, u32[]{:S(2)}, u32[]{:S(2)}) collective-permute-start(bf16[256,1024]{1,0:T(8,128)(2,1)S(1)} %get-tuple-element.466), channel_id=1, source_target_pairs={{0,2},{1,3},{2,0},{3,1},{4,6},{5,7},{6,4},{7,5},{8,10},{9,11},{10,... | collective-permute-start | bytes 1572872 | tf_op jit(solution)/shard_map/ppermute | solution.py:37
  348.7 12.5 %collective-permute-start.57 = (bf16[256,1024]{1,0:T(8,128)(2,1)S(1)}, bf16[256,1024]{1,0:T(8,128)(2,1)S(1)}, u32[]{:S(2)}, u32[]{:S(2)}) collective-permute-start(bf16[256,1024]{1,0:T(8,128)(2,1)S(1)} %get-tuple-element.459), channel_id=1, source_target_pairs={{0,16},{8,24},{16,0},{24,8},{1,17},{9,25},{17,1},{25,9},{2,18},{10... | collective-permute-start | bytes 1572872 | tf_op jit(solution)/shard_map/ppermute | solution.py:37
  363.7 7.1 %collective-permute-start.62 = (bf16[128,1024]{1,0:T(8,128)(2,1)S(1)}, bf16[128,1024]{1,0:T(8,128)(2,1)S(1)}, u32[]{:S(2)}, u32[]{:S(2)}) collective-permute-start(bf16[128,1024]{1,0:T(8,128)(2,1)S(1)} %get-tuple-element.494), channel_id=1, source_target_pairs={{0,1},{1,0},{2,3},{3,2},{4,5},{5,4},{6,7},{7,6},{8,9},{9,8},{10,11... | collective-permute-start | bytes 786440 | tf_op jit(solution)/shard_map/ppermute | solution.py:37
  370.9 13.8 %collective-permute-start.63 = (bf16[512,384]{1,0:T(8,128)(2,1)S(1)}, bf16[512,384]{1,0:T(8,128)(2,1)S(1)}, u32[]{:S(2)}, u32[]{:S(2)}) collective-permute-start(bf16[512,384]{1,0:T(8,128)(2,1)S(1)} %get-tuple-element.536), channel_id=1, source_target_pairs={{0,0},{4,1},{1,2},{5,3},{2,4},{6,5},{3,6},{7,7},{8,8},{12,9},{9,10... | collective-permute-start | bytes 1179656 | tf_op jit(solution)/shard_map/ppermute | solution.py:1156
  371.6 23.1 %collective-permute-start.64 = (bf16[512,384]{1,0:T(8,128)(2,1)S(1)}, bf16[512,384]{1,0:T(8,128)(2,1)S(1)}, u32[]{:S(2)}, u32[]{:S(2)}) collective-permute-start(bf16[512,384]{1,0:T(8,128)(2,1)S(1)} %get-tuple-element.537), channel_id=1, source_target_pairs={{4,0},{0,1},{5,2},{1,3},{6,4},{2,5},{7,6},{3,7},{12,8},{8,9},{13,1... | collective-permute-start | bytes 1179656 | tf_op jit(solution)/shard_map/ppermute | solution.py:1156
  377.3 18.1 %collective-permute-start.68 = (bf16[256,1024]{1,0:T(8,128)(2,1)S(1)}, bf16[256,1024]{1,0:T(8,128)(2,1)S(1)}, u32[]{:S(2)}, u32[]{:S(2)}) collective-permute-start(bf16[256,1024]{1,0:T(8,128)(2,1)S(1)} %get-tuple-element.498), channel_id=1, source_target_pairs={{0,16},{8,24},{16,0},{24,8},{1,17},{9,25},{17,1},{25,9},{2,18},{10... | collective-permute-start | bytes 1572872 | tf_op jit(solution)/shard_map/ppermute | solution.py:37
  382.4 14.0 %collective-permute-start.69 = (bf16[1024,256]{1,0:T(8,128)(2,1)S(1)}, bf16[1024,256]{1,0:T(8,128)(2,1)}, u32[]{:S(2)}, u32[]{:S(2)}) collective-permute-start(bf16[1024,256]{1,0:T(8,128)(2,1)S(1)} %turned.1), channel_id=1, source_target_pairs={{0,8},{8,0},{16,24},{24,16},{1,9},{9,1},{17,25},{25,17},{2,10},{10... | collective-permute-start | bytes 1572872 | tf_op jit(solution)/shard_map/ppermute | solution.py:37
  396.8 7.3 %collective-permute-start.76 = (bf16[64,1024]{1,0:T(8,128)(2,1)}, bf16[64,1024]{1,0:T(8,128)(2,1)}, u32[]{:S(2)}, u32[]{:S(2)}) collective-permute-start(bf16[64,1024]{1,0:T(8,128)(2,1)} %add_add_fusion), channel_id=1, source_target_pairs={{0,2},{1,3},{2,0},{3,1},{4,6},{5,7},{6,4},{7,5},{8,10},{9,11},{10,... | collective-permute-start | bytes 393224 | tf_op jit(solution)/shard_map/ppermute | solution.py:37
  397.4 7.9 %collective-permute-start.77 = (bf16[64,1024]{1,0:T(8,128)(2,1)}, bf16[64,1024]{1,0:T(8,128)(2,1)}, u32[]{:S(2)}, u32[]{:S(2)}) collective-permute-start(bf16[64,1024]{1,0:T(8,128)(2,1)} %add_add_fusion), channel_id=1, source_target_pairs={{0,3},{1,2},{2,1},{3,0},{4,7},{5,6},{6,5},{7,4},{8,11},{9,10},{10,... | collective-permute-start | bytes 393224 | tf_op jit(solution)/shard_map/ppermute | solution.py:37
  399.9 16.5 %collective-permute-start.74 = (bf16[256,1024]{1,0:T(8,128)(2,1)}, bf16[256,1024]{1,0:T(8,128)(2,1)S(1)}, u32[]{:S(2)}, u32[]{:S(2)}) collective-permute-start(bf16[256,1024]{1,0:T(8,128)(2,1)} %add_convert_fusion.2), channel_id=1, source_target_pairs={{0,8},{8,0},{16,24},{24,16},{1,9},{9,1},{17,25},{25,17},{2,10},{10... | collective-permute-start | bytes 1572872 | tf_op jit(solution)/shard_map/ppermute | solution.py:37
  400.0 10.5 %collective-permute-start.73 = (bf16[32,1024]{1,0:T(8,128)(2,1)}, bf16[32,1024]{1,0:T(8,128)(2,1)S(1)}, u32[]{:S(2)}, u32[]{:S(2)}) collective-permute-start(bf16[32,1024]{1,0:T(8,128)(2,1)} %reduce-scatter.2.cloned.1.call-done), channel_id=1, source_target_pairs={{0,16},{8,24},{16,0},{24,8},{1,17},{9,25},{17,1},{25,9},{2,18},{10... | collective-permute-start | bytes 196616 | tf_op jit(solution)/shard_map/ppermute | solution.py:37
  403.1 13.3 %collective-permute-start.70 = (bf16[512,384]{1,0:T(8,128)(2,1)S(1)}, bf16[512,384]{1,0:T(8,128)(2,1)S(1)}, u32[]{:S(2)}, u32[]{:S(2)}) collective-permute-start(bf16[512,384]{1,0:T(8,128)(2,1)S(1)} %add_convert_fusion.5), channel_id=1, source_target_pairs={{0,16},{8,24},{16,0},{24,8},{1,17},{9,25},{17,1},{25,9},{2,18},{10... | collective-permute-start | bytes 1179656 | tf_op jit(solution)/shard_map/ppermute | solution.py:37
  404.1 14.1 %collective-permute-start.71 = (bf16[256,1024]{1,0:T(8,128)(2,1)}, bf16[256,1024]{1,0:T(8,128)(2,1)S(1)}, u32[]{:S(2)}, u32[]{:S(2)}) collective-permute-start(bf16[256,1024]{1,0:T(8,128)(2,1)} %copy-done.78), channel_id=1, source_target_pairs={{0,1},{1,0},{2,3},{3,2},{4,5},{5,4},{6,7},{7,6},{8,9},{9,8},{10,11... | collective-permute-start | bytes 1572872 | tf_op jit(solution)/shard_map/ppermute | solution.py:37
  406.4 7.0 %collective-permute-start.78 = (bf16[64,1024]{1,0:T(8,128)(2,1)S(1)}, bf16[64,1024]{1,0:T(8,128)(2,1)S(1)}, u32[]{:S(2)}, u32[]{:S(2)}) collective-permute-start(bf16[64,1024]{1,0:T(8,128)(2,1)S(1)} %add_convert_fusion.6), channel_id=1, source_target_pairs={{0,4},{1,5},{2,6},{3,7},{4,0},{5,1},{6,2},{7,3},{8,12},{9,13},{10,... | collective-permute-start | bytes 393224 | tf_op jit(solution)/shard_map/ppermute | solution.py:37
  410.5 12.8 %collective-permute-start.72 = (bf16[256,1024]{1,0:T(8,128)(2,1)S(1)}, bf16[256,1024]{1,0:T(8,128)(2,1)S(1)}, u32[]{:S(2)}, u32[]{:S(2)}) collective-permute-start(bf16[256,1024]{1,0:T(8,128)(2,1)S(1)} %get-tuple-element.508), channel_id=1, source_target_pairs={{0,2},{1,3},{2,0},{3,1},{4,6},{5,7},{6,4},{7,5},{8,10},{9,11},{10,... | collective-permute-start | bytes 1572872 | tf_op jit(solution)/shard_map/ppermute | solution.py:37
  (143 other events, 904.9 us)
Sparse Core Ops, SparseCore 0:
  46.9 44.0 all-gather.2
  317.9 61.6 reduce-scatter.1
